TPU v7x, 512 devices: a whole 4x4x16 slice. The times are simulated.
512 devices in a mesh: rep: 32 (over y, z_lo), tp: 16 (over z_hi, x, core).
Axes of the slice: x: 4, y: 4, z: 16 (z_hi: 2, z_lo: 8; z = z_hi * 8 + z_lo), core: 2. Of those that a mesh axis runs over, the one named last changes fastest.
Arguments:
- hidden: bfloat16 [14336, 7168], P('rep', 'tp'), may hold values from -6 to 6
- upstream: bfloat16 [14336, 2048], P('rep', 'tp'), may hold values from -6 to 6
- weights: bfloat16 [7168, 8192], P('tp', 'rep'), may hold values from -2 to 2
- first_moment: float32 [7168, 8192], P('tp', 'rep'), may hold values from -0.12 to 0.12
- second_moment: float32 [7168, 8192], P('tp', 'rep'), may hold values from 1e-06 to 0.001
- step_index: int32 [1], replicated, may hold values from 0 to 63
Outputs:
- mixed_weights: bfloat16 [7168, 8192], P('tp', 'rep')
- new_first: float32 [7168, 8192], P('tp', 'rep')
- new_second: float32 [7168, 8192], P('tp', 'rep')
- hidden_grad: bfloat16 [14336, 7168], P('rep', 'tp')
All inputs are finite; a program needn't handle non-finite values.
Results may differ from a plain program's by a relative error of at most 0.0052.
Values may be sent and summed in bfloat16 or wider, within the bound.
No kernel may reach another device: no remote copies, remote signals or barrier semaphores. Data moves between devices by JAX's collectives and lax.ppermute only.
A program may use at most 64 MiB of HBM per device.

v0:
```python
import math

import jax
import jax.numpy as jnp
from jax import lax
from jax.sharding import PartitionSpec as P

REPLICAS = 4


def from_partner(value, axis, distance):
    return lax.ppermute(value, axis, [(i, i ^ 1 << distance) for i in range(lax.axis_size(axis))])


def passed_along(block, axis, distance):
    devices = range(lax.axis_size(axis))
    route = [((i - distance) % len(devices), i) for i in devices]
    return lax.ppermute(block, axis, route)


def body(hidden, upstream, weights, first_moment, second_moment, step_index):
    group = lax.axis_size("rep") // REPLICAS
    levels = group.bit_length() - 1
    place = lax.axis_index("rep") % group
    units = hidden.shape[1] * lax.axis_size("tp")
    scale_hid = 1.0 / math.sqrt(units)
    block_width = weights.shape[1]
    full_up = lax.all_gather(upstream, "tp", axis=1, tiled=True)
    partial_value = jnp.dot(hidden.T, full_up, preferred_element_type=jnp.float32) * scale_hid
    total = partial_value
    for level in range(levels):
        total = total + from_partner(total, "rep", level)
    grads = lax.dynamic_slice_in_dim(total, place * block_width, block_width, 1)
    gathered = weights
    for level in range(levels):
        other = from_partner(gathered, "rep", level)
        upper_side = place >> level & 1 == 1
        gathered = jnp.where(
            upper_side,
            jnp.concatenate([other, gathered], axis=1),
            jnp.concatenate([gathered, other], axis=1),
        )
    in_grad = (jnp.dot(full_up, gathered.T, preferred_element_type=jnp.float32) * scale_hid).astype(
        jnp.bfloat16
    )
    count = (step_index[0] + 1).astype(jnp.float32)
    first_new = 0.9 * first_moment + 0.1 * grads
    second_new = 0.999 * second_moment + 0.001 * grads * grads
    correct_one = 1.0 - jnp.power(jnp.float32(0.9), count)
    correct_two = 1.0 - jnp.power(jnp.float32(0.999), count)
    weights_f = weights.astype(jnp.float32)
    step_size = (
        first_new / correct_one / (jnp.sqrt(second_new / correct_two) + 1e-08) + 0.1 * weights_f
    )
    updated = (weights_f - 0.05 * step_size).astype(jnp.bfloat16)
    half_rows = updated.shape[0] // 2
    lower_rows = updated[:half_rows]
    upper_rows = updated[half_rows:]
    even_step = step_index[0] % 2 == 0
    near_send = jnp.where(even_step, lower_rows, upper_rows)
    far_send = jnp.where(even_step, upper_rows, lower_rows)
    near_back = passed_along(near_send, "rep", group)
    far_back = passed_along(far_send, "rep", 2 * group)
    partner = jnp.concatenate(
        [jnp.where(even_step, near_back, far_back), jnp.where(even_step, far_back, near_back)],
        axis=0,
    )
    mixed = ((updated.astype(jnp.float32) + partner.astype(jnp.float32)) * 0.5).astype(jnp.bfloat16)
    return (mixed, first_new, second_new, in_grad)


def solution(mesh):
    in_specs = (P("rep", "tp"), P("rep", "tp"), P("tp", "rep"), P("tp", "rep"), P("tp", "rep"), P())
    out_specs = (P("tp", "rep"), P("tp", "rep"), P("tp", "rep"), P("rep", "tp"))
    return jax.shard_map(body, mesh=mesh, in_specs=in_specs, out_specs=out_specs, check_vma=False)
```

profile of v0, /device:TPU:1, one launch (start us, length us, event | category | flops | bytes accessed | tf_op | source)
XLA Modules:
  0.0 786.8 jit_solution(328131145723133337)
XLA Ops:
  7.2 0.0 copy-start
  7.2 0.0 all-gather.2.cloned.1.call-start
  7.2 0.7 all-gather.2.cloned.1.call-update
  7.9 95.5 %all-gather.2.cloned.1.call-done = bf16[448,2048]{1,0:T(8,128)(2,1)} async-done(((bf16[448,128]{1,0:T(8,128)(2,1)}), bf16[448,2048]{1,0:T(8,128)(2,1)}) %all-gather.2.cloned.1.call-update) | async-done | bytes 1835024 | tf_op jit(solution)/shard_map/all_gather | solution.py:28
  103.4 0.0 copy-done
  103.4 2.6 convolution_multiply_fusion
  106.0 1.9 collective-permute-start
  108.0 80.6 %collective-permute-done = f32[448,2048]{1,0:T(8,128)S(1)} collective-permute-done((f32[448,2048]{1,0:T(8,128)S(1)}, f32[448,2048]{1,0:T(8,128)S(1)}, u32[]{:S(2)}, u32[]{:S(2)}) %collective-permute-start) | collective-permute-done | bytes 3670048 | tf_op jit(solution)/shard_map/ppermute | solution.py:12
  188.6 0.9 add.40
  189.5 0.0 copy-start.2
  189.5 2.1 collective-permute-start.1
  191.6 160.7 %collective-permute-done.1 = f32[448,2048]{1,0:T(8,128)S(1)} collective-permute-done((f32[448,2048]{1,0:T(8,128)S(1)}, f32[448,2048]{1,0:T(8,128)S(1)}, u32[]{:S(2)}, u32[]{:S(2)}) %collective-permute-start.1) | collective-permute-done | bytes 3670048 | tf_op jit(solution)/shard_map/ppermute | solution.py:12
  352.3 2.5 add.41
  354.8 2.0 collective-permute-start.2
  356.9 1.9 collective-permute-start.5
  358.8 81.5 %collective-permute-done.5 = bf16[448,256]{1,0:T(8,128)(2,1)S(1)} collective-permute-done((bf16[448,256]{1,0:T(8,128)(2,1)S(1)}, bf16[448,256]{1,0:T(8,128)(2,1)S(1)}, u32[]{:S(2)}, u32[]{:S(2)}) %collective-permute-start.5) | collective-permute-done | bytes 229408 | tf_op jit(solution)/shard_map/ppermute | solution.py:12
  440.4 0.1 maximum_select_fusion.9
  440.5 157.8 %collective-permute-start.6 = (bf16[448,512]{1,0:T(8,128)(2,1)S(1)}, bf16[448,512]{1,0:T(8,128)(2,1)S(1)}, u32[]{:S(2)}, u32[]{:S(2)}) collective-permute-start(bf16[448,512]{1,0:T(8,128)(2,1)S(1)} %maximum_select_fusion.9), channel_id=1, source_target_pairs={{0,32},{16,48},{32,0},{48,16},{64,96},{80,112},{96,64},{112,80},{1... | collective-permute-start | bytes 1376264 | tf_op jit(solution)/shard_map/ppermute | solution.py:12
  598.3 95.8 %collective-permute-done.6 = bf16[448,512]{1,0:T(8,128)(2,1)S(1)} collective-permute-done((bf16[448,512]{1,0:T(8,128)(2,1)S(1)}, bf16[448,512]{1,0:T(8,128)(2,1)S(1)}, u32[]{:S(2)}, u32[]{:S(2)}) %collective-permute-start.6) | collective-permute-done | bytes 458784 | tf_op jit(solution)/shard_map/ppermute | solution.py:12
  694.1 0.3 maximum_select_fusion.8
  694.3 1.9 collective-permute-start.7
  697.0 0.0 copy-start.1
  697.0 0.0 collective-permute-done.2
  697.0 2.6 fusion.12
  699.7 3.1 collective-permute-start.3
  702.8 4.3 collective-permute-start.4
  707.1 68.4 %collective-permute-done.7 = bf16[448,1024]{1,0:T(8,128)(2,1)} collective-permute-done((bf16[448,1024]{1,0:T(8,128)(2,1)S(1)}, bf16[448,1024]{1,0:T(8,128)(2,1)}, u32[]{:S(2)}, u32[]{:S(2)}) %collective-permute-start.7) | collective-permute-done | bytes 917536 | tf_op jit(solution)/shard_map/ppermute | solution.py:12
  775.6 2.6 fusion.9
  778.2 1.0 copy.10
  779.1 0.0 collective-permute-done.3
  779.1 0.0 collective-permute-done.4
  779.2 0.8 multiply_convert_fusion
  (8 shorter events, 0.1 us)
Async XLA Ops:
  7.2 96.2 %copy-start = (bf16[448,448]{1,0:T(8,128)(2,1)S(1)}, bf16[448,448]{1,0:T(8,128)(2,1)}, u32[]{:S(2)}) copy-start(bf16[448,448]{1,0:T(8,128)(2,1)} %param.6) | copy-start | bytes 1204228
  7.2 96.2 %all-gather.2.cloned.1.call-start = ((), (), s32[]{:S(2)}) async-start(), calls=%async_computation | async-start | bytes 1949696 | tf_op jit(solution)/shard_map/all_gather | solution.py:28
  106.0 82.6 %collective-permute-start = (f32[448,2048]{1,0:T(8,128)S(1)}, f32[448,2048]{1,0:T(8,128)S(1)}, u32[]{:S(2)}, u32[]{:S(2)}) collective-permute-start(f32[448,2048]{1,0:T(8,128)S(1)} %convolution_multiply_fusion), channel_id=1, source_target_pairs={{0,16},{16,0},{32,48},{48,32},{64,80},{80,64},{96,112},{112,96},{1... | collective-permute-start | bytes 11010056 | tf_op jit(solution)/shard_map/ppermute | solution.py:12
  189.5 167.4 %copy-start.2 = (bf16[448,256]{1,0:T(8,128)(2,1)S(1)}, bf16[448,256]{1,0:T(8,128)(2,1)}, u32[]{:S(2)}) copy-start(bf16[448,256]{1,0:T(8,128)(2,1)} %param.8) | copy-start | bytes 688132
  189.5 162.8 %collective-permute-start.1 = (f32[448,2048]{1,0:T(8,128)S(1)}, f32[448,2048]{1,0:T(8,128)S(1)}, u32[]{:S(2)}, u32[]{:S(2)}) collective-permute-start(f32[448,2048]{1,0:T(8,128)S(1)} %add.40), channel_id=1, source_target_pairs={{0,32},{16,48},{32,0},{48,16},{64,96},{80,112},{96,64},{112,80},{1... | collective-permute-start | bytes 11010056 | tf_op jit(solution)/shard_map/ppermute | solution.py:12
  354.8 342.2 %copy-start.3 = (f32[448,256]{1,0:T(8,128)S(1)}, f32[448,256]{1,0:T(8,128)}, u32[]{:S(2)}) copy-start(f32[448,256]{1,0:T(8,128)} %param.10) | copy-start | bytes 1376260
  354.8 342.2 %copy-start.4 = (f32[448,256]{1,0:T(8,128)S(1)}, f32[448,256]{1,0:T(8,128)}, u32[]{:S(2)}) copy-start(f32[448,256]{1,0:T(8,128)} %param.9) | copy-start | bytes 1376260
  354.8 342.2 %collective-permute-start.2 = (f32[448,2048]{1,0:T(8,128)}, f32[448,2048]{1,0:T(8,128)}, u32[]{:S(2)}, u32[]{:S(2)}) collective-permute-start(f32[448,2048]{1,0:T(8,128)} %add.41), channel_id=1, source_target_pairs={{0,64},{16,80},{32,96},{48,112},{64,0},{80,16},{96,32},{112,48},{1... | collective-permute-start | bytes 11010056 | tf_op jit(solution)/shard_map/ppermute | solution.py:12
  356.9 83.5 %collective-permute-start.5 = (bf16[448,256]{1,0:T(8,128)(2,1)S(1)}, bf16[448,256]{1,0:T(8,128)(2,1)S(1)}, u32[]{:S(2)}, u32[]{:S(2)}) collective-permute-start(bf16[448,256]{1,0:T(8,128)(2,1)S(1)} %copy-done.2), channel_id=1, source_target_pairs={{0,16},{16,0},{32,48},{48,32},{64,80},{80,64},{96,112},{112,96},{1... | collective-permute-start | bytes 688136 | tf_op jit(solution)/shard_map/ppermute | solution.py:12
  440.5 253.6 %collective-permute-start.6 = (bf16[448,512]{1,0:T(8,128)(2,1)S(1)}, bf16[448,512]{1,0:T(8,128)(2,1)S(1)}, u32[]{:S(2)}, u32[]{:S(2)}) collective-permute-start(bf16[448,512]{1,0:T(8,128)(2,1)S(1)} %maximum_select_fusion.9), channel_id=1, source_target_pairs={{0,32},{16,48},{32,0},{48,16},{64,96},{80,112},{96,64},{112,80},{1... | collective-permute-start | bytes 1376264 | tf_op jit(solution)/shard_map/ppermute | solution.py:12
  694.3 81.2 %collective-permute-start.7 = (bf16[448,1024]{1,0:T(8,128)(2,1)S(1)}, bf16[448,1024]{1,0:T(8,128)(2,1)}, u32[]{:S(2)}, u32[]{:S(2)}) collective-permute-start(bf16[448,1024]{1,0:T(8,128)(2,1)S(1)} %maximum_select_fusion.8), channel_id=1, source_target_pairs={{0,64},{16,80},{32,96},{48,112},{64,0},{80,16},{96,32},{112,48},{1... | collective-permute-start | bytes 2752520 | tf_op jit(solution)/shard_map/ppermute | solution.py:12
  697.0 78.6 %copy-start.1 = (bf16[448,2048]{1,0:T(8,128)(2,1)S(1)}, bf16[448,2048]{1,0:T(8,128)(2,1)}, u32[]{:S(2)}) copy-start(bf16[448,2048]{1,0:T(8,128)(2,1)} %all-gather.2.cloned.1.call-done) | copy-start | bytes 5505028
  699.7 79.5 %collective-permute-start.3 = (bf16[224,256]{1,0:T(8,128)(2,1)S(1)}, bf16[224,256]{1,0:T(8,128)(2,1)S(1)}, u32[]{:S(2)}, u32[]{:S(2)}) collective-permute-start(bf16[224,256]{1,0:T(8,128)(2,1)S(1)} %get-tuple-element.13), channel_id=1, source_target_pairs={{384,0},{400,16},{416,32},{432,48},{448,64},{464,80},{480,96},{496... | collective-permute-start | bytes 344072 | tf_op jit(solution)/shard_map/ppermute | solution.py:18
  702.8 76.4 %collective-permute-start.4 = (bf16[224,256]{1,0:T(8,128)(2,1)S(1)}, bf16[224,256]{1,0:T(8,128)(2,1)S(1)}, u32[]{:S(2)}, u32[]{:S(2)}) collective-permute-start(bf16[224,256]{1,0:T(8,128)(2,1)S(1)} %get-tuple-element.14), channel_id=1, source_target_pairs={{256,0},{272,16},{288,32},{304,48},{320,64},{336,80},{352,96},{368... | collective-permute-start | bytes 344072 | tf_op jit(solution)/shard_map/ppermute | solution.py:18
Sparse Core Ops, SparseCore 0:
  11.2 92.1 all-gather.1
where the time goes:
time: 787 us
  waiting for transfers between devices  583 us (74%)
  starting transfers between devices  175 us (22%)
  between operations  15 us (2%)
    ppermute x6, waiting for transfers between devices, from_partner(): lax.ppermute(value, axis, [(i, i ^ 1 << distance) for i in range(lax.axis...  487 us
    ppermute x6, starting transfers between devices, from_partner(): lax.ppermute(value, axis, [(i, i ^ 1 << distance) for i in range(lax.axis...  168 us
    all_gather x1, waiting for transfers between devices, body(): full_up = lax.all_gather(upstream, 'tp', axis=1, tiled=True)  95.5 us
  transfers between devices with their start and end apart: 9, of which 6 were waited for; matrix products, arithmetic and copies ran while one was open for 1% of the time, Pallas kernels for 0%

commit v1 on v0

v1 whole, which is shorter than its diff:
```python
import math

import jax
import jax.numpy as jnp
from jax import lax
from jax.sharding import Mesh, PartitionSpec as P

BF = jnp.bfloat16
F32 = jnp.float32
LINE = 8
LEAD = 1


def swap_cores(value):
    return lax.ppermute(value, "c", [(0, 1), (1, 0)])


def hop(value, odd):
    pairs = []
    for chip in range(LINE - 1):
        low, high = chip * 2 + odd, (chip + 1) * 2 + 1 - odd
        pairs += [(low, high), (high, low)]
    return lax.ppermute(value, ("zl", "c"), pairs)


def contract(left, right, dims):
    return lax.dot_general(left, right, (dims, ((), ())), preferred_element_type=F32)


def body(hidden, upstream, weights, first_moment, second_moment, step_index):
    tokens, units = hidden.shape
    width = weights.shape[1]
    place, core, far_half = lax.axis_index("zl"), lax.axis_index("c"), lax.axis_index("zh")
    first_core = core == 0
    scale_hid = 1.0 / math.sqrt(7168)

    weights_other = swap_cores(weights)
    both_weights = jnp.where(
        first_core,
        jnp.concatenate([weights, weights_other], 0),
        jnp.concatenate([weights_other, weights], 0),
    )
    hidden_other = swap_cores(hidden)
    both_hidden = jnp.where(
        first_core,
        jnp.concatenate([hidden, hidden_other], 1),
        jnp.concatenate([hidden_other, hidden], 1),
    )

    up_other = lax.ppermute(upstream, "zh", [(0, 1), (1, 0)])
    near_up = lax.all_gather(upstream, ("x", "c"), axis=1, tiled=True)
    far_up = lax.all_gather(up_other, ("x", "c"), axis=1, tiled=True)
    full_up = jnp.concatenate([near_up, far_up], axis=1)

    def up_block(index):
        at = jnp.bitwise_xor(index, 4 * far_half) * width
        return lax.dynamic_slice_in_dim(full_up, at, width, 1)

    carried = both_weights
    hg_total = jnp.zeros((tokens, 2 * units), F32)
    for step in range(LINE - 1 + LEAD):
        upward = core == step % 2
        turn = step - LEAD
        payload = carried
        if turn >= 0:
            position = jnp.where(upward, place, LINE - 1 - place)
            block = jnp.clip(LINE - 1 - turn + position, 0, LINE - 1)
            block = jnp.where(upward, block, LINE - 1 - block)
            part = contract(both_hidden, up_block(block), ((0,), (0,)))
            part = lax.optimization_barrier(part)
            payload = jnp.where(position <= turn, (carried.astype(F32) + part).astype(BF), carried)
        carried = hop(payload, step % 2)
        if step < LINE - 1:
            position = jnp.where(upward, LINE - 1 - place, place)
            source = position - 1 - step
            valid = source >= 0
            source = jnp.clip(source, 0, LINE - 1)
            source = jnp.where(upward, LINE - 1 - source, source)
            features = jnp.where(valid, up_block(source), jnp.zeros((), BF))
            hg_total = hg_total + contract(features, carried, ((1,), (1,)))

    own_up = up_block(place)
    mine = lax.dynamic_slice_in_dim(carried, core * units, units, 0)
    theirs = lax.dynamic_slice_in_dim(carried, (1 - core) * units, units, 0)
    own_part = contract(hidden, own_up, ((0,), (0,)))
    grads = (mine.astype(F32) + own_part + swap_cores(theirs).astype(F32)) * scale_hid

    count = (step_index[0] + 1).astype(F32)
    first_new = 0.9 * first_moment + 0.1 * grads
    second_new = 0.999 * second_moment + 0.001 * grads * grads
    correct_one = 1.0 - jnp.power(F32(0.9), count)
    correct_two = 1.0 - jnp.power(F32(0.999), count)
    weights_f = weights.astype(F32)
    step_size = first_new / correct_one / (jnp.sqrt(second_new / correct_two) + 1e-08) + 0.1 * weights_f
    updated = (weights_f - 0.05 * step_size).astype(BF)

    half = units // 2
    even_step = step_index[0] % 2 == 0
    lower, upper = updated[:half], updated[half:]
    near = lax.ppermute(jnp.where(even_step, lower, upper), "y", [(i, (i + 1) % 4) for i in range(4)])
    far = lax.ppermute(jnp.where(even_step, upper, lower), "y", [(i, (i + 2) % 4) for i in range(4)])
    partner = jnp.concatenate([jnp.where(even_step, near, far), jnp.where(even_step, far, near)], 0)
    mixed = ((updated.astype(F32) + partner.astype(F32)) * 0.5).astype(BF)

    hg_mine = lax.dynamic_slice_in_dim(hg_total, core * units, units, 1)
    hg_theirs = lax.dynamic_slice_in_dim(hg_total, (1 - core) * units, units, 1)
    hg_own = contract(own_up, weights, ((1,), (1,)))
    in_grad = ((hg_mine + hg_own + swap_cores(hg_theirs)) * scale_hid).astype(BF)
    return mixed, first_new, second_new, in_grad


def solution(mesh):
    split = Mesh(mesh.devices.reshape(4, LINE, 2, 4, 2), ("y", "zl", "zh", "x", "c"))
    rep, tp = ("y", "zl"), ("zh", "x", "c")
    in_specs = (P(rep, tp), P(rep, tp), P(tp, rep), P(tp, rep), P(tp, rep), P())
    out_specs = (P(tp, rep), P(tp, rep), P(tp, rep), P(rep, tp))
    return jax.shard_map(body, mesh=split, in_specs=in_specs, out_specs=out_specs, check_vma=False)
```

time: 787 us -> 152 us (0.19)
  the two profiles are of different devices: /device:TPU:1 before, /device:TPU:98 now
where the time goes in v1:
time: 152 us; the launch traced here: 151 us
  starting transfers between devices  53.1 us (35%)
  waiting for transfers between devices  41 us (27%)
  blocking collectives  28.8 us (19%)
  matrix products  18.3 us (12%)
  other arithmetic  6.64 us (4%)
  between operations  2.05 us (1%)
    ppermute x8, waiting for transfers between devices, hop(): return lax.ppermute(value, ('zl', 'c'), pairs)  37.3 us
    ppermute x8, starting transfers between devices, hop(): return lax.ppermute(value, ('zl', 'c'), pairs)  22 us
    dot_general x16, matrix products, contract(): lax.dot_general(left, right, (dims, ((), ())), preferred_element_type=F32)  18.3 us
    all_gather x1, blocking collectives, body(): near_up = lax.all_gather(upstream, ('x', 'c'), axis=1, tiled=True)  14.8 us
    all_gather x1, blocking collectives, body(): far_up = lax.all_gather(up_other, ('x', 'c'), axis=1, tiled=True)  14.1 us
    ppermute x1, starting transfers between devices, body(): up_other = lax.ppermute(upstream, 'zh', [(0, 1), (1, 0)])  13.2 us
    ppermute x4, starting transfers between devices, swap_cores(): return lax.ppermute(value, 'c', [(0, 1), (1, 0)])  9.72 us
    ppermute x1, starting transfers between devices, body(): lax.ppermute(jnp.where(even_step, upper, lower), 'y', [(i, (i + 2) % 4) f...  4.81 us
  transfers between devices with their start and end apart: 15, of which 9 were waited for; matrix products, arithmetic and copies ran while one was open for 14% of the time, Pallas kernels for 0%

profile of v1, /device:TPU:98, one launch (start us, length us, event | category | flops | bytes accessed | tf_op | source)
XLA Modules:
  0.0 151.1 jit_solution(11094273909297865881)
XLA Ops:
  0.6 13.2 %collective-permute-start.3 = (bf16[448,128]{1,0:T(8,128)(2,1)}, bf16[448,128]{1,0:T(8,128)(2,1)S(1)}, u32[]{:S(2)}, u32[]{:S(2)}) collective-permute-start(bf16[448,128]{1,0:T(8,128)(2,1)} %param.7), channel_id=1, source_target_pairs={{0,8},{8,0},{1,9},{9,1},{2,10},{10,2},{3,11},{11,3},{4,12},{12,4},... | collective-permute-start | bytes 344072 | tf_op jit(solution)/shard_map/ppermute | solution.py:50
  13.8 1.9 %collective-permute-start.2 = (bf16[448,448]{1,0:T(8,128)(2,1)}, bf16[448,448]{1,0:T(8,128)(2,1)}, u32[]{:S(2)}, u32[]{:S(2)}) collective-permute-start(bf16[448,448]{1,0:T(8,128)(2,1)} %param.6), channel_id=1, source_target_pairs={{0,1},{1,0},{2,3},{3,2},{4,5},{5,4},{6,7},{7,6},{8,9},{9,8},{10,11... | collective-permute-start | bytes 1204232 | tf_op jit(solution)/shard_map/ppermute | solution.py:15
  15.7 2.4 %collective-permute-start = (bf16[448,256]{1,0:T(8,128)(2,1)}, bf16[448,256]{1,0:T(8,128)(2,1)S(1)}, u32[]{:S(2)}, u32[]{:S(2)}) collective-permute-start(bf16[448,256]{1,0:T(8,128)(2,1)} %param.8), channel_id=1, source_target_pairs={{0,1},{1,0},{2,3},{3,2},{4,5},{5,4},{6,7},{7,6},{8,9},{9,8},{10,11... | collective-permute-start | bytes 688136 | tf_op jit(solution)/shard_map/ppermute | solution.py:15
  18.2 14.8 %all_gather.6 = bf16[448,1024]{1,0:T(8,128)(2,1)S(1)} all-gather(bf16[448,128]{1,0:T(8,128)(2,1)} %param.7), channel_id=1, replica_groups=mesh['y'=4,'zl'=8,'zh'=2,'x'=4,'c'=2] {'x','c'}, dimensions={1}, use_global_device_ids=true | all-gather | bytes 1032192 | tf_op jit(solution)/shard_map/all_gather | solution.py:51
  33.2 2.7 %collective-permute-start.1 = (bf16[896,256]{1,0:T(8,128)(2,1)S(1)}, bf16[896,256]{1,0:T(8,128)(2,1)S(1)}, u32[]{:S(2)}, u32[]{:S(2)}) collective-permute-start(bf16[896,256]{1,0:T(8,128)(2,1)S(1)} %maximum_select_fusion.1), channel_id=1, source_target_pairs={{0,17},{17,0},{16,33},{33,16},{32,49},{49,32},{48,65},{65,48},{64,... | collective-permute-start | bytes 1376264 | tf_op jit(solution)/shard_map/ppermute | solution.py:23
  35.9 14.1 %all_gather.7 = bf16[448,1024]{1,0:T(8,128)(2,1)S(1)} all-gather(bf16[448,128]{1,0:T(8,128)(2,1)S(1)} %collective-permute-done.3), channel_id=1, replica_groups=mesh['y'=4,'zl'=8,'zh'=2,'x'=4,'c'=2] {'x','c'}, dimensions={1}, use_global_device_ids=true | all-gather | bytes 1032192 | tf_op jit(solution)/shard_map/all_gather | solution.py:52
  50.1 2.0 %fusion.45 = f32[896,256]{1,0:T(8,128)S(1)} fusion(bf16[448,2048]{1,0:T(8,128)(2,1)S(1)} %constant_dynamic-update-slice_fusion, s32[]{:T(128)S(6)} %select_n.260, bf16[448,448]{1,0:T(8,128)(2,1)} %collective-permute-done.2, bf16[448,448]{1,0:T(8,128)(2,1)S(1)} %copy-done.9, pred[]{:T(512)S(6)} %eq.8), kind=kOutput, calls=%fused_computation.61 | convolution fusion | flops 209133568 | bytes 2007045 | tf_op jit(solution)/shard_map/dot_general | solution.py:27
  53.0 2.5 %collective-permute-start.4 = (bf16[896,256]{1,0:T(8,128)(2,1)}, bf16[896,256]{1,0:T(8,128)(2,1)S(1)}, u32[]{:S(2)}, u32[]{:S(2)}) collective-permute-start(bf16[896,256]{1,0:T(8,128)(2,1)} %fusion), channel_id=1, source_target_pairs={{1,16},{16,1},{17,32},{32,17},{33,48},{48,33},{49,64},{64,49},{65,... | collective-permute-start | bytes 1376264 | tf_op jit(solution)/shard_map/ppermute | solution.py:23
  55.5 2.0 %fusion.43 = f32[896,256]{1,0:T(8,128)S(1)} fusion(bf16[448,2048]{1,0:T(8,128)(2,1)S(1)} %constant_dynamic-update-slice_fusion, s32[]{:T(128)S(6)} %select_n.263, bf16[448,448]{1,0:T(8,128)(2,1)} %collective-permute-done.2, bf16[448,448]{1,0:T(8,128)(2,1)S(1)} %copy-done.10, pred[]{:T(512)S(6)} %eq.8), kind=kOutput, calls=%fused_computation.59 | convolution fusion | flops 209133568 | bytes 2007045 | tf_op jit(solution)/shard_map/dot_general | solution.py:27
  57.5 5.5 %collective-permute-done.4 = bf16[896,256]{1,0:T(8,128)(2,1)S(1)} collective-permute-done((bf16[896,256]{1,0:T(8,128)(2,1)}, bf16[896,256]{1,0:T(8,128)(2,1)S(1)}, u32[]{:S(2)}, u32[]{:S(2)}) %collective-permute-start.4) | collective-permute-done | bytes 458784 | tf_op jit(solution)/shard_map/ppermute | solution.py:23
  63.9 3.3 %collective-permute-start.5 = (bf16[896,256]{1,0:T(8,128)(2,1)}, bf16[896,256]{1,0:T(8,128)(2,1)S(1)}, u32[]{:S(2)}, u32[]{:S(2)}) collective-permute-start(bf16[896,256]{1,0:T(8,128)(2,1)} %fusion.1), channel_id=1, source_target_pairs={{0,17},{17,0},{16,33},{33,16},{32,49},{49,32},{48,65},{65,48},{64,... | collective-permute-start | bytes 1376264 | tf_op jit(solution)/shard_map/ppermute | solution.py:23
  67.2 2.2 %fusion.41 = f32[896,256]{1,0:T(8,128)S(1)} fusion(bf16[448,2048]{1,0:T(8,128)(2,1)S(1)} %constant_dynamic-update-slice_fusion, s32[]{:T(128)S(6)} %select_n.266, bf16[448,448]{1,0:T(8,128)(2,1)} %collective-permute-done.2, bf16[448,448]{1,0:T(8,128)(2,1)} %param.6, pred[]{:T(512)S(6)} %eq.8), kind=kOutput, calls=%fused_computation.57 | convolution fusion | flops 209133568 | bytes 1949701 | tf_op jit(solution)/shard_map/dot_general | solution.py:27
  69.5 5.6 %collective-permute-done.5 = bf16[896,256]{1,0:T(8,128)(2,1)S(1)} collective-permute-done((bf16[896,256]{1,0:T(8,128)(2,1)}, bf16[896,256]{1,0:T(8,128)(2,1)S(1)}, u32[]{:S(2)}, u32[]{:S(2)}) %collective-permute-start.5) | collective-permute-done | bytes 458784 | tf_op jit(solution)/shard_map/ppermute | solution.py:23
  76.0 1.9 %collective-permute-start.6 = (bf16[896,256]{1,0:T(8,128)(2,1)}, bf16[896,256]{1,0:T(8,128)(2,1)S(1)}, u32[]{:S(2)}, u32[]{:S(2)}) collective-permute-start(bf16[896,256]{1,0:T(8,128)(2,1)} %fusion.2), channel_id=1, source_target_pairs={{1,16},{16,1},{17,32},{32,17},{33,48},{48,33},{49,64},{64,49},{65,... | collective-permute-start | bytes 1376264 | tf_op jit(solution)/shard_map/ppermute | solution.py:23
  78.8 2.2 %fusion.39 = f32[896,256]{1,0:T(8,128)S(1)} fusion(bf16[448,2048]{1,0:T(8,128)(2,1)S(1)} %constant_dynamic-update-slice_fusion, s32[]{:T(128)S(6)} %select_n.269, bf16[448,448]{1,0:T(8,128)(2,1)} %collective-permute-done.2, bf16[448,448]{1,0:T(8,128)(2,1)} %param.6, pred[]{:T(512)S(6)} %eq.8), kind=kOutput, calls=%fused_computation.55 | convolution fusion | flops 209133568 | bytes 1949701 | tf_op jit(solution)/shard_map/dot_general | solution.py:27
  81.1 4.9 %collective-permute-done.6 = bf16[896,256]{1,0:T(8,128)(2,1)S(1)} collective-permute-done((bf16[896,256]{1,0:T(8,128)(2,1)}, bf16[896,256]{1,0:T(8,128)(2,1)S(1)}, u32[]{:S(2)}, u32[]{:S(2)}) %collective-permute-start.6) | collective-permute-done | bytes 458784 | tf_op jit(solution)/shard_map/ppermute | solution.py:23
  86.8 3.6 %collective-permute-start.7 = (bf16[896,256]{1,0:T(8,128)(2,1)S(1)}, bf16[896,256]{1,0:T(8,128)(2,1)S(1)}, u32[]{:S(2)}, u32[]{:S(2)}) collective-permute-start(bf16[896,256]{1,0:T(8,128)(2,1)S(1)} %fusion.3), channel_id=1, source_target_pairs={{0,17},{17,0},{16,33},{33,16},{32,49},{49,32},{48,65},{65,48},{64,... | collective-permute-start | bytes 1376264 | tf_op jit(solution)/shard_map/ppermute | solution.py:23
  90.7 2.0 %fusion.37 = f32[896,256]{1,0:T(8,128)S(1)} fusion(bf16[448,2048]{1,0:T(8,128)(2,1)S(1)} %constant_dynamic-update-slice_fusion, s32[]{:T(128)S(6)} %select_n.272, bf16[448,448]{1,0:T(8,128)(2,1)} %collective-permute-done.2, bf16[448,448]{1,0:T(8,128)(2,1)S(1)} %copy-done.11, pred[]{:T(512)S(6)} %eq.8), kind=kOutput, calls=%fused_computation.53 | convolution fusion | flops 209133568 | bytes 2007045 | tf_op jit(solution)/shard_map/dot_general | solution.py:27
  92.7 2.0 %fusion.35 = f32[896,256]{1,0:T(8,128)S(1)} fusion(bf16[448,2048]{1,0:T(8,128)(2,1)S(1)} %constant_dynamic-update-slice_fusion, s32[]{:T(128)S(6)} %select_n.275, bf16[448,448]{1,0:T(8,128)(2,1)} %collective-permute-done.2, bf16[448,448]{1,0:T(8,128)(2,1)S(1)} %copy-done.11, pred[]{:T(512)S(6)} %eq.8), kind=kOutput, calls=%fused_computation.51 | convolution fusion | flops 209133568 | bytes 2007045 | tf_op jit(solution)/shard_map/dot_general | solution.py:27
  94.7 2.0 %fusion.33 = f32[896,256]{1,0:T(8,128)S(1)} fusion(bf16[448,2048]{1,0:T(8,128)(2,1)S(1)} %constant_dynamic-update-slice_fusion, s32[]{:T(128)S(6)} %select_n.278, bf16[448,448]{1,0:T(8,128)(2,1)} %collective-permute-done.2, bf16[448,448]{1,0:T(8,128)(2,1)S(1)} %copy-done.11, pred[]{:T(512)S(6)} %eq.8), kind=kOutput, calls=%fused_computation.49 | convolution fusion | flops 209133568 | bytes 2007045 | tf_op jit(solution)/shard_map/dot_general | solution.py:27
  97.9 2.1 %collective-permute-start.8 = (bf16[896,256]{1,0:T(8,128)(2,1)S(1)}, bf16[896,256]{1,0:T(8,128)(2,1)S(1)}, u32[]{:S(2)}, u32[]{:S(2)}) collective-permute-start(bf16[896,256]{1,0:T(8,128)(2,1)S(1)} %fusion.4), channel_id=1, source_target_pairs={{1,16},{16,1},{17,32},{32,17},{33,48},{48,33},{49,64},{64,49},{65,... | collective-permute-start | bytes 1376264 | tf_op jit(solution)/shard_map/ppermute | solution.py:23
  100.8 7.0 %collective-permute-done.8 = bf16[896,256]{1,0:T(8,128)(2,1)S(1)} collective-permute-done((bf16[896,256]{1,0:T(8,128)(2,1)S(1)}, bf16[896,256]{1,0:T(8,128)(2,1)S(1)}, u32[]{:S(2)}, u32[]{:S(2)}) %collective-permute-start.8) | collective-permute-done | bytes 458784 | tf_op jit(solution)/shard_map/ppermute | solution.py:23
  107.9 4.0 %collective-permute-start.9 = (bf16[896,256]{1,0:T(8,128)(2,1)S(1)}, bf16[896,256]{1,0:T(8,128)(2,1)S(1)}, u32[]{:S(2)}, u32[]{:S(2)}) collective-permute-start(bf16[896,256]{1,0:T(8,128)(2,1)S(1)} %fusion.5), channel_id=1, source_target_pairs={{0,17},{17,0},{16,33},{33,16},{32,49},{49,32},{48,65},{65,48},{64,... | collective-permute-start | bytes 1376264 | tf_op jit(solution)/shard_map/ppermute | solution.py:23
  112.9 6.2 %collective-permute-done.9 = bf16[896,256]{1,0:T(8,128)(2,1)S(1)} collective-permute-done((bf16[896,256]{1,0:T(8,128)(2,1)S(1)}, bf16[896,256]{1,0:T(8,128)(2,1)S(1)}, u32[]{:S(2)}, u32[]{:S(2)}) %collective-permute-start.9) | collective-permute-done | bytes 458784 | tf_op jit(solution)/shard_map/ppermute | solution.py:23
  119.2 1.9 %collective-permute-start.10 = (bf16[896,256]{1,0:T(8,128)(2,1)S(1)}, bf16[896,256]{1,0:T(8,128)(2,1)S(1)}, u32[]{:S(2)}, u32[]{:S(2)}) collective-permute-start(bf16[896,256]{1,0:T(8,128)(2,1)S(1)} %fusion.6), channel_id=1, source_target_pairs={{1,16},{16,1},{17,32},{32,17},{33,48},{48,33},{49,64},{64,49},{65,... | collective-permute-start | bytes 1376264 | tf_op jit(solution)/shard_map/ppermute | solution.py:23
  122.0 7.0 %collective-permute-done.10 = bf16[896,256]{1,0:T(8,128)(2,1)S(1)} collective-permute-done((bf16[896,256]{1,0:T(8,128)(2,1)S(1)}, bf16[896,256]{1,0:T(8,128)(2,1)S(1)}, u32[]{:S(2)}, u32[]{:S(2)}) %collective-permute-start.10) | collective-permute-done | bytes 458784 | tf_op jit(solution)/shard_map/ppermute | solution.py:23
  129.0 3.5 %collective-permute-start.11 = (bf16[448,256]{1,0:T(8,128)(2,1)S(1)}, bf16[448,256]{1,0:T(8,128)(2,1)S(1)}, u32[]{:S(2)}, u32[]{:S(2)}) collective-permute-start(bf16[448,256]{1,0:T(8,128)(2,1)S(1)} %constant_dynamic-slice_fusion.1), channel_id=1, source_target_pairs={{0,1},{1,0},{2,3},{3,2},{4,5},{5,4},{6,7},{7,6},{8,9},{9,8},{10,11... | collective-permute-start | bytes 688136 | tf_op jit(solution)/shard_map/ppermute | solution.py:15
  133.5 1.9 %collective-permute-start.14 = (f32[448,448]{1,0:T(8,128)S(1)}, f32[448,448]{1,0:T(8,128)S(1)}, u32[]{:S(2)}, u32[]{:S(2)}) collective-permute-start(f32[448,448]{1,0:T(8,128)S(1)} %constant_dynamic-slice_fusion), channel_id=1, source_target_pairs={{0,1},{1,0},{2,3},{3,2},{4,5},{5,4},{6,7},{7,6},{8,9},{9,8},{10,11... | collective-permute-start | bytes 2408456 | tf_op jit(solution)/shard_map/ppermute | solution.py:15
  135.5 1.4 fusion.9
  136.9 3.5 %collective-permute-start.12 = (bf16[224,256]{1,0:T(8,128)(2,1)S(1)}, bf16[224,256]{1,0:T(8,128)(2,1)S(1)}, u32[]{:S(2)}, u32[]{:S(2)}) collective-permute-start(bf16[224,256]{1,0:T(8,128)(2,1)S(1)} %get-tuple-element.9), channel_id=1, source_target_pairs={{0,128},{128,256},{256,384},{384,0},{1,129},{129,257},{257,385},{3... | collective-permute-start | bytes 344072 | tf_op jit(solution)/shard_map/ppermute | solution.py:100
  140.3 4.8 %collective-permute-start.13 = (bf16[224,256]{1,0:T(8,128)(2,1)S(1)}, bf16[224,256]{1,0:T(8,128)(2,1)S(1)}, u32[]{:S(2)}, u32[]{:S(2)}) collective-permute-start(bf16[224,256]{1,0:T(8,128)(2,1)S(1)} %get-tuple-element.10), channel_id=1, source_target_pairs={{0,256},{128,384},{256,0},{384,128},{1,257},{129,385},{257,1},{385... | collective-permute-start | bytes 344072 | tf_op jit(solution)/shard_map/ppermute | solution.py:101
  145.6 3.6 %collective-permute-done.13 = bf16[224,256]{1,0:T(8,128)(2,1)S(1)} collective-permute-done((bf16[224,256]{1,0:T(8,128)(2,1)S(1)}, bf16[224,256]{1,0:T(8,128)(2,1)S(1)}, u32[]{:S(2)}, u32[]{:S(2)}) %collective-permute-start.13) | collective-permute-done | bytes 114720 | tf_op jit(solution)/shard_map/ppermute | solution.py:101
  (57 shorter events, 11.6 us)
Async XLA Ops:
  0.6 32.4 %copy-start = (bf16[448,256]{1,0:T(8,128)(2,1)S(1)}, bf16[448,256]{1,0:T(8,128)(2,1)}, u32[]{:S(2)}) copy-start(bf16[448,256]{1,0:T(8,128)(2,1)} %param.8) | copy-start | bytes 688132
  0.6 35.3 %collective-permute-start.3 = (bf16[448,128]{1,0:T(8,128)(2,1)}, bf16[448,128]{1,0:T(8,128)(2,1)S(1)}, u32[]{:S(2)}, u32[]{:S(2)}) collective-permute-start(bf16[448,128]{1,0:T(8,128)(2,1)} %param.7), channel_id=1, source_target_pairs={{0,8},{8,0},{1,9},{9,1},{2,10},{10,2},{3,11},{11,3},{4,12},{12,4},... | collective-permute-start | bytes 344072 | tf_op jit(solution)/shard_map/ppermute | solution.py:50
  13.8 36.3 %collective-permute-start.2 = (bf16[448,448]{1,0:T(8,128)(2,1)}, bf16[448,448]{1,0:T(8,128)(2,1)}, u32[]{:S(2)}, u32[]{:S(2)}) collective-permute-start(bf16[448,448]{1,0:T(8,128)(2,1)} %param.6), channel_id=1, source_target_pairs={{0,1},{1,0},{2,3},{3,2},{4,5},{5,4},{6,7},{7,6},{8,9},{9,8},{10,11... | collective-permute-start | bytes 1204232 | tf_op jit(solution)/shard_map/ppermute | solution.py:15
  15.7 17.3 %collective-permute-start = (bf16[448,256]{1,0:T(8,128)(2,1)}, bf16[448,256]{1,0:T(8,128)(2,1)S(1)}, u32[]{:S(2)}, u32[]{:S(2)}) collective-permute-start(bf16[448,256]{1,0:T(8,128)(2,1)} %param.8), channel_id=1, source_target_pairs={{0,1},{1,0},{2,3},{3,2},{4,5},{5,4},{6,7},{7,6},{8,9},{9,8},{10,11... | collective-permute-start | bytes 688136 | tf_op jit(solution)/shard_map/ppermute | solution.py:15
  33.2 16.9 %copy-start.9 = (bf16[448,448]{1,0:T(8,128)(2,1)S(1)}, bf16[448,448]{1,0:T(8,128)(2,1)}, u32[]{:S(2)}) copy-start(bf16[448,448]{1,0:T(8,128)(2,1)} %param.6) | copy-start | bytes 1204228
  33.2 18.8 %collective-permute-start.1 = (bf16[896,256]{1,0:T(8,128)(2,1)S(1)}, bf16[896,256]{1,0:T(8,128)(2,1)S(1)}, u32[]{:S(2)}, u32[]{:S(2)}) collective-permute-start(bf16[896,256]{1,0:T(8,128)(2,1)S(1)} %maximum_select_fusion.1), channel_id=1, source_target_pairs={{0,17},{17,0},{16,33},{33,16},{32,49},{49,32},{48,65},{65,48},{64,... | collective-permute-start | bytes 1376264 | tf_op jit(solution)/shard_map/ppermute | solution.py:23
  52.1 3.4 %copy-start.10 = (bf16[448,448]{1,0:T(8,128)(2,1)S(1)}, bf16[448,448]{1,0:T(8,128)(2,1)}, u32[]{:S(2)}) copy-start(bf16[448,448]{1,0:T(8,128)(2,1)} %param.6) | copy-start | bytes 1204228
  53.0 10.0 %collective-permute-start.4 = (bf16[896,256]{1,0:T(8,128)(2,1)}, bf16[896,256]{1,0:T(8,128)(2,1)S(1)}, u32[]{:S(2)}, u32[]{:S(2)}) collective-permute-start(bf16[896,256]{1,0:T(8,128)(2,1)} %fusion), channel_id=1, source_target_pairs={{1,16},{16,1},{17,32},{32,17},{33,48},{48,33},{49,64},{64,49},{65,... | collective-permute-start | bytes 1376264 | tf_op jit(solution)/shard_map/ppermute | solution.py:23
  63.0 6.5 %copy-start.1 = (bf16[896,256]{1,0:T(8,128)(2,1)}, bf16[896,256]{1,0:T(8,128)(2,1)S(1)}, u32[]{:S(2)}) copy-start(bf16[896,256]{1,0:T(8,128)(2,1)S(1)} %collective-permute-done.4) | copy-start | bytes 1376260
  63.9 11.2 %collective-permute-start.5 = (bf16[896,256]{1,0:T(8,128)(2,1)}, bf16[896,256]{1,0:T(8,128)(2,1)S(1)}, u32[]{:S(2)}, u32[]{:S(2)}) collective-permute-start(bf16[896,256]{1,0:T(8,128)(2,1)} %fusion.1), channel_id=1, source_target_pairs={{0,17},{17,0},{16,33},{33,16},{32,49},{49,32},{48,65},{65,48},{64,... | collective-permute-start | bytes 1376264 | tf_op jit(solution)/shard_map/ppermute | solution.py:23
  75.1 6.0 %copy-start.3 = (bf16[896,256]{1,0:T(8,128)(2,1)}, bf16[896,256]{1,0:T(8,128)(2,1)S(1)}, u32[]{:S(2)}) copy-start(bf16[896,256]{1,0:T(8,128)(2,1)S(1)} %collective-permute-done.5) | copy-start | bytes 1376260
  76.0 10.0 %collective-permute-start.6 = (bf16[896,256]{1,0:T(8,128)(2,1)}, bf16[896,256]{1,0:T(8,128)(2,1)S(1)}, u32[]{:S(2)}, u32[]{:S(2)}) collective-permute-start(bf16[896,256]{1,0:T(8,128)(2,1)} %fusion.2), channel_id=1, source_target_pairs={{1,16},{16,1},{17,32},{32,17},{33,48},{48,33},{49,64},{64,49},{65,... | collective-permute-start | bytes 1376264 | tf_op jit(solution)/shard_map/ppermute | solution.py:23
  81.1 9.3 %copy-start.11 = (bf16[448,448]{1,0:T(8,128)(2,1)S(1)}, bf16[448,448]{1,0:T(8,128)(2,1)}, u32[]{:S(2)}) copy-start(bf16[448,448]{1,0:T(8,128)(2,1)} %param.6) | copy-start | bytes 1204228
  86.0 0.8 copy-start.5
  86.8 11.0 %collective-permute-start.7 = (bf16[896,256]{1,0:T(8,128)(2,1)S(1)}, bf16[896,256]{1,0:T(8,128)(2,1)S(1)}, u32[]{:S(2)}, u32[]{:S(2)}) collective-permute-start(bf16[896,256]{1,0:T(8,128)(2,1)S(1)} %fusion.3), channel_id=1, source_target_pairs={{0,17},{17,0},{16,33},{33,16},{32,49},{49,32},{48,65},{65,48},{64,... | collective-permute-start | bytes 1376264 | tf_op jit(solution)/shard_map/ppermute | solution.py:23
  97.9 2.5 %copy-start.2 = (bf16[896,256]{1,0:T(8,128)(2,1)S(1)}, bf16[896,256]{1,0:T(8,128)(2,1)}, u32[]{:S(2)}) copy-start(bf16[896,256]{1,0:T(8,128)(2,1)} %copy-done.1) | copy-start | bytes 1376260
  97.9 9.9 %collective-permute-start.8 = (bf16[896,256]{1,0:T(8,128)(2,1)S(1)}, bf16[896,256]{1,0:T(8,128)(2,1)S(1)}, u32[]{:S(2)}, u32[]{:S(2)}) collective-permute-start(bf16[896,256]{1,0:T(8,128)(2,1)S(1)} %fusion.4), channel_id=1, source_target_pairs={{1,16},{16,1},{17,32},{32,17},{33,48},{48,33},{49,64},{64,49},{65,... | collective-permute-start | bytes 1376264 | tf_op jit(solution)/shard_map/ppermute | solution.py:23
  100.4 11.6 %copy-start.4 = (bf16[896,256]{1,0:T(8,128)(2,1)S(1)}, bf16[896,256]{1,0:T(8,128)(2,1)}, u32[]{:S(2)}) copy-start(bf16[896,256]{1,0:T(8,128)(2,1)} %copy-done.3) | copy-start | bytes 1376260
  107.9 4.5 %copy-start.6 = (bf16[896,256]{1,0:T(8,128)(2,1)S(1)}, bf16[896,256]{1,0:T(8,128)(2,1)}, u32[]{:S(2)}) copy-start(bf16[896,256]{1,0:T(8,128)(2,1)} %copy-done.5) | copy-start | bytes 1376260
  107.9 11.1 %collective-permute-start.9 = (bf16[896,256]{1,0:T(8,128)(2,1)S(1)}, bf16[896,256]{1,0:T(8,128)(2,1)S(1)}, u32[]{:S(2)}, u32[]{:S(2)}) collective-permute-start(bf16[896,256]{1,0:T(8,128)(2,1)S(1)} %fusion.5), channel_id=1, source_target_pairs={{0,17},{17,0},{16,33},{33,16},{32,49},{49,32},{48,65},{65,48},{64,... | collective-permute-start | bytes 1376264 | tf_op jit(solution)/shard_map/ppermute | solution.py:23
  119.2 9.8 %collective-permute-start.10 = (bf16[896,256]{1,0:T(8,128)(2,1)S(1)}, bf16[896,256]{1,0:T(8,128)(2,1)S(1)}, u32[]{:S(2)}, u32[]{:S(2)}) collective-permute-start(bf16[896,256]{1,0:T(8,128)(2,1)S(1)} %fusion.6), channel_id=1, source_target_pairs={{1,16},{16,1},{17,32},{32,17},{33,48},{48,33},{49,64},{64,49},{65,... | collective-permute-start | bytes 1376264 | tf_op jit(solution)/shard_map/ppermute | solution.py:23
  129.0 6.4 %collective-permute-start.11 = (bf16[448,256]{1,0:T(8,128)(2,1)S(1)}, bf16[448,256]{1,0:T(8,128)(2,1)S(1)}, u32[]{:S(2)}, u32[]{:S(2)}) collective-permute-start(bf16[448,256]{1,0:T(8,128)(2,1)S(1)} %constant_dynamic-slice_fusion.1), channel_id=1, source_target_pairs={{0,1},{1,0},{2,3},{3,2},{4,5},{5,4},{6,7},{7,6},{8,9},{9,8},{10,11... | collective-permute-start | bytes 688136 | tf_op jit(solution)/shard_map/ppermute | solution.py:15
  133.2 2.3 %copy-start.7 = (f32[448,256]{1,0:T(8,128)S(1)}, f32[448,256]{1,0:T(8,128)}, u32[]{:S(2)}) copy-start(f32[448,256]{1,0:T(8,128)} %param.10) | copy-start | bytes 1376260
  133.2 2.3 %copy-start.8 = (f32[448,256]{1,0:T(8,128)S(1)}, f32[448,256]{1,0:T(8,128)}, u32[]{:S(2)}) copy-start(f32[448,256]{1,0:T(8,128)} %param.9) | copy-start | bytes 1376260
  133.5 16.5 %collective-permute-start.14 = (f32[448,448]{1,0:T(8,128)S(1)}, f32[448,448]{1,0:T(8,128)S(1)}, u32[]{:S(2)}, u32[]{:S(2)}) collective-permute-start(f32[448,448]{1,0:T(8,128)S(1)} %constant_dynamic-slice_fusion), channel_id=1, source_target_pairs={{0,1},{1,0},{2,3},{3,2},{4,5},{5,4},{6,7},{7,6},{8,9},{9,8},{10,11... | collective-permute-start | bytes 2408456 | tf_op jit(solution)/shard_map/ppermute | solution.py:15
  136.9 8.7 %collective-permute-start.12 = (bf16[224,256]{1,0:T(8,128)(2,1)S(1)}, bf16[224,256]{1,0:T(8,128)(2,1)S(1)}, u32[]{:S(2)}, u32[]{:S(2)}) collective-permute-start(bf16[224,256]{1,0:T(8,128)(2,1)S(1)} %get-tuple-element.9), channel_id=1, source_target_pairs={{0,128},{128,256},{256,384},{384,0},{1,129},{129,257},{257,385},{3... | collective-permute-start | bytes 344072 | tf_op jit(solution)/shard_map/ppermute | solution.py:100
  140.3 8.9 %collective-permute-start.13 = (bf16[224,256]{1,0:T(8,128)(2,1)S(1)}, bf16[224,256]{1,0:T(8,128)(2,1)S(1)}, u32[]{:S(2)}, u32[]{:S(2)}) collective-permute-start(bf16[224,256]{1,0:T(8,128)(2,1)S(1)} %get-tuple-element.10), channel_id=1, source_target_pairs={{0,256},{128,384},{256,0},{384,128},{1,257},{129,385},{257,1},{385... | collective-permute-start | bytes 344072 | tf_op jit(solution)/shard_map/ppermute | solution.py:101

commit v2 on v1

v2 whole, which is shorter than its diff:
```python
import math

import jax
import jax.numpy as jnp
from jax import lax
from jax.sharding import Mesh, PartitionSpec as P

BF = jnp.bfloat16
F32 = jnp.float32
LINE = 8
LEAD = 1


def along(value, way):
    return lax.ppermute(value, "zl", [(i, i + way) for i in range(LINE) if 0 <= i + way < LINE])


def contract(left, right, dims):
    return lax.dot_general(left, right, (dims, ((), ())), preferred_element_type=F32)


def after(value, other):
    mark = other[0, 0]
    return jnp.where(mark != mark, jnp.zeros((), value.dtype), value)


def body(hidden, upstream, weights, first_moment, second_moment, step_index):
    width = weights.shape[1]
    place, far_half = lax.axis_index("zl"), lax.axis_index("zh")
    scale_hid = 1.0 / math.sqrt(7168)

    up_other = lax.ppermute(upstream, "zh", [(0, 1), (1, 0)])
    near_up = lax.all_gather(upstream, ("x", "c"), axis=1, tiled=True)
    far_up = lax.all_gather(up_other, ("x", "c"), axis=1, tiled=True)
    full_up = jnp.concatenate([near_up, far_up], axis=1)
    hidden_t = lax.optimization_barrier(hidden.T)

    def up_block(index):
        at = jnp.bitwise_xor(index, 4 * far_half) * width
        return lax.dynamic_slice_in_dim(full_up, at, width, 1)

    own_up = up_block(place)
    hg_total = contract(own_up, weights, ((1,), (1,)))
    start = after(weights, near_up)
    carried = {1: start, -1: start}
    for step in range(LINE - 1 + LEAD):
        turn = step - LEAD
        for way in (1, -1):
            position = place if way == 1 else LINE - 1 - place
            payload = carried[way]
            if turn >= 0:
                block = jnp.clip(LINE - 1 - turn + position, 0, LINE - 1)
                block = block if way == 1 else LINE - 1 - block
                part = lax.optimization_barrier(contract(hidden_t, up_block(block), ((1,), (0,))))
                payload = jnp.where(position <= turn, (payload.astype(F32) + part).astype(BF), payload)
            carried[way] = along(payload, way)
        for way in (1, -1):
            if step < LINE - 1:
                position = place if way == 1 else LINE - 1 - place
                source = position - 1 - step
                valid = source >= 0
                source = jnp.clip(source, 0, LINE - 1)
                source = source if way == 1 else LINE - 1 - source
                features = jnp.where(valid, up_block(source), jnp.zeros((), BF))
                hg_total = hg_total + contract(features, carried[way], ((1,), (1,)))

    own_part = lax.optimization_barrier(contract(hidden_t, own_up, ((1,), (0,))))
    grads = (own_part + carried[1].astype(F32) + carried[-1].astype(F32)) * scale_hid

    count = (step_index[0] + 1).astype(F32)
    first_new = 0.9 * first_moment + 0.1 * grads
    second_new = 0.999 * second_moment + 0.001 * grads * grads
    correct_one = 1.0 - jnp.power(F32(0.9), count)
    correct_two = 1.0 - jnp.power(F32(0.999), count)
    weights_f = weights.astype(F32)
    step_size = first_new / correct_one / (jnp.sqrt(second_new / correct_two) + 1e-08) + 0.1 * weights_f
    updated = (weights_f - 0.05 * step_size).astype(BF)

    half = updated.shape[0] // 2
    even_step = step_index[0] % 2 == 0
    lower, upper = updated[:half], updated[half:]
    near = lax.ppermute(jnp.where(even_step, lower, upper), "y", [(i, (i + 1) % 4) for i in range(4)])
    far = lax.ppermute(jnp.where(even_step, upper, lower), "y", [(i, (i + 2) % 4) for i in range(4)])
    partner = jnp.concatenate([jnp.where(even_step, near, far), jnp.where(even_step, far, near)], 0)
    mixed = ((updated.astype(F32) + partner.astype(F32)) * 0.5).astype(BF)

    in_grad = (hg_total * scale_hid).astype(BF)
    return mixed, first_new, second_new, in_grad


def solution(mesh):
    split = Mesh(mesh.devices.reshape(4, LINE, 2, 4, 2), ("y", "zl", "zh", "x", "c"))
    rep, tp = ("y", "zl"), ("zh", "x", "c")
    in_specs = (P(rep, tp), P(rep, tp), P(tp, rep), P(tp, rep), P(tp, rep), P())
    out_specs = (P(tp, rep), P(tp, rep), P(tp, rep), P(rep, tp))
    return jax.shard_map(body, mesh=split, in_specs=in_specs, out_specs=out_specs, check_vma=False)
```

time: 152 us -> 144 us (0.947)
  the two profiles are of different devices: /device:TPU:98 before, /device:TPU:96 now
where the time goes in v2:
time: 144 us; the launch traced here: 143 us
  starting transfers between devices  79.2 us (55%)
  blocking collectives  27.9 us (19%)
  waiting for transfers between devices  16.9 us (12%)
  matrix products  11 us (8%)
  other arithmetic  3.96 us (3%)
  between operations  3.55 us (2%)
    ppermute x16, starting transfers between devices, along(): lax.ppermute(value, 'zl', [(i, i + way) for i in range(LINE) if 0 <= i +...  57.8 us
    ppermute x16, waiting for transfers between devices, along(): lax.ppermute(value, 'zl', [(i, i + way) for i in range(LINE) if 0 <= i +...  15 us
    all_gather x1, blocking collectives, body(): near_up = lax.all_gather(upstream, ('x', 'c'), axis=1, tiled=True)  14.5 us
    all_gather x1, blocking collectives, body(): far_up = lax.all_gather(up_other, ('x', 'c'), axis=1, tiled=True)  13.3 us
    ppermute x1, starting transfers between devices, body(): up_other = lax.ppermute(upstream, 'zh', [(0, 1), (1, 0)])  13.2 us
    dot_general x30, matrix products, contract(): lax.dot_general(left, right, (dims, ((), ())), preferred_element_type=F32)  11 us
    ppermute x1, starting transfers between devices, body(): lax.ppermute(jnp.where(even_step, upper, lower), 'y', [(i, (i + 2) % 4) f...  4.79 us
    ppermute x1, starting transfers between devices, body(): lax.ppermute(jnp.where(even_step, lower, upper), 'y', [(i, (i + 1) % 4) f...  3.49 us
  transfers between devices with their start and end apart: 19, of which 9 were waited for; matrix products, arithmetic and copies ran while one was open for 9% of the time, Pallas kernels for 0%

profile of v2, /device:TPU:96, one launch (start us, length us, event | category | flops | bytes accessed | tf_op | source)
XLA Modules:
  0.0 143.1 jit_solution(9731839071862217776)
XLA Ops:
  0.6 13.2 %collective-permute-start = (bf16[448,128]{1,0:T(8,128)(2,1)}, bf16[448,128]{1,0:T(8,128)(2,1)S(1)}, u32[]{:S(2)}, u32[]{:S(2)}) collective-permute-start(bf16[448,128]{1,0:T(8,128)(2,1)} %param.7), channel_id=1, source_target_pairs={{0,8},{8,0},{1,9},{9,1},{2,10},{10,2},{3,11},{11,3},{4,12},{12,4},... | collective-permute-start | bytes 344072 | tf_op jit(solution)/shard_map/ppermute | solution.py:32
  13.8 14.5 %all_gather.6 = bf16[448,1024]{1,0:T(8,128)(2,1)S(1)} all-gather(bf16[448,128]{1,0:T(8,128)(2,1)} %param.7), channel_id=1, replica_groups=mesh['y'=4,'zl'=8,'zh'=2,'x'=4,'c'=2] {'x','c'}, dimensions={1}, use_global_device_ids=true | all-gather | bytes 1032192 | tf_op jit(solution)/shard_map/all_gather | solution.py:33
  30.1 1.0 broadcast_select_fusion
  31.1 2.7 %collective-permute-start.1 = (bf16[448,256]{1,0:T(8,128)(2,1)S(1)}, bf16[448,256]{1,0:T(8,128)(2,1)S(1)}, u32[]{:S(2)}, u32[]{:S(2)}) collective-permute-start(bf16[448,256]{1,0:T(8,128)(2,1)S(1)} %broadcast_select_fusion), channel_id=1, source_target_pairs={{0,16},{16,32},{32,48},{48,64},{64,80},{80,96},{96,112},{1,17},{17... | collective-permute-start | bytes 688136 | tf_op jit(solution)/shard_map/ppermute | solution.py:15
  33.8 3.2 %collective-permute-start.9 = (bf16[448,256]{1,0:T(8,128)(2,1)S(1)}, bf16[448,256]{1,0:T(8,128)(2,1)S(1)}, u32[]{:S(2)}, u32[]{:S(2)}) collective-permute-start(bf16[448,256]{1,0:T(8,128)(2,1)S(1)} %broadcast_select_fusion), channel_id=1, source_target_pairs={{16,0},{32,16},{48,32},{64,48},{80,64},{96,80},{112,96},{17,1},{33... | collective-permute-start | bytes 688136 | tf_op jit(solution)/shard_map/ppermute | solution.py:15
  38.2 13.3 %all_gather.7 = bf16[448,1024]{1,0:T(8,128)(2,1)S(1)} all-gather(bf16[448,128]{1,0:T(8,128)(2,1)S(1)} %collective-permute-done), channel_id=1, replica_groups=mesh['y'=4,'zl'=8,'zh'=2,'x'=4,'c'=2] {'x','c'}, dimensions={1}, use_global_device_ids=true | all-gather | bytes 1032192 | tf_op jit(solution)/shard_map/all_gather | solution.py:34
  57.0 4.8 %collective-permute-start.2 = (bf16[448,256]{1,0:T(8,128)(2,1)S(1)}, bf16[448,256]{1,0:T(8,128)(2,1)S(1)}, u32[]{:S(2)}, u32[]{:S(2)}) collective-permute-start(bf16[448,256]{1,0:T(8,128)(2,1)S(1)} %fusion.18), channel_id=1, source_target_pairs={{0,16},{16,32},{32,48},{48,64},{64,80},{80,96},{96,112},{1,17},{17... | collective-permute-start | bytes 688136 | tf_op jit(solution)/shard_map/ppermute | solution.py:15
  61.9 1.9 %collective-permute-start.10 = (bf16[448,256]{1,0:T(8,128)(2,1)S(1)}, bf16[448,256]{1,0:T(8,128)(2,1)S(1)}, u32[]{:S(2)}, u32[]{:S(2)}) collective-permute-start(bf16[448,256]{1,0:T(8,128)(2,1)S(1)} %fusion.25), channel_id=1, source_target_pairs={{16,0},{32,16},{48,32},{64,48},{80,64},{96,80},{112,96},{17,1},{33... | collective-permute-start | bytes 688136 | tf_op jit(solution)/shard_map/ppermute | solution.py:15
  64.4 2.7 %collective-permute-done.2 = bf16[448,256]{1,0:T(8,128)(2,1)S(1)} collective-permute-done((bf16[448,256]{1,0:T(8,128)(2,1)S(1)}, bf16[448,256]{1,0:T(8,128)(2,1)S(1)}, u32[]{:S(2)}, u32[]{:S(2)}) %collective-permute-start.2) | collective-permute-done | bytes 229408 | tf_op jit(solution)/shard_map/ppermute | solution.py:15
  67.2 5.6 %collective-permute-start.3 = (bf16[448,256]{1,0:T(8,128)(2,1)S(1)}, bf16[448,256]{1,0:T(8,128)(2,1)S(1)}, u32[]{:S(2)}, u32[]{:S(2)}) collective-permute-start(bf16[448,256]{1,0:T(8,128)(2,1)S(1)} %fusion.19), channel_id=1, source_target_pairs={{0,16},{16,32},{32,48},{48,64},{64,80},{80,96},{96,112},{1,17},{17... | collective-permute-start | bytes 688136 | tf_op jit(solution)/shard_map/ppermute | solution.py:15
  72.9 1.9 %collective-permute-start.11 = (bf16[448,256]{1,0:T(8,128)(2,1)S(1)}, bf16[448,256]{1,0:T(8,128)(2,1)S(1)}, u32[]{:S(2)}, u32[]{:S(2)}) collective-permute-start(bf16[448,256]{1,0:T(8,128)(2,1)S(1)} %fusion.26), channel_id=1, source_target_pairs={{16,0},{32,16},{48,32},{64,48},{80,64},{96,80},{112,96},{17,1},{33... | collective-permute-start | bytes 688136 | tf_op jit(solution)/shard_map/ppermute | solution.py:15
  75.4 1.9 %collective-permute-done.3 = bf16[448,256]{1,0:T(8,128)(2,1)S(1)} collective-permute-done((bf16[448,256]{1,0:T(8,128)(2,1)S(1)}, bf16[448,256]{1,0:T(8,128)(2,1)S(1)}, u32[]{:S(2)}, u32[]{:S(2)}) %collective-permute-start.3) | collective-permute-done | bytes 229408 | tf_op jit(solution)/shard_map/ppermute | solution.py:15
  77.4 5.6 %collective-permute-start.4 = (bf16[448,256]{1,0:T(8,128)(2,1)S(1)}, bf16[448,256]{1,0:T(8,128)(2,1)S(1)}, u32[]{:S(2)}, u32[]{:S(2)}) collective-permute-start(bf16[448,256]{1,0:T(8,128)(2,1)S(1)} %fusion.20), channel_id=1, source_target_pairs={{0,16},{16,32},{32,48},{48,64},{64,80},{80,96},{96,112},{1,17},{17... | collective-permute-start | bytes 688136 | tf_op jit(solution)/shard_map/ppermute | solution.py:15
  83.1 1.9 %collective-permute-start.12 = (bf16[448,256]{1,0:T(8,128)(2,1)S(1)}, bf16[448,256]{1,0:T(8,128)(2,1)S(1)}, u32[]{:S(2)}, u32[]{:S(2)}) collective-permute-start(bf16[448,256]{1,0:T(8,128)(2,1)S(1)} %fusion.27), channel_id=1, source_target_pairs={{16,0},{32,16},{48,32},{64,48},{80,64},{96,80},{112,96},{17,1},{33... | collective-permute-start | bytes 688136 | tf_op jit(solution)/shard_map/ppermute | solution.py:15
  85.6 1.0 collective-permute-done.4
  86.7 5.6 %collective-permute-start.5 = (bf16[448,256]{1,0:T(8,128)(2,1)S(1)}, bf16[448,256]{1,0:T(8,128)(2,1)S(1)}, u32[]{:S(2)}, u32[]{:S(2)}) collective-permute-start(bf16[448,256]{1,0:T(8,128)(2,1)S(1)} %fusion.21), channel_id=1, source_target_pairs={{0,16},{16,32},{32,48},{48,64},{64,80},{80,96},{96,112},{1,17},{17... | collective-permute-start | bytes 688136 | tf_op jit(solution)/shard_map/ppermute | solution.py:15
  92.4 1.9 %collective-permute-start.13 = (bf16[448,256]{1,0:T(8,128)(2,1)S(1)}, bf16[448,256]{1,0:T(8,128)(2,1)S(1)}, u32[]{:S(2)}, u32[]{:S(2)}) collective-permute-start(bf16[448,256]{1,0:T(8,128)(2,1)S(1)} %fusion.28), channel_id=1, source_target_pairs={{16,0},{32,16},{48,32},{64,48},{80,64},{96,80},{112,96},{17,1},{33... | collective-permute-start | bytes 688136 | tf_op jit(solution)/shard_map/ppermute | solution.py:15
  94.9 0.9 collective-permute-done.5
  95.9 5.6 %collective-permute-start.6 = (bf16[448,256]{1,0:T(8,128)(2,1)S(1)}, bf16[448,256]{1,0:T(8,128)(2,1)S(1)}, u32[]{:S(2)}, u32[]{:S(2)}) collective-permute-start(bf16[448,256]{1,0:T(8,128)(2,1)S(1)} %fusion.22), channel_id=1, source_target_pairs={{0,16},{16,32},{32,48},{48,64},{64,80},{80,96},{96,112},{1,17},{17... | collective-permute-start | bytes 688136 | tf_op jit(solution)/shard_map/ppermute | solution.py:15
  101.6 1.9 %collective-permute-start.14 = (bf16[448,256]{1,0:T(8,128)(2,1)S(1)}, bf16[448,256]{1,0:T(8,128)(2,1)S(1)}, u32[]{:S(2)}, u32[]{:S(2)}) collective-permute-start(bf16[448,256]{1,0:T(8,128)(2,1)S(1)} %fusion.29), channel_id=1, source_target_pairs={{16,0},{32,16},{48,32},{64,48},{80,64},{96,80},{112,96},{17,1},{33... | collective-permute-start | bytes 688136 | tf_op jit(solution)/shard_map/ppermute | solution.py:15
  104.1 0.9 collective-permute-done.6
  105.1 5.6 %collective-permute-start.7 = (bf16[448,256]{1,0:T(8,128)(2,1)S(1)}, bf16[448,256]{1,0:T(8,128)(2,1)S(1)}, u32[]{:S(2)}, u32[]{:S(2)}) collective-permute-start(bf16[448,256]{1,0:T(8,128)(2,1)S(1)} %fusion.23), channel_id=1, source_target_pairs={{0,16},{16,32},{32,48},{48,64},{64,80},{80,96},{96,112},{1,17},{17... | collective-permute-start | bytes 688136 | tf_op jit(solution)/shard_map/ppermute | solution.py:15
  110.8 1.9 %collective-permute-start.15 = (bf16[448,256]{1,0:T(8,128)(2,1)S(1)}, bf16[448,256]{1,0:T(8,128)(2,1)S(1)}, u32[]{:S(2)}, u32[]{:S(2)}) collective-permute-start(bf16[448,256]{1,0:T(8,128)(2,1)S(1)} %fusion.30), channel_id=1, source_target_pairs={{16,0},{32,16},{48,32},{64,48},{80,64},{96,80},{112,96},{17,1},{33... | collective-permute-start | bytes 688136 | tf_op jit(solution)/shard_map/ppermute | solution.py:15
  113.3 0.9 collective-permute-done.7
  114.3 5.7 %collective-permute-start.8 = (bf16[448,256]{1,0:T(8,128)(2,1)S(1)}, bf16[448,256]{1,0:T(8,128)(2,1)S(1)}, u32[]{:S(2)}, u32[]{:S(2)}) collective-permute-start(bf16[448,256]{1,0:T(8,128)(2,1)S(1)} %fusion.24), channel_id=1, source_target_pairs={{0,16},{16,32},{32,48},{48,64},{64,80},{80,96},{96,112},{1,17},{17... | collective-permute-start | bytes 688136 | tf_op jit(solution)/shard_map/ppermute | solution.py:15
  120.1 1.9 %collective-permute-start.16 = (bf16[448,256]{1,0:T(8,128)(2,1)S(1)}, bf16[448,256]{1,0:T(8,128)(2,1)S(1)}, u32[]{:S(2)}, u32[]{:S(2)}) collective-permute-start(bf16[448,256]{1,0:T(8,128)(2,1)S(1)} %fusion.31), channel_id=1, source_target_pairs={{16,0},{32,16},{48,32},{64,48},{80,64},{96,80},{112,96},{17,1},{33... | collective-permute-start | bytes 688136 | tf_op jit(solution)/shard_map/ppermute | solution.py:15
  123.6 5.7 %collective-permute-done.16 = bf16[448,256]{1,0:T(8,128)(2,1)S(1)} collective-permute-done((bf16[448,256]{1,0:T(8,128)(2,1)S(1)}, bf16[448,256]{1,0:T(8,128)(2,1)S(1)}, u32[]{:S(2)}, u32[]{:S(2)}) %collective-permute-start.16) | collective-permute-done | bytes 229408 | tf_op jit(solution)/shard_map/ppermute | solution.py:15
  129.3 1.4 fusion.17
  130.6 3.5 %collective-permute-start.17 = (bf16[224,256]{1,0:T(8,128)(2,1)S(1)}, bf16[224,256]{1,0:T(8,128)(2,1)S(1)}, u32[]{:S(2)}, u32[]{:S(2)}) collective-permute-start(bf16[224,256]{1,0:T(8,128)(2,1)S(1)} %get-tuple-element.9), channel_id=1, source_target_pairs={{0,128},{128,256},{256,384},{384,0},{1,129},{129,257},{257,385},{3... | collective-permute-start | bytes 344072 | tf_op jit(solution)/shard_map/ppermute | solution.py:82
  134.1 4.8 %collective-permute-start.18 = (bf16[224,256]{1,0:T(8,128)(2,1)S(1)}, bf16[224,256]{1,0:T(8,128)(2,1)S(1)}, u32[]{:S(2)}, u32[]{:S(2)}) collective-permute-start(bf16[224,256]{1,0:T(8,128)(2,1)S(1)} %get-tuple-element.10), channel_id=1, source_target_pairs={{0,256},{128,384},{256,0},{384,128},{1,257},{129,385},{257,1},{385... | collective-permute-start | bytes 344072 | tf_op jit(solution)/shard_map/ppermute | solution.py:83
  138.9 1.5 %fusion.14 = bf16[448,448]{1,0:T(8,128)(2,1)} fusion(f32[448,448]{1,0:T(8,128)S(1)} %fusion.32, f32[448,448]{1,0:T(8,128)S(1)} %fusion.35, f32[448,448]{1,0:T(8,128)S(1)} %fusion.38, f32[448,448]{1,0:T(8,128)S(1)} %fusion.41, f32[448,448]{1,0:T(8,128)S(1)} %fusion.44, f32[448,448]{1,0:T(8,128)S(1)} %fusion.47, f32[448,448]{1,0:T(8,128)S(1)} %fusion.50, ...), kind=kOutput, calls=%fused_computation.15 | convolution fusion | flops 105971712 | bytes 13705220 | tf_op jit(solution)/shard_map/dot_general | solution.py:19
  140.5 1.9 %collective-permute-done.18 = bf16[224,256]{1,0:T(8,128)(2,1)S(1)} collective-permute-done((bf16[224,256]{1,0:T(8,128)(2,1)S(1)}, bf16[224,256]{1,0:T(8,128)(2,1)S(1)}, u32[]{:S(2)}, u32[]{:S(2)}) %collective-permute-start.18) | collective-permute-done | bytes 114720 | tf_op jit(solution)/shard_map/ppermute | solution.py:83
  (68 shorter events, 12.7 us)
Async XLA Ops:
  0.6 37.2 %copy-start = (bf16[448,448]{1,0:T(8,128)(2,1)S(1)}, bf16[448,448]{1,0:T(8,128)(2,1)}, u32[]{:S(2)}) copy-start(bf16[448,448]{1,0:T(8,128)(2,1)} %param.6) | copy-start | bytes 1204228
  0.6 37.5 %collective-permute-start = (bf16[448,128]{1,0:T(8,128)(2,1)}, bf16[448,128]{1,0:T(8,128)(2,1)S(1)}, u32[]{:S(2)}, u32[]{:S(2)}) collective-permute-start(bf16[448,128]{1,0:T(8,128)(2,1)} %param.7), channel_id=1, source_target_pairs={{0,8},{8,0},{1,9},{9,1},{2,10},{10,2},{3,11},{11,3},{4,12},{12,4},... | collective-permute-start | bytes 344072 | tf_op jit(solution)/shard_map/ppermute | solution.py:32
  31.1 25.8 %collective-permute-start.1 = (bf16[448,256]{1,0:T(8,128)(2,1)S(1)}, bf16[448,256]{1,0:T(8,128)(2,1)S(1)}, u32[]{:S(2)}, u32[]{:S(2)}) collective-permute-start(bf16[448,256]{1,0:T(8,128)(2,1)S(1)} %broadcast_select_fusion), channel_id=1, source_target_pairs={{0,16},{16,32},{32,48},{48,64},{64,80},{80,96},{96,112},{1,17},{17... | collective-permute-start | bytes 688136 | tf_op jit(solution)/shard_map/ppermute | solution.py:15
  33.8 28.0 %collective-permute-start.9 = (bf16[448,256]{1,0:T(8,128)(2,1)S(1)}, bf16[448,256]{1,0:T(8,128)(2,1)S(1)}, u32[]{:S(2)}, u32[]{:S(2)}) collective-permute-start(bf16[448,256]{1,0:T(8,128)(2,1)S(1)} %broadcast_select_fusion), channel_id=1, source_target_pairs={{16,0},{32,16},{48,32},{64,48},{80,64},{96,80},{112,96},{17,1},{33... | collective-permute-start | bytes 688136 | tf_op jit(solution)/shard_map/ppermute | solution.py:15
  57.0 10.1 %collective-permute-start.2 = (bf16[448,256]{1,0:T(8,128)(2,1)S(1)}, bf16[448,256]{1,0:T(8,128)(2,1)S(1)}, u32[]{:S(2)}, u32[]{:S(2)}) collective-permute-start(bf16[448,256]{1,0:T(8,128)(2,1)S(1)} %fusion.18), channel_id=1, source_target_pairs={{0,16},{16,32},{32,48},{48,64},{64,80},{80,96},{96,112},{1,17},{17... | collective-permute-start | bytes 688136 | tf_op jit(solution)/shard_map/ppermute | solution.py:15
  61.9 10.9 %collective-permute-start.10 = (bf16[448,256]{1,0:T(8,128)(2,1)S(1)}, bf16[448,256]{1,0:T(8,128)(2,1)S(1)}, u32[]{:S(2)}, u32[]{:S(2)}) collective-permute-start(bf16[448,256]{1,0:T(8,128)(2,1)S(1)} %fusion.25), channel_id=1, source_target_pairs={{16,0},{32,16},{48,32},{64,48},{80,64},{96,80},{112,96},{17,1},{33... | collective-permute-start | bytes 688136 | tf_op jit(solution)/shard_map/ppermute | solution.py:15
  67.2 10.2 %collective-permute-start.3 = (bf16[448,256]{1,0:T(8,128)(2,1)S(1)}, bf16[448,256]{1,0:T(8,128)(2,1)S(1)}, u32[]{:S(2)}, u32[]{:S(2)}) collective-permute-start(bf16[448,256]{1,0:T(8,128)(2,1)S(1)} %fusion.19), channel_id=1, source_target_pairs={{0,16},{16,32},{32,48},{48,64},{64,80},{80,96},{96,112},{1,17},{17... | collective-permute-start | bytes 688136 | tf_op jit(solution)/shard_map/ppermute | solution.py:15
  72.9 10.1 %collective-permute-start.11 = (bf16[448,256]{1,0:T(8,128)(2,1)S(1)}, bf16[448,256]{1,0:T(8,128)(2,1)S(1)}, u32[]{:S(2)}, u32[]{:S(2)}) collective-permute-start(bf16[448,256]{1,0:T(8,128)(2,1)S(1)} %fusion.26), channel_id=1, source_target_pairs={{16,0},{32,16},{48,32},{64,48},{80,64},{96,80},{112,96},{17,1},{33... | collective-permute-start | bytes 688136 | tf_op jit(solution)/shard_map/ppermute | solution.py:15
  77.4 9.2 %collective-permute-start.4 = (bf16[448,256]{1,0:T(8,128)(2,1)S(1)}, bf16[448,256]{1,0:T(8,128)(2,1)S(1)}, u32[]{:S(2)}, u32[]{:S(2)}) collective-permute-start(bf16[448,256]{1,0:T(8,128)(2,1)S(1)} %fusion.20), channel_id=1, source_target_pairs={{0,16},{16,32},{32,48},{48,64},{64,80},{80,96},{96,112},{1,17},{17... | collective-permute-start | bytes 688136 | tf_op jit(solution)/shard_map/ppermute | solution.py:15
  83.1 9.2 %collective-permute-start.12 = (bf16[448,256]{1,0:T(8,128)(2,1)S(1)}, bf16[448,256]{1,0:T(8,128)(2,1)S(1)}, u32[]{:S(2)}, u32[]{:S(2)}) collective-permute-start(bf16[448,256]{1,0:T(8,128)(2,1)S(1)} %fusion.27), channel_id=1, source_target_pairs={{16,0},{32,16},{48,32},{64,48},{80,64},{96,80},{112,96},{17,1},{33... | collective-permute-start | bytes 688136 | tf_op jit(solution)/shard_map/ppermute | solution.py:15
  86.7 9.1 %collective-permute-start.5 = (bf16[448,256]{1,0:T(8,128)(2,1)S(1)}, bf16[448,256]{1,0:T(8,128)(2,1)S(1)}, u32[]{:S(2)}, u32[]{:S(2)}) collective-permute-start(bf16[448,256]{1,0:T(8,128)(2,1)S(1)} %fusion.21), channel_id=1, source_target_pairs={{0,16},{16,32},{32,48},{48,64},{64,80},{80,96},{96,112},{1,17},{17... | collective-permute-start | bytes 688136 | tf_op jit(solution)/shard_map/ppermute | solution.py:15
  92.4 9.1 %collective-permute-start.13 = (bf16[448,256]{1,0:T(8,128)(2,1)S(1)}, bf16[448,256]{1,0:T(8,128)(2,1)S(1)}, u32[]{:S(2)}, u32[]{:S(2)}) collective-permute-start(bf16[448,256]{1,0:T(8,128)(2,1)S(1)} %fusion.28), channel_id=1, source_target_pairs={{16,0},{32,16},{48,32},{64,48},{80,64},{96,80},{112,96},{17,1},{33... | collective-permute-start | bytes 688136 | tf_op jit(solution)/shard_map/ppermute | solution.py:15
  95.9 9.1 %collective-permute-start.6 = (bf16[448,256]{1,0:T(8,128)(2,1)S(1)}, bf16[448,256]{1,0:T(8,128)(2,1)S(1)}, u32[]{:S(2)}, u32[]{:S(2)}) collective-permute-start(bf16[448,256]{1,0:T(8,128)(2,1)S(1)} %fusion.22), channel_id=1, source_target_pairs={{0,16},{16,32},{32,48},{48,64},{64,80},{80,96},{96,112},{1,17},{17... | collective-permute-start | bytes 688136 | tf_op jit(solution)/shard_map/ppermute | solution.py:15
  101.6 9.1 %collective-permute-start.14 = (bf16[448,256]{1,0:T(8,128)(2,1)S(1)}, bf16[448,256]{1,0:T(8,128)(2,1)S(1)}, u32[]{:S(2)}, u32[]{:S(2)}) collective-permute-start(bf16[448,256]{1,0:T(8,128)(2,1)S(1)} %fusion.29), channel_id=1, source_target_pairs={{16,0},{32,16},{48,32},{64,48},{80,64},{96,80},{112,96},{17,1},{33... | collective-permute-start | bytes 688136 | tf_op jit(solution)/shard_map/ppermute | solution.py:15
  105.1 9.1 %collective-permute-start.7 = (bf16[448,256]{1,0:T(8,128)(2,1)S(1)}, bf16[448,256]{1,0:T(8,128)(2,1)S(1)}, u32[]{:S(2)}, u32[]{:S(2)}) collective-permute-start(bf16[448,256]{1,0:T(8,128)(2,1)S(1)} %fusion.23), channel_id=1, source_target_pairs={{0,16},{16,32},{32,48},{48,64},{64,80},{80,96},{96,112},{1,17},{17... | collective-permute-start | bytes 688136 | tf_op jit(solution)/shard_map/ppermute | solution.py:15
  110.8 9.3 %collective-permute-start.15 = (bf16[448,256]{1,0:T(8,128)(2,1)S(1)}, bf16[448,256]{1,0:T(8,128)(2,1)S(1)}, u32[]{:S(2)}, u32[]{:S(2)}) collective-permute-start(bf16[448,256]{1,0:T(8,128)(2,1)S(1)} %fusion.30), channel_id=1, source_target_pairs={{16,0},{32,16},{48,32},{64,48},{80,64},{96,80},{112,96},{17,1},{33... | collective-permute-start | bytes 688136 | tf_op jit(solution)/shard_map/ppermute | solution.py:15
  114.3 15.0 %copy-start.1 = (bf16[448,256]{1,0:T(8,128)(2,1)S(1)}, bf16[448,256]{1,0:T(8,128)(2,1)}, u32[]{:S(2)}) copy-start(bf16[448,256]{1,0:T(8,128)(2,1)} %param.8) | copy-start | bytes 688132
  114.3 15.0 %copy-start.2 = (f32[448,256]{1,0:T(8,128)S(1)}, f32[448,256]{1,0:T(8,128)}, u32[]{:S(2)}) copy-start(f32[448,256]{1,0:T(8,128)} %param.10) | copy-start | bytes 1376260
  114.3 15.0 %copy-start.3 = (f32[448,256]{1,0:T(8,128)S(1)}, f32[448,256]{1,0:T(8,128)}, u32[]{:S(2)}) copy-start(f32[448,256]{1,0:T(8,128)} %param.9) | copy-start | bytes 1376260
  114.3 9.3 %collective-permute-start.8 = (bf16[448,256]{1,0:T(8,128)(2,1)S(1)}, bf16[448,256]{1,0:T(8,128)(2,1)S(1)}, u32[]{:S(2)}, u32[]{:S(2)}) collective-permute-start(bf16[448,256]{1,0:T(8,128)(2,1)S(1)} %fusion.24), channel_id=1, source_target_pairs={{0,16},{16,32},{32,48},{48,64},{64,80},{80,96},{96,112},{1,17},{17... | collective-permute-start | bytes 688136 | tf_op jit(solution)/shard_map/ppermute | solution.py:15
  120.1 9.1 %collective-permute-start.16 = (bf16[448,256]{1,0:T(8,128)(2,1)S(1)}, bf16[448,256]{1,0:T(8,128)(2,1)S(1)}, u32[]{:S(2)}, u32[]{:S(2)}) collective-permute-start(bf16[448,256]{1,0:T(8,128)(2,1)S(1)} %fusion.31), channel_id=1, source_target_pairs={{16,0},{32,16},{48,32},{64,48},{80,64},{96,80},{112,96},{17,1},{33... | collective-permute-start | bytes 688136 | tf_op jit(solution)/shard_map/ppermute | solution.py:15
  130.6 9.8 %collective-permute-start.17 = (bf16[224,256]{1,0:T(8,128)(2,1)S(1)}, bf16[224,256]{1,0:T(8,128)(2,1)S(1)}, u32[]{:S(2)}, u32[]{:S(2)}) collective-permute-start(bf16[224,256]{1,0:T(8,128)(2,1)S(1)} %get-tuple-element.9), channel_id=1, source_target_pairs={{0,128},{128,256},{256,384},{384,0},{1,129},{129,257},{257,385},{3... | collective-permute-start | bytes 344072 | tf_op jit(solution)/shard_map/ppermute | solution.py:82
  134.1 8.2 %collective-permute-start.18 = (bf16[224,256]{1,0:T(8,128)(2,1)S(1)}, bf16[224,256]{1,0:T(8,128)(2,1)S(1)}, u32[]{:S(2)}, u32[]{:S(2)}) collective-permute-start(bf16[224,256]{1,0:T(8,128)(2,1)S(1)} %get-tuple-element.10), channel_id=1, source_target_pairs={{0,256},{128,384},{256,0},{384,128},{1,257},{129,385},{257,1},{385... | collective-permute-start | bytes 344072 | tf_op jit(solution)/shard_map/ppermute | solution.py:83

commit v3 on v2

v3 whole, which is shorter than its diff:
```python
import math

import jax
import jax.numpy as jnp
from jax import lax
from jax.sharding import Mesh, PartitionSpec as P

BF = jnp.bfloat16
F32 = jnp.float32
LINE = 8


def along(value, way, step):
    chips = range(step + 1) if way == 1 else range(LINE - 1, LINE - 2 - step, -1)
    return lax.ppermute(value, "zl", [(chip, chip + way) for chip in chips])


def contract(left, right, dims):
    return lax.dot_general(left, right, (dims, ((), ())), preferred_element_type=F32)


def body(hidden, upstream, weights, first_moment, second_moment, step_index):
    width = weights.shape[1]
    place, far_half = lax.axis_index("zl"), lax.axis_index("zh")
    scale_hid = 1.0 / math.sqrt(7168)
    never = step_index[0] < 0

    all_weights = lax.all_gather(weights, "zl", axis=1, tiled=True)
    up_other = lax.ppermute(upstream, "zh", [(0, 1), (1, 0)])
    near_up = lax.all_gather(upstream, ("x", "c"), axis=1, tiled=True)
    far_up = lax.all_gather(up_other, ("x", "c"), axis=1, tiled=True)
    full_up = jnp.concatenate([near_up, far_up], axis=1)
    hidden_t = lax.optimization_barrier(hidden.T)

    def up_block(index):
        at = jnp.bitwise_xor(index, 4 * far_half) * width
        return lax.dynamic_slice_in_dim(full_up, at, width, 1)

    carried, sent = {}, {}
    for step in range(LINE - 1):
        for way in (1, -1):
            position = place if way == 1 else LINE - 1 - place
            block = jnp.clip(LINE - 1 - step + position, 0, LINE - 1)
            block = block if way == 1 else LINE - 1 - block
            features = up_block(block)
            if step > 0:
                features = jnp.where(never, sent[way], features)
            part = lax.optimization_barrier(contract(hidden_t, features, ((1,), (0,))))
            sent[way] = (part + carried[way].astype(F32) if step > 0 else part).astype(BF)
            carried[way] = along(sent[way], way, step)

    own_up = jnp.where(never, sent[1], up_block(place))
    own_part = lax.optimization_barrier(contract(hidden_t, own_up, ((1,), (0,))))
    grads = (own_part + carried[1].astype(F32) + carried[-1].astype(F32)) * scale_hid

    count = (step_index[0] + 1).astype(F32)
    first_new = 0.9 * first_moment + 0.1 * grads
    second_new = 0.999 * second_moment + 0.001 * grads * grads
    correct_one = 1.0 - jnp.power(F32(0.9), count)
    correct_two = 1.0 - jnp.power(F32(0.999), count)
    weights_f = weights.astype(F32)
    step_size = first_new / correct_one / (jnp.sqrt(second_new / correct_two) + 1e-08) + 0.1 * weights_f
    updated = (weights_f - 0.05 * step_size).astype(BF)

    half = updated.shape[0] // 2
    even_step = step_index[0] % 2 == 0
    lower, upper = updated[:half], updated[half:]
    near = lax.ppermute(jnp.where(even_step, lower, upper), "y", [(i, (i + 1) % 4) for i in range(4)])
    far = lax.ppermute(jnp.where(even_step, upper, lower), "y", [(i, (i + 2) % 4) for i in range(4)])
    partner = jnp.concatenate([jnp.where(even_step, near, far), jnp.where(even_step, far, near)], 0)
    mixed = ((updated.astype(F32) + partner.astype(F32)) * 0.5).astype(BF)

    ordered_up = jnp.where(far_half == 0, full_up, jnp.concatenate([far_up, near_up], axis=1))
    in_grad = (contract(ordered_up, all_weights, ((1,), (1,))) * scale_hid).astype(BF)
    return mixed, first_new, second_new, in_grad


def solution(mesh):
    split = Mesh(mesh.devices.reshape(4, LINE, 2, 4, 2), ("y", "zl", "zh", "x", "c"))
    rep, tp = ("y", "zl"), ("zh", "x", "c")
    in_specs = (P(rep, tp), P(rep, tp), P(tp, rep), P(tp, rep), P(tp, rep), P())
    out_specs = (P(tp, rep), P(tp, rep), P(tp, rep), P(rep, tp))
    return jax.shard_map(body, mesh=split, in_specs=in_specs, out_specs=out_specs, check_vma=False)
```

time: 144 us -> 157 us (1.090)
  the two profiles are of different devices: /device:TPU:96 before, /device:TPU:14 now
where the time goes in v3:
time: 157 us
  starting transfers between devices  57.2 us (36%)
  waiting for transfers between devices  44 us (28%)
  blocking collectives  27 us (17%)
  between operations  15.3 us (10%)
  matrix products  8.98 us (6%)
  other arithmetic  4.37 us (3%)
    ppermute x14, waiting for transfers between devices, along(): return lax.ppermute(value, 'zl', [(chip, chip + way) for chip in chips])  37.7 us
    ppermute x14, starting transfers between devices, along(): return lax.ppermute(value, 'zl', [(chip, chip + way) for chip in chips])  34.9 us
    ppermute x1, starting transfers between devices, body(): up_other = lax.ppermute(upstream, 'zh', [(0, 1), (1, 0)])  15.9 us
    all_gather x1, blocking collectives, body(): near_up = lax.all_gather(upstream, ('x', 'c'), axis=1, tiled=True)  13.6 us
    all_gather x1, blocking collectives, body(): far_up = lax.all_gather(up_other, ('x', 'c'), axis=1, tiled=True)  13.4 us
    dot_general x16, matrix products, contract(): lax.dot_general(left, right, (dims, ((), ())), preferred_element_type=F32)  8.98 us
    ppermute x1, waiting for transfers between devices, body(): lax.ppermute(jnp.where(even_step, upper, lower), 'y', [(i, (i + 2) % 4) f...  5.81 us
    ppermute x1, starting transfers between devices, body(): lax.ppermute(jnp.where(even_step, lower, upper), 'y', [(i, (i + 1) % 4) f...  4.18 us
  transfers between devices with their start and end apart: 18, of which 10 were waited for; matrix products, arithmetic and copies ran while one was open for 6% of the time, Pallas kernels for 0%

profile of v3, /device:TPU:14, one launch (start us, length us, event | category | flops | bytes accessed | tf_op | source)
XLA Modules:
  0.0 157.0 jit_solution(7803839825928341890)
XLA Ops:
  7.2 15.9 %collective-permute-start = (bf16[448,128]{1,0:T(8,128)(2,1)}, bf16[448,128]{1,0:T(8,128)(2,1)S(1)}, u32[]{:S(2)}, u32[]{:S(2)}) collective-permute-start(bf16[448,128]{1,0:T(8,128)(2,1)} %param.7), channel_id=1, source_target_pairs={{0,8},{8,0},{1,9},{9,1},{2,10},{10,2},{3,11},{11,3},{4,12},{12,4},... | collective-permute-start | bytes 344072 | tf_op jit(solution)/shard_map/ppermute | solution.py:29
  23.1 13.6 %all_gather.9 = bf16[448,1024]{1,0:T(8,128)(2,1)S(1)} all-gather(bf16[448,128]{1,0:T(8,128)(2,1)} %param.7), channel_id=1, replica_groups=mesh['y'=4,'zl'=8,'zh'=2,'x'=4,'c'=2] {'x','c'}, dimensions={1}, use_global_device_ids=true | all-gather | bytes 1032192 | tf_op jit(solution)/shard_map/all_gather | solution.py:30
  37.6 13.4 %all_gather.10 = bf16[448,1024]{1,0:T(8,128)(2,1)S(1)} all-gather(bf16[448,128]{1,0:T(8,128)(2,1)S(1)} %collective-permute-done), channel_id=1, replica_groups=mesh['y'=4,'zl'=8,'zh'=2,'x'=4,'c'=2] {'x','c'}, dimensions={1}, use_global_device_ids=true | all-gather | bytes 1032192 | tf_op jit(solution)/shard_map/all_gather | solution.py:31
  51.4 3.2 %collective-permute-start.1 = (bf16[448,256]{1,0:T(8,128)(2,1)S(1)}, bf16[448,256]{1,0:T(8,128)(2,1)S(1)}, u32[]{:S(2)}, u32[]{:S(2)}) collective-permute-start(bf16[448,256]{1,0:T(8,128)(2,1)S(1)} %convolution_bitcast_fusion.14), channel_id=1, source_target_pairs={{0,16},{1,17},{2,18},{3,19},{4,20},{5,21},{6,22},{7,23},{8,24},{9,... | collective-permute-start | bytes 688136 | tf_op jit(solution)/shard_map/ppermute | solution.py:15
  55.4 0.7 collective-permute-start.8
  56.4 8.5 %collective-permute-done.1 = bf16[448,256]{1,0:T(8,128)(2,1)S(1)} collective-permute-done((bf16[448,256]{1,0:T(8,128)(2,1)S(1)}, bf16[448,256]{1,0:T(8,128)(2,1)S(1)}, u32[]{:S(2)}, u32[]{:S(2)}) %collective-permute-start.1) | collective-permute-done | bytes 229408 | tf_op jit(solution)/shard_map/ppermute | solution.py:15
  65.0 4.4 %collective-permute-start.2 = (bf16[448,256]{1,0:T(8,128)(2,1)S(1)}, bf16[448,256]{1,0:T(8,128)(2,1)S(1)}, u32[]{:S(2)}, u32[]{:S(2)}) collective-permute-start(bf16[448,256]{1,0:T(8,128)(2,1)S(1)} %add_convert_fusion.11), channel_id=1, source_target_pairs={{0,16},{16,32},{1,17},{17,33},{2,18},{18,34},{3,19},{19,35},{4,20}... | collective-permute-start | bytes 688136 | tf_op jit(solution)/shard_map/ppermute | solution.py:15
  69.8 0.7 collective-permute-start.9
  70.9 7.1 %collective-permute-done.2 = bf16[448,256]{1,0:T(8,128)(2,1)S(1)} collective-permute-done((bf16[448,256]{1,0:T(8,128)(2,1)S(1)}, bf16[448,256]{1,0:T(8,128)(2,1)S(1)}, u32[]{:S(2)}, u32[]{:S(2)}) %collective-permute-start.2) | collective-permute-done | bytes 229408 | tf_op jit(solution)/shard_map/ppermute | solution.py:15
  78.1 4.4 %collective-permute-start.3 = (bf16[448,256]{1,0:T(8,128)(2,1)S(1)}, bf16[448,256]{1,0:T(8,128)(2,1)S(1)}, u32[]{:S(2)}, u32[]{:S(2)}) collective-permute-start(bf16[448,256]{1,0:T(8,128)(2,1)S(1)} %add_convert_fusion.10), channel_id=1, source_target_pairs={{0,16},{16,32},{32,48},{1,17},{17,33},{33,49},{2,18},{18,34},{34,5... | collective-permute-start | bytes 688136 | tf_op jit(solution)/shard_map/ppermute | solution.py:15
  82.9 0.7 collective-permute-start.10
  84.0 7.5 %collective-permute-done.3 = bf16[448,256]{1,0:T(8,128)(2,1)S(1)} collective-permute-done((bf16[448,256]{1,0:T(8,128)(2,1)S(1)}, bf16[448,256]{1,0:T(8,128)(2,1)S(1)}, u32[]{:S(2)}, u32[]{:S(2)}) %collective-permute-start.3) | collective-permute-done | bytes 229408 | tf_op jit(solution)/shard_map/ppermute | solution.py:15
  91.6 4.4 %collective-permute-start.4 = (bf16[448,256]{1,0:T(8,128)(2,1)S(1)}, bf16[448,256]{1,0:T(8,128)(2,1)S(1)}, u32[]{:S(2)}, u32[]{:S(2)}) collective-permute-start(bf16[448,256]{1,0:T(8,128)(2,1)S(1)} %add_convert_fusion.9), channel_id=1, source_target_pairs={{0,16},{16,32},{32,48},{48,64},{1,17},{17,33},{33,49},{49,65},{2,1... | collective-permute-start | bytes 688136 | tf_op jit(solution)/shard_map/ppermute | solution.py:15
  96.4 0.7 collective-permute-start.11
  97.5 2.0 %collective-permute-done.4 = bf16[448,256]{1,0:T(8,128)(2,1)S(1)} collective-permute-done((bf16[448,256]{1,0:T(8,128)(2,1)S(1)}, bf16[448,256]{1,0:T(8,128)(2,1)S(1)}, u32[]{:S(2)}, u32[]{:S(2)}) %collective-permute-start.4) | collective-permute-done | bytes 229408 | tf_op jit(solution)/shard_map/ppermute | solution.py:15
  99.5 4.4 %collective-permute-start.5 = (bf16[448,256]{1,0:T(8,128)(2,1)S(1)}, bf16[448,256]{1,0:T(8,128)(2,1)S(1)}, u32[]{:S(2)}, u32[]{:S(2)}) collective-permute-start(bf16[448,256]{1,0:T(8,128)(2,1)S(1)} %add_convert_fusion.8), channel_id=1, source_target_pairs={{0,16},{16,32},{32,48},{48,64},{64,80},{1,17},{17,33},{33,49},{49,... | collective-permute-start | bytes 688136 | tf_op jit(solution)/shard_map/ppermute | solution.py:15
  104.4 0.7 collective-permute-start.12
  105.4 2.5 %collective-permute-done.5 = bf16[448,256]{1,0:T(8,128)(2,1)S(1)} collective-permute-done((bf16[448,256]{1,0:T(8,128)(2,1)S(1)}, bf16[448,256]{1,0:T(8,128)(2,1)S(1)}, u32[]{:S(2)}, u32[]{:S(2)}) %collective-permute-start.5) | collective-permute-done | bytes 229408 | tf_op jit(solution)/shard_map/ppermute | solution.py:15
  108.0 4.4 %collective-permute-start.6 = (bf16[448,256]{1,0:T(8,128)(2,1)S(1)}, bf16[448,256]{1,0:T(8,128)(2,1)S(1)}, u32[]{:S(2)}, u32[]{:S(2)}) collective-permute-start(bf16[448,256]{1,0:T(8,128)(2,1)S(1)} %add_convert_fusion.7), channel_id=1, source_target_pairs={{0,16},{16,32},{32,48},{48,64},{64,80},{80,96},{1,17},{17,33},{33,... | collective-permute-start | bytes 688136 | tf_op jit(solution)/shard_map/ppermute | solution.py:15
  113.9 3.6 %collective-permute-done.6 = bf16[448,256]{1,0:T(8,128)(2,1)S(1)} collective-permute-done((bf16[448,256]{1,0:T(8,128)(2,1)S(1)}, bf16[448,256]{1,0:T(8,128)(2,1)S(1)}, u32[]{:S(2)}, u32[]{:S(2)}) %collective-permute-start.6) | collective-permute-done | bytes 229408 | tf_op jit(solution)/shard_map/ppermute | solution.py:15
  117.6 4.4 %collective-permute-start.7 = (bf16[448,256]{1,0:T(8,128)(2,1)S(1)}, bf16[448,256]{1,0:T(8,128)(2,1)S(1)}, u32[]{:S(2)}, u32[]{:S(2)}) collective-permute-start(bf16[448,256]{1,0:T(8,128)(2,1)S(1)} %add_convert_fusion.6), channel_id=1, source_target_pairs={{0,16},{16,32},{32,48},{48,64},{64,80},{80,96},{96,112},{1,17},{17... | collective-permute-start | bytes 688136 | tf_op jit(solution)/shard_map/ppermute | solution.py:15
  122.0 1.3 collective-permute-start.14
  123.7 1.8 %collective-permute-done.7 = bf16[448,256]{1,0:T(8,128)(2,1)S(1)} collective-permute-done((bf16[448,256]{1,0:T(8,128)(2,1)S(1)}, bf16[448,256]{1,0:T(8,128)(2,1)S(1)}, u32[]{:S(2)}, u32[]{:S(2)}) %collective-permute-start.7) | collective-permute-done | bytes 229408 | tf_op jit(solution)/shard_map/ppermute | solution.py:15
  125.5 4.5 %collective-permute-done.14 = bf16[448,256]{1,0:T(8,128)(2,1)S(1)} collective-permute-done((bf16[448,256]{1,0:T(8,128)(2,1)S(1)}, bf16[448,256]{1,0:T(8,128)(2,1)S(1)}, u32[]{:S(2)}, u32[]{:S(2)}) %collective-permute-start.14) | collective-permute-done | bytes 229408 | tf_op jit(solution)/shard_map/ppermute | solution.py:15
  130.0 1.4 fusion.8
  131.3 0.7 broadcast_select_fusion.3
  132.0 4.2 %collective-permute-start.15 = (bf16[224,256]{1,0:T(8,128)(2,1)}, bf16[224,256]{1,0:T(8,128)(2,1)S(1)}, u32[]{:S(2)}, u32[]{:S(2)}) collective-permute-start(bf16[224,256]{1,0:T(8,128)(2,1)} %get-tuple-element.9), channel_id=1, source_target_pairs={{0,128},{128,256},{256,384},{384,0},{1,129},{129,257},{257,385},{3... | collective-permute-start | bytes 344072 | tf_op jit(solution)/shard_map/ppermute | solution.py:68
  136.2 2.2 %collective-permute-start.16 = (bf16[224,256]{1,0:T(8,128)(2,1)}, bf16[224,256]{1,0:T(8,128)(2,1)}, u32[]{:S(2)}, u32[]{:S(2)}) collective-permute-start(bf16[224,256]{1,0:T(8,128)(2,1)} %get-tuple-element.10), channel_id=1, source_target_pairs={{0,256},{128,384},{256,0},{384,128},{1,257},{129,385},{257,1},{385... | collective-permute-start | bytes 344072 | tf_op jit(solution)/shard_map/ppermute | solution.py:69
  138.9 5.8 %collective-permute-done.16 = bf16[224,256]{1,0:T(8,128)(2,1)} collective-permute-done((bf16[224,256]{1,0:T(8,128)(2,1)}, bf16[224,256]{1,0:T(8,128)(2,1)}, u32[]{:S(2)}, u32[]{:S(2)}) %collective-permute-start.16) | collective-permute-done | bytes 114720 | tf_op jit(solution)/shard_map/ppermute | solution.py:69
  144.7 0.9 broadcast_select_fusion.1
  145.6 0.8 multiply_convert_fusion
  146.4 3.7 %fusion.5 = bf16[448,448]{1,0:T(8,128)(2,1)} fusion(bf16[448,2048]{1,0:T(8,128)(2,1)} %all-gather.2.cloned.1.call-done, bf16[448,2048]{1,0:T(8,128)(2,1)S(1)} %constant_dynamic-update-slice_fusion, bf16[448,1024]{1,0:T(8,128)(2,1)S(1)} %all_gather.9, bf16[448,1024]{1,0:T(8,128)(2,1)} %copy-done.1, pred[]{:T(512)S(6)} %eq.9), kind=kOutput, calls=%fused_computation.6 | convolution fusion | flops 827072512 | bytes 5906433 | tf_op jit(solution)/shard_map/dot_general | solution.py:19
  (51 shorter events, 7.4 us)
Async XLA Ops:
  7.2 30.2 %copy-start = (bf16[448,448]{1,0:T(8,128)(2,1)S(1)}, bf16[448,448]{1,0:T(8,128)(2,1)}, u32[]{:S(2)}) copy-start(bf16[448,448]{1,0:T(8,128)(2,1)} %param.6) | copy-start | bytes 1204228
  7.2 139.2 %all-gather.2.cloned.1.call-start = ((), (), s32[]{:S(2)}) async-start(), calls=%async_computation | async-start | bytes 2064384 | tf_op jit(solution)/shard_map/all_gather | solution.py:28
  7.2 30.4 %collective-permute-start = (bf16[448,128]{1,0:T(8,128)(2,1)}, bf16[448,128]{1,0:T(8,128)(2,1)S(1)}, u32[]{:S(2)}, u32[]{:S(2)}) collective-permute-start(bf16[448,128]{1,0:T(8,128)(2,1)} %param.7), channel_id=1, source_target_pairs={{0,8},{8,0},{1,9},{9,1},{2,10},{10,2},{3,11},{11,3},{4,12},{12,4},... | collective-permute-start | bytes 344072 | tf_op jit(solution)/shard_map/ppermute | solution.py:29
  51.0 4.0 %copy-start.1 = (bf16[448,1024]{1,0:T(8,128)(2,1)}, bf16[448,1024]{1,0:T(8,128)(2,1)S(1)}, u32[]{:S(2)}) copy-start(bf16[448,1024]{1,0:T(8,128)(2,1)S(1)} %all_gather.10) | copy-start | bytes 2752516
  51.4 13.5 %collective-permute-start.1 = (bf16[448,256]{1,0:T(8,128)(2,1)S(1)}, bf16[448,256]{1,0:T(8,128)(2,1)S(1)}, u32[]{:S(2)}, u32[]{:S(2)}) collective-permute-start(bf16[448,256]{1,0:T(8,128)(2,1)S(1)} %convolution_bitcast_fusion.14), channel_id=1, source_target_pairs={{0,16},{1,17},{2,18},{3,19},{4,20},{5,21},{6,22},{7,23},{8,24},{9,... | collective-permute-start | bytes 688136 | tf_op jit(solution)/shard_map/ppermute | solution.py:15
  55.4 14.4 %collective-permute-start.8 = (bf16[448,256]{1,0:T(8,128)(2,1)S(1)}, bf16[448,256]{1,0:T(8,128)(2,1)S(1)}, u32[]{:S(2)}, u32[]{:S(2)}) collective-permute-start(bf16[448,256]{1,0:T(8,128)(2,1)S(1)} %convolution_bitcast_fusion.6), channel_id=1, source_target_pairs={{112,96},{113,97},{114,98},{115,99},{116,100},{117,101},{118,102},... | collective-permute-start | bytes 688136 | tf_op jit(solution)/shard_map/ppermute | solution.py:15
  65.0 13.0 %collective-permute-start.2 = (bf16[448,256]{1,0:T(8,128)(2,1)S(1)}, bf16[448,256]{1,0:T(8,128)(2,1)S(1)}, u32[]{:S(2)}, u32[]{:S(2)}) collective-permute-start(bf16[448,256]{1,0:T(8,128)(2,1)S(1)} %add_convert_fusion.11), channel_id=1, source_target_pairs={{0,16},{16,32},{1,17},{17,33},{2,18},{18,34},{3,19},{19,35},{4,20}... | collective-permute-start | bytes 688136 | tf_op jit(solution)/shard_map/ppermute | solution.py:15
  69.8 13.0 %collective-permute-start.9 = (bf16[448,256]{1,0:T(8,128)(2,1)S(1)}, bf16[448,256]{1,0:T(8,128)(2,1)S(1)}, u32[]{:S(2)}, u32[]{:S(2)}) collective-permute-start(bf16[448,256]{1,0:T(8,128)(2,1)S(1)} %add_convert_fusion.5), channel_id=1, source_target_pairs={{112,96},{96,80},{113,97},{97,81},{114,98},{98,82},{115,99},{99,83... | collective-permute-start | bytes 688136 | tf_op jit(solution)/shard_map/ppermute | solution.py:15
  78.1 13.4 %collective-permute-start.3 = (bf16[448,256]{1,0:T(8,128)(2,1)S(1)}, bf16[448,256]{1,0:T(8,128)(2,1)S(1)}, u32[]{:S(2)}, u32[]{:S(2)}) collective-permute-start(bf16[448,256]{1,0:T(8,128)(2,1)S(1)} %add_convert_fusion.10), channel_id=1, source_target_pairs={{0,16},{16,32},{32,48},{1,17},{17,33},{33,49},{2,18},{18,34},{34,5... | collective-permute-start | bytes 688136 | tf_op jit(solution)/shard_map/ppermute | solution.py:15
  82.9 13.4 %collective-permute-start.10 = (bf16[448,256]{1,0:T(8,128)(2,1)S(1)}, bf16[448,256]{1,0:T(8,128)(2,1)S(1)}, u32[]{:S(2)}, u32[]{:S(2)}) collective-permute-start(bf16[448,256]{1,0:T(8,128)(2,1)S(1)} %add_convert_fusion.4), channel_id=1, source_target_pairs={{112,96},{96,80},{80,64},{113,97},{97,81},{81,65},{114,98},{98,82}... | collective-permute-start | bytes 688136 | tf_op jit(solution)/shard_map/ppermute | solution.py:15
  91.6 7.9 %collective-permute-start.4 = (bf16[448,256]{1,0:T(8,128)(2,1)S(1)}, bf16[448,256]{1,0:T(8,128)(2,1)S(1)}, u32[]{:S(2)}, u32[]{:S(2)}) collective-permute-start(bf16[448,256]{1,0:T(8,128)(2,1)S(1)} %add_convert_fusion.9), channel_id=1, source_target_pairs={{0,16},{16,32},{32,48},{48,64},{1,17},{17,33},{33,49},{49,65},{2,1... | collective-permute-start | bytes 688136 | tf_op jit(solution)/shard_map/ppermute | solution.py:15
  96.4 7.9 %collective-permute-start.11 = (bf16[448,256]{1,0:T(8,128)(2,1)S(1)}, bf16[448,256]{1,0:T(8,128)(2,1)S(1)}, u32[]{:S(2)}, u32[]{:S(2)}) collective-permute-start(bf16[448,256]{1,0:T(8,128)(2,1)S(1)} %add_convert_fusion.3), channel_id=1, source_target_pairs={{112,96},{96,80},{80,64},{64,48},{113,97},{97,81},{81,65},{65,49},... | collective-permute-start | bytes 688136 | tf_op jit(solution)/shard_map/ppermute | solution.py:15
  99.5 8.4 %collective-permute-start.5 = (bf16[448,256]{1,0:T(8,128)(2,1)S(1)}, bf16[448,256]{1,0:T(8,128)(2,1)S(1)}, u32[]{:S(2)}, u32[]{:S(2)}) collective-permute-start(bf16[448,256]{1,0:T(8,128)(2,1)S(1)} %add_convert_fusion.8), channel_id=1, source_target_pairs={{0,16},{16,32},{32,48},{48,64},{64,80},{1,17},{17,33},{33,49},{49,... | collective-permute-start | bytes 688136 | tf_op jit(solution)/shard_map/ppermute | solution.py:15
  104.4 8.4 %collective-permute-start.12 = (bf16[448,256]{1,0:T(8,128)(2,1)S(1)}, bf16[448,256]{1,0:T(8,128)(2,1)S(1)}, u32[]{:S(2)}, u32[]{:S(2)}) collective-permute-start(bf16[448,256]{1,0:T(8,128)(2,1)S(1)} %add_convert_fusion.2), channel_id=1, source_target_pairs={{112,96},{96,80},{80,64},{64,48},{48,32},{113,97},{97,81},{81,65},... | collective-permute-start | bytes 688136 | tf_op jit(solution)/shard_map/ppermute | solution.py:15
  108.0 9.5 %collective-permute-start.6 = (bf16[448,256]{1,0:T(8,128)(2,1)S(1)}, bf16[448,256]{1,0:T(8,128)(2,1)S(1)}, u32[]{:S(2)}, u32[]{:S(2)}) collective-permute-start(bf16[448,256]{1,0:T(8,128)(2,1)S(1)} %add_convert_fusion.7), channel_id=1, source_target_pairs={{0,16},{16,32},{32,48},{48,64},{64,80},{80,96},{1,17},{17,33},{33,... | collective-permute-start | bytes 688136 | tf_op jit(solution)/shard_map/ppermute | solution.py:15
  112.8 9.2 %collective-permute-start.13 = (bf16[448,256]{1,0:T(8,128)(2,1)S(1)}, bf16[448,256]{1,0:T(8,128)(2,1)S(1)}, u32[]{:S(2)}, u32[]{:S(2)}) collective-permute-start(bf16[448,256]{1,0:T(8,128)(2,1)S(1)} %add_convert_fusion.1), channel_id=1, source_target_pairs={{112,96},{96,80},{80,64},{64,48},{48,32},{32,16},{113,97},{97,81},... | collective-permute-start | bytes 688136 | tf_op jit(solution)/shard_map/ppermute | solution.py:15
  113.8 16.1 %copy-start.2 = (bf16[448,256]{1,0:T(8,128)(2,1)S(1)}, bf16[448,256]{1,0:T(8,128)(2,1)}, u32[]{:S(2)}) copy-start(bf16[448,256]{1,0:T(8,128)(2,1)} %param.8) | copy-start | bytes 688132
  113.9 16.1 %copy-start.3 = (f32[448,256]{1,0:T(8,128)S(1)}, f32[448,256]{1,0:T(8,128)}, u32[]{:S(2)}) copy-start(f32[448,256]{1,0:T(8,128)} %param.10) | copy-start | bytes 1376260
  113.9 16.1 %copy-start.4 = (f32[448,256]{1,0:T(8,128)S(1)}, f32[448,256]{1,0:T(8,128)}, u32[]{:S(2)}) copy-start(f32[448,256]{1,0:T(8,128)} %param.9) | copy-start | bytes 1376260
  117.6 7.9 %collective-permute-start.7 = (bf16[448,256]{1,0:T(8,128)(2,1)S(1)}, bf16[448,256]{1,0:T(8,128)(2,1)S(1)}, u32[]{:S(2)}, u32[]{:S(2)}) collective-permute-start(bf16[448,256]{1,0:T(8,128)(2,1)S(1)} %add_convert_fusion.6), channel_id=1, source_target_pairs={{0,16},{16,32},{32,48},{48,64},{64,80},{80,96},{96,112},{1,17},{17... | collective-permute-start | bytes 688136 | tf_op jit(solution)/shard_map/ppermute | solution.py:15
  122.0 7.9 %collective-permute-start.14 = (bf16[448,256]{1,0:T(8,128)(2,1)S(1)}, bf16[448,256]{1,0:T(8,128)(2,1)S(1)}, u32[]{:S(2)}, u32[]{:S(2)}) collective-permute-start(bf16[448,256]{1,0:T(8,128)(2,1)S(1)} %add_convert_fusion), channel_id=1, source_target_pairs={{112,96},{96,80},{80,64},{64,48},{48,32},{32,16},{16,0},{113,97},{... | collective-permute-start | bytes 688136 | tf_op jit(solution)/shard_map/ppermute | solution.py:15
  132.0 6.9 %collective-permute-start.15 = (bf16[224,256]{1,0:T(8,128)(2,1)}, bf16[224,256]{1,0:T(8,128)(2,1)S(1)}, u32[]{:S(2)}, u32[]{:S(2)}) collective-permute-start(bf16[224,256]{1,0:T(8,128)(2,1)} %get-tuple-element.9), channel_id=1, source_target_pairs={{0,128},{128,256},{256,384},{384,0},{1,129},{129,257},{257,385},{3... | collective-permute-start | bytes 344072 | tf_op jit(solution)/shard_map/ppermute | solution.py:68
  136.2 8.5 %collective-permute-start.16 = (bf16[224,256]{1,0:T(8,128)(2,1)}, bf16[224,256]{1,0:T(8,128)(2,1)}, u32[]{:S(2)}, u32[]{:S(2)}) collective-permute-start(bf16[224,256]{1,0:T(8,128)(2,1)} %get-tuple-element.10), channel_id=1, source_target_pairs={{0,256},{128,384},{256,0},{384,128},{1,257},{129,385},{257,1},{385... | collective-permute-start | bytes 344072 | tf_op jit(solution)/shard_map/ppermute | solution.py:69
Sparse Core Ops, SparseCore 0:
  23.2 75.3 all-gather.1

commit v4 on v2

--- a/solution.py
+++ b/solution.py
@@ -19,15 +19,13 @@
     return lax.dot_general(left, right, (dims, ((), ())), preferred_element_type=F32)
 
 
-def after(value, other):
-    mark = other[0, 0]
-    return jnp.where(mark != mark, jnp.zeros((), value.dtype), value)
-
-
 def body(hidden, upstream, weights, first_moment, second_moment, step_index):
     width = weights.shape[1]
     place, far_half = lax.axis_index("zl"), lax.axis_index("zh")
     scale_hid = 1.0 / math.sqrt(7168)
+
+    def behind(value, other):
+        return jnp.where(step_index[0] < 0, other, value)
 
     up_other = lax.ppermute(upstream, "zh", [(0, 1), (1, 0)])
     near_up = lax.all_gather(upstream, ("x", "c"), axis=1, tiled=True)
@@ -39,10 +37,9 @@
         at = jnp.bitwise_xor(index, 4 * far_half) * width
         return lax.dynamic_slice_in_dim(full_up, at, width, 1)
 
-    own_up = up_block(place)
-    hg_total = contract(own_up, weights, ((1,), (1,)))
-    start = after(weights, near_up)
-    carried = {1: start, -1: start}
+    start = behind(weights, near_up[:, :width])
+    carried, sent = {1: start, -1: start}, {}
+    hg_total = contract(behind(up_block(place), start), weights, ((1,), (1,)))
     for step in range(LINE - 1 + LEAD):
         turn = step - LEAD
         for way in (1, -1):
@@ -51,8 +48,12 @@
             if turn >= 0:
                 block = jnp.clip(LINE - 1 - turn + position, 0, LINE - 1)
                 block = block if way == 1 else LINE - 1 - block
-                part = lax.optimization_barrier(contract(hidden_t, up_block(block), ((1,), (0,))))
+                features = up_block(block)
+                if turn > 0:
+                    features = behind(features, sent[way])
+                part = lax.optimization_barrier(contract(hidden_t, features, ((1,), (0,))))
                 payload = jnp.where(position <= turn, (payload.astype(F32) + part).astype(BF), payload)
+            sent[way] = payload
             carried[way] = along(payload, way)
         for way in (1, -1):
             if step < LINE - 1:
@@ -64,6 +65,7 @@
                 features = jnp.where(valid, up_block(source), jnp.zeros((), BF))
                 hg_total = hg_total + contract(features, carried[way], ((1,), (1,)))
 
+    own_up = behind(up_block(place), sent[1])
     own_part = lax.optimization_barrier(contract(hidden_t, own_up, ((1,), (0,))))
     grads = (own_part + carried[1].astype(F32) + carried[-1].astype(F32)) * scale_hid
 

time: 144 us -> 138 us (0.958)
  the two profiles are of different devices: /device:TPU:96 before, /device:TPU:104 now
where the time goes in v4:
time: 138 us; the launch traced here: 137 us
  starting transfers between devices  77.2 us (56%)
  blocking collectives  27.9 us (20%)
  waiting for transfers between devices  14.5 us (11%)
  matrix products  11 us (8%)
  other arithmetic  4.04 us (3%)
  between operations  2.28 us (2%)
    ppermute x16, starting transfers between devices, along(): lax.ppermute(value, 'zl', [(i, i + way) for i in range(LINE) if 0 <= i +...  57.7 us
    all_gather x1, blocking collectives, body(): near_up = lax.all_gather(upstream, ('x', 'c'), axis=1, tiled=True)  14.5 us
    all_gather x1, blocking collectives, body(): far_up = lax.all_gather(up_other, ('x', 'c'), axis=1, tiled=True)  13.3 us
    ppermute x1, starting transfers between devices, body(): up_other = lax.ppermute(upstream, 'zh', [(0, 1), (1, 0)])  13.2 us
    dot_general x30, matrix products, contract(): lax.dot_general(left, right, (dims, ((), ())), preferred_element_type=F32)  11 us
    ppermute x16, waiting for transfers between devices, along(): lax.ppermute(value, 'zl', [(i, i + way) for i in range(LINE) if 0 <= i +...  10.7 us
    ppermute x1, waiting for transfers between devices, body(): lax.ppermute(jnp.where(even_step, upper, lower), 'y', [(i, (i + 2) % 4) f...  3.85 us
    ppermute x1, starting transfers between devices, body(): lax.ppermute(jnp.where(even_step, lower, upper), 'y', [(i, (i + 1) % 4) f...  3.49 us
  transfers between devices with their start and end apart: 19, of which 9 were waited for; matrix products, arithmetic and copies ran while one was open for 10% of the time, Pallas kernels for 0%

profile of v4, /device:TPU:104, one launch (start us, length us, event | category | flops | bytes accessed | tf_op | source)
XLA Modules:
  0.0 137.1 jit_solution(16790942593613446709)
XLA Ops:
  0.6 13.2 %collective-permute-start.1 = (bf16[448,128]{1,0:T(8,128)(2,1)}, bf16[448,128]{1,0:T(8,128)(2,1)S(1)}, u32[]{:S(2)}, u32[]{:S(2)}) collective-permute-start(bf16[448,128]{1,0:T(8,128)(2,1)} %param.7), channel_id=1, source_target_pairs={{0,8},{8,0},{1,9},{9,1},{2,10},{10,2},{3,11},{11,3},{4,12},{12,4},... | collective-permute-start | bytes 344072 | tf_op jit(solution)/shard_map/ppermute | solution.py:30
  13.8 14.5 %all_gather.6 = bf16[448,1024]{1,0:T(8,128)(2,1)S(1)} all-gather(bf16[448,128]{1,0:T(8,128)(2,1)} %param.7), channel_id=1, replica_groups=mesh['y'=4,'zl'=8,'zh'=2,'x'=4,'c'=2] {'x','c'}, dimensions={1}, use_global_device_ids=true | all-gather | bytes 1032192 | tf_op jit(solution)/shard_map/all_gather | solution.py:31
  29.0 1.0 slice_select_fusion
  30.0 2.7 %collective-permute-start = (bf16[448,256]{1,0:T(8,128)(2,1)S(1)}, bf16[448,256]{1,0:T(8,128)(2,1)S(1)}, u32[]{:S(2)}, u32[]{:S(2)}) collective-permute-start(bf16[448,256]{1,0:T(8,128)(2,1)S(1)} %slice_select_fusion), channel_id=1, source_target_pairs={{0,16},{16,32},{32,48},{48,64},{64,80},{80,96},{96,112},{1,17},{17... | collective-permute-start | bytes 688136 | tf_op jit(solution)/shard_map/ppermute | solution.py:15
  32.6 3.2 %collective-permute-start.9 = (bf16[448,256]{1,0:T(8,128)(2,1)S(1)}, bf16[448,256]{1,0:T(8,128)(2,1)S(1)}, u32[]{:S(2)}, u32[]{:S(2)}) collective-permute-start(bf16[448,256]{1,0:T(8,128)(2,1)S(1)} %slice_select_fusion), channel_id=1, source_target_pairs={{16,0},{32,16},{48,32},{64,48},{80,64},{96,80},{112,96},{17,1},{33... | collective-permute-start | bytes 688136 | tf_op jit(solution)/shard_map/ppermute | solution.py:15
  36.4 13.3 %all_gather.7 = bf16[448,1024]{1,0:T(8,128)(2,1)S(1)} all-gather(bf16[448,128]{1,0:T(8,128)(2,1)S(1)} %collective-permute-done.1), channel_id=1, replica_groups=mesh['y'=4,'zl'=8,'zh'=2,'x'=4,'c'=2] {'x','c'}, dimensions={1}, use_global_device_ids=true | all-gather | bytes 1032192 | tf_op jit(solution)/shard_map/all_gather | solution.py:32
  50.6 4.8 %collective-permute-start.2 = (bf16[448,256]{1,0:T(8,128)(2,1)S(1)}, bf16[448,256]{1,0:T(8,128)(2,1)S(1)}, u32[]{:S(2)}, u32[]{:S(2)}) collective-permute-start(bf16[448,256]{1,0:T(8,128)(2,1)S(1)} %fusion.17), channel_id=1, source_target_pairs={{0,16},{16,32},{32,48},{48,64},{64,80},{80,96},{96,112},{1,17},{17... | collective-permute-start | bytes 688136 | tf_op jit(solution)/shard_map/ppermute | solution.py:15
  55.8 2.1 %collective-permute-start.10 = (bf16[448,256]{1,0:T(8,128)(2,1)S(1)}, bf16[448,256]{1,0:T(8,128)(2,1)S(1)}, u32[]{:S(2)}, u32[]{:S(2)}) collective-permute-start(bf16[448,256]{1,0:T(8,128)(2,1)S(1)} %fusion.24), channel_id=1, source_target_pairs={{16,0},{32,16},{48,32},{64,48},{80,64},{96,80},{112,96},{17,1},{33... | collective-permute-start | bytes 688136 | tf_op jit(solution)/shard_map/ppermute | solution.py:15
  58.9 1.9 %collective-permute-done.2 = bf16[448,256]{1,0:T(8,128)(2,1)S(1)} collective-permute-done((bf16[448,256]{1,0:T(8,128)(2,1)S(1)}, bf16[448,256]{1,0:T(8,128)(2,1)S(1)}, u32[]{:S(2)}, u32[]{:S(2)}) %collective-permute-start.2) | collective-permute-done | bytes 229408 | tf_op jit(solution)/shard_map/ppermute | solution.py:15
  60.8 5.6 %collective-permute-start.3 = (bf16[448,256]{1,0:T(8,128)(2,1)S(1)}, bf16[448,256]{1,0:T(8,128)(2,1)S(1)}, u32[]{:S(2)}, u32[]{:S(2)}) collective-permute-start(bf16[448,256]{1,0:T(8,128)(2,1)S(1)} %fusion.18), channel_id=1, source_target_pairs={{0,16},{16,32},{32,48},{48,64},{64,80},{80,96},{96,112},{1,17},{17... | collective-permute-start | bytes 688136 | tf_op jit(solution)/shard_map/ppermute | solution.py:15
  66.8 1.9 %collective-permute-start.11 = (bf16[448,256]{1,0:T(8,128)(2,1)S(1)}, bf16[448,256]{1,0:T(8,128)(2,1)S(1)}, u32[]{:S(2)}, u32[]{:S(2)}) collective-permute-start(bf16[448,256]{1,0:T(8,128)(2,1)S(1)} %fusion.25), channel_id=1, source_target_pairs={{16,0},{32,16},{48,32},{64,48},{80,64},{96,80},{112,96},{17,1},{33... | collective-permute-start | bytes 688136 | tf_op jit(solution)/shard_map/ppermute | solution.py:15
  69.7 1.2 collective-permute-done.3
  71.0 5.6 %collective-permute-start.4 = (bf16[448,256]{1,0:T(8,128)(2,1)S(1)}, bf16[448,256]{1,0:T(8,128)(2,1)S(1)}, u32[]{:S(2)}, u32[]{:S(2)}) collective-permute-start(bf16[448,256]{1,0:T(8,128)(2,1)S(1)} %fusion.19), channel_id=1, source_target_pairs={{0,16},{16,32},{32,48},{48,64},{64,80},{80,96},{96,112},{1,17},{17... | collective-permute-start | bytes 688136 | tf_op jit(solution)/shard_map/ppermute | solution.py:15
  77.1 1.9 %collective-permute-start.12 = (bf16[448,256]{1,0:T(8,128)(2,1)S(1)}, bf16[448,256]{1,0:T(8,128)(2,1)S(1)}, u32[]{:S(2)}, u32[]{:S(2)}) collective-permute-start(bf16[448,256]{1,0:T(8,128)(2,1)S(1)} %fusion.26), channel_id=1, source_target_pairs={{16,0},{32,16},{48,32},{64,48},{80,64},{96,80},{112,96},{17,1},{33... | collective-permute-start | bytes 688136 | tf_op jit(solution)/shard_map/ppermute | solution.py:15
  80.3 5.6 %collective-permute-start.5 = (bf16[448,256]{1,0:T(8,128)(2,1)S(1)}, bf16[448,256]{1,0:T(8,128)(2,1)S(1)}, u32[]{:S(2)}, u32[]{:S(2)}) collective-permute-start(bf16[448,256]{1,0:T(8,128)(2,1)S(1)} %fusion.20), channel_id=1, source_target_pairs={{0,16},{16,32},{32,48},{48,64},{64,80},{80,96},{96,112},{1,17},{17... | collective-permute-start | bytes 688136 | tf_op jit(solution)/shard_map/ppermute | solution.py:15
  86.4 1.9 %collective-permute-start.13 = (bf16[448,256]{1,0:T(8,128)(2,1)S(1)}, bf16[448,256]{1,0:T(8,128)(2,1)S(1)}, u32[]{:S(2)}, u32[]{:S(2)}) collective-permute-start(bf16[448,256]{1,0:T(8,128)(2,1)S(1)} %fusion.27), channel_id=1, source_target_pairs={{16,0},{32,16},{48,32},{64,48},{80,64},{96,80},{112,96},{17,1},{33... | collective-permute-start | bytes 688136 | tf_op jit(solution)/shard_map/ppermute | solution.py:15
  89.5 5.6 %collective-permute-start.6 = (bf16[448,256]{1,0:T(8,128)(2,1)S(1)}, bf16[448,256]{1,0:T(8,128)(2,1)S(1)}, u32[]{:S(2)}, u32[]{:S(2)}) collective-permute-start(bf16[448,256]{1,0:T(8,128)(2,1)S(1)} %fusion.21), channel_id=1, source_target_pairs={{0,16},{16,32},{32,48},{48,64},{64,80},{80,96},{96,112},{1,17},{17... | collective-permute-start | bytes 688136 | tf_op jit(solution)/shard_map/ppermute | solution.py:15
  95.2 0.4 convolution_bitcast_fusion.9
  95.6 1.9 %collective-permute-start.14 = (bf16[448,256]{1,0:T(8,128)(2,1)S(1)}, bf16[448,256]{1,0:T(8,128)(2,1)S(1)}, u32[]{:S(2)}, u32[]{:S(2)}) collective-permute-start(bf16[448,256]{1,0:T(8,128)(2,1)S(1)} %fusion.28), channel_id=1, source_target_pairs={{16,0},{32,16},{48,32},{64,48},{80,64},{96,80},{112,96},{17,1},{33... | collective-permute-start | bytes 688136 | tf_op jit(solution)/shard_map/ppermute | solution.py:15
  98.7 5.6 %collective-permute-start.7 = (bf16[448,256]{1,0:T(8,128)(2,1)S(1)}, bf16[448,256]{1,0:T(8,128)(2,1)S(1)}, u32[]{:S(2)}, u32[]{:S(2)}) collective-permute-start(bf16[448,256]{1,0:T(8,128)(2,1)S(1)} %fusion.22), channel_id=1, source_target_pairs={{0,16},{16,32},{32,48},{48,64},{64,80},{80,96},{96,112},{1,17},{17... | collective-permute-start | bytes 688136 | tf_op jit(solution)/shard_map/ppermute | solution.py:15
  104.3 0.4 collective-permute-done.14
  104.8 1.9 %collective-permute-start.15 = (bf16[448,256]{1,0:T(8,128)(2,1)S(1)}, bf16[448,256]{1,0:T(8,128)(2,1)S(1)}, u32[]{:S(2)}, u32[]{:S(2)}) collective-permute-start(bf16[448,256]{1,0:T(8,128)(2,1)S(1)} %fusion.29), channel_id=1, source_target_pairs={{16,0},{32,16},{48,32},{64,48},{80,64},{96,80},{112,96},{17,1},{33... | collective-permute-start | bytes 688136 | tf_op jit(solution)/shard_map/ppermute | solution.py:15
  108.1 5.4 %collective-permute-start.8 = (bf16[448,256]{1,0:T(8,128)(2,1)S(1)}, bf16[448,256]{1,0:T(8,128)(2,1)S(1)}, u32[]{:S(2)}, u32[]{:S(2)}) collective-permute-start(bf16[448,256]{1,0:T(8,128)(2,1)S(1)} %fusion.23), channel_id=1, source_target_pairs={{0,16},{16,32},{32,48},{48,64},{64,80},{80,96},{96,112},{1,17},{17... | collective-permute-start | bytes 688136 | tf_op jit(solution)/shard_map/ppermute | solution.py:15
  114.0 2.1 %collective-permute-start.16 = (bf16[448,256]{1,0:T(8,128)(2,1)S(1)}, bf16[448,256]{1,0:T(8,128)(2,1)S(1)}, u32[]{:S(2)}, u32[]{:S(2)}) collective-permute-start(bf16[448,256]{1,0:T(8,128)(2,1)S(1)} %fusion.30), channel_id=1, source_target_pairs={{16,0},{32,16},{48,32},{64,48},{80,64},{96,80},{112,96},{17,1},{33... | collective-permute-start | bytes 688136 | tf_op jit(solution)/shard_map/ppermute | solution.py:15
  116.7 0.4 collective-permute-done.8
  117.1 6.2 %collective-permute-done.16 = bf16[448,256]{1,0:T(8,128)(2,1)S(1)} collective-permute-done((bf16[448,256]{1,0:T(8,128)(2,1)S(1)}, bf16[448,256]{1,0:T(8,128)(2,1)S(1)}, u32[]{:S(2)}, u32[]{:S(2)}) %collective-permute-start.16) | collective-permute-done | bytes 229408 | tf_op jit(solution)/shard_map/ppermute | solution.py:15
  123.3 1.4 fusion.16
  124.6 3.5 %collective-permute-start.17 = (bf16[224,256]{1,0:T(8,128)(2,1)S(1)}, bf16[224,256]{1,0:T(8,128)(2,1)S(1)}, u32[]{:S(2)}, u32[]{:S(2)}) collective-permute-start(bf16[224,256]{1,0:T(8,128)(2,1)S(1)} %get-tuple-element.9), channel_id=1, source_target_pairs={{0,128},{128,256},{256,384},{384,0},{1,129},{129,257},{257,385},{3... | collective-permute-start | bytes 344072 | tf_op jit(solution)/shard_map/ppermute | solution.py:84
  128.1 2.8 %collective-permute-start.18 = (bf16[224,256]{1,0:T(8,128)(2,1)S(1)}, bf16[224,256]{1,0:T(8,128)(2,1)S(1)}, u32[]{:S(2)}, u32[]{:S(2)}) collective-permute-start(bf16[224,256]{1,0:T(8,128)(2,1)S(1)} %get-tuple-element.10), channel_id=1, source_target_pairs={{0,256},{128,384},{256,0},{384,128},{1,257},{129,385},{257,1},{385... | collective-permute-start | bytes 344072 | tf_op jit(solution)/shard_map/ppermute | solution.py:85
  131.0 1.5 %fusion.13 = bf16[448,448]{1,0:T(8,128)(2,1)} fusion(f32[448,448]{1,0:T(8,128)S(1)} %fusion.31, f32[448,448]{1,0:T(8,128)S(1)} %fusion.34, f32[448,448]{1,0:T(8,128)S(1)} %fusion.37, f32[448,448]{1,0:T(8,128)S(1)} %fusion.40, f32[448,448]{1,0:T(8,128)S(1)} %fusion.43, f32[448,448]{1,0:T(8,128)S(1)} %fusion.46, f32[448,448]{1,0:T(8,128)S(1)} %fusion.49, ...), kind=kOutput, calls=%fused_computation.15 | convolution fusion | flops 105885696 | bytes 12787717 | tf_op jit(solution)/shard_map/dot_general | solution.py:19
  132.5 3.9 %collective-permute-done.18 = bf16[224,256]{1,0:T(8,128)(2,1)S(1)} collective-permute-done((bf16[224,256]{1,0:T(8,128)(2,1)S(1)}, bf16[224,256]{1,0:T(8,128)(2,1)S(1)}, u32[]{:S(2)}, u32[]{:S(2)}) %collective-permute-start.18) | collective-permute-done | bytes 114720 | tf_op jit(solution)/shard_map/ppermute | solution.py:85
  136.4 0.8 multiply_convert_fusion
  (67 shorter events, 11.0 us)
Async XLA Ops:
  0.6 35.4 %copy-start = (bf16[448,448]{1,0:T(8,128)(2,1)S(1)}, bf16[448,448]{1,0:T(8,128)(2,1)}, u32[]{:S(2)}) copy-start(bf16[448,448]{1,0:T(8,128)(2,1)} %param.6) | copy-start | bytes 1204228
  0.6 35.7 %collective-permute-start.1 = (bf16[448,128]{1,0:T(8,128)(2,1)}, bf16[448,128]{1,0:T(8,128)(2,1)S(1)}, u32[]{:S(2)}, u32[]{:S(2)}) collective-permute-start(bf16[448,128]{1,0:T(8,128)(2,1)} %param.7), channel_id=1, source_target_pairs={{0,8},{8,0},{1,9},{9,1},{2,10},{10,2},{3,11},{11,3},{4,12},{12,4},... | collective-permute-start | bytes 344072 | tf_op jit(solution)/shard_map/ppermute | solution.py:30
  30.0 20.6 %collective-permute-start = (bf16[448,256]{1,0:T(8,128)(2,1)S(1)}, bf16[448,256]{1,0:T(8,128)(2,1)S(1)}, u32[]{:S(2)}, u32[]{:S(2)}) collective-permute-start(bf16[448,256]{1,0:T(8,128)(2,1)S(1)} %slice_select_fusion), channel_id=1, source_target_pairs={{0,16},{16,32},{32,48},{48,64},{64,80},{80,96},{96,112},{1,17},{17... | collective-permute-start | bytes 688136 | tf_op jit(solution)/shard_map/ppermute | solution.py:15
  32.6 23.1 %collective-permute-start.9 = (bf16[448,256]{1,0:T(8,128)(2,1)S(1)}, bf16[448,256]{1,0:T(8,128)(2,1)S(1)}, u32[]{:S(2)}, u32[]{:S(2)}) collective-permute-start(bf16[448,256]{1,0:T(8,128)(2,1)S(1)} %slice_select_fusion), channel_id=1, source_target_pairs={{16,0},{32,16},{48,32},{64,48},{80,64},{96,80},{112,96},{17,1},{33... | collective-permute-start | bytes 688136 | tf_op jit(solution)/shard_map/ppermute | solution.py:15
  50.6 10.1 %collective-permute-start.2 = (bf16[448,256]{1,0:T(8,128)(2,1)S(1)}, bf16[448,256]{1,0:T(8,128)(2,1)S(1)}, u32[]{:S(2)}, u32[]{:S(2)}) collective-permute-start(bf16[448,256]{1,0:T(8,128)(2,1)S(1)} %fusion.17), channel_id=1, source_target_pairs={{0,16},{16,32},{32,48},{48,64},{64,80},{80,96},{96,112},{1,17},{17... | collective-permute-start | bytes 688136 | tf_op jit(solution)/shard_map/ppermute | solution.py:15
  55.7 2.8 %copy-start.1 = (bf16[448,256]{1,0:T(8,128)(2,1)S(1)}, bf16[448,256]{1,0:T(8,128)(2,1)}, u32[]{:S(2)}) copy-start(bf16[448,256]{1,0:T(8,128)(2,1)} %param.8) | copy-start | bytes 688132
  55.8 10.9 %collective-permute-start.10 = (bf16[448,256]{1,0:T(8,128)(2,1)S(1)}, bf16[448,256]{1,0:T(8,128)(2,1)S(1)}, u32[]{:S(2)}, u32[]{:S(2)}) collective-permute-start(bf16[448,256]{1,0:T(8,128)(2,1)S(1)} %fusion.24), channel_id=1, source_target_pairs={{16,0},{32,16},{48,32},{64,48},{80,64},{96,80},{112,96},{17,1},{33... | collective-permute-start | bytes 688136 | tf_op jit(solution)/shard_map/ppermute | solution.py:15
  60.8 10.2 %collective-permute-start.3 = (bf16[448,256]{1,0:T(8,128)(2,1)S(1)}, bf16[448,256]{1,0:T(8,128)(2,1)S(1)}, u32[]{:S(2)}, u32[]{:S(2)}) collective-permute-start(bf16[448,256]{1,0:T(8,128)(2,1)S(1)} %fusion.18), channel_id=1, source_target_pairs={{0,16},{16,32},{32,48},{48,64},{64,80},{80,96},{96,112},{1,17},{17... | collective-permute-start | bytes 688136 | tf_op jit(solution)/shard_map/ppermute | solution.py:15
  66.8 10.2 %collective-permute-start.11 = (bf16[448,256]{1,0:T(8,128)(2,1)S(1)}, bf16[448,256]{1,0:T(8,128)(2,1)S(1)}, u32[]{:S(2)}, u32[]{:S(2)}) collective-permute-start(bf16[448,256]{1,0:T(8,128)(2,1)S(1)} %fusion.25), channel_id=1, source_target_pairs={{16,0},{32,16},{48,32},{64,48},{80,64},{96,80},{112,96},{17,1},{33... | collective-permute-start | bytes 688136 | tf_op jit(solution)/shard_map/ppermute | solution.py:15
  71.0 9.2 %collective-permute-start.4 = (bf16[448,256]{1,0:T(8,128)(2,1)S(1)}, bf16[448,256]{1,0:T(8,128)(2,1)S(1)}, u32[]{:S(2)}, u32[]{:S(2)}) collective-permute-start(bf16[448,256]{1,0:T(8,128)(2,1)S(1)} %fusion.19), channel_id=1, source_target_pairs={{0,16},{16,32},{32,48},{48,64},{64,80},{80,96},{96,112},{1,17},{17... | collective-permute-start | bytes 688136 | tf_op jit(solution)/shard_map/ppermute | solution.py:15
  77.1 9.2 %collective-permute-start.12 = (bf16[448,256]{1,0:T(8,128)(2,1)S(1)}, bf16[448,256]{1,0:T(8,128)(2,1)S(1)}, u32[]{:S(2)}, u32[]{:S(2)}) collective-permute-start(bf16[448,256]{1,0:T(8,128)(2,1)S(1)} %fusion.26), channel_id=1, source_target_pairs={{16,0},{32,16},{48,32},{64,48},{80,64},{96,80},{112,96},{17,1},{33... | collective-permute-start | bytes 688136 | tf_op jit(solution)/shard_map/ppermute | solution.py:15
  80.3 9.1 %collective-permute-start.5 = (bf16[448,256]{1,0:T(8,128)(2,1)S(1)}, bf16[448,256]{1,0:T(8,128)(2,1)S(1)}, u32[]{:S(2)}, u32[]{:S(2)}) collective-permute-start(bf16[448,256]{1,0:T(8,128)(2,1)S(1)} %fusion.20), channel_id=1, source_target_pairs={{0,16},{16,32},{32,48},{48,64},{64,80},{80,96},{96,112},{1,17},{17... | collective-permute-start | bytes 688136 | tf_op jit(solution)/shard_map/ppermute | solution.py:15
  86.4 9.1 %collective-permute-start.13 = (bf16[448,256]{1,0:T(8,128)(2,1)S(1)}, bf16[448,256]{1,0:T(8,128)(2,1)S(1)}, u32[]{:S(2)}, u32[]{:S(2)}) collective-permute-start(bf16[448,256]{1,0:T(8,128)(2,1)S(1)} %fusion.27), channel_id=1, source_target_pairs={{16,0},{32,16},{48,32},{64,48},{80,64},{96,80},{112,96},{17,1},{33... | collective-permute-start | bytes 688136 | tf_op jit(solution)/shard_map/ppermute | solution.py:15
  89.5 9.1 %collective-permute-start.6 = (bf16[448,256]{1,0:T(8,128)(2,1)S(1)}, bf16[448,256]{1,0:T(8,128)(2,1)S(1)}, u32[]{:S(2)}, u32[]{:S(2)}) collective-permute-start(bf16[448,256]{1,0:T(8,128)(2,1)S(1)} %fusion.21), channel_id=1, source_target_pairs={{0,16},{16,32},{32,48},{48,64},{64,80},{80,96},{96,112},{1,17},{17... | collective-permute-start | bytes 688136 | tf_op jit(solution)/shard_map/ppermute | solution.py:15
  95.6 9.1 %collective-permute-start.14 = (bf16[448,256]{1,0:T(8,128)(2,1)S(1)}, bf16[448,256]{1,0:T(8,128)(2,1)S(1)}, u32[]{:S(2)}, u32[]{:S(2)}) collective-permute-start(bf16[448,256]{1,0:T(8,128)(2,1)S(1)} %fusion.28), channel_id=1, source_target_pairs={{16,0},{32,16},{48,32},{64,48},{80,64},{96,80},{112,96},{17,1},{33... | collective-permute-start | bytes 688136 | tf_op jit(solution)/shard_map/ppermute | solution.py:15
  98.7 9.3 %collective-permute-start.7 = (bf16[448,256]{1,0:T(8,128)(2,1)S(1)}, bf16[448,256]{1,0:T(8,128)(2,1)S(1)}, u32[]{:S(2)}, u32[]{:S(2)}) collective-permute-start(bf16[448,256]{1,0:T(8,128)(2,1)S(1)} %fusion.22), channel_id=1, source_target_pairs={{0,16},{16,32},{32,48},{48,64},{64,80},{80,96},{96,112},{1,17},{17... | collective-permute-start | bytes 688136 | tf_op jit(solution)/shard_map/ppermute | solution.py:15
  104.8 9.1 %collective-permute-start.15 = (bf16[448,256]{1,0:T(8,128)(2,1)S(1)}, bf16[448,256]{1,0:T(8,128)(2,1)S(1)}, u32[]{:S(2)}, u32[]{:S(2)}) collective-permute-start(bf16[448,256]{1,0:T(8,128)(2,1)S(1)} %fusion.29), channel_id=1, source_target_pairs={{16,0},{32,16},{48,32},{64,48},{80,64},{96,80},{112,96},{17,1},{33... | collective-permute-start | bytes 688136 | tf_op jit(solution)/shard_map/ppermute | solution.py:15
  108.1 8.9 %collective-permute-start.8 = (bf16[448,256]{1,0:T(8,128)(2,1)S(1)}, bf16[448,256]{1,0:T(8,128)(2,1)S(1)}, u32[]{:S(2)}, u32[]{:S(2)}) collective-permute-start(bf16[448,256]{1,0:T(8,128)(2,1)S(1)} %fusion.23), channel_id=1, source_target_pairs={{0,16},{16,32},{32,48},{48,64},{64,80},{80,96},{96,112},{1,17},{17... | collective-permute-start | bytes 688136 | tf_op jit(solution)/shard_map/ppermute | solution.py:15
  113.9 9.4 %copy-start.2 = (f32[448,256]{1,0:T(8,128)S(1)}, f32[448,256]{1,0:T(8,128)}, u32[]{:S(2)}) copy-start(f32[448,256]{1,0:T(8,128)} %param.10) | copy-start | bytes 1376260
  113.9 9.3 %copy-start.3 = (f32[448,256]{1,0:T(8,128)S(1)}, f32[448,256]{1,0:T(8,128)}, u32[]{:S(2)}) copy-start(f32[448,256]{1,0:T(8,128)} %param.9) | copy-start | bytes 1376260
  114.0 9.3 %collective-permute-start.16 = (bf16[448,256]{1,0:T(8,128)(2,1)S(1)}, bf16[448,256]{1,0:T(8,128)(2,1)S(1)}, u32[]{:S(2)}, u32[]{:S(2)}) collective-permute-start(bf16[448,256]{1,0:T(8,128)(2,1)S(1)} %fusion.30), channel_id=1, source_target_pairs={{16,0},{32,16},{48,32},{64,48},{80,64},{96,80},{112,96},{17,1},{33... | collective-permute-start | bytes 688136 | tf_op jit(solution)/shard_map/ppermute | solution.py:15
  124.6 7.8 %collective-permute-start.17 = (bf16[224,256]{1,0:T(8,128)(2,1)S(1)}, bf16[224,256]{1,0:T(8,128)(2,1)S(1)}, u32[]{:S(2)}, u32[]{:S(2)}) collective-permute-start(bf16[224,256]{1,0:T(8,128)(2,1)S(1)} %get-tuple-element.9), channel_id=1, source_target_pairs={{0,128},{128,256},{256,384},{384,0},{1,129},{129,257},{257,385},{3... | collective-permute-start | bytes 344072 | tf_op jit(solution)/shard_map/ppermute | solution.py:84
  128.1 8.2 %collective-permute-start.18 = (bf16[224,256]{1,0:T(8,128)(2,1)S(1)}, bf16[224,256]{1,0:T(8,128)(2,1)S(1)}, u32[]{:S(2)}, u32[]{:S(2)}) collective-permute-start(bf16[224,256]{1,0:T(8,128)(2,1)S(1)} %get-tuple-element.10), channel_id=1, source_target_pairs={{0,256},{128,384},{256,0},{384,128},{1,257},{129,385},{257,1},{385... | collective-permute-start | bytes 344072 | tf_op jit(solution)/shard_map/ppermute | solution.py:85

commit v5 on v3

v5 whole, which is shorter than its diff:
```python
import math

import jax
import jax.numpy as jnp
from jax import lax
from jax.sharding import Mesh, PartitionSpec as P

BF = jnp.bfloat16
F32 = jnp.float32
LINE = 8


def along(value, early):
    pairs = []
    for half in range(2):
        way = 1 if (half == 1) == early else -1
        pairs += [(i * 2 + half, (i + way) * 2 + half) for i in range(LINE) if 0 <= i + way < LINE]
    return lax.ppermute(value, ("zl", "zh"), pairs)


def contract(left, right, dims):
    return lax.dot_general(left, right, (dims, ((), ())), preferred_element_type=F32)


def body(hidden, upstream, weights, first_moment, second_moment, step_index):
    width = weights.shape[1]
    place, far_half = lax.axis_index("zl"), lax.axis_index("zh")
    scale_hid = 1.0 / math.sqrt(7168)

    def behind(value, other):
        return jnp.where(step_index[0] < 0, other, value)

    last = LINE - 1
    early_up = far_half == 1
    position = jnp.where(early_up, place, last - place)

    up_other = lax.ppermute(upstream, "zh", [(0, 1), (1, 0)])
    hidden_t = lax.optimization_barrier(hidden.T)
    got = {True: [along(weights, True)], False: []}
    sent = {}

    def send(early, turn, part):
        here = position if early else last - position
        arrived = got[early][-1]
        total = (arrived.astype(F32) + part).astype(BF)
        sent[early, turn] = jnp.where(here <= turn, total, arrived)
        got[early].append(along(sent[early, turn], early))

    def product(features):
        return lax.optimization_barrier(contract(hidden_t, features, ((1,), (0,))))

    near_up = lax.all_gather(upstream, ("x", "c"), axis=1, tiled=True)
    got[False].append(along(behind(weights, near_up[:, :width]), False))
    first = lax.dynamic_slice_in_dim(near_up, jnp.where(early_up, 3, 0) * width, width, 1)
    send(True, 0, product(first))
    up_other = behind(up_other, sent[True, 0][:, : up_other.shape[1]])
    far_up = lax.all_gather(up_other, ("x", "c"), axis=1, tiled=True)
    full_up = jnp.concatenate([near_up, far_up], axis=1)

    def up_block(index):
        at = jnp.bitwise_xor(index, 4 * far_half) * width
        return lax.dynamic_slice_in_dim(full_up, at, width, 1)

    def features_of(pair):
        index = jnp.where(pair >= position, last - pair + position, position - 1 - pair)
        return up_block(jnp.where(early_up, index, last - index))

    parts = {}

    def part_of(pair, after):
        if pair not in parts:
            features = features_of(pair)
            parts[pair] = product(features if after is None else behind(features, sent[after]))
        return parts[pair]

    hg_total = contract(behind(up_block(place), sent[True, 0]), weights, ((1,), (1,)))
    for turn in range(last):
        send(False, turn, part_of(last - 1 - turn, (False, turn - 1) if 0 < turn < last - 1 else (False, 3) if turn else None))
        if turn < last - 1:
            send(True, turn + 1, part_of(turn + 1, (True, turn) if turn else None))
        for pair in {turn, last - 1 - turn} if turn >= last // 2 else ():
            block = jnp.where(pair < position, got[True][pair], got[False][last - 1 - pair])
            hg_total = hg_total + contract(features_of(pair), block, ((1,), (1,)))

    own_part = product(behind(up_block(place), sent[False, 4]))
    grads = (own_part + got[True][-1].astype(F32) + got[False][-1].astype(F32)) * scale_hid

    count = (step_index[0] + 1).astype(F32)
    first_new = 0.9 * first_moment + 0.1 * grads
    second_new = 0.999 * second_moment + 0.001 * grads * grads
    correct_one = 1.0 - jnp.power(F32(0.9), count)
    correct_two = 1.0 - jnp.power(F32(0.999), count)
    weights_f = weights.astype(F32)
    step_size = first_new / correct_one / (jnp.sqrt(second_new / correct_two) + 1e-08) + 0.1 * weights_f
    updated = (weights_f - 0.05 * step_size).astype(BF)

    half = updated.shape[0] // 2
    even_step = step_index[0] % 2 == 0
    lower, upper = updated[:half], updated[half:]
    near = lax.ppermute(jnp.where(even_step, lower, upper), "y", [(i, (i + 1) % 4) for i in range(4)])
    far = lax.ppermute(jnp.where(even_step, upper, lower), "y", [(i, (i + 2) % 4) for i in range(4)])
    partner = jnp.concatenate([jnp.where(even_step, near, far), jnp.where(even_step, far, near)], 0)
    mixed = ((updated.astype(F32) + partner.astype(F32)) * 0.5).astype(BF)

    in_grad = (hg_total * scale_hid).astype(BF)
    return mixed, first_new, second_new, in_grad


def solution(mesh):
    split = Mesh(mesh.devices.reshape(4, LINE, 2, 4, 2), ("y", "zl", "zh", "x", "c"))
    rep, tp = ("y", "zl"), ("zh", "x", "c")
    in_specs = (P(rep, tp), P(rep, tp), P(tp, rep), P(tp, rep), P(tp, rep), P())
    out_specs = (P(tp, rep), P(tp, rep), P(tp, rep), P(rep, tp))
    return jax.shard_map(body, mesh=split, in_specs=in_specs, out_specs=out_specs, check_vma=False)
```

time: 157 us -> 148 us (0.943)
  the two profiles are of different devices: /device:TPU:14 before, /device:TPU:128 now
where the time goes in v5:
time: 148 us; the launch traced here: 147 us
  starting transfers between devices  74.7 us (50%)
  waiting for transfers between devices  31 us (21%)
  blocking collectives  28.5 us (19%)
  matrix products  6.63 us (4%)
  other arithmetic  4.04 us (3%)
  between operations  2 us (1%)
    ppermute x16, starting transfers between devices, along(): return lax.ppermute(value, ('zl', 'zh'), pairs)  54.6 us
    ppermute x16, waiting for transfers between devices, along(): return lax.ppermute(value, ('zl', 'zh'), pairs)  28.9 us
    all_gather x1, blocking collectives, body(): near_up = lax.all_gather(upstream, ('x', 'c'), axis=1, tiled=True)  14.4 us
    all_gather x1, blocking collectives, body(): far_up = lax.all_gather(up_other, ('x', 'c'), axis=1, tiled=True)  14.1 us
    ppermute x1, starting transfers between devices, body(): up_other = lax.ppermute(upstream, 'zh', [(0, 1), (1, 0)])  11.8 us
    dot_general x17, matrix products, contract(): lax.dot_general(left, right, (dims, ((), ())), preferred_element_type=F32)  6.63 us
    ppermute x1, starting transfers between devices, body(): lax.ppermute(jnp.where(even_step, upper, lower), 'y', [(i, (i + 2) % 4) f...  4.81 us
    ppermute x1, starting transfers between devices, body(): lax.ppermute(jnp.where(even_step, lower, upper), 'y', [(i, (i + 1) % 4) f...  3.48 us
  transfers between devices with their start and end apart: 19, of which 9 were waited for; matrix products, arithmetic and copies ran while one was open for 6% of the time, Pallas kernels for 0%

profile of v5, /device:TPU:128, one launch (start us, length us, event | category | flops | bytes accessed | tf_op | source)
XLA Modules:
  0.0 147.0 jit_solution(11081641647622902537)
XLA Ops:
  0.6 2.2 %collective-permute-start.1 = (bf16[448,256]{1,0:T(8,128)(2,1)}, bf16[448,256]{1,0:T(8,128)(2,1)S(1)}, u32[]{:S(2)}, u32[]{:S(2)}) collective-permute-start(bf16[448,256]{1,0:T(8,128)(2,1)} %param.8), channel_id=1, source_target_pairs={{16,0},{32,16},{48,32},{64,48},{80,64},{96,80},{112,96},{8,24},{24... | collective-permute-start | bytes 688136 | tf_op jit(solution)/shard_map/ppermute | solution.py:18
  2.8 11.8 %collective-permute-start.2 = (bf16[448,128]{1,0:T(8,128)(2,1)}, bf16[448,128]{1,0:T(8,128)(2,1)S(1)}, u32[]{:S(2)}, u32[]{:S(2)}) collective-permute-start(bf16[448,128]{1,0:T(8,128)(2,1)} %param.7), channel_id=1, source_target_pairs={{0,8},{8,0},{1,9},{9,1},{2,10},{10,2},{3,11},{11,3},{4,12},{12,4},... | collective-permute-start | bytes 344072 | tf_op jit(solution)/shard_map/ppermute | solution.py:37
  14.6 14.4 %all_gather.6 = bf16[448,1024]{1,0:T(8,128)(2,1)S(1)} all-gather(bf16[448,128]{1,0:T(8,128)(2,1)} %param.7), channel_id=1, replica_groups=mesh['y'=4,'zl'=8,'zh'=2,'x'=4,'c'=2] {'x','c'}, dimensions={1}, use_global_device_ids=true | all-gather | bytes 1032192 | tf_op jit(solution)/shard_map/all_gather | solution.py:52
  29.7 1.0 slice_select_fusion
  30.6 3.1 %collective-permute-start = (bf16[448,256]{1,0:T(8,128)(2,1)S(1)}, bf16[448,256]{1,0:T(8,128)(2,1)S(1)}, u32[]{:S(2)}, u32[]{:S(2)}) collective-permute-start(bf16[448,256]{1,0:T(8,128)(2,1)S(1)} %slice_select_fusion), channel_id=1, source_target_pairs={{0,16},{16,32},{32,48},{48,64},{64,80},{80,96},{96,112},{24,8},{40... | collective-permute-start | bytes 688136 | tf_op jit(solution)/shard_map/ppermute | solution.py:18
  34.5 4.0 %collective-permute-start.6 = (bf16[448,256]{1,0:T(8,128)(2,1)S(1)}, bf16[448,256]{1,0:T(8,128)(2,1)S(1)}, u32[]{:S(2)}, u32[]{:S(2)}) collective-permute-start(bf16[448,256]{1,0:T(8,128)(2,1)S(1)} %fusion.11), channel_id=1, source_target_pairs={{16,0},{32,16},{48,32},{64,48},{80,64},{96,80},{112,96},{8,24},{24... | collective-permute-start | bytes 688136 | tf_op jit(solution)/shard_map/ppermute | solution.py:18
  38.5 14.1 %all_gather.7 = bf16[448,1024]{1,0:T(8,128)(2,1)S(1)} all-gather(bf16[448,128]{1,0:T(8,128)(2,1)S(1)} %slice_select_fusion.1), channel_id=1, replica_groups=mesh['y'=4,'zl'=8,'zh'=2,'x'=4,'c'=2] {'x','c'}, dimensions={1}, use_global_device_ids=true | all-gather | bytes 1032192 | tf_op jit(solution)/shard_map/all_gather | solution.py:57
  53.5 1.9 %collective-permute-start.3 = (bf16[448,256]{1,0:T(8,128)(2,1)S(1)}, bf16[448,256]{1,0:T(8,128)(2,1)S(1)}, u32[]{:S(2)}, u32[]{:S(2)}) collective-permute-start(bf16[448,256]{1,0:T(8,128)(2,1)S(1)} %fusion.12), channel_id=1, source_target_pairs={{0,16},{16,32},{32,48},{48,64},{64,80},{80,96},{96,112},{24,8},{40... | collective-permute-start | bytes 688136 | tf_op jit(solution)/shard_map/ppermute | solution.py:18
  55.9 5.1 %collective-permute-start.7 = (bf16[448,256]{1,0:T(8,128)(2,1)S(1)}, bf16[448,256]{1,0:T(8,128)(2,1)S(1)}, u32[]{:S(2)}, u32[]{:S(2)}) collective-permute-start(bf16[448,256]{1,0:T(8,128)(2,1)S(1)} %fusion.15), channel_id=1, source_target_pairs={{16,0},{32,16},{48,32},{64,48},{80,64},{96,80},{112,96},{8,24},{24... | collective-permute-start | bytes 688136 | tf_op jit(solution)/shard_map/ppermute | solution.py:18
  61.4 3.1 %collective-permute-done.3 = bf16[448,256]{1,0:T(8,128)(2,1)S(1)} collective-permute-done((bf16[448,256]{1,0:T(8,128)(2,1)S(1)}, bf16[448,256]{1,0:T(8,128)(2,1)S(1)}, u32[]{:S(2)}, u32[]{:S(2)}) %collective-permute-start.3) | collective-permute-done | bytes 229408 | tf_op jit(solution)/shard_map/ppermute | solution.py:18
  64.5 1.9 %collective-permute-start.4 = (bf16[448,256]{1,0:T(8,128)(2,1)S(1)}, bf16[448,256]{1,0:T(8,128)(2,1)S(1)}, u32[]{:S(2)}, u32[]{:S(2)}) collective-permute-start(bf16[448,256]{1,0:T(8,128)(2,1)S(1)} %fusion.13), channel_id=1, source_target_pairs={{0,16},{16,32},{32,48},{48,64},{64,80},{80,96},{96,112},{24,8},{40... | collective-permute-start | bytes 688136 | tf_op jit(solution)/shard_map/ppermute | solution.py:18
  66.6 5.2 %collective-permute-start.9 = (bf16[448,256]{1,0:T(8,128)(2,1)S(1)}, bf16[448,256]{1,0:T(8,128)(2,1)S(1)}, u32[]{:S(2)}, u32[]{:S(2)}) collective-permute-start(bf16[448,256]{1,0:T(8,128)(2,1)S(1)} %fusion.16), channel_id=1, source_target_pairs={{16,0},{32,16},{48,32},{64,48},{80,64},{96,80},{112,96},{8,24},{24... | collective-permute-start | bytes 688136 | tf_op jit(solution)/shard_map/ppermute | solution.py:18
  72.1 3.9 %collective-permute-done.9 = bf16[448,256]{1,0:T(8,128)(2,1)S(1)} collective-permute-done((bf16[448,256]{1,0:T(8,128)(2,1)S(1)}, bf16[448,256]{1,0:T(8,128)(2,1)S(1)}, u32[]{:S(2)}, u32[]{:S(2)}) %collective-permute-start.9) | collective-permute-done | bytes 229408 | tf_op jit(solution)/shard_map/ppermute | solution.py:18
  76.1 5.6 %collective-permute-start.10 = (bf16[448,256]{1,0:T(8,128)(2,1)S(1)}, bf16[448,256]{1,0:T(8,128)(2,1)S(1)}, u32[]{:S(2)}, u32[]{:S(2)}) collective-permute-start(bf16[448,256]{1,0:T(8,128)(2,1)S(1)} %fusion.19), channel_id=1, source_target_pairs={{16,0},{32,16},{48,32},{64,48},{80,64},{96,80},{112,96},{8,24},{24... | collective-permute-start | bytes 688136 | tf_op jit(solution)/shard_map/ppermute | solution.py:18
  82.1 3.1 %collective-permute-done.10 = bf16[448,256]{1,0:T(8,128)(2,1)S(1)} collective-permute-done((bf16[448,256]{1,0:T(8,128)(2,1)S(1)}, bf16[448,256]{1,0:T(8,128)(2,1)S(1)}, u32[]{:S(2)}, u32[]{:S(2)}) %collective-permute-start.10) | collective-permute-done | bytes 229408 | tf_op jit(solution)/shard_map/ppermute | solution.py:18
  85.3 1.9 %collective-permute-start.5 = (bf16[448,256]{1,0:T(8,128)(2,1)S(1)}, bf16[448,256]{1,0:T(8,128)(2,1)S(1)}, u32[]{:S(2)}, u32[]{:S(2)}) collective-permute-start(bf16[448,256]{1,0:T(8,128)(2,1)S(1)} %get-tuple-element.8), channel_id=1, source_target_pairs={{0,16},{16,32},{32,48},{48,64},{64,80},{80,96},{96,112},{24,8},{40... | collective-permute-start | bytes 688136 | tf_op jit(solution)/shard_map/ppermute | solution.py:18
  87.2 5.6 %collective-permute-start.11 = (bf16[448,256]{1,0:T(8,128)(2,1)S(1)}, bf16[448,256]{1,0:T(8,128)(2,1)S(1)}, u32[]{:S(2)}, u32[]{:S(2)}) collective-permute-start(bf16[448,256]{1,0:T(8,128)(2,1)S(1)} %get-tuple-element.7), channel_id=1, source_target_pairs={{16,0},{32,16},{48,32},{64,48},{80,64},{96,80},{112,96},{8,24},{24... | collective-permute-start | bytes 688136 | tf_op jit(solution)/shard_map/ppermute | solution.py:18
  93.2 1.7 %collective-permute-done.5 = bf16[448,256]{1,0:T(8,128)(2,1)S(1)} collective-permute-done((bf16[448,256]{1,0:T(8,128)(2,1)S(1)}, bf16[448,256]{1,0:T(8,128)(2,1)S(1)}, u32[]{:S(2)}, u32[]{:S(2)}) %collective-permute-start.5) | collective-permute-done | bytes 229408 | tf_op jit(solution)/shard_map/ppermute | solution.py:18
  95.0 1.9 %collective-permute-start.8 = (bf16[448,256]{1,0:T(8,128)(2,1)S(1)}, bf16[448,256]{1,0:T(8,128)(2,1)S(1)}, u32[]{:S(2)}, u32[]{:S(2)}) collective-permute-start(bf16[448,256]{1,0:T(8,128)(2,1)S(1)} %fusion.17), channel_id=1, source_target_pairs={{0,16},{16,32},{32,48},{48,64},{64,80},{80,96},{96,112},{24,8},{40... | collective-permute-start | bytes 688136 | tf_op jit(solution)/shard_map/ppermute | solution.py:18
  97.3 5.1 %collective-permute-start.12 = (bf16[448,256]{1,0:T(8,128)(2,1)S(1)}, bf16[448,256]{1,0:T(8,128)(2,1)S(1)}, u32[]{:S(2)}, u32[]{:S(2)}) collective-permute-start(bf16[448,256]{1,0:T(8,128)(2,1)S(1)} %fusion.21), channel_id=1, source_target_pairs={{16,0},{32,16},{48,32},{64,48},{80,64},{96,80},{112,96},{8,24},{24... | collective-permute-start | bytes 688136 | tf_op jit(solution)/shard_map/ppermute | solution.py:18
  103.1 1.0 collective-permute-done.8
  104.2 1.9 %collective-permute-start.14 = (bf16[448,256]{1,0:T(8,128)(2,1)S(1)}, bf16[448,256]{1,0:T(8,128)(2,1)S(1)}, u32[]{:S(2)}, u32[]{:S(2)}) collective-permute-start(bf16[448,256]{1,0:T(8,128)(2,1)S(1)} %fusion.18), channel_id=1, source_target_pairs={{0,16},{16,32},{32,48},{48,64},{64,80},{80,96},{96,112},{24,8},{40... | collective-permute-start | bytes 688136 | tf_op jit(solution)/shard_map/ppermute | solution.py:18
  106.5 5.1 %collective-permute-start.13 = (bf16[448,256]{1,0:T(8,128)(2,1)S(1)}, bf16[448,256]{1,0:T(8,128)(2,1)S(1)}, u32[]{:S(2)}, u32[]{:S(2)}) collective-permute-start(bf16[448,256]{1,0:T(8,128)(2,1)S(1)} %fusion.22), channel_id=1, source_target_pairs={{16,0},{32,16},{48,32},{64,48},{80,64},{96,80},{112,96},{8,24},{24... | collective-permute-start | bytes 688136 | tf_op jit(solution)/shard_map/ppermute | solution.py:18
  113.4 2.1 %collective-permute-start.15 = (bf16[448,256]{1,0:T(8,128)(2,1)S(1)}, bf16[448,256]{1,0:T(8,128)(2,1)S(1)}, u32[]{:S(2)}, u32[]{:S(2)}) collective-permute-start(bf16[448,256]{1,0:T(8,128)(2,1)S(1)} %fusion.23), channel_id=1, source_target_pairs={{0,16},{16,32},{32,48},{48,64},{64,80},{80,96},{96,112},{24,8},{40... | collective-permute-start | bytes 688136 | tf_op jit(solution)/shard_map/ppermute | solution.py:18
  115.8 8.2 %collective-permute-done.15 = bf16[448,256]{1,0:T(8,128)(2,1)S(1)} collective-permute-done((bf16[448,256]{1,0:T(8,128)(2,1)S(1)}, bf16[448,256]{1,0:T(8,128)(2,1)S(1)}, u32[]{:S(2)}, u32[]{:S(2)}) %collective-permute-start.15) | collective-permute-done | bytes 229408 | tf_op jit(solution)/shard_map/ppermute | solution.py:18
  124.0 1.9 %collective-permute-start.16 = (bf16[448,256]{1,0:T(8,128)(2,1)S(1)}, bf16[448,256]{1,0:T(8,128)(2,1)S(1)}, u32[]{:S(2)}, u32[]{:S(2)}) collective-permute-start(bf16[448,256]{1,0:T(8,128)(2,1)S(1)} %fusion.24), channel_id=1, source_target_pairs={{0,16},{16,32},{32,48},{48,64},{64,80},{80,96},{96,112},{24,8},{40... | collective-permute-start | bytes 688136 | tf_op jit(solution)/shard_map/ppermute | solution.py:18
  126.3 6.9 %collective-permute-done.16 = bf16[448,256]{1,0:T(8,128)(2,1)S(1)} collective-permute-done((bf16[448,256]{1,0:T(8,128)(2,1)S(1)}, bf16[448,256]{1,0:T(8,128)(2,1)S(1)}, u32[]{:S(2)}, u32[]{:S(2)}) %collective-permute-start.16) | collective-permute-done | bytes 229408 | tf_op jit(solution)/shard_map/ppermute | solution.py:18
  133.2 1.4 fusion.10
  134.6 3.5 %collective-permute-start.17 = (bf16[224,256]{1,0:T(8,128)(2,1)S(1)}, bf16[224,256]{1,0:T(8,128)(2,1)S(1)}, u32[]{:S(2)}, u32[]{:S(2)}) collective-permute-start(bf16[224,256]{1,0:T(8,128)(2,1)S(1)} %get-tuple-element.11), channel_id=1, source_target_pairs={{0,128},{128,256},{256,384},{384,0},{1,129},{129,257},{257,385},{3... | collective-permute-start | bytes 344072 | tf_op jit(solution)/shard_map/ppermute | solution.py:100
  138.0 4.8 %collective-permute-start.18 = (bf16[224,256]{1,0:T(8,128)(2,1)S(1)}, bf16[224,256]{1,0:T(8,128)(2,1)S(1)}, u32[]{:S(2)}, u32[]{:S(2)}) collective-permute-start(bf16[224,256]{1,0:T(8,128)(2,1)S(1)} %get-tuple-element.12), channel_id=1, source_target_pairs={{0,256},{128,384},{256,0},{384,128},{1,257},{129,385},{257,1},{385... | collective-permute-start | bytes 344072 | tf_op jit(solution)/shard_map/ppermute | solution.py:101
  142.9 1.3 fusion.7
  144.1 2.1 %collective-permute-done.18 = bf16[224,256]{1,0:T(8,128)(2,1)S(1)} collective-permute-done((bf16[224,256]{1,0:T(8,128)(2,1)S(1)}, bf16[224,256]{1,0:T(8,128)(2,1)S(1)}, u32[]{:S(2)}, u32[]{:S(2)}) %collective-permute-start.18) | collective-permute-done | bytes 114720 | tf_op jit(solution)/shard_map/ppermute | solution.py:101
  (54 shorter events, 8.2 us)
Async XLA Ops:
  0.6 33.1 %copy-start = (bf16[448,448]{1,0:T(8,128)(2,1)S(1)}, bf16[448,448]{1,0:T(8,128)(2,1)}, u32[]{:S(2)}) copy-start(bf16[448,448]{1,0:T(8,128)(2,1)} %param.6) | copy-start | bytes 1204228
  0.6 33.8 %collective-permute-start.1 = (bf16[448,256]{1,0:T(8,128)(2,1)}, bf16[448,256]{1,0:T(8,128)(2,1)S(1)}, u32[]{:S(2)}, u32[]{:S(2)}) collective-permute-start(bf16[448,256]{1,0:T(8,128)(2,1)} %param.8), channel_id=1, source_target_pairs={{16,0},{32,16},{48,32},{64,48},{80,64},{96,80},{112,96},{8,24},{24... | collective-permute-start | bytes 688136 | tf_op jit(solution)/shard_map/ppermute | solution.py:18
  2.8 35.7 %collective-permute-start.2 = (bf16[448,128]{1,0:T(8,128)(2,1)}, bf16[448,128]{1,0:T(8,128)(2,1)S(1)}, u32[]{:S(2)}, u32[]{:S(2)}) collective-permute-start(bf16[448,128]{1,0:T(8,128)(2,1)} %param.7), channel_id=1, source_target_pairs={{0,8},{8,0},{1,9},{9,1},{2,10},{10,2},{3,11},{11,3},{4,12},{12,4},... | collective-permute-start | bytes 344072 | tf_op jit(solution)/shard_map/ppermute | solution.py:37
  30.6 22.8 %collective-permute-start = (bf16[448,256]{1,0:T(8,128)(2,1)S(1)}, bf16[448,256]{1,0:T(8,128)(2,1)S(1)}, u32[]{:S(2)}, u32[]{:S(2)}) collective-permute-start(bf16[448,256]{1,0:T(8,128)(2,1)S(1)} %slice_select_fusion), channel_id=1, source_target_pairs={{0,16},{16,32},{32,48},{48,64},{64,80},{80,96},{96,112},{24,8},{40... | collective-permute-start | bytes 688136 | tf_op jit(solution)/shard_map/ppermute | solution.py:18
  34.5 21.3 %collective-permute-start.6 = (bf16[448,256]{1,0:T(8,128)(2,1)S(1)}, bf16[448,256]{1,0:T(8,128)(2,1)S(1)}, u32[]{:S(2)}, u32[]{:S(2)}) collective-permute-start(bf16[448,256]{1,0:T(8,128)(2,1)S(1)} %fusion.11), channel_id=1, source_target_pairs={{16,0},{32,16},{48,32},{64,48},{80,64},{96,80},{112,96},{8,24},{24... | collective-permute-start | bytes 688136 | tf_op jit(solution)/shard_map/ppermute | solution.py:18
  53.5 11.0 %collective-permute-start.3 = (bf16[448,256]{1,0:T(8,128)(2,1)S(1)}, bf16[448,256]{1,0:T(8,128)(2,1)S(1)}, u32[]{:S(2)}, u32[]{:S(2)}) collective-permute-start(bf16[448,256]{1,0:T(8,128)(2,1)S(1)} %fusion.12), channel_id=1, source_target_pairs={{0,16},{16,32},{32,48},{48,64},{64,80},{80,96},{96,112},{24,8},{40... | collective-permute-start | bytes 688136 | tf_op jit(solution)/shard_map/ppermute | solution.py:18
  55.9 10.6 %collective-permute-start.7 = (bf16[448,256]{1,0:T(8,128)(2,1)S(1)}, bf16[448,256]{1,0:T(8,128)(2,1)S(1)}, u32[]{:S(2)}, u32[]{:S(2)}) collective-permute-start(bf16[448,256]{1,0:T(8,128)(2,1)S(1)} %fusion.15), channel_id=1, source_target_pairs={{16,0},{32,16},{48,32},{64,48},{80,64},{96,80},{112,96},{8,24},{24... | collective-permute-start | bytes 688136 | tf_op jit(solution)/shard_map/ppermute | solution.py:18
  64.5 17.5 %collective-permute-start.4 = (bf16[448,256]{1,0:T(8,128)(2,1)S(1)}, bf16[448,256]{1,0:T(8,128)(2,1)S(1)}, u32[]{:S(2)}, u32[]{:S(2)}) collective-permute-start(bf16[448,256]{1,0:T(8,128)(2,1)S(1)} %fusion.13), channel_id=1, source_target_pairs={{0,16},{16,32},{32,48},{48,64},{64,80},{80,96},{96,112},{24,8},{40... | collective-permute-start | bytes 688136 | tf_op jit(solution)/shard_map/ppermute | solution.py:18
  66.6 9.5 %collective-permute-start.9 = (bf16[448,256]{1,0:T(8,128)(2,1)S(1)}, bf16[448,256]{1,0:T(8,128)(2,1)S(1)}, u32[]{:S(2)}, u32[]{:S(2)}) collective-permute-start(bf16[448,256]{1,0:T(8,128)(2,1)S(1)} %fusion.16), channel_id=1, source_target_pairs={{16,0},{32,16},{48,32},{64,48},{80,64},{96,80},{112,96},{8,24},{24... | collective-permute-start | bytes 688136 | tf_op jit(solution)/shard_map/ppermute | solution.py:18
  76.1 9.1 %collective-permute-start.10 = (bf16[448,256]{1,0:T(8,128)(2,1)S(1)}, bf16[448,256]{1,0:T(8,128)(2,1)S(1)}, u32[]{:S(2)}, u32[]{:S(2)}) collective-permute-start(bf16[448,256]{1,0:T(8,128)(2,1)S(1)} %fusion.19), channel_id=1, source_target_pairs={{16,0},{32,16},{48,32},{64,48},{80,64},{96,80},{112,96},{8,24},{24... | collective-permute-start | bytes 688136 | tf_op jit(solution)/shard_map/ppermute | solution.py:18
  85.3 9.6 %collective-permute-start.5 = (bf16[448,256]{1,0:T(8,128)(2,1)S(1)}, bf16[448,256]{1,0:T(8,128)(2,1)S(1)}, u32[]{:S(2)}, u32[]{:S(2)}) collective-permute-start(bf16[448,256]{1,0:T(8,128)(2,1)S(1)} %get-tuple-element.8), channel_id=1, source_target_pairs={{0,16},{16,32},{32,48},{48,64},{64,80},{80,96},{96,112},{24,8},{40... | collective-permute-start | bytes 688136 | tf_op jit(solution)/shard_map/ppermute | solution.py:18
  87.2 10.0 %collective-permute-start.11 = (bf16[448,256]{1,0:T(8,128)(2,1)S(1)}, bf16[448,256]{1,0:T(8,128)(2,1)S(1)}, u32[]{:S(2)}, u32[]{:S(2)}) collective-permute-start(bf16[448,256]{1,0:T(8,128)(2,1)S(1)} %get-tuple-element.7), channel_id=1, source_target_pairs={{16,0},{32,16},{48,32},{64,48},{80,64},{96,80},{112,96},{8,24},{24... | collective-permute-start | bytes 688136 | tf_op jit(solution)/shard_map/ppermute | solution.py:18
  95.0 9.1 %collective-permute-start.8 = (bf16[448,256]{1,0:T(8,128)(2,1)S(1)}, bf16[448,256]{1,0:T(8,128)(2,1)S(1)}, u32[]{:S(2)}, u32[]{:S(2)}) collective-permute-start(bf16[448,256]{1,0:T(8,128)(2,1)S(1)} %fusion.17), channel_id=1, source_target_pairs={{0,16},{16,32},{32,48},{48,64},{64,80},{80,96},{96,112},{24,8},{40... | collective-permute-start | bytes 688136 | tf_op jit(solution)/shard_map/ppermute | solution.py:18
  97.3 9.1 %collective-permute-start.12 = (bf16[448,256]{1,0:T(8,128)(2,1)S(1)}, bf16[448,256]{1,0:T(8,128)(2,1)S(1)}, u32[]{:S(2)}, u32[]{:S(2)}) collective-permute-start(bf16[448,256]{1,0:T(8,128)(2,1)S(1)} %fusion.21), channel_id=1, source_target_pairs={{16,0},{32,16},{48,32},{64,48},{80,64},{96,80},{112,96},{8,24},{24... | collective-permute-start | bytes 688136 | tf_op jit(solution)/shard_map/ppermute | solution.py:18
  104.2 9.1 %collective-permute-start.14 = (bf16[448,256]{1,0:T(8,128)(2,1)S(1)}, bf16[448,256]{1,0:T(8,128)(2,1)S(1)}, u32[]{:S(2)}, u32[]{:S(2)}) collective-permute-start(bf16[448,256]{1,0:T(8,128)(2,1)S(1)} %fusion.18), channel_id=1, source_target_pairs={{0,16},{16,32},{32,48},{48,64},{64,80},{80,96},{96,112},{24,8},{40... | collective-permute-start | bytes 688136 | tf_op jit(solution)/shard_map/ppermute | solution.py:18
  106.5 19.7 %collective-permute-start.13 = (bf16[448,256]{1,0:T(8,128)(2,1)S(1)}, bf16[448,256]{1,0:T(8,128)(2,1)S(1)}, u32[]{:S(2)}, u32[]{:S(2)}) collective-permute-start(bf16[448,256]{1,0:T(8,128)(2,1)S(1)} %fusion.22), channel_id=1, source_target_pairs={{16,0},{32,16},{48,32},{64,48},{80,64},{96,80},{112,96},{8,24},{24... | collective-permute-start | bytes 688136 | tf_op jit(solution)/shard_map/ppermute | solution.py:18
  113.4 19.8 %copy-start.1 = (bf16[448,256]{1,0:T(8,128)(2,1)S(1)}, bf16[448,256]{1,0:T(8,128)(2,1)}, u32[]{:S(2)}) copy-start(bf16[448,256]{1,0:T(8,128)(2,1)} %param.8) | copy-start | bytes 688132
  113.4 19.8 %copy-start.2 = (f32[448,256]{1,0:T(8,128)S(1)}, f32[448,256]{1,0:T(8,128)}, u32[]{:S(2)}) copy-start(f32[448,256]{1,0:T(8,128)} %param.10) | copy-start | bytes 1376260
  113.4 19.8 %copy-start.3 = (f32[448,256]{1,0:T(8,128)S(1)}, f32[448,256]{1,0:T(8,128)}, u32[]{:S(2)}) copy-start(f32[448,256]{1,0:T(8,128)} %param.9) | copy-start | bytes 1376260
  113.4 10.6 %collective-permute-start.15 = (bf16[448,256]{1,0:T(8,128)(2,1)S(1)}, bf16[448,256]{1,0:T(8,128)(2,1)S(1)}, u32[]{:S(2)}, u32[]{:S(2)}) collective-permute-start(bf16[448,256]{1,0:T(8,128)(2,1)S(1)} %fusion.23), channel_id=1, source_target_pairs={{0,16},{16,32},{32,48},{48,64},{64,80},{80,96},{96,112},{24,8},{40... | collective-permute-start | bytes 688136 | tf_op jit(solution)/shard_map/ppermute | solution.py:18
  124.0 9.1 %collective-permute-start.16 = (bf16[448,256]{1,0:T(8,128)(2,1)S(1)}, bf16[448,256]{1,0:T(8,128)(2,1)S(1)}, u32[]{:S(2)}, u32[]{:S(2)}) collective-permute-start(bf16[448,256]{1,0:T(8,128)(2,1)S(1)} %fusion.24), channel_id=1, source_target_pairs={{0,16},{16,32},{32,48},{48,64},{64,80},{80,96},{96,112},{24,8},{40... | collective-permute-start | bytes 688136 | tf_op jit(solution)/shard_map/ppermute | solution.py:18
  134.6 9.6 %collective-permute-start.17 = (bf16[224,256]{1,0:T(8,128)(2,1)S(1)}, bf16[224,256]{1,0:T(8,128)(2,1)S(1)}, u32[]{:S(2)}, u32[]{:S(2)}) collective-permute-start(bf16[224,256]{1,0:T(8,128)(2,1)S(1)} %get-tuple-element.11), channel_id=1, source_target_pairs={{0,128},{128,256},{256,384},{384,0},{1,129},{129,257},{257,385},{3... | collective-permute-start | bytes 344072 | tf_op jit(solution)/shard_map/ppermute | solution.py:100
  138.0 8.2 %collective-permute-start.18 = (bf16[224,256]{1,0:T(8,128)(2,1)S(1)}, bf16[224,256]{1,0:T(8,128)(2,1)S(1)}, u32[]{:S(2)}, u32[]{:S(2)}) collective-permute-start(bf16[224,256]{1,0:T(8,128)(2,1)S(1)} %get-tuple-element.12), channel_id=1, source_target_pairs={{0,256},{128,384},{256,0},{384,128},{1,257},{129,385},{257,1},{385... | collective-permute-start | bytes 344072 | tf_op jit(solution)/shard_map/ppermute | solution.py:101

commit v6 on v5

--- a/solution.py
+++ b/solution.py
@@ -42,8 +42,10 @@
     def send(early, turn, part):
         here = position if early else last - position
         arrived = got[early][-1]
+        if sent:
+            arrived = behind(arrived, list(sent.values())[-1])
         total = (arrived.astype(F32) + part).astype(BF)
-        sent[early, turn] = jnp.where(here <= turn, total, arrived)
+        sent[early, turn] = lax.optimization_barrier(jnp.where(here <= turn, total, arrived))
         got[early].append(along(sent[early, turn], early))
 
     def product(features):

time: 148 us -> 137 us (0.926)
  waiting for transfers between devices: 31 us -> 19.1 us
    ppermute x16, waiting for transfers between devices: 28.9 us -> 17 us  [along(): return lax.ppermute(value, ('zl', 'zh'), pairs)]
  transfers between devices with their start and end apart: 19 -> 19, of which waited for: 9 -> 8; matrix products, arithmetic and copies ran while one was open for 6% -> 7% of each run, Pallas kernels for 0% -> 0%
where the time goes in v6:
time: 137 us; the launch traced here: 136 us
  starting transfers between devices  75.4 us (55%)
  blocking collectives  28.6 us (21%)
  waiting for transfers between devices  19.1 us (14%)
  matrix products  6.65 us (5%)
  other arithmetic  4.48 us (3%)
  between operations  2.02 us (1%)
    ppermute x16, starting transfers between devices, along(): return lax.ppermute(value, ('zl', 'zh'), pairs)  56 us
    ppermute x16, waiting for transfers between devices, along(): return lax.ppermute(value, ('zl', 'zh'), pairs)  17 us
    all_gather x1, blocking collectives, body(): far_up = lax.all_gather(up_other, ('x', 'c'), axis=1, tiled=True)  14.4 us
    all_gather x1, blocking collectives, body(): near_up = lax.all_gather(upstream, ('x', 'c'), axis=1, tiled=True)  14.2 us
    ppermute x1, starting transfers between devices, body(): up_other = lax.ppermute(upstream, 'zh', [(0, 1), (1, 0)])  11 us
    dot_general x17, matrix products, contract(): lax.dot_general(left, right, (dims, ((), ())), preferred_element_type=F32)  6.65 us
    ppermute x1, starting transfers between devices, body(): lax.ppermute(jnp.where(even_step, upper, lower), 'y', [(i, (i + 2) % 4) f...  4.81 us
    ppermute x1, starting transfers between devices, body(): lax.ppermute(jnp.where(even_step, lower, upper), 'y', [(i, (i + 1) % 4) f...  3.49 us
  transfers between devices with their start and end apart: 19, of which 8 were waited for; matrix products, arithmetic and copies ran while one was open for 7% of the time, Pallas kernels for 0%

profile of v6, /device:TPU:128, one launch (start us, length us, event | category | flops | bytes accessed | tf_op | source)
XLA Modules:
  0.0 136.4 jit_solution(15123730607751529707)
XLA Ops:
  0.6 11.0 %collective-permute-start.2 = (bf16[448,128]{1,0:T(8,128)(2,1)}, bf16[448,128]{1,0:T(8,128)(2,1)S(1)}, u32[]{:S(2)}, u32[]{:S(2)}) collective-permute-start(bf16[448,128]{1,0:T(8,128)(2,1)} %param.7), channel_id=1, source_target_pairs={{0,8},{8,0},{1,9},{9,1},{2,10},{10,2},{3,11},{11,3},{4,12},{12,4},... | collective-permute-start | bytes 344072 | tf_op jit(solution)/shard_map/ppermute | solution.py:37
  11.7 4.1 %collective-permute-start = (bf16[448,256]{1,0:T(8,128)(2,1)}, bf16[448,256]{1,0:T(8,128)(2,1)S(1)}, u32[]{:S(2)}, u32[]{:S(2)}) collective-permute-start(bf16[448,256]{1,0:T(8,128)(2,1)} %param.8), channel_id=1, source_target_pairs={{16,0},{32,16},{48,32},{64,48},{80,64},{96,80},{112,96},{8,24},{24... | collective-permute-start | bytes 688136 | tf_op jit(solution)/shard_map/ppermute | solution.py:18
  15.8 14.2 %all_gather.6 = bf16[448,1024]{1,0:T(8,128)(2,1)S(1)} all-gather(bf16[448,128]{1,0:T(8,128)(2,1)} %param.7), channel_id=1, replica_groups=mesh['y'=4,'zl'=8,'zh'=2,'x'=4,'c'=2] {'x','c'}, dimensions={1}, use_global_device_ids=true | all-gather | bytes 1032192 | tf_op jit(solution)/shard_map/all_gather | solution.py:54
  30.7 1.0 slice_select_fusion
  31.7 1.9 %collective-permute-start.1 = (bf16[448,256]{1,0:T(8,128)(2,1)S(1)}, bf16[448,256]{1,0:T(8,128)(2,1)S(1)}, u32[]{:S(2)}, u32[]{:S(2)}) collective-permute-start(bf16[448,256]{1,0:T(8,128)(2,1)S(1)} %slice_select_fusion), channel_id=1, source_target_pairs={{0,16},{16,32},{32,48},{48,64},{64,80},{80,96},{96,112},{24,8},{40... | collective-permute-start | bytes 688136 | tf_op jit(solution)/shard_map/ppermute | solution.py:18
  34.4 5.1 %collective-permute-start.3 = (bf16[448,256]{1,0:T(8,128)(2,1)S(1)}, bf16[448,256]{1,0:T(8,128)(2,1)S(1)}, u32[]{:S(2)}, u32[]{:S(2)}) collective-permute-start(bf16[448,256]{1,0:T(8,128)(2,1)S(1)} %fusion.11), channel_id=1, source_target_pairs={{16,0},{32,16},{48,32},{64,48},{80,64},{96,80},{112,96},{8,24},{24... | collective-permute-start | bytes 688136 | tf_op jit(solution)/shard_map/ppermute | solution.py:18
  39.6 14.4 %all_gather.7 = bf16[448,1024]{1,0:T(8,128)(2,1)S(1)} all-gather(bf16[448,128]{1,0:T(8,128)(2,1)S(1)} %slice_select_fusion.1), channel_id=1, replica_groups=mesh['y'=4,'zl'=8,'zh'=2,'x'=4,'c'=2] {'x','c'}, dimensions={1}, use_global_device_ids=true | all-gather | bytes 1032192 | tf_op jit(solution)/shard_map/all_gather | solution.py:59
  54.9 1.9 %collective-permute-start.4 = (bf16[448,256]{1,0:T(8,128)(2,1)S(1)}, bf16[448,256]{1,0:T(8,128)(2,1)S(1)}, u32[]{:S(2)}, u32[]{:S(2)}) collective-permute-start(bf16[448,256]{1,0:T(8,128)(2,1)S(1)} %fusion.12), channel_id=1, source_target_pairs={{0,16},{16,32},{32,48},{48,64},{64,80},{80,96},{96,112},{24,8},{40... | collective-permute-start | bytes 688136 | tf_op jit(solution)/shard_map/ppermute | solution.py:18
  57.3 5.1 %collective-permute-start.5 = (bf16[448,256]{1,0:T(8,128)(2,1)S(1)}, bf16[448,256]{1,0:T(8,128)(2,1)S(1)}, u32[]{:S(2)}, u32[]{:S(2)}) collective-permute-start(bf16[448,256]{1,0:T(8,128)(2,1)S(1)} %fusion.13), channel_id=1, source_target_pairs={{16,0},{32,16},{48,32},{64,48},{80,64},{96,80},{112,96},{8,24},{24... | collective-permute-start | bytes 688136 | tf_op jit(solution)/shard_map/ppermute | solution.py:18
  62.8 3.1 %collective-permute-done.4 = bf16[448,256]{1,0:T(8,128)(2,1)S(1)} collective-permute-done((bf16[448,256]{1,0:T(8,128)(2,1)S(1)}, bf16[448,256]{1,0:T(8,128)(2,1)S(1)}, u32[]{:S(2)}, u32[]{:S(2)}) %collective-permute-start.4) | collective-permute-done | bytes 229408 | tf_op jit(solution)/shard_map/ppermute | solution.py:18
  66.0 1.9 %collective-permute-start.6 = (bf16[448,256]{1,0:T(8,128)(2,1)S(1)}, bf16[448,256]{1,0:T(8,128)(2,1)S(1)}, u32[]{:S(2)}, u32[]{:S(2)}) collective-permute-start(bf16[448,256]{1,0:T(8,128)(2,1)S(1)} %fusion.14), channel_id=1, source_target_pairs={{0,16},{16,32},{32,48},{48,64},{64,80},{80,96},{96,112},{24,8},{40... | collective-permute-start | bytes 688136 | tf_op jit(solution)/shard_map/ppermute | solution.py:18
  68.3 5.1 %collective-permute-start.7 = (bf16[448,256]{1,0:T(8,128)(2,1)S(1)}, bf16[448,256]{1,0:T(8,128)(2,1)S(1)}, u32[]{:S(2)}, u32[]{:S(2)}) collective-permute-start(bf16[448,256]{1,0:T(8,128)(2,1)S(1)} %fusion.15), channel_id=1, source_target_pairs={{16,0},{32,16},{48,32},{64,48},{80,64},{96,80},{112,96},{8,24},{24... | collective-permute-start | bytes 688136 | tf_op jit(solution)/shard_map/ppermute | solution.py:18
  73.9 2.3 %collective-permute-done.6 = bf16[448,256]{1,0:T(8,128)(2,1)S(1)} collective-permute-done((bf16[448,256]{1,0:T(8,128)(2,1)S(1)}, bf16[448,256]{1,0:T(8,128)(2,1)S(1)}, u32[]{:S(2)}, u32[]{:S(2)}) %collective-permute-start.6) | collective-permute-done | bytes 229408 | tf_op jit(solution)/shard_map/ppermute | solution.py:18
  76.2 1.9 %collective-permute-start.8 = (bf16[448,256]{1,0:T(8,128)(2,1)S(1)}, bf16[448,256]{1,0:T(8,128)(2,1)S(1)}, u32[]{:S(2)}, u32[]{:S(2)}) collective-permute-start(bf16[448,256]{1,0:T(8,128)(2,1)S(1)} %fusion.16), channel_id=1, source_target_pairs={{0,16},{16,32},{32,48},{48,64},{64,80},{80,96},{96,112},{24,8},{40... | collective-permute-start | bytes 688136 | tf_op jit(solution)/shard_map/ppermute | solution.py:18
  78.2 5.2 %collective-permute-start.9 = (bf16[448,256]{1,0:T(8,128)(2,1)S(1)}, bf16[448,256]{1,0:T(8,128)(2,1)S(1)}, u32[]{:S(2)}, u32[]{:S(2)}) collective-permute-start(bf16[448,256]{1,0:T(8,128)(2,1)S(1)} %fusion.17), channel_id=1, source_target_pairs={{16,0},{32,16},{48,32},{64,48},{80,64},{96,80},{112,96},{8,24},{24... | collective-permute-start | bytes 688136 | tf_op jit(solution)/shard_map/ppermute | solution.py:18
  83.5 2.0 %collective-permute-done.8 = bf16[448,256]{1,0:T(8,128)(2,1)S(1)} collective-permute-done((bf16[448,256]{1,0:T(8,128)(2,1)S(1)}, bf16[448,256]{1,0:T(8,128)(2,1)S(1)}, u32[]{:S(2)}, u32[]{:S(2)}) %collective-permute-start.8) | collective-permute-done | bytes 229408 | tf_op jit(solution)/shard_map/ppermute | solution.py:18
  85.6 1.9 %collective-permute-start.10 = (bf16[448,256]{1,0:T(8,128)(2,1)S(1)}, bf16[448,256]{1,0:T(8,128)(2,1)S(1)}, u32[]{:S(2)}, u32[]{:S(2)}) collective-permute-start(bf16[448,256]{1,0:T(8,128)(2,1)S(1)} %fusion.18), channel_id=1, source_target_pairs={{0,16},{16,32},{32,48},{48,64},{64,80},{80,96},{96,112},{24,8},{40... | collective-permute-start | bytes 688136 | tf_op jit(solution)/shard_map/ppermute | solution.py:18
  88.3 5.1 %collective-permute-start.11 = (bf16[448,256]{1,0:T(8,128)(2,1)S(1)}, bf16[448,256]{1,0:T(8,128)(2,1)S(1)}, u32[]{:S(2)}, u32[]{:S(2)}) collective-permute-start(bf16[448,256]{1,0:T(8,128)(2,1)S(1)} %fusion.19), channel_id=1, source_target_pairs={{16,0},{32,16},{48,32},{64,48},{80,64},{96,80},{112,96},{8,24},{24... | collective-permute-start | bytes 688136 | tf_op jit(solution)/shard_map/ppermute | solution.py:18
  93.4 1.3 collective-permute-done.10
  94.8 1.9 %collective-permute-start.12 = (bf16[448,256]{1,0:T(8,128)(2,1)S(1)}, bf16[448,256]{1,0:T(8,128)(2,1)S(1)}, u32[]{:S(2)}, u32[]{:S(2)}) collective-permute-start(bf16[448,256]{1,0:T(8,128)(2,1)S(1)} %fusion.20), channel_id=1, source_target_pairs={{0,16},{16,32},{32,48},{48,64},{64,80},{80,96},{96,112},{24,8},{40... | collective-permute-start | bytes 688136 | tf_op jit(solution)/shard_map/ppermute | solution.py:18
  97.8 5.1 %collective-permute-start.13 = (bf16[448,256]{1,0:T(8,128)(2,1)S(1)}, bf16[448,256]{1,0:T(8,128)(2,1)S(1)}, u32[]{:S(2)}, u32[]{:S(2)}) collective-permute-start(bf16[448,256]{1,0:T(8,128)(2,1)S(1)} %fusion.21), channel_id=1, source_target_pairs={{16,0},{32,16},{48,32},{64,48},{80,64},{96,80},{112,96},{8,24},{24... | collective-permute-start | bytes 688136 | tf_op jit(solution)/shard_map/ppermute | solution.py:18
  103.0 0.9 collective-permute-done.12
  104.0 1.9 %collective-permute-start.15 = (bf16[448,256]{1,0:T(8,128)(2,1)S(1)}, bf16[448,256]{1,0:T(8,128)(2,1)S(1)}, u32[]{:S(2)}, u32[]{:S(2)}) collective-permute-start(bf16[448,256]{1,0:T(8,128)(2,1)S(1)} %fusion.22), channel_id=1, source_target_pairs={{0,16},{16,32},{32,48},{48,64},{64,80},{80,96},{96,112},{24,8},{40... | collective-permute-start | bytes 688136 | tf_op jit(solution)/shard_map/ppermute | solution.py:18
  106.7 5.5 %collective-permute-start.14 = (bf16[448,256]{1,0:T(8,128)(2,1)S(1)}, bf16[448,256]{1,0:T(8,128)(2,1)S(1)}, u32[]{:S(2)}, u32[]{:S(2)}) collective-permute-start(bf16[448,256]{1,0:T(8,128)(2,1)S(1)} %fusion.23), channel_id=1, source_target_pairs={{16,0},{32,16},{48,32},{64,48},{80,64},{96,80},{112,96},{8,24},{24... | collective-permute-start | bytes 688136 | tf_op jit(solution)/shard_map/ppermute | solution.py:18
  112.2 0.9 collective-permute-done.15
  113.3 2.1 %collective-permute-start.16 = (bf16[448,256]{1,0:T(8,128)(2,1)S(1)}, bf16[448,256]{1,0:T(8,128)(2,1)S(1)}, u32[]{:S(2)}, u32[]{:S(2)}) collective-permute-start(bf16[448,256]{1,0:T(8,128)(2,1)S(1)} %fusion.24), channel_id=1, source_target_pairs={{0,16},{16,32},{32,48},{48,64},{64,80},{80,96},{96,112},{24,8},{40... | collective-permute-start | bytes 688136 | tf_op jit(solution)/shard_map/ppermute | solution.py:18
  116.0 6.5 %collective-permute-done.16 = bf16[448,256]{1,0:T(8,128)(2,1)S(1)} collective-permute-done((bf16[448,256]{1,0:T(8,128)(2,1)S(1)}, bf16[448,256]{1,0:T(8,128)(2,1)S(1)}, u32[]{:S(2)}, u32[]{:S(2)}) %collective-permute-start.16) | collective-permute-done | bytes 229408 | tf_op jit(solution)/shard_map/ppermute | solution.py:18
  122.5 1.4 %fusion.10 = (bf16[448,256]{1,0:T(8,128)(2,1)S(1)}, f32[448,256]{1,0:T(8,128)}, f32[448,256]{1,0:T(8,128)}) fusion(bf16[448,256]{1,0:T(8,128)(2,1)S(1)} %copy-done.1, f32[]{:T(128)S(6)} %sub.106, f32[]{:T(128)S(6)} %sub.105, bf16[448,256]{1,0:T(8,128)(2,1)S(1)} %collective-permute-done.16, f32[448,256]{1,0:T(8,128)S(1)} %convolution_bitcast_fusion.1, ...), kind=kLoop, calls=%fused_computation.22 | loop fusion | flops 2523136 | bytes 3211272 | tf_op jit(solution)/shard_map/convert_element_type | solution.py:97
  123.9 3.5 %collective-permute-start.17 = (bf16[224,256]{1,0:T(8,128)(2,1)S(1)}, bf16[224,256]{1,0:T(8,128)(2,1)S(1)}, u32[]{:S(2)}, u32[]{:S(2)}) collective-permute-start(bf16[224,256]{1,0:T(8,128)(2,1)S(1)} %get-tuple-element.9), channel_id=1, source_target_pairs={{0,128},{128,256},{256,384},{384,0},{1,129},{129,257},{257,385},{3... | collective-permute-start | bytes 344072 | tf_op jit(solution)/shard_map/ppermute | solution.py:102
  127.4 4.8 %collective-permute-start.18 = (bf16[224,256]{1,0:T(8,128)(2,1)S(1)}, bf16[224,256]{1,0:T(8,128)(2,1)S(1)}, u32[]{:S(2)}, u32[]{:S(2)}) collective-permute-start(bf16[224,256]{1,0:T(8,128)(2,1)S(1)} %get-tuple-element.10), channel_id=1, source_target_pairs={{0,256},{128,384},{256,0},{384,128},{1,257},{129,385},{257,1},{385... | collective-permute-start | bytes 344072 | tf_op jit(solution)/shard_map/ppermute | solution.py:103
  132.2 1.3 fusion.7
  133.5 2.1 %collective-permute-done.18 = bf16[224,256]{1,0:T(8,128)(2,1)S(1)} collective-permute-done((bf16[224,256]{1,0:T(8,128)(2,1)S(1)}, bf16[224,256]{1,0:T(8,128)(2,1)S(1)}, u32[]{:S(2)}, u32[]{:S(2)}) %collective-permute-start.18) | collective-permute-done | bytes 114720 | tf_op jit(solution)/shard_map/ppermute | solution.py:103
  (55 shorter events, 7.7 us)
Async XLA Ops:
  0.6 33.0 %copy-start = (bf16[448,448]{1,0:T(8,128)(2,1)S(1)}, bf16[448,448]{1,0:T(8,128)(2,1)}, u32[]{:S(2)}) copy-start(bf16[448,448]{1,0:T(8,128)(2,1)} %param.6) | copy-start | bytes 1204228
  0.6 38.9 %collective-permute-start.2 = (bf16[448,128]{1,0:T(8,128)(2,1)}, bf16[448,128]{1,0:T(8,128)(2,1)S(1)}, u32[]{:S(2)}, u32[]{:S(2)}) collective-permute-start(bf16[448,128]{1,0:T(8,128)(2,1)} %param.7), channel_id=1, source_target_pairs={{0,8},{8,0},{1,9},{9,1},{2,10},{10,2},{3,11},{11,3},{4,12},{12,4},... | collective-permute-start | bytes 344072 | tf_op jit(solution)/shard_map/ppermute | solution.py:37
  11.7 22.6 %collective-permute-start = (bf16[448,256]{1,0:T(8,128)(2,1)}, bf16[448,256]{1,0:T(8,128)(2,1)S(1)}, u32[]{:S(2)}, u32[]{:S(2)}) collective-permute-start(bf16[448,256]{1,0:T(8,128)(2,1)} %param.8), channel_id=1, source_target_pairs={{16,0},{32,16},{48,32},{64,48},{80,64},{96,80},{112,96},{8,24},{24... | collective-permute-start | bytes 688136 | tf_op jit(solution)/shard_map/ppermute | solution.py:18
  31.7 23.1 %collective-permute-start.1 = (bf16[448,256]{1,0:T(8,128)(2,1)S(1)}, bf16[448,256]{1,0:T(8,128)(2,1)S(1)}, u32[]{:S(2)}, u32[]{:S(2)}) collective-permute-start(bf16[448,256]{1,0:T(8,128)(2,1)S(1)} %slice_select_fusion), channel_id=1, source_target_pairs={{0,16},{16,32},{32,48},{48,64},{64,80},{80,96},{96,112},{24,8},{40... | collective-permute-start | bytes 688136 | tf_op jit(solution)/shard_map/ppermute | solution.py:18
  34.4 22.8 %collective-permute-start.3 = (bf16[448,256]{1,0:T(8,128)(2,1)S(1)}, bf16[448,256]{1,0:T(8,128)(2,1)S(1)}, u32[]{:S(2)}, u32[]{:S(2)}) collective-permute-start(bf16[448,256]{1,0:T(8,128)(2,1)S(1)} %fusion.11), channel_id=1, source_target_pairs={{16,0},{32,16},{48,32},{64,48},{80,64},{96,80},{112,96},{8,24},{24... | collective-permute-start | bytes 688136 | tf_op jit(solution)/shard_map/ppermute | solution.py:18
  54.9 11.0 %collective-permute-start.4 = (bf16[448,256]{1,0:T(8,128)(2,1)S(1)}, bf16[448,256]{1,0:T(8,128)(2,1)S(1)}, u32[]{:S(2)}, u32[]{:S(2)}) collective-permute-start(bf16[448,256]{1,0:T(8,128)(2,1)S(1)} %fusion.12), channel_id=1, source_target_pairs={{0,16},{16,32},{32,48},{48,64},{64,80},{80,96},{96,112},{24,8},{40... | collective-permute-start | bytes 688136 | tf_op jit(solution)/shard_map/ppermute | solution.py:18
  57.3 11.0 %collective-permute-start.5 = (bf16[448,256]{1,0:T(8,128)(2,1)S(1)}, bf16[448,256]{1,0:T(8,128)(2,1)S(1)}, u32[]{:S(2)}, u32[]{:S(2)}) collective-permute-start(bf16[448,256]{1,0:T(8,128)(2,1)S(1)} %fusion.13), channel_id=1, source_target_pairs={{16,0},{32,16},{48,32},{64,48},{80,64},{96,80},{112,96},{8,24},{24... | collective-permute-start | bytes 688136 | tf_op jit(solution)/shard_map/ppermute | solution.py:18
  66.0 10.2 %collective-permute-start.6 = (bf16[448,256]{1,0:T(8,128)(2,1)S(1)}, bf16[448,256]{1,0:T(8,128)(2,1)S(1)}, u32[]{:S(2)}, u32[]{:S(2)}) collective-permute-start(bf16[448,256]{1,0:T(8,128)(2,1)S(1)} %fusion.14), channel_id=1, source_target_pairs={{0,16},{16,32},{32,48},{48,64},{64,80},{80,96},{96,112},{24,8},{40... | collective-permute-start | bytes 688136 | tf_op jit(solution)/shard_map/ppermute | solution.py:18
  68.3 9.8 %collective-permute-start.7 = (bf16[448,256]{1,0:T(8,128)(2,1)S(1)}, bf16[448,256]{1,0:T(8,128)(2,1)S(1)}, u32[]{:S(2)}, u32[]{:S(2)}) collective-permute-start(bf16[448,256]{1,0:T(8,128)(2,1)S(1)} %fusion.15), channel_id=1, source_target_pairs={{16,0},{32,16},{48,32},{64,48},{80,64},{96,80},{112,96},{8,24},{24... | collective-permute-start | bytes 688136 | tf_op jit(solution)/shard_map/ppermute | solution.py:18
  76.2 9.2 %collective-permute-start.8 = (bf16[448,256]{1,0:T(8,128)(2,1)S(1)}, bf16[448,256]{1,0:T(8,128)(2,1)S(1)}, u32[]{:S(2)}, u32[]{:S(2)}) collective-permute-start(bf16[448,256]{1,0:T(8,128)(2,1)S(1)} %fusion.16), channel_id=1, source_target_pairs={{0,16},{16,32},{32,48},{48,64},{64,80},{80,96},{96,112},{24,8},{40... | collective-permute-start | bytes 688136 | tf_op jit(solution)/shard_map/ppermute | solution.py:18
  78.2 9.9 %collective-permute-start.9 = (bf16[448,256]{1,0:T(8,128)(2,1)S(1)}, bf16[448,256]{1,0:T(8,128)(2,1)S(1)}, u32[]{:S(2)}, u32[]{:S(2)}) collective-permute-start(bf16[448,256]{1,0:T(8,128)(2,1)S(1)} %fusion.17), channel_id=1, source_target_pairs={{16,0},{32,16},{48,32},{64,48},{80,64},{96,80},{112,96},{8,24},{24... | collective-permute-start | bytes 688136 | tf_op jit(solution)/shard_map/ppermute | solution.py:18
  85.6 9.1 %collective-permute-start.10 = (bf16[448,256]{1,0:T(8,128)(2,1)S(1)}, bf16[448,256]{1,0:T(8,128)(2,1)S(1)}, u32[]{:S(2)}, u32[]{:S(2)}) collective-permute-start(bf16[448,256]{1,0:T(8,128)(2,1)S(1)} %fusion.18), channel_id=1, source_target_pairs={{0,16},{16,32},{32,48},{48,64},{64,80},{80,96},{96,112},{24,8},{40... | collective-permute-start | bytes 688136 | tf_op jit(solution)/shard_map/ppermute | solution.py:18
  88.3 9.5 %collective-permute-start.11 = (bf16[448,256]{1,0:T(8,128)(2,1)S(1)}, bf16[448,256]{1,0:T(8,128)(2,1)S(1)}, u32[]{:S(2)}, u32[]{:S(2)}) collective-permute-start(bf16[448,256]{1,0:T(8,128)(2,1)S(1)} %fusion.19), channel_id=1, source_target_pairs={{16,0},{32,16},{48,32},{64,48},{80,64},{96,80},{112,96},{8,24},{24... | collective-permute-start | bytes 688136 | tf_op jit(solution)/shard_map/ppermute | solution.py:18
  94.8 9.1 %collective-permute-start.12 = (bf16[448,256]{1,0:T(8,128)(2,1)S(1)}, bf16[448,256]{1,0:T(8,128)(2,1)S(1)}, u32[]{:S(2)}, u32[]{:S(2)}) collective-permute-start(bf16[448,256]{1,0:T(8,128)(2,1)S(1)} %fusion.20), channel_id=1, source_target_pairs={{0,16},{16,32},{32,48},{48,64},{64,80},{80,96},{96,112},{24,8},{40... | collective-permute-start | bytes 688136 | tf_op jit(solution)/shard_map/ppermute | solution.py:18
  97.8 8.7 %collective-permute-start.13 = (bf16[448,256]{1,0:T(8,128)(2,1)S(1)}, bf16[448,256]{1,0:T(8,128)(2,1)S(1)}, u32[]{:S(2)}, u32[]{:S(2)}) collective-permute-start(bf16[448,256]{1,0:T(8,128)(2,1)S(1)} %fusion.21), channel_id=1, source_target_pairs={{16,0},{32,16},{48,32},{64,48},{80,64},{96,80},{112,96},{8,24},{24... | collective-permute-start | bytes 688136 | tf_op jit(solution)/shard_map/ppermute | solution.py:18
  104.0 9.1 %collective-permute-start.15 = (bf16[448,256]{1,0:T(8,128)(2,1)S(1)}, bf16[448,256]{1,0:T(8,128)(2,1)S(1)}, u32[]{:S(2)}, u32[]{:S(2)}) collective-permute-start(bf16[448,256]{1,0:T(8,128)(2,1)S(1)} %fusion.22), channel_id=1, source_target_pairs={{0,16},{16,32},{32,48},{48,64},{64,80},{80,96},{96,112},{24,8},{40... | collective-permute-start | bytes 688136 | tf_op jit(solution)/shard_map/ppermute | solution.py:18
  106.7 9.3 %collective-permute-start.14 = (bf16[448,256]{1,0:T(8,128)(2,1)S(1)}, bf16[448,256]{1,0:T(8,128)(2,1)S(1)}, u32[]{:S(2)}, u32[]{:S(2)}) collective-permute-start(bf16[448,256]{1,0:T(8,128)(2,1)S(1)} %fusion.23), channel_id=1, source_target_pairs={{16,0},{32,16},{48,32},{64,48},{80,64},{96,80},{112,96},{8,24},{24... | collective-permute-start | bytes 688136 | tf_op jit(solution)/shard_map/ppermute | solution.py:18
  113.2 9.3 %copy-start.1 = (bf16[448,256]{1,0:T(8,128)(2,1)S(1)}, bf16[448,256]{1,0:T(8,128)(2,1)}, u32[]{:S(2)}) copy-start(bf16[448,256]{1,0:T(8,128)(2,1)} %param.8) | copy-start | bytes 688132
  113.2 9.3 %copy-start.2 = (f32[448,256]{1,0:T(8,128)S(1)}, f32[448,256]{1,0:T(8,128)}, u32[]{:S(2)}) copy-start(f32[448,256]{1,0:T(8,128)} %param.10) | copy-start | bytes 1376260
  113.3 9.3 %copy-start.3 = (f32[448,256]{1,0:T(8,128)S(1)}, f32[448,256]{1,0:T(8,128)}, u32[]{:S(2)}) copy-start(f32[448,256]{1,0:T(8,128)} %param.9) | copy-start | bytes 1376260
  113.3 9.3 %collective-permute-start.16 = (bf16[448,256]{1,0:T(8,128)(2,1)S(1)}, bf16[448,256]{1,0:T(8,128)(2,1)S(1)}, u32[]{:S(2)}, u32[]{:S(2)}) collective-permute-start(bf16[448,256]{1,0:T(8,128)(2,1)S(1)} %fusion.24), channel_id=1, source_target_pairs={{0,16},{16,32},{32,48},{48,64},{64,80},{80,96},{96,112},{24,8},{40... | collective-permute-start | bytes 688136 | tf_op jit(solution)/shard_map/ppermute | solution.py:18
  123.9 9.6 %collective-permute-start.17 = (bf16[224,256]{1,0:T(8,128)(2,1)S(1)}, bf16[224,256]{1,0:T(8,128)(2,1)S(1)}, u32[]{:S(2)}, u32[]{:S(2)}) collective-permute-start(bf16[224,256]{1,0:T(8,128)(2,1)S(1)} %get-tuple-element.9), channel_id=1, source_target_pairs={{0,128},{128,256},{256,384},{384,0},{1,129},{129,257},{257,385},{3... | collective-permute-start | bytes 344072 | tf_op jit(solution)/shard_map/ppermute | solution.py:102
  127.4 8.2 %collective-permute-start.18 = (bf16[224,256]{1,0:T(8,128)(2,1)S(1)}, bf16[224,256]{1,0:T(8,128)(2,1)S(1)}, u32[]{:S(2)}, u32[]{:S(2)}) collective-permute-start(bf16[224,256]{1,0:T(8,128)(2,1)S(1)} %get-tuple-element.10), channel_id=1, source_target_pairs={{0,256},{128,384},{256,0},{384,128},{1,257},{129,385},{257,1},{385... | collective-permute-start | bytes 344072 | tf_op jit(solution)/shard_map/ppermute | solution.py:103

commit v7 on v6

v7 whole, which is shorter than its diff:
```python
import math

import jax
import jax.numpy as jnp
from jax import lax
from jax.sharding import Mesh, PartitionSpec as P

BF = jnp.bfloat16
F32 = jnp.float32
LINE = 8


def along(value, way):
    return lax.ppermute(value, "zl", [(i, i + way) for i in range(LINE) if 0 <= i + way < LINE])


def contract(left, right, dims):
    return lax.dot_general(left, right, (dims, ((), ())), preferred_element_type=F32)


def body(hidden, upstream, weights, first_moment, second_moment, step_index):
    width = weights.shape[1]
    place, far_half = lax.axis_index("zl"), lax.axis_index("zh")
    scale_hid = 1.0 / math.sqrt(7168)

    def behind(value, other):
        return jnp.where(step_index[0] < 0, other, value)

    last = LINE - 1
    piece = width // 2
    second_core = lax.axis_index("c") == 1

    up_other = lax.ppermute(upstream, "zh", [(0, 1), (1, 0)])
    hidden_t = lax.optimization_barrier(hidden.T)
    got = {True: [along(weights, 1)], False: [along(weights, -1)]}
    sent = {}

    for hop in (got[True][0], got[False][0]):
        up_other = behind(up_other, hop[:, : up_other.shape[1]])
    of_core = lax.all_gather(jnp.concatenate([upstream, up_other], 1), "x", axis=1, tiled=True)
    of_other = lax.ppermute(of_core, "c", [(0, 1), (1, 0)])
    of_first = jnp.where(second_core, of_other, of_core)
    of_second = jnp.where(second_core, of_core, of_other)
    cuts = range(0, of_core.shape[1], piece)
    full_up = jnp.concatenate([part[:, at : at + piece] for at in cuts for part in (of_first, of_second)], 1)
    full_up = lax.optimization_barrier(full_up)

    def up_block(index):
        at = 2 * jnp.bitwise_and(index, 3) + jnp.bitwise_xor(index // 4, far_half)
        return lax.dynamic_slice_in_dim(full_up, at * width, width, 1)

    def send(up, turn, part):
        arrived = got[up][-1]
        if sent:
            arrived = behind(arrived, list(sent.values())[-1])
        total = (arrived.astype(F32) + part).astype(BF)
        ready = (place if up else last - place) <= turn
        sent[up, turn] = lax.optimization_barrier(jnp.where(ready, total, arrived))
        got[up].append(along(sent[up, turn], 1 if up else -1))

    def product(features):
        return lax.optimization_barrier(contract(hidden_t, features, ((1,), (0,))))

    def features_of(pair):
        return up_block(jnp.where(pair >= place, last - pair + place, place - 1 - pair))

    parts = {}

    def part_of(pair, after):
        if pair not in parts:
            features = features_of(pair)
            parts[pair] = product(behind(features, sent[after]) if after in sent else features)
        return parts[pair]

    hg_total = 0.0
    for turn in range(last):
        send(True, turn, part_of(turn, (True, turn - 1)))
        send(False, turn, part_of(last - 1 - turn, (False, turn - 1)))
        for pair in sorted({turn, last - 1 - turn}) if turn >= last // 2 else ():
            block = jnp.where(pair < place, got[True][pair], got[False][last - 1 - pair])
            hg_total = hg_total + contract(features_of(pair), block, ((1,), (1,)))

    own_up = behind(up_block(place), sent[True, 4])
    hg_total = hg_total + contract(own_up, weights, ((1,), (1,)))
    own_part = product(own_up)
    grads = (own_part + got[True][-1].astype(F32) + got[False][-1].astype(F32)) * scale_hid

    count = (step_index[0] + 1).astype(F32)
    first_new = 0.9 * first_moment + 0.1 * grads
    second_new = 0.999 * second_moment + 0.001 * grads * grads
    correct_one = 1.0 - jnp.power(F32(0.9), count)
    correct_two = 1.0 - jnp.power(F32(0.999), count)
    weights_f = weights.astype(F32)
    step_size = first_new / correct_one / (jnp.sqrt(second_new / correct_two) + 1e-08) + 0.1 * weights_f
    updated = (weights_f - 0.05 * step_size).astype(BF)

    half = updated.shape[0] // 2
    even_step = step_index[0] % 2 == 0
    lower, upper = updated[:half], updated[half:]
    near = lax.ppermute(jnp.where(even_step, lower, upper), "y", [(i, (i + 1) % 4) for i in range(4)])
    far = lax.ppermute(jnp.where(even_step, upper, lower), "y", [(i, (i + 2) % 4) for i in range(4)])
    partner = jnp.concatenate([jnp.where(even_step, near, far), jnp.where(even_step, far, near)], 0)
    mixed = ((updated.astype(F32) + partner.astype(F32)) * 0.5).astype(BF)

    in_grad = (hg_total * scale_hid).astype(BF)
    return mixed, first_new, second_new, in_grad


def solution(mesh):
    split = Mesh(mesh.devices.reshape(4, LINE, 2, 4, 2), ("y", "zl", "zh", "x", "c"))
    rep, tp = ("y", "zl"), ("zh", "x", "c")
    in_specs = (P(rep, tp), P(rep, tp), P(tp, rep), P(tp, rep), P(tp, rep), P())
    out_specs = (P(tp, rep), P(tp, rep), P(tp, rep), P(rep, tp))
    return jax.shard_map(body, mesh=split, in_specs=in_specs, out_specs=out_specs, check_vma=False)
```

time: 137 us -> 139 us (1.015)
  the two profiles are of different devices: /device:TPU:128 before, /device:TPU:106 now
where the time goes in v7:
time: 139 us; the launch traced here: 138 us
  starting transfers between devices  77.6 us (56%)
  waiting for transfers between devices  33.3 us (24%)
  blocking collectives  13.6 us (10%)
  matrix products  6.3 us (5%)
  other arithmetic  4.61 us (3%)
  between operations  2.17 us (2%)
    ppermute x16, starting transfers between devices, along(): lax.ppermute(value, 'zl', [(i, i + way) for i in range(LINE) if 0 <= i +...  57.5 us
    ppermute x16, waiting for transfers between devices, along(): lax.ppermute(value, 'zl', [(i, i + way) for i in range(LINE) if 0 <= i +...  15.7 us
    all_gather x1, blocking collectives, body(): lax.all_gather(jnp.concatenate([upstream, up_other], 1), 'x', axis=1, til...  13.6 us
    ppermute x1, starting transfers between devices, body(): up_other = lax.ppermute(upstream, 'zh', [(0, 1), (1, 0)])  11.9 us
    ppermute x1, waiting for transfers between devices, body(): up_other = lax.ppermute(upstream, 'zh', [(0, 1), (1, 0)])  11.6 us
    dot_general x16, matrix products, contract(): lax.dot_general(left, right, (dims, ((), ())), preferred_element_type=F32)  6.3 us
    ppermute x1, waiting for transfers between devices, body(): lax.ppermute(jnp.where(even_step, upper, lower), 'y', [(i, (i + 2) % 4) f...  4.05 us
    ppermute x1, starting transfers between devices, body(): lax.ppermute(jnp.where(even_step, lower, upper), 'y', [(i, (i + 1) % 4) f...  3.49 us
  transfers between devices with their start and end apart: 20, of which 12 were waited for; matrix products, arithmetic and copies ran while one was open for 5% of the time, Pallas kernels for 0%

profile of v7, /device:TPU:106, one launch (start us, length us, event | category | flops | bytes accessed | tf_op | source)
XLA Modules:
  0.0 138.4 jit_solution(13047637602390032898)
XLA Ops:
  0.6 5.2 %collective-permute-start = (bf16[448,256]{1,0:T(8,128)(2,1)}, bf16[448,256]{1,0:T(8,128)(2,1)S(1)}, u32[]{:S(2)}, u32[]{:S(2)}) collective-permute-start(bf16[448,256]{1,0:T(8,128)(2,1)} %param.8), channel_id=1, source_target_pairs={{0,16},{16,32},{32,48},{48,64},{64,80},{80,96},{96,112},{1,17},{17... | collective-permute-start | bytes 688136 | tf_op jit(solution)/shard_map/ppermute | solution.py:14
  5.8 1.9 %collective-permute-start.1 = (bf16[448,256]{1,0:T(8,128)(2,1)}, bf16[448,256]{1,0:T(8,128)(2,1)S(1)}, u32[]{:S(2)}, u32[]{:S(2)}) collective-permute-start(bf16[448,256]{1,0:T(8,128)(2,1)} %param.8), channel_id=1, source_target_pairs={{16,0},{32,16},{48,32},{64,48},{80,64},{96,80},{112,96},{17,1},{33... | collective-permute-start | bytes 688136 | tf_op jit(solution)/shard_map/ppermute | solution.py:14
  7.8 11.9 %collective-permute-start.2 = (bf16[448,128]{1,0:T(8,128)(2,1)}, bf16[448,128]{1,0:T(8,128)(2,1)S(1)}, u32[]{:S(2)}, u32[]{:S(2)}) collective-permute-start(bf16[448,128]{1,0:T(8,128)(2,1)} %param.7), channel_id=1, source_target_pairs={{0,8},{8,0},{1,9},{9,1},{2,10},{10,2},{3,11},{11,3},{4,12},{12,4},... | collective-permute-start | bytes 344072 | tf_op jit(solution)/shard_map/ppermute | solution.py:33
  20.3 11.6 %collective-permute-done.2 = bf16[448,128]{1,0:T(8,128)(2,1)S(1)} collective-permute-done((bf16[448,128]{1,0:T(8,128)(2,1)}, bf16[448,128]{1,0:T(8,128)(2,1)S(1)}, u32[]{:S(2)}, u32[]{:S(2)}) %collective-permute-start.2) | collective-permute-done | bytes 114720 | tf_op jit(solution)/shard_map/ppermute | solution.py:33
  31.9 0.9 pad_maximum_fusion
  32.8 13.6 %all_gather.3 = bf16[448,1024]{1,0:T(8,128)(2,1)S(1)} all-gather(bf16[448,256]{1,0:T(8,128)(2,1)S(1)} %pad_maximum_fusion), channel_id=1, replica_groups=mesh['y'=4,'zl'=8,'zh'=2,'x'=4,'c'=2] {'x'}, dimensions={1}, use_global_device_ids=true | all-gather | bytes 1146880 | tf_op jit(solution)/shard_map/all_gather | solution.py:40
  46.5 1.9 %collective-permute-start.3 = (bf16[448,1024]{1,0:T(8,128)(2,1)S(1)}, bf16[448,1024]{1,0:T(8,128)(2,1)S(1)}, u32[]{:S(2)}, u32[]{:S(2)}) collective-permute-start(bf16[448,1024]{1,0:T(8,128)(2,1)S(1)} %all_gather.3), channel_id=1, source_target_pairs={{0,1},{1,0},{2,3},{3,2},{4,5},{5,4},{6,7},{7,6},{8,9},{9,8},{10,11... | collective-permute-start | bytes 2752520 | tf_op jit(solution)/shard_map/ppermute | solution.py:41
  48.8 2.0 %collective-permute-done.3 = bf16[448,1024]{1,0:T(8,128)(2,1)S(1)} collective-permute-done((bf16[448,1024]{1,0:T(8,128)(2,1)S(1)}, bf16[448,1024]{1,0:T(8,128)(2,1)S(1)}, u32[]{:S(2)}, u32[]{:S(2)}) %collective-permute-start.3) | collective-permute-done | bytes 917536 | tf_op jit(solution)/shard_map/ppermute | solution.py:41
  52.5 3.7 %collective-permute-start.4 = (bf16[448,256]{1,0:T(8,128)(2,1)S(1)}, bf16[448,256]{1,0:T(8,128)(2,1)S(1)}, u32[]{:S(2)}, u32[]{:S(2)}) collective-permute-start(bf16[448,256]{1,0:T(8,128)(2,1)S(1)} %fusion.11), channel_id=1, source_target_pairs={{0,16},{16,32},{32,48},{48,64},{64,80},{80,96},{96,112},{1,17},{17... | collective-permute-start | bytes 688136 | tf_op jit(solution)/shard_map/ppermute | solution.py:14
  56.3 2.2 %collective-permute-start.5 = (bf16[448,256]{1,0:T(8,128)(2,1)S(1)}, bf16[448,256]{1,0:T(8,128)(2,1)S(1)}, u32[]{:S(2)}, u32[]{:S(2)}) collective-permute-start(bf16[448,256]{1,0:T(8,128)(2,1)S(1)} %fusion.12), channel_id=1, source_target_pairs={{16,0},{32,16},{48,32},{64,48},{80,64},{96,80},{112,96},{17,1},{33... | collective-permute-start | bytes 688136 | tf_op jit(solution)/shard_map/ppermute | solution.py:14
  59.2 2.9 %collective-permute-done.4 = bf16[448,256]{1,0:T(8,128)(2,1)S(1)} collective-permute-done((bf16[448,256]{1,0:T(8,128)(2,1)S(1)}, bf16[448,256]{1,0:T(8,128)(2,1)S(1)}, u32[]{:S(2)}, u32[]{:S(2)}) %collective-permute-start.4) | collective-permute-done | bytes 229408 | tf_op jit(solution)/shard_map/ppermute | solution.py:14
  62.2 4.9 %collective-permute-start.6 = (bf16[448,256]{1,0:T(8,128)(2,1)S(1)}, bf16[448,256]{1,0:T(8,128)(2,1)S(1)}, u32[]{:S(2)}, u32[]{:S(2)}) collective-permute-start(bf16[448,256]{1,0:T(8,128)(2,1)S(1)} %fusion.13), channel_id=1, source_target_pairs={{0,16},{16,32},{32,48},{48,64},{64,80},{80,96},{96,112},{1,17},{17... | collective-permute-start | bytes 688136 | tf_op jit(solution)/shard_map/ppermute | solution.py:14
  67.2 1.9 %collective-permute-start.7 = (bf16[448,256]{1,0:T(8,128)(2,1)S(1)}, bf16[448,256]{1,0:T(8,128)(2,1)S(1)}, u32[]{:S(2)}, u32[]{:S(2)}) collective-permute-start(bf16[448,256]{1,0:T(8,128)(2,1)S(1)} %fusion.14), channel_id=1, source_target_pairs={{16,0},{32,16},{48,32},{64,48},{80,64},{96,80},{112,96},{17,1},{33... | collective-permute-start | bytes 688136 | tf_op jit(solution)/shard_map/ppermute | solution.py:14
  69.8 1.5 %collective-permute-done.6 = bf16[448,256]{1,0:T(8,128)(2,1)S(1)} collective-permute-done((bf16[448,256]{1,0:T(8,128)(2,1)S(1)}, bf16[448,256]{1,0:T(8,128)(2,1)S(1)}, u32[]{:S(2)}, u32[]{:S(2)}) %collective-permute-start.6) | collective-permute-done | bytes 229408 | tf_op jit(solution)/shard_map/ppermute | solution.py:14
  71.5 5.6 %collective-permute-start.8 = (bf16[448,256]{1,0:T(8,128)(2,1)S(1)}, bf16[448,256]{1,0:T(8,128)(2,1)S(1)}, u32[]{:S(2)}, u32[]{:S(2)}) collective-permute-start(bf16[448,256]{1,0:T(8,128)(2,1)S(1)} %fusion.15), channel_id=1, source_target_pairs={{0,16},{16,32},{32,48},{48,64},{64,80},{80,96},{96,112},{1,17},{17... | collective-permute-start | bytes 688136 | tf_op jit(solution)/shard_map/ppermute | solution.py:14
  77.2 1.9 %collective-permute-start.9 = (bf16[448,256]{1,0:T(8,128)(2,1)S(1)}, bf16[448,256]{1,0:T(8,128)(2,1)S(1)}, u32[]{:S(2)}, u32[]{:S(2)}) collective-permute-start(bf16[448,256]{1,0:T(8,128)(2,1)S(1)} %fusion.16), channel_id=1, source_target_pairs={{16,0},{32,16},{48,32},{64,48},{80,64},{96,80},{112,96},{17,1},{33... | collective-permute-start | bytes 688136 | tf_op jit(solution)/shard_map/ppermute | solution.py:14
  79.5 1.1 collective-permute-done.8
  80.7 5.6 %collective-permute-start.10 = (bf16[448,256]{1,0:T(8,128)(2,1)S(1)}, bf16[448,256]{1,0:T(8,128)(2,1)S(1)}, u32[]{:S(2)}, u32[]{:S(2)}) collective-permute-start(bf16[448,256]{1,0:T(8,128)(2,1)S(1)} %fusion.17), channel_id=1, source_target_pairs={{0,16},{16,32},{32,48},{48,64},{64,80},{80,96},{96,112},{1,17},{17... | collective-permute-start | bytes 688136 | tf_op jit(solution)/shard_map/ppermute | solution.py:14
  86.4 1.9 %collective-permute-start.11 = (bf16[448,256]{1,0:T(8,128)(2,1)S(1)}, bf16[448,256]{1,0:T(8,128)(2,1)S(1)}, u32[]{:S(2)}, u32[]{:S(2)}) collective-permute-start(bf16[448,256]{1,0:T(8,128)(2,1)S(1)} %fusion.18), channel_id=1, source_target_pairs={{16,0},{32,16},{48,32},{64,48},{80,64},{96,80},{112,96},{17,1},{33... | collective-permute-start | bytes 688136 | tf_op jit(solution)/shard_map/ppermute | solution.py:14
  88.3 1.5 %collective-permute-done.10 = bf16[448,256]{1,0:T(8,128)(2,1)S(1)} collective-permute-done((bf16[448,256]{1,0:T(8,128)(2,1)S(1)}, bf16[448,256]{1,0:T(8,128)(2,1)S(1)}, u32[]{:S(2)}, u32[]{:S(2)}) %collective-permute-start.10) | collective-permute-done | bytes 229408 | tf_op jit(solution)/shard_map/ppermute | solution.py:14
  89.9 5.6 %collective-permute-start.12 = (bf16[448,256]{1,0:T(8,128)(2,1)S(1)}, bf16[448,256]{1,0:T(8,128)(2,1)S(1)}, u32[]{:S(2)}, u32[]{:S(2)}) collective-permute-start(bf16[448,256]{1,0:T(8,128)(2,1)S(1)} %fusion.19), channel_id=1, source_target_pairs={{0,16},{16,32},{32,48},{48,64},{64,80},{80,96},{96,112},{1,17},{17... | collective-permute-start | bytes 688136 | tf_op jit(solution)/shard_map/ppermute | solution.py:14
  96.3 1.9 %collective-permute-start.13 = (bf16[448,256]{1,0:T(8,128)(2,1)S(1)}, bf16[448,256]{1,0:T(8,128)(2,1)S(1)}, u32[]{:S(2)}, u32[]{:S(2)}) collective-permute-start(bf16[448,256]{1,0:T(8,128)(2,1)S(1)} %fusion.20), channel_id=1, source_target_pairs={{16,0},{32,16},{48,32},{64,48},{80,64},{96,80},{112,96},{17,1},{33... | collective-permute-start | bytes 688136 | tf_op jit(solution)/shard_map/ppermute | solution.py:14
  99.1 5.6 %collective-permute-start.14 = (bf16[448,256]{1,0:T(8,128)(2,1)S(1)}, bf16[448,256]{1,0:T(8,128)(2,1)S(1)}, u32[]{:S(2)}, u32[]{:S(2)}) collective-permute-start(bf16[448,256]{1,0:T(8,128)(2,1)S(1)} %fusion.21), channel_id=1, source_target_pairs={{0,16},{16,32},{32,48},{48,64},{64,80},{80,96},{96,112},{1,17},{17... | collective-permute-start | bytes 688136 | tf_op jit(solution)/shard_map/ppermute | solution.py:14
  105.5 1.9 %collective-permute-start.16 = (bf16[448,256]{1,0:T(8,128)(2,1)S(1)}, bf16[448,256]{1,0:T(8,128)(2,1)S(1)}, u32[]{:S(2)}, u32[]{:S(2)}) collective-permute-start(bf16[448,256]{1,0:T(8,128)(2,1)S(1)} %fusion.22), channel_id=1, source_target_pairs={{16,0},{32,16},{48,32},{64,48},{80,64},{96,80},{112,96},{17,1},{33... | collective-permute-start | bytes 688136 | tf_op jit(solution)/shard_map/ppermute | solution.py:14
  108.7 5.6 %collective-permute-start.15 = (bf16[448,256]{1,0:T(8,128)(2,1)S(1)}, bf16[448,256]{1,0:T(8,128)(2,1)S(1)}, u32[]{:S(2)}, u32[]{:S(2)}) collective-permute-start(bf16[448,256]{1,0:T(8,128)(2,1)S(1)} %fusion.23), channel_id=1, source_target_pairs={{0,16},{16,32},{32,48},{48,64},{64,80},{80,96},{96,112},{1,17},{17... | collective-permute-start | bytes 688136 | tf_op jit(solution)/shard_map/ppermute | solution.py:14
  115.3 2.1 %collective-permute-start.17 = (bf16[448,256]{1,0:T(8,128)(2,1)S(1)}, bf16[448,256]{1,0:T(8,128)(2,1)S(1)}, u32[]{:S(2)}, u32[]{:S(2)}) collective-permute-start(bf16[448,256]{1,0:T(8,128)(2,1)S(1)} %fusion.24), channel_id=1, source_target_pairs={{16,0},{32,16},{48,32},{64,48},{80,64},{96,80},{112,96},{17,1},{33... | collective-permute-start | bytes 688136 | tf_op jit(solution)/shard_map/ppermute | solution.py:14
  118.0 6.6 %collective-permute-done.17 = bf16[448,256]{1,0:T(8,128)(2,1)S(1)} collective-permute-done((bf16[448,256]{1,0:T(8,128)(2,1)S(1)}, bf16[448,256]{1,0:T(8,128)(2,1)S(1)}, u32[]{:S(2)}, u32[]{:S(2)}) %collective-permute-start.17) | collective-permute-done | bytes 229408 | tf_op jit(solution)/shard_map/ppermute | solution.py:14
  124.5 1.4 fusion.10
  125.9 3.5 %collective-permute-start.18 = (bf16[224,256]{1,0:T(8,128)(2,1)S(1)}, bf16[224,256]{1,0:T(8,128)(2,1)S(1)}, u32[]{:S(2)}, u32[]{:S(2)}) collective-permute-start(bf16[224,256]{1,0:T(8,128)(2,1)S(1)} %get-tuple-element.11), channel_id=1, source_target_pairs={{0,128},{128,256},{256,384},{384,0},{1,129},{129,257},{257,385},{3... | collective-permute-start | bytes 344072 | tf_op jit(solution)/shard_map/ppermute | solution.py:100
  129.4 2.8 %collective-permute-start.19 = (bf16[224,256]{1,0:T(8,128)(2,1)S(1)}, bf16[224,256]{1,0:T(8,128)(2,1)S(1)}, u32[]{:S(2)}, u32[]{:S(2)}) collective-permute-start(bf16[224,256]{1,0:T(8,128)(2,1)S(1)} %get-tuple-element.12), channel_id=1, source_target_pairs={{0,256},{128,384},{256,0},{384,128},{1,257},{129,385},{257,1},{385... | collective-permute-start | bytes 344072 | tf_op jit(solution)/shard_map/ppermute | solution.py:101
  132.3 1.3 fusion.7
  133.5 4.0 %collective-permute-done.19 = bf16[224,256]{1,0:T(8,128)(2,1)S(1)} collective-permute-done((bf16[224,256]{1,0:T(8,128)(2,1)S(1)}, bf16[224,256]{1,0:T(8,128)(2,1)S(1)}, u32[]{:S(2)}, u32[]{:S(2)}) %collective-permute-start.19) | collective-permute-done | bytes 114720 | tf_op jit(solution)/shard_map/ppermute | solution.py:101
  (70 shorter events, 10.2 us)
Async XLA Ops:
  0.6 48.1 %copy-start = (bf16[448,448]{1,0:T(8,128)(2,1)S(1)}, bf16[448,448]{1,0:T(8,128)(2,1)}, u32[]{:S(2)}) copy-start(bf16[448,448]{1,0:T(8,128)(2,1)} %param.6) | copy-start | bytes 1204228
  0.6 31.2 %collective-permute-start = (bf16[448,256]{1,0:T(8,128)(2,1)}, bf16[448,256]{1,0:T(8,128)(2,1)S(1)}, u32[]{:S(2)}, u32[]{:S(2)}) collective-permute-start(bf16[448,256]{1,0:T(8,128)(2,1)} %param.8), channel_id=1, source_target_pairs={{0,16},{16,32},{32,48},{48,64},{64,80},{80,96},{96,112},{1,17},{17... | collective-permute-start | bytes 688136 | tf_op jit(solution)/shard_map/ppermute | solution.py:14
  5.8 26.1 %collective-permute-start.1 = (bf16[448,256]{1,0:T(8,128)(2,1)}, bf16[448,256]{1,0:T(8,128)(2,1)S(1)}, u32[]{:S(2)}, u32[]{:S(2)}) collective-permute-start(bf16[448,256]{1,0:T(8,128)(2,1)} %param.8), channel_id=1, source_target_pairs={{16,0},{32,16},{48,32},{64,48},{80,64},{96,80},{112,96},{17,1},{33... | collective-permute-start | bytes 688136 | tf_op jit(solution)/shard_map/ppermute | solution.py:14
  7.8 24.1 %collective-permute-start.2 = (bf16[448,128]{1,0:T(8,128)(2,1)}, bf16[448,128]{1,0:T(8,128)(2,1)S(1)}, u32[]{:S(2)}, u32[]{:S(2)}) collective-permute-start(bf16[448,128]{1,0:T(8,128)(2,1)} %param.7), channel_id=1, source_target_pairs={{0,8},{8,0},{1,9},{9,1},{2,10},{10,2},{3,11},{11,3},{4,12},{12,4},... | collective-permute-start | bytes 344072 | tf_op jit(solution)/shard_map/ppermute | solution.py:33
  46.5 4.4 %collective-permute-start.3 = (bf16[448,1024]{1,0:T(8,128)(2,1)S(1)}, bf16[448,1024]{1,0:T(8,128)(2,1)S(1)}, u32[]{:S(2)}, u32[]{:S(2)}) collective-permute-start(bf16[448,1024]{1,0:T(8,128)(2,1)S(1)} %all_gather.3), channel_id=1, source_target_pairs={{0,1},{1,0},{2,3},{3,2},{4,5},{5,4},{6,7},{7,6},{8,9},{9,8},{10,11... | collective-permute-start | bytes 2752520 | tf_op jit(solution)/shard_map/ppermute | solution.py:41
  52.5 9.5 %collective-permute-start.4 = (bf16[448,256]{1,0:T(8,128)(2,1)S(1)}, bf16[448,256]{1,0:T(8,128)(2,1)S(1)}, u32[]{:S(2)}, u32[]{:S(2)}) collective-permute-start(bf16[448,256]{1,0:T(8,128)(2,1)S(1)} %fusion.11), channel_id=1, source_target_pairs={{0,16},{16,32},{32,48},{48,64},{64,80},{80,96},{96,112},{1,17},{17... | collective-permute-start | bytes 688136 | tf_op jit(solution)/shard_map/ppermute | solution.py:14
  56.3 10.7 %collective-permute-start.5 = (bf16[448,256]{1,0:T(8,128)(2,1)S(1)}, bf16[448,256]{1,0:T(8,128)(2,1)S(1)}, u32[]{:S(2)}, u32[]{:S(2)}) collective-permute-start(bf16[448,256]{1,0:T(8,128)(2,1)S(1)} %fusion.12), channel_id=1, source_target_pairs={{16,0},{32,16},{48,32},{64,48},{80,64},{96,80},{112,96},{17,1},{33... | collective-permute-start | bytes 688136 | tf_op jit(solution)/shard_map/ppermute | solution.py:14
  62.2 9.2 %collective-permute-start.6 = (bf16[448,256]{1,0:T(8,128)(2,1)S(1)}, bf16[448,256]{1,0:T(8,128)(2,1)S(1)}, u32[]{:S(2)}, u32[]{:S(2)}) collective-permute-start(bf16[448,256]{1,0:T(8,128)(2,1)S(1)} %fusion.13), channel_id=1, source_target_pairs={{0,16},{16,32},{32,48},{48,64},{64,80},{80,96},{96,112},{1,17},{17... | collective-permute-start | bytes 688136 | tf_op jit(solution)/shard_map/ppermute | solution.py:14
  67.2 9.9 %collective-permute-start.7 = (bf16[448,256]{1,0:T(8,128)(2,1)S(1)}, bf16[448,256]{1,0:T(8,128)(2,1)S(1)}, u32[]{:S(2)}, u32[]{:S(2)}) collective-permute-start(bf16[448,256]{1,0:T(8,128)(2,1)S(1)} %fusion.14), channel_id=1, source_target_pairs={{16,0},{32,16},{48,32},{64,48},{80,64},{96,80},{112,96},{17,1},{33... | collective-permute-start | bytes 688136 | tf_op jit(solution)/shard_map/ppermute | solution.py:14
  71.5 9.1 %collective-permute-start.8 = (bf16[448,256]{1,0:T(8,128)(2,1)S(1)}, bf16[448,256]{1,0:T(8,128)(2,1)S(1)}, u32[]{:S(2)}, u32[]{:S(2)}) collective-permute-start(bf16[448,256]{1,0:T(8,128)(2,1)S(1)} %fusion.15), channel_id=1, source_target_pairs={{0,16},{16,32},{32,48},{48,64},{64,80},{80,96},{96,112},{1,17},{17... | collective-permute-start | bytes 688136 | tf_op jit(solution)/shard_map/ppermute | solution.py:14
  77.2 9.1 %collective-permute-start.9 = (bf16[448,256]{1,0:T(8,128)(2,1)S(1)}, bf16[448,256]{1,0:T(8,128)(2,1)S(1)}, u32[]{:S(2)}, u32[]{:S(2)}) collective-permute-start(bf16[448,256]{1,0:T(8,128)(2,1)S(1)} %fusion.16), channel_id=1, source_target_pairs={{16,0},{32,16},{48,32},{64,48},{80,64},{96,80},{112,96},{17,1},{33... | collective-permute-start | bytes 688136 | tf_op jit(solution)/shard_map/ppermute | solution.py:14
  79.5 16.0 %copy-start.1 = (bf16[448,256]{1,0:T(8,128)(2,1)S(1)}, bf16[448,256]{1,0:T(8,128)(2,1)}, u32[]{:S(2)}) copy-start(bf16[448,256]{1,0:T(8,128)(2,1)} %param.8) | copy-start | bytes 688132
  80.7 9.1 %collective-permute-start.10 = (bf16[448,256]{1,0:T(8,128)(2,1)S(1)}, bf16[448,256]{1,0:T(8,128)(2,1)S(1)}, u32[]{:S(2)}, u32[]{:S(2)}) collective-permute-start(bf16[448,256]{1,0:T(8,128)(2,1)S(1)} %fusion.17), channel_id=1, source_target_pairs={{0,16},{16,32},{32,48},{48,64},{64,80},{80,96},{96,112},{1,17},{17... | collective-permute-start | bytes 688136 | tf_op jit(solution)/shard_map/ppermute | solution.py:14
  86.4 9.8 %collective-permute-start.11 = (bf16[448,256]{1,0:T(8,128)(2,1)S(1)}, bf16[448,256]{1,0:T(8,128)(2,1)S(1)}, u32[]{:S(2)}, u32[]{:S(2)}) collective-permute-start(bf16[448,256]{1,0:T(8,128)(2,1)S(1)} %fusion.18), channel_id=1, source_target_pairs={{16,0},{32,16},{48,32},{64,48},{80,64},{96,80},{112,96},{17,1},{33... | collective-permute-start | bytes 688136 | tf_op jit(solution)/shard_map/ppermute | solution.py:14
  89.9 9.1 %collective-permute-start.12 = (bf16[448,256]{1,0:T(8,128)(2,1)S(1)}, bf16[448,256]{1,0:T(8,128)(2,1)S(1)}, u32[]{:S(2)}, u32[]{:S(2)}) collective-permute-start(bf16[448,256]{1,0:T(8,128)(2,1)S(1)} %fusion.19), channel_id=1, source_target_pairs={{0,16},{16,32},{32,48},{48,64},{64,80},{80,96},{96,112},{1,17},{17... | collective-permute-start | bytes 688136 | tf_op jit(solution)/shard_map/ppermute | solution.py:14
  96.3 9.1 %collective-permute-start.13 = (bf16[448,256]{1,0:T(8,128)(2,1)S(1)}, bf16[448,256]{1,0:T(8,128)(2,1)S(1)}, u32[]{:S(2)}, u32[]{:S(2)}) collective-permute-start(bf16[448,256]{1,0:T(8,128)(2,1)S(1)} %fusion.20), channel_id=1, source_target_pairs={{16,0},{32,16},{48,32},{64,48},{80,64},{96,80},{112,96},{17,1},{33... | collective-permute-start | bytes 688136 | tf_op jit(solution)/shard_map/ppermute | solution.py:14
  99.1 9.5 %collective-permute-start.14 = (bf16[448,256]{1,0:T(8,128)(2,1)S(1)}, bf16[448,256]{1,0:T(8,128)(2,1)S(1)}, u32[]{:S(2)}, u32[]{:S(2)}) collective-permute-start(bf16[448,256]{1,0:T(8,128)(2,1)S(1)} %fusion.21), channel_id=1, source_target_pairs={{0,16},{16,32},{32,48},{48,64},{64,80},{80,96},{96,112},{1,17},{17... | collective-permute-start | bytes 688136 | tf_op jit(solution)/shard_map/ppermute | solution.py:14
  105.5 9.6 %collective-permute-start.16 = (bf16[448,256]{1,0:T(8,128)(2,1)S(1)}, bf16[448,256]{1,0:T(8,128)(2,1)S(1)}, u32[]{:S(2)}, u32[]{:S(2)}) collective-permute-start(bf16[448,256]{1,0:T(8,128)(2,1)S(1)} %fusion.22), channel_id=1, source_target_pairs={{16,0},{32,16},{48,32},{64,48},{80,64},{96,80},{112,96},{17,1},{33... | collective-permute-start | bytes 688136 | tf_op jit(solution)/shard_map/ppermute | solution.py:14
  108.7 15.8 %collective-permute-start.15 = (bf16[448,256]{1,0:T(8,128)(2,1)S(1)}, bf16[448,256]{1,0:T(8,128)(2,1)S(1)}, u32[]{:S(2)}, u32[]{:S(2)}) collective-permute-start(bf16[448,256]{1,0:T(8,128)(2,1)S(1)} %fusion.23), channel_id=1, source_target_pairs={{0,16},{16,32},{32,48},{48,64},{64,80},{80,96},{96,112},{1,17},{17... | collective-permute-start | bytes 688136 | tf_op jit(solution)/shard_map/ppermute | solution.py:14
  115.2 9.3 %copy-start.2 = (f32[448,256]{1,0:T(8,128)S(1)}, f32[448,256]{1,0:T(8,128)}, u32[]{:S(2)}) copy-start(f32[448,256]{1,0:T(8,128)} %param.10) | copy-start | bytes 1376260
  115.2 9.3 %copy-start.3 = (f32[448,256]{1,0:T(8,128)S(1)}, f32[448,256]{1,0:T(8,128)}, u32[]{:S(2)}) copy-start(f32[448,256]{1,0:T(8,128)} %param.9) | copy-start | bytes 1376260
  115.3 9.3 %collective-permute-start.17 = (bf16[448,256]{1,0:T(8,128)(2,1)S(1)}, bf16[448,256]{1,0:T(8,128)(2,1)S(1)}, u32[]{:S(2)}, u32[]{:S(2)}) collective-permute-start(bf16[448,256]{1,0:T(8,128)(2,1)S(1)} %fusion.24), channel_id=1, source_target_pairs={{16,0},{32,16},{48,32},{64,48},{80,64},{96,80},{112,96},{17,1},{33... | collective-permute-start | bytes 688136 | tf_op jit(solution)/shard_map/ppermute | solution.py:14
  125.9 7.6 %collective-permute-start.18 = (bf16[224,256]{1,0:T(8,128)(2,1)S(1)}, bf16[224,256]{1,0:T(8,128)(2,1)S(1)}, u32[]{:S(2)}, u32[]{:S(2)}) collective-permute-start(bf16[224,256]{1,0:T(8,128)(2,1)S(1)} %get-tuple-element.11), channel_id=1, source_target_pairs={{0,128},{128,256},{256,384},{384,0},{1,129},{129,257},{257,385},{3... | collective-permute-start | bytes 344072 | tf_op jit(solution)/shard_map/ppermute | solution.py:100
  129.4 8.2 %collective-permute-start.19 = (bf16[224,256]{1,0:T(8,128)(2,1)S(1)}, bf16[224,256]{1,0:T(8,128)(2,1)S(1)}, u32[]{:S(2)}, u32[]{:S(2)}) collective-permute-start(bf16[224,256]{1,0:T(8,128)(2,1)S(1)} %get-tuple-element.12), channel_id=1, source_target_pairs={{0,256},{128,384},{256,0},{384,128},{1,257},{129,385},{257,1},{385... | collective-permute-start | bytes 344072 | tf_op jit(solution)/shard_map/ppermute | solution.py:101

commit v8 on v7

--- a/solution.py
+++ b/solution.py
@@ -32,13 +32,16 @@
 
     up_other = lax.ppermute(upstream, "zh", [(0, 1), (1, 0)])
     hidden_t = lax.optimization_barrier(hidden.T)
-    got = {True: [along(weights, 1)], False: [along(weights, -1)]}
+    both_up = lax.optimization_barrier(jnp.concatenate([upstream, up_other], 1))
+    weights_after = lax.optimization_barrier(behind(weights, both_up))
+    got = {True: [along(weights_after, 1)], False: [along(weights_after, -1)]}
     sent = {}
 
+    of_core = lax.all_gather(behind(both_up, weights_after), "x", axis=1, tiled=True)
+    to_other = of_core
     for hop in (got[True][0], got[False][0]):
-        up_other = behind(up_other, hop[:, : up_other.shape[1]])
-    of_core = lax.all_gather(jnp.concatenate([upstream, up_other], 1), "x", axis=1, tiled=True)
-    of_other = lax.ppermute(of_core, "c", [(0, 1), (1, 0)])
+        to_other = behind(to_other, jnp.concatenate([hop] * (of_core.shape[1] // width), 1))
+    of_other = lax.ppermute(to_other, "c", [(0, 1), (1, 0)])
     of_first = jnp.where(second_core, of_other, of_core)
     of_second = jnp.where(second_core, of_core, of_other)
     cuts = range(0, of_core.shape[1], piece)
@@ -97,8 +100,8 @@
     half = updated.shape[0] // 2
     even_step = step_index[0] % 2 == 0
     lower, upper = updated[:half], updated[half:]
+    far = lax.ppermute(jnp.where(even_step, upper, lower), "y", [(i, (i + 2) % 4) for i in range(4)])
     near = lax.ppermute(jnp.where(even_step, lower, upper), "y", [(i, (i + 1) % 4) for i in range(4)])
-    far = lax.ppermute(jnp.where(even_step, upper, lower), "y", [(i, (i + 2) % 4) for i in range(4)])
     partner = jnp.concatenate([jnp.where(even_step, near, far), jnp.where(even_step, far, near)], 0)
     mixed = ((updated.astype(F32) + partner.astype(F32)) * 0.5).astype(BF)
 

time: 139 us -> 140 us (level)
  the two profiles are of different devices: /device:TPU:106 before, /device:TPU:104 now
where the time goes in v8:
time: 140 us; the launch traced here: 139 us
  starting transfers between devices  83.3 us (60%)
  waiting for transfers between devices  24.8 us (18%)
  blocking collectives  14.8 us (11%)
  other arithmetic  7.11 us (5%)
  matrix products  6.29 us (4%)
  between operations  2.18 us (2%)
    ppermute x16, starting transfers between devices, along(): lax.ppermute(value, 'zl', [(i, i + way) for i in range(LINE) if 0 <= i +...  61.9 us
    ppermute x16, waiting for transfers between devices, along(): lax.ppermute(value, 'zl', [(i, i + way) for i in range(LINE) if 0 <= i +...  15.7 us
    all_gather x1, blocking collectives, body(): lax.all_gather(behind(both_up, weights_after), 'x', axis=1, tiled=True)  14.8 us
    ppermute x1, starting transfers between devices, body(): up_other = lax.ppermute(upstream, 'zh', [(0, 1), (1, 0)])  13.2 us
    dot_general x16, matrix products, contract(): lax.dot_general(left, right, (dims, ((), ())), preferred_element_type=F32)  6.29 us
    ppermute x1, waiting for transfers between devices, body(): lax.ppermute(jnp.where(even_step, upper, lower), 'y', [(i, (i + 2) % 4) f...  4.05 us
    ppermute x1, starting transfers between devices, body(): lax.ppermute(jnp.where(even_step, lower, upper), 'y', [(i, (i + 1) % 4) f...  3.48 us
    ppermute x1, waiting for transfers between devices, body(): up_other = lax.ppermute(upstream, 'zh', [(0, 1), (1, 0)])  2.93 us
  transfers between devices with their start and end apart: 20, of which 12 were waited for; matrix products, arithmetic and copies ran while one was open for 5% of the time, Pallas kernels for 0%

profile of v8, /device:TPU:104, one launch (start us, length us, event | category | flops | bytes accessed | tf_op | source)
XLA Modules:
  0.0 139.2 jit_solution(17710104107345550795)
XLA Ops:
  0.6 13.2 %collective-permute-start = (bf16[448,128]{1,0:T(8,128)(2,1)}, bf16[448,128]{1,0:T(8,128)(2,1)S(1)}, u32[]{:S(2)}, u32[]{:S(2)}) collective-permute-start(bf16[448,128]{1,0:T(8,128)(2,1)} %param.7), channel_id=1, source_target_pairs={{0,8},{8,0},{1,9},{9,1},{2,10},{10,2},{3,11},{11,3},{4,12},{12,4},... | collective-permute-start | bytes 344072 | tf_op jit(solution)/shard_map/ppermute | solution.py:33
  14.5 2.9 %collective-permute-done = bf16[448,128]{1,0:T(8,128)(2,1)S(1)} collective-permute-done((bf16[448,128]{1,0:T(8,128)(2,1)}, bf16[448,128]{1,0:T(8,128)(2,1)S(1)}, u32[]{:S(2)}, u32[]{:S(2)}) %collective-permute-start) | collective-permute-done | bytes 114720 | tf_op jit(solution)/shard_map/ppermute | solution.py:33
  19.3 5.4 %collective-permute-start.2 = (bf16[448,256]{1,0:T(8,128)(2,1)S(1)}, bf16[448,256]{1,0:T(8,128)(2,1)S(1)}, u32[]{:S(2)}, u32[]{:S(2)}) collective-permute-start(bf16[448,256]{1,0:T(8,128)(2,1)S(1)} %broadcast_select_fusion.3), channel_id=1, source_target_pairs={{16,0},{32,16},{48,32},{64,48},{80,64},{96,80},{112,96},{17,1},{33... | collective-permute-start | bytes 688136 | tf_op jit(solution)/shard_map/ppermute | solution.py:14
  24.7 5.9 %collective-permute-start.1 = (bf16[448,256]{1,0:T(8,128)(2,1)S(1)}, bf16[448,256]{1,0:T(8,128)(2,1)S(1)}, u32[]{:S(2)}, u32[]{:S(2)}) collective-permute-start(bf16[448,256]{1,0:T(8,128)(2,1)S(1)} %broadcast_select_fusion.3), channel_id=1, source_target_pairs={{0,16},{16,32},{32,48},{48,64},{64,80},{80,96},{96,112},{1,17},{17... | collective-permute-start | bytes 688136 | tf_op jit(solution)/shard_map/ppermute | solution.py:14
  30.6 14.8 %all_gather.3 = bf16[448,1024]{1,0:T(8,128)(2,1)S(1)} all-gather(bf16[448,256]{1,0:T(8,128)(2,1)S(1)} %broadcast_select_fusion.2), channel_id=1, replica_groups=mesh['y'=4,'zl'=8,'zh'=2,'x'=4,'c'=2] {'x'}, dimensions={1}, use_global_device_ids=true | all-gather | bytes 1146880 | tf_op jit(solution)/shard_map/all_gather | solution.py:40
  45.7 1.9 %collective-permute-start.3 = (bf16[448,1024]{1,0:T(8,128)(2,1)S(1)}, bf16[448,1024]{1,0:T(8,128)(2,1)}, u32[]{:S(2)}, u32[]{:S(2)}) collective-permute-start(bf16[448,1024]{1,0:T(8,128)(2,1)S(1)} %maximum_select_fusion), channel_id=1, source_target_pairs={{0,1},{1,0},{2,3},{3,2},{4,5},{5,4},{6,7},{7,6},{8,9},{9,8},{10,11... | collective-permute-start | bytes 2752520 | tf_op jit(solution)/shard_map/ppermute | solution.py:44
  48.1 2.2 %collective-permute-done.3 = bf16[448,1024]{1,0:T(8,128)(2,1)} collective-permute-done((bf16[448,1024]{1,0:T(8,128)(2,1)S(1)}, bf16[448,1024]{1,0:T(8,128)(2,1)}, u32[]{:S(2)}, u32[]{:S(2)}) %collective-permute-start.3) | collective-permute-done | bytes 917536 | tf_op jit(solution)/shard_map/ppermute | solution.py:44
  50.2 1.3 broadcast_select_fusion
  53.1 3.9 %collective-permute-start.4 = (bf16[448,256]{1,0:T(8,128)(2,1)S(1)}, bf16[448,256]{1,0:T(8,128)(2,1)S(1)}, u32[]{:S(2)}, u32[]{:S(2)}) collective-permute-start(bf16[448,256]{1,0:T(8,128)(2,1)S(1)} %fusion.11), channel_id=1, source_target_pairs={{0,16},{16,32},{32,48},{48,64},{64,80},{80,96},{96,112},{1,17},{17... | collective-permute-start | bytes 688136 | tf_op jit(solution)/shard_map/ppermute | solution.py:14
  57.1 1.9 %collective-permute-start.5 = (bf16[448,256]{1,0:T(8,128)(2,1)S(1)}, bf16[448,256]{1,0:T(8,128)(2,1)S(1)}, u32[]{:S(2)}, u32[]{:S(2)}) collective-permute-start(bf16[448,256]{1,0:T(8,128)(2,1)S(1)} %fusion.12), channel_id=1, source_target_pairs={{16,0},{32,16},{48,32},{64,48},{80,64},{96,80},{112,96},{17,1},{33... | collective-permute-start | bytes 688136 | tf_op jit(solution)/shard_map/ppermute | solution.py:14
  59.8 2.8 %collective-permute-done.4 = bf16[448,256]{1,0:T(8,128)(2,1)S(1)} collective-permute-done((bf16[448,256]{1,0:T(8,128)(2,1)S(1)}, bf16[448,256]{1,0:T(8,128)(2,1)S(1)}, u32[]{:S(2)}, u32[]{:S(2)}) %collective-permute-start.4) | collective-permute-done | bytes 229408 | tf_op jit(solution)/shard_map/ppermute | solution.py:14
  62.8 5.1 %collective-permute-start.6 = (bf16[448,256]{1,0:T(8,128)(2,1)S(1)}, bf16[448,256]{1,0:T(8,128)(2,1)S(1)}, u32[]{:S(2)}, u32[]{:S(2)}) collective-permute-start(bf16[448,256]{1,0:T(8,128)(2,1)S(1)} %fusion.13), channel_id=1, source_target_pairs={{0,16},{16,32},{32,48},{48,64},{64,80},{80,96},{96,112},{1,17},{17... | collective-permute-start | bytes 688136 | tf_op jit(solution)/shard_map/ppermute | solution.py:14
  68.0 1.9 %collective-permute-start.7 = (bf16[448,256]{1,0:T(8,128)(2,1)S(1)}, bf16[448,256]{1,0:T(8,128)(2,1)S(1)}, u32[]{:S(2)}, u32[]{:S(2)}) collective-permute-start(bf16[448,256]{1,0:T(8,128)(2,1)S(1)} %fusion.14), channel_id=1, source_target_pairs={{16,0},{32,16},{48,32},{64,48},{80,64},{96,80},{112,96},{17,1},{33... | collective-permute-start | bytes 688136 | tf_op jit(solution)/shard_map/ppermute | solution.py:14
  70.7 1.5 %collective-permute-done.6 = bf16[448,256]{1,0:T(8,128)(2,1)S(1)} collective-permute-done((bf16[448,256]{1,0:T(8,128)(2,1)S(1)}, bf16[448,256]{1,0:T(8,128)(2,1)S(1)}, u32[]{:S(2)}, u32[]{:S(2)}) %collective-permute-start.6) | collective-permute-done | bytes 229408 | tf_op jit(solution)/shard_map/ppermute | solution.py:14
  72.3 5.6 %collective-permute-start.8 = (bf16[448,256]{1,0:T(8,128)(2,1)S(1)}, bf16[448,256]{1,0:T(8,128)(2,1)S(1)}, u32[]{:S(2)}, u32[]{:S(2)}) collective-permute-start(bf16[448,256]{1,0:T(8,128)(2,1)S(1)} %fusion.15), channel_id=1, source_target_pairs={{0,16},{16,32},{32,48},{48,64},{64,80},{80,96},{96,112},{1,17},{17... | collective-permute-start | bytes 688136 | tf_op jit(solution)/shard_map/ppermute | solution.py:14
  78.1 1.9 %collective-permute-start.9 = (bf16[448,256]{1,0:T(8,128)(2,1)S(1)}, bf16[448,256]{1,0:T(8,128)(2,1)S(1)}, u32[]{:S(2)}, u32[]{:S(2)}) collective-permute-start(bf16[448,256]{1,0:T(8,128)(2,1)S(1)} %fusion.16), channel_id=1, source_target_pairs={{16,0},{32,16},{48,32},{64,48},{80,64},{96,80},{112,96},{17,1},{33... | collective-permute-start | bytes 688136 | tf_op jit(solution)/shard_map/ppermute | solution.py:14
  80.4 1.1 collective-permute-done.8
  81.6 5.6 %collective-permute-start.10 = (bf16[448,256]{1,0:T(8,128)(2,1)S(1)}, bf16[448,256]{1,0:T(8,128)(2,1)S(1)}, u32[]{:S(2)}, u32[]{:S(2)}) collective-permute-start(bf16[448,256]{1,0:T(8,128)(2,1)S(1)} %fusion.17), channel_id=1, source_target_pairs={{0,16},{16,32},{32,48},{48,64},{64,80},{80,96},{96,112},{1,17},{17... | collective-permute-start | bytes 688136 | tf_op jit(solution)/shard_map/ppermute | solution.py:14
  87.3 1.9 %collective-permute-start.11 = (bf16[448,256]{1,0:T(8,128)(2,1)S(1)}, bf16[448,256]{1,0:T(8,128)(2,1)S(1)}, u32[]{:S(2)}, u32[]{:S(2)}) collective-permute-start(bf16[448,256]{1,0:T(8,128)(2,1)S(1)} %fusion.18), channel_id=1, source_target_pairs={{16,0},{32,16},{48,32},{64,48},{80,64},{96,80},{112,96},{17,1},{33... | collective-permute-start | bytes 688136 | tf_op jit(solution)/shard_map/ppermute | solution.py:14
  89.2 1.5 %collective-permute-done.10 = bf16[448,256]{1,0:T(8,128)(2,1)S(1)} collective-permute-done((bf16[448,256]{1,0:T(8,128)(2,1)S(1)}, bf16[448,256]{1,0:T(8,128)(2,1)S(1)}, u32[]{:S(2)}, u32[]{:S(2)}) %collective-permute-start.10) | collective-permute-done | bytes 229408 | tf_op jit(solution)/shard_map/ppermute | solution.py:14
  90.8 5.6 %collective-permute-start.12 = (bf16[448,256]{1,0:T(8,128)(2,1)S(1)}, bf16[448,256]{1,0:T(8,128)(2,1)S(1)}, u32[]{:S(2)}, u32[]{:S(2)}) collective-permute-start(bf16[448,256]{1,0:T(8,128)(2,1)S(1)} %fusion.19), channel_id=1, source_target_pairs={{0,16},{16,32},{32,48},{48,64},{64,80},{80,96},{96,112},{1,17},{17... | collective-permute-start | bytes 688136 | tf_op jit(solution)/shard_map/ppermute | solution.py:14
  97.2 1.9 %collective-permute-start.13 = (bf16[448,256]{1,0:T(8,128)(2,1)S(1)}, bf16[448,256]{1,0:T(8,128)(2,1)S(1)}, u32[]{:S(2)}, u32[]{:S(2)}) collective-permute-start(bf16[448,256]{1,0:T(8,128)(2,1)S(1)} %fusion.20), channel_id=1, source_target_pairs={{16,0},{32,16},{48,32},{64,48},{80,64},{96,80},{112,96},{17,1},{33... | collective-permute-start | bytes 688136 | tf_op jit(solution)/shard_map/ppermute | solution.py:14
  100.0 5.6 %collective-permute-start.14 = (bf16[448,256]{1,0:T(8,128)(2,1)S(1)}, bf16[448,256]{1,0:T(8,128)(2,1)S(1)}, u32[]{:S(2)}, u32[]{:S(2)}) collective-permute-start(bf16[448,256]{1,0:T(8,128)(2,1)S(1)} %fusion.21), channel_id=1, source_target_pairs={{0,16},{16,32},{32,48},{48,64},{64,80},{80,96},{96,112},{1,17},{17... | collective-permute-start | bytes 688136 | tf_op jit(solution)/shard_map/ppermute | solution.py:14
  106.4 1.9 %collective-permute-start.16 = (bf16[448,256]{1,0:T(8,128)(2,1)S(1)}, bf16[448,256]{1,0:T(8,128)(2,1)S(1)}, u32[]{:S(2)}, u32[]{:S(2)}) collective-permute-start(bf16[448,256]{1,0:T(8,128)(2,1)S(1)} %fusion.22), channel_id=1, source_target_pairs={{16,0},{32,16},{48,32},{64,48},{80,64},{96,80},{112,96},{17,1},{33... | collective-permute-start | bytes 688136 | tf_op jit(solution)/shard_map/ppermute | solution.py:14
  109.6 5.6 %collective-permute-start.15 = (bf16[448,256]{1,0:T(8,128)(2,1)S(1)}, bf16[448,256]{1,0:T(8,128)(2,1)S(1)}, u32[]{:S(2)}, u32[]{:S(2)}) collective-permute-start(bf16[448,256]{1,0:T(8,128)(2,1)S(1)} %fusion.23), channel_id=1, source_target_pairs={{0,16},{16,32},{32,48},{48,64},{64,80},{80,96},{96,112},{1,17},{17... | collective-permute-start | bytes 688136 | tf_op jit(solution)/shard_map/ppermute | solution.py:14
  116.1 2.1 %collective-permute-start.17 = (bf16[448,256]{1,0:T(8,128)(2,1)S(1)}, bf16[448,256]{1,0:T(8,128)(2,1)S(1)}, u32[]{:S(2)}, u32[]{:S(2)}) collective-permute-start(bf16[448,256]{1,0:T(8,128)(2,1)S(1)} %fusion.24), channel_id=1, source_target_pairs={{16,0},{32,16},{48,32},{64,48},{80,64},{96,80},{112,96},{17,1},{33... | collective-permute-start | bytes 688136 | tf_op jit(solution)/shard_map/ppermute | solution.py:14
  118.8 6.6 %collective-permute-done.17 = bf16[448,256]{1,0:T(8,128)(2,1)S(1)} collective-permute-done((bf16[448,256]{1,0:T(8,128)(2,1)S(1)}, bf16[448,256]{1,0:T(8,128)(2,1)S(1)}, u32[]{:S(2)}, u32[]{:S(2)}) %collective-permute-start.17) | collective-permute-done | bytes 229408 | tf_op jit(solution)/shard_map/ppermute | solution.py:14
  125.4 1.4 fusion.10
  126.8 3.5 %collective-permute-start.18 = (bf16[224,256]{1,0:T(8,128)(2,1)S(1)}, bf16[224,256]{1,0:T(8,128)(2,1)S(1)}, u32[]{:S(2)}, u32[]{:S(2)}) collective-permute-start(bf16[224,256]{1,0:T(8,128)(2,1)S(1)} %get-tuple-element.11), channel_id=1, source_target_pairs={{0,128},{128,256},{256,384},{384,0},{1,129},{129,257},{257,385},{3... | collective-permute-start | bytes 344072 | tf_op jit(solution)/shard_map/ppermute | solution.py:104
  130.3 2.8 %collective-permute-start.19 = (bf16[224,256]{1,0:T(8,128)(2,1)S(1)}, bf16[224,256]{1,0:T(8,128)(2,1)S(1)}, u32[]{:S(2)}, u32[]{:S(2)}) collective-permute-start(bf16[224,256]{1,0:T(8,128)(2,1)S(1)} %get-tuple-element.12), channel_id=1, source_target_pairs={{0,256},{128,384},{256,0},{384,128},{1,257},{129,385},{257,1},{385... | collective-permute-start | bytes 344072 | tf_op jit(solution)/shard_map/ppermute | solution.py:103
  133.1 1.3 fusion.7
  134.4 4.0 %collective-permute-done.19 = bf16[224,256]{1,0:T(8,128)(2,1)S(1)} collective-permute-done((bf16[224,256]{1,0:T(8,128)(2,1)S(1)}, bf16[224,256]{1,0:T(8,128)(2,1)S(1)}, u32[]{:S(2)}, u32[]{:S(2)}) %collective-permute-start.19) | collective-permute-done | bytes 114720 | tf_op jit(solution)/shard_map/ppermute | solution.py:103
  (72 shorter events, 12.4 us)
Async XLA Ops:
  0.6 47.4 %copy-start = (bf16[448,448]{1,0:T(8,128)(2,1)S(1)}, bf16[448,448]{1,0:T(8,128)(2,1)}, u32[]{:S(2)}) copy-start(bf16[448,448]{1,0:T(8,128)(2,1)} %param.6) | copy-start | bytes 1204228
  0.6 16.7 %collective-permute-start = (bf16[448,128]{1,0:T(8,128)(2,1)}, bf16[448,128]{1,0:T(8,128)(2,1)S(1)}, u32[]{:S(2)}, u32[]{:S(2)}) collective-permute-start(bf16[448,128]{1,0:T(8,128)(2,1)} %param.7), channel_id=1, source_target_pairs={{0,8},{8,0},{1,9},{9,1},{2,10},{10,2},{3,11},{11,3},{4,12},{12,4},... | collective-permute-start | bytes 344072 | tf_op jit(solution)/shard_map/ppermute | solution.py:33
  19.3 26.1 %collective-permute-start.2 = (bf16[448,256]{1,0:T(8,128)(2,1)S(1)}, bf16[448,256]{1,0:T(8,128)(2,1)S(1)}, u32[]{:S(2)}, u32[]{:S(2)}) collective-permute-start(bf16[448,256]{1,0:T(8,128)(2,1)S(1)} %broadcast_select_fusion.3), channel_id=1, source_target_pairs={{16,0},{32,16},{48,32},{64,48},{80,64},{96,80},{112,96},{17,1},{33... | collective-permute-start | bytes 688136 | tf_op jit(solution)/shard_map/ppermute | solution.py:14
  24.7 20.7 %collective-permute-start.1 = (bf16[448,256]{1,0:T(8,128)(2,1)S(1)}, bf16[448,256]{1,0:T(8,128)(2,1)S(1)}, u32[]{:S(2)}, u32[]{:S(2)}) collective-permute-start(bf16[448,256]{1,0:T(8,128)(2,1)S(1)} %broadcast_select_fusion.3), channel_id=1, source_target_pairs={{0,16},{16,32},{32,48},{48,64},{64,80},{80,96},{96,112},{1,17},{17... | collective-permute-start | bytes 688136 | tf_op jit(solution)/shard_map/ppermute | solution.py:14
  45.7 4.5 %collective-permute-start.3 = (bf16[448,1024]{1,0:T(8,128)(2,1)S(1)}, bf16[448,1024]{1,0:T(8,128)(2,1)}, u32[]{:S(2)}, u32[]{:S(2)}) collective-permute-start(bf16[448,1024]{1,0:T(8,128)(2,1)S(1)} %maximum_select_fusion), channel_id=1, source_target_pairs={{0,1},{1,0},{2,3},{3,2},{4,5},{5,4},{6,7},{7,6},{8,9},{9,8},{10,11... | collective-permute-start | bytes 2752520 | tf_op jit(solution)/shard_map/ppermute | solution.py:44
  53.1 9.5 %collective-permute-start.4 = (bf16[448,256]{1,0:T(8,128)(2,1)S(1)}, bf16[448,256]{1,0:T(8,128)(2,1)S(1)}, u32[]{:S(2)}, u32[]{:S(2)}) collective-permute-start(bf16[448,256]{1,0:T(8,128)(2,1)S(1)} %fusion.11), channel_id=1, source_target_pairs={{0,16},{16,32},{32,48},{48,64},{64,80},{80,96},{96,112},{1,17},{17... | collective-permute-start | bytes 688136 | tf_op jit(solution)/shard_map/ppermute | solution.py:14
  57.1 10.8 %collective-permute-start.5 = (bf16[448,256]{1,0:T(8,128)(2,1)S(1)}, bf16[448,256]{1,0:T(8,128)(2,1)S(1)}, u32[]{:S(2)}, u32[]{:S(2)}) collective-permute-start(bf16[448,256]{1,0:T(8,128)(2,1)S(1)} %fusion.12), channel_id=1, source_target_pairs={{16,0},{32,16},{48,32},{64,48},{80,64},{96,80},{112,96},{17,1},{33... | collective-permute-start | bytes 688136 | tf_op jit(solution)/shard_map/ppermute | solution.py:14
  62.8 9.5 %collective-permute-start.6 = (bf16[448,256]{1,0:T(8,128)(2,1)S(1)}, bf16[448,256]{1,0:T(8,128)(2,1)S(1)}, u32[]{:S(2)}, u32[]{:S(2)}) collective-permute-start(bf16[448,256]{1,0:T(8,128)(2,1)S(1)} %fusion.13), channel_id=1, source_target_pairs={{0,16},{16,32},{32,48},{48,64},{64,80},{80,96},{96,112},{1,17},{17... | collective-permute-start | bytes 688136 | tf_op jit(solution)/shard_map/ppermute | solution.py:14
  68.0 9.9 %collective-permute-start.7 = (bf16[448,256]{1,0:T(8,128)(2,1)S(1)}, bf16[448,256]{1,0:T(8,128)(2,1)S(1)}, u32[]{:S(2)}, u32[]{:S(2)}) collective-permute-start(bf16[448,256]{1,0:T(8,128)(2,1)S(1)} %fusion.14), channel_id=1, source_target_pairs={{16,0},{32,16},{48,32},{64,48},{80,64},{96,80},{112,96},{17,1},{33... | collective-permute-start | bytes 688136 | tf_op jit(solution)/shard_map/ppermute | solution.py:14
  72.3 9.1 %collective-permute-start.8 = (bf16[448,256]{1,0:T(8,128)(2,1)S(1)}, bf16[448,256]{1,0:T(8,128)(2,1)S(1)}, u32[]{:S(2)}, u32[]{:S(2)}) collective-permute-start(bf16[448,256]{1,0:T(8,128)(2,1)S(1)} %fusion.15), channel_id=1, source_target_pairs={{0,16},{16,32},{32,48},{48,64},{64,80},{80,96},{96,112},{1,17},{17... | collective-permute-start | bytes 688136 | tf_op jit(solution)/shard_map/ppermute | solution.py:14
  78.1 9.1 %collective-permute-start.9 = (bf16[448,256]{1,0:T(8,128)(2,1)S(1)}, bf16[448,256]{1,0:T(8,128)(2,1)S(1)}, u32[]{:S(2)}, u32[]{:S(2)}) collective-permute-start(bf16[448,256]{1,0:T(8,128)(2,1)S(1)} %fusion.16), channel_id=1, source_target_pairs={{16,0},{32,16},{48,32},{64,48},{80,64},{96,80},{112,96},{17,1},{33... | collective-permute-start | bytes 688136 | tf_op jit(solution)/shard_map/ppermute | solution.py:14
  80.4 16.0 %copy-start.1 = (bf16[448,256]{1,0:T(8,128)(2,1)S(1)}, bf16[448,256]{1,0:T(8,128)(2,1)}, u32[]{:S(2)}) copy-start(bf16[448,256]{1,0:T(8,128)(2,1)} %param.8) | copy-start | bytes 688132
  81.6 9.1 %collective-permute-start.10 = (bf16[448,256]{1,0:T(8,128)(2,1)S(1)}, bf16[448,256]{1,0:T(8,128)(2,1)S(1)}, u32[]{:S(2)}, u32[]{:S(2)}) collective-permute-start(bf16[448,256]{1,0:T(8,128)(2,1)S(1)} %fusion.17), channel_id=1, source_target_pairs={{0,16},{16,32},{32,48},{48,64},{64,80},{80,96},{96,112},{1,17},{17... | collective-permute-start | bytes 688136 | tf_op jit(solution)/shard_map/ppermute | solution.py:14
  87.3 9.8 %collective-permute-start.11 = (bf16[448,256]{1,0:T(8,128)(2,1)S(1)}, bf16[448,256]{1,0:T(8,128)(2,1)S(1)}, u32[]{:S(2)}, u32[]{:S(2)}) collective-permute-start(bf16[448,256]{1,0:T(8,128)(2,1)S(1)} %fusion.18), channel_id=1, source_target_pairs={{16,0},{32,16},{48,32},{64,48},{80,64},{96,80},{112,96},{17,1},{33... | collective-permute-start | bytes 688136 | tf_op jit(solution)/shard_map/ppermute | solution.py:14
  90.8 9.1 %collective-permute-start.12 = (bf16[448,256]{1,0:T(8,128)(2,1)S(1)}, bf16[448,256]{1,0:T(8,128)(2,1)S(1)}, u32[]{:S(2)}, u32[]{:S(2)}) collective-permute-start(bf16[448,256]{1,0:T(8,128)(2,1)S(1)} %fusion.19), channel_id=1, source_target_pairs={{0,16},{16,32},{32,48},{48,64},{64,80},{80,96},{96,112},{1,17},{17... | collective-permute-start | bytes 688136 | tf_op jit(solution)/shard_map/ppermute | solution.py:14
  97.2 9.1 %collective-permute-start.13 = (bf16[448,256]{1,0:T(8,128)(2,1)S(1)}, bf16[448,256]{1,0:T(8,128)(2,1)S(1)}, u32[]{:S(2)}, u32[]{:S(2)}) collective-permute-start(bf16[448,256]{1,0:T(8,128)(2,1)S(1)} %fusion.20), channel_id=1, source_target_pairs={{16,0},{32,16},{48,32},{64,48},{80,64},{96,80},{112,96},{17,1},{33... | collective-permute-start | bytes 688136 | tf_op jit(solution)/shard_map/ppermute | solution.py:14
  100.0 9.5 %collective-permute-start.14 = (bf16[448,256]{1,0:T(8,128)(2,1)S(1)}, bf16[448,256]{1,0:T(8,128)(2,1)S(1)}, u32[]{:S(2)}, u32[]{:S(2)}) collective-permute-start(bf16[448,256]{1,0:T(8,128)(2,1)S(1)} %fusion.21), channel_id=1, source_target_pairs={{0,16},{16,32},{32,48},{48,64},{64,80},{80,96},{96,112},{1,17},{17... | collective-permute-start | bytes 688136 | tf_op jit(solution)/shard_map/ppermute | solution.py:14
  106.4 9.6 %collective-permute-start.16 = (bf16[448,256]{1,0:T(8,128)(2,1)S(1)}, bf16[448,256]{1,0:T(8,128)(2,1)S(1)}, u32[]{:S(2)}, u32[]{:S(2)}) collective-permute-start(bf16[448,256]{1,0:T(8,128)(2,1)S(1)} %fusion.22), channel_id=1, source_target_pairs={{16,0},{32,16},{48,32},{64,48},{80,64},{96,80},{112,96},{17,1},{33... | collective-permute-start | bytes 688136 | tf_op jit(solution)/shard_map/ppermute | solution.py:14
  109.6 15.8 %collective-permute-start.15 = (bf16[448,256]{1,0:T(8,128)(2,1)S(1)}, bf16[448,256]{1,0:T(8,128)(2,1)S(1)}, u32[]{:S(2)}, u32[]{:S(2)}) collective-permute-start(bf16[448,256]{1,0:T(8,128)(2,1)S(1)} %fusion.23), channel_id=1, source_target_pairs={{0,16},{16,32},{32,48},{48,64},{64,80},{80,96},{96,112},{1,17},{17... | collective-permute-start | bytes 688136 | tf_op jit(solution)/shard_map/ppermute | solution.py:14
  116.1 9.3 %copy-start.2 = (f32[448,256]{1,0:T(8,128)S(1)}, f32[448,256]{1,0:T(8,128)}, u32[]{:S(2)}) copy-start(f32[448,256]{1,0:T(8,128)} %param.10) | copy-start | bytes 1376260
  116.1 9.3 %copy-start.3 = (f32[448,256]{1,0:T(8,128)S(1)}, f32[448,256]{1,0:T(8,128)}, u32[]{:S(2)}) copy-start(f32[448,256]{1,0:T(8,128)} %param.9) | copy-start | bytes 1376260
  116.1 9.3 %collective-permute-start.17 = (bf16[448,256]{1,0:T(8,128)(2,1)S(1)}, bf16[448,256]{1,0:T(8,128)(2,1)S(1)}, u32[]{:S(2)}, u32[]{:S(2)}) collective-permute-start(bf16[448,256]{1,0:T(8,128)(2,1)S(1)} %fusion.24), channel_id=1, source_target_pairs={{16,0},{32,16},{48,32},{64,48},{80,64},{96,80},{112,96},{17,1},{33... | collective-permute-start | bytes 688136 | tf_op jit(solution)/shard_map/ppermute | solution.py:14
  126.8 7.6 %collective-permute-start.18 = (bf16[224,256]{1,0:T(8,128)(2,1)S(1)}, bf16[224,256]{1,0:T(8,128)(2,1)S(1)}, u32[]{:S(2)}, u32[]{:S(2)}) collective-permute-start(bf16[224,256]{1,0:T(8,128)(2,1)S(1)} %get-tuple-element.11), channel_id=1, source_target_pairs={{0,128},{128,256},{256,384},{384,0},{1,129},{129,257},{257,385},{3... | collective-permute-start | bytes 344072 | tf_op jit(solution)/shard_map/ppermute | solution.py:104
  130.3 8.2 %collective-permute-start.19 = (bf16[224,256]{1,0:T(8,128)(2,1)S(1)}, bf16[224,256]{1,0:T(8,128)(2,1)S(1)}, u32[]{:S(2)}, u32[]{:S(2)}) collective-permute-start(bf16[224,256]{1,0:T(8,128)(2,1)S(1)} %get-tuple-element.12), channel_id=1, source_target_pairs={{0,256},{128,384},{256,0},{384,128},{1,257},{129,385},{257,1},{385... | collective-permute-start | bytes 344072 | tf_op jit(solution)/shard_map/ppermute | solution.py:103

commit v9 on v6

--- a/solution.py
+++ b/solution.py
@@ -36,14 +36,13 @@
 
     up_other = lax.ppermute(upstream, "zh", [(0, 1), (1, 0)])
     hidden_t = lax.optimization_barrier(hidden.T)
-    got = {True: [along(weights, True)], False: []}
+    got = {True: [along(weights, True)], False: [along(weights, False)]}
     sent = {}
 
     def send(early, turn, part):
         here = position if early else last - position
         arrived = got[early][-1]
-        if sent:
-            arrived = behind(arrived, list(sent.values())[-1])
+        arrived = behind(arrived, list(sent.values())[-1] if sent else got[not early][-1])
         total = (arrived.astype(F32) + part).astype(BF)
         sent[early, turn] = lax.optimization_barrier(jnp.where(here <= turn, total, arrived))
         got[early].append(along(sent[early, turn], early))
@@ -52,7 +51,6 @@
         return lax.optimization_barrier(contract(hidden_t, features, ((1,), (0,))))
 
     near_up = lax.all_gather(upstream, ("x", "c"), axis=1, tiled=True)
-    got[False].append(along(behind(weights, near_up[:, :width]), False))
     first = lax.dynamic_slice_in_dim(near_up, jnp.where(early_up, 3, 0) * width, width, 1)
     send(True, 0, product(first))
     up_other = behind(up_other, sent[True, 0][:, : up_other.shape[1]])

time: 137 us -> 136 us (level)
    ppermute x16, starting transfers between devices: 56 us -> 57.6 us  [along(): return lax.ppermute(value, ('zl', 'zh'), pairs)]
  transfers between devices with their start and end apart: 19 -> 19, of which waited for: 8 -> 8; matrix products, arithmetic and copies ran while one was open for 7% -> 6% of each run, Pallas kernels for 0% -> 0%
where the time goes in v9:
time: 136 us; the launch traced here: 135 us
  starting transfers between devices  75.8 us (56%)
  blocking collectives  28.4 us (21%)
  waiting for transfers between devices  18.7 us (14%)
  matrix products  6.6 us (5%)
  other arithmetic  3.48 us (3%)
  between operations  2.02 us (1%)
    ppermute x16, starting transfers between devices, along(): return lax.ppermute(value, ('zl', 'zh'), pairs)  57.6 us
    ppermute x16, waiting for transfers between devices, along(): return lax.ppermute(value, ('zl', 'zh'), pairs)  16.6 us
    all_gather x1, blocking collectives, body(): near_up = lax.all_gather(upstream, ('x', 'c'), axis=1, tiled=True)  14.4 us
    all_gather x1, blocking collectives, body(): far_up = lax.all_gather(up_other, ('x', 'c'), axis=1, tiled=True)  14 us
    ppermute x1, starting transfers between devices, body(): up_other = lax.ppermute(upstream, 'zh', [(0, 1), (1, 0)])  9.91 us
    dot_general x17, matrix products, contract(): lax.dot_general(left, right, (dims, ((), ())), preferred_element_type=F32)  6.6 us
    ppermute x1, starting transfers between devices, body(): lax.ppermute(jnp.where(even_step, upper, lower), 'y', [(i, (i + 2) % 4) f...  4.81 us
    ppermute x1, starting transfers between devices, body(): lax.ppermute(jnp.where(even_step, lower, upper), 'y', [(i, (i + 1) % 4) f...  3.48 us
  transfers between devices with their start and end apart: 19, of which 8 were waited for; matrix products, arithmetic and copies ran while one was open for 6% of the time, Pallas kernels for 0%

profile of v9, /device:TPU:128, one launch (start us, length us, event | category | flops | bytes accessed | tf_op | source)
XLA Modules:
  0.0 135.2 jit_solution(3833161056846876903)
XLA Ops:
  0.6 4.0 %collective-permute-start = (bf16[448,256]{1,0:T(8,128)(2,1)}, bf16[448,256]{1,0:T(8,128)(2,1)S(1)}, u32[]{:S(2)}, u32[]{:S(2)}) collective-permute-start(bf16[448,256]{1,0:T(8,128)(2,1)} %param.8), channel_id=1, source_target_pairs={{0,16},{16,32},{32,48},{48,64},{64,80},{80,96},{96,112},{24,8},{40... | collective-permute-start | bytes 688136 | tf_op jit(solution)/shard_map/ppermute | solution.py:18
  4.6 3.2 %collective-permute-start.1 = (bf16[448,256]{1,0:T(8,128)(2,1)}, bf16[448,256]{1,0:T(8,128)(2,1)S(1)}, u32[]{:S(2)}, u32[]{:S(2)}) collective-permute-start(bf16[448,256]{1,0:T(8,128)(2,1)} %param.8), channel_id=1, source_target_pairs={{16,0},{32,16},{48,32},{64,48},{80,64},{96,80},{112,96},{8,24},{24... | collective-permute-start | bytes 688136 | tf_op jit(solution)/shard_map/ppermute | solution.py:18
  7.8 9.9 %collective-permute-start.2 = (bf16[448,128]{1,0:T(8,128)(2,1)}, bf16[448,128]{1,0:T(8,128)(2,1)S(1)}, u32[]{:S(2)}, u32[]{:S(2)}) collective-permute-start(bf16[448,128]{1,0:T(8,128)(2,1)} %param.7), channel_id=1, source_target_pairs={{0,8},{8,0},{1,9},{9,1},{2,10},{10,2},{3,11},{11,3},{4,12},{12,4},... | collective-permute-start | bytes 344072 | tf_op jit(solution)/shard_map/ppermute | solution.py:37
  17.8 14.4 %all_gather.6 = bf16[448,1024]{1,0:T(8,128)(2,1)S(1)} all-gather(bf16[448,128]{1,0:T(8,128)(2,1)} %param.7), channel_id=1, replica_groups=mesh['y'=4,'zl'=8,'zh'=2,'x'=4,'c'=2] {'x','c'}, dimensions={1}, use_global_device_ids=true | all-gather | bytes 1032192 | tf_op jit(solution)/shard_map/all_gather | solution.py:53
  33.6 5.1 %collective-permute-start.3 = (bf16[448,256]{1,0:T(8,128)(2,1)S(1)}, bf16[448,256]{1,0:T(8,128)(2,1)S(1)}, u32[]{:S(2)}, u32[]{:S(2)}) collective-permute-start(bf16[448,256]{1,0:T(8,128)(2,1)S(1)} %fusion.10), channel_id=1, source_target_pairs={{16,0},{32,16},{48,32},{64,48},{80,64},{96,80},{112,96},{8,24},{24... | collective-permute-start | bytes 688136 | tf_op jit(solution)/shard_map/ppermute | solution.py:18
  38.8 14.0 %all_gather.7 = bf16[448,1024]{1,0:T(8,128)(2,1)S(1)} all-gather(bf16[448,128]{1,0:T(8,128)(2,1)S(1)} %slice_select_fusion), channel_id=1, replica_groups=mesh['y'=4,'zl'=8,'zh'=2,'x'=4,'c'=2] {'x','c'}, dimensions={1}, use_global_device_ids=true | all-gather | bytes 1032192 | tf_op jit(solution)/shard_map/all_gather | solution.py:57
  53.7 1.9 %collective-permute-start.4 = (bf16[448,256]{1,0:T(8,128)(2,1)S(1)}, bf16[448,256]{1,0:T(8,128)(2,1)S(1)}, u32[]{:S(2)}, u32[]{:S(2)}) collective-permute-start(bf16[448,256]{1,0:T(8,128)(2,1)S(1)} %fusion.11), channel_id=1, source_target_pairs={{0,16},{16,32},{32,48},{48,64},{64,80},{80,96},{96,112},{24,8},{40... | collective-permute-start | bytes 688136 | tf_op jit(solution)/shard_map/ppermute | solution.py:18
  56.1 5.1 %collective-permute-start.5 = (bf16[448,256]{1,0:T(8,128)(2,1)S(1)}, bf16[448,256]{1,0:T(8,128)(2,1)S(1)}, u32[]{:S(2)}, u32[]{:S(2)}) collective-permute-start(bf16[448,256]{1,0:T(8,128)(2,1)S(1)} %fusion.12), channel_id=1, source_target_pairs={{16,0},{32,16},{48,32},{64,48},{80,64},{96,80},{112,96},{8,24},{24... | collective-permute-start | bytes 688136 | tf_op jit(solution)/shard_map/ppermute | solution.py:18
  61.6 3.1 %collective-permute-done.4 = bf16[448,256]{1,0:T(8,128)(2,1)S(1)} collective-permute-done((bf16[448,256]{1,0:T(8,128)(2,1)S(1)}, bf16[448,256]{1,0:T(8,128)(2,1)S(1)}, u32[]{:S(2)}, u32[]{:S(2)}) %collective-permute-start.4) | collective-permute-done | bytes 229408 | tf_op jit(solution)/shard_map/ppermute | solution.py:18
  64.8 1.9 %collective-permute-start.6 = (bf16[448,256]{1,0:T(8,128)(2,1)S(1)}, bf16[448,256]{1,0:T(8,128)(2,1)S(1)}, u32[]{:S(2)}, u32[]{:S(2)}) collective-permute-start(bf16[448,256]{1,0:T(8,128)(2,1)S(1)} %fusion.13), channel_id=1, source_target_pairs={{0,16},{16,32},{32,48},{48,64},{64,80},{80,96},{96,112},{24,8},{40... | collective-permute-start | bytes 688136 | tf_op jit(solution)/shard_map/ppermute | solution.py:18
  67.1 5.1 %collective-permute-start.7 = (bf16[448,256]{1,0:T(8,128)(2,1)S(1)}, bf16[448,256]{1,0:T(8,128)(2,1)S(1)}, u32[]{:S(2)}, u32[]{:S(2)}) collective-permute-start(bf16[448,256]{1,0:T(8,128)(2,1)S(1)} %fusion.14), channel_id=1, source_target_pairs={{16,0},{32,16},{48,32},{64,48},{80,64},{96,80},{112,96},{8,24},{24... | collective-permute-start | bytes 688136 | tf_op jit(solution)/shard_map/ppermute | solution.py:18
  72.6 2.3 %collective-permute-done.6 = bf16[448,256]{1,0:T(8,128)(2,1)S(1)} collective-permute-done((bf16[448,256]{1,0:T(8,128)(2,1)S(1)}, bf16[448,256]{1,0:T(8,128)(2,1)S(1)}, u32[]{:S(2)}, u32[]{:S(2)}) %collective-permute-start.6) | collective-permute-done | bytes 229408 | tf_op jit(solution)/shard_map/ppermute | solution.py:18
  75.0 1.9 %collective-permute-start.8 = (bf16[448,256]{1,0:T(8,128)(2,1)S(1)}, bf16[448,256]{1,0:T(8,128)(2,1)S(1)}, u32[]{:S(2)}, u32[]{:S(2)}) collective-permute-start(bf16[448,256]{1,0:T(8,128)(2,1)S(1)} %fusion.15), channel_id=1, source_target_pairs={{0,16},{16,32},{32,48},{48,64},{64,80},{80,96},{96,112},{24,8},{40... | collective-permute-start | bytes 688136 | tf_op jit(solution)/shard_map/ppermute | solution.py:18
  77.1 5.3 %collective-permute-start.9 = (bf16[448,256]{1,0:T(8,128)(2,1)S(1)}, bf16[448,256]{1,0:T(8,128)(2,1)S(1)}, u32[]{:S(2)}, u32[]{:S(2)}) collective-permute-start(bf16[448,256]{1,0:T(8,128)(2,1)S(1)} %fusion.16), channel_id=1, source_target_pairs={{16,0},{32,16},{48,32},{64,48},{80,64},{96,80},{112,96},{8,24},{24... | collective-permute-start | bytes 688136 | tf_op jit(solution)/shard_map/ppermute | solution.py:18
  82.4 1.8 %collective-permute-done.8 = bf16[448,256]{1,0:T(8,128)(2,1)S(1)} collective-permute-done((bf16[448,256]{1,0:T(8,128)(2,1)S(1)}, bf16[448,256]{1,0:T(8,128)(2,1)S(1)}, u32[]{:S(2)}, u32[]{:S(2)}) %collective-permute-start.8) | collective-permute-done | bytes 229408 | tf_op jit(solution)/shard_map/ppermute | solution.py:18
  84.3 1.9 %collective-permute-start.10 = (bf16[448,256]{1,0:T(8,128)(2,1)S(1)}, bf16[448,256]{1,0:T(8,128)(2,1)S(1)}, u32[]{:S(2)}, u32[]{:S(2)}) collective-permute-start(bf16[448,256]{1,0:T(8,128)(2,1)S(1)} %fusion.17), channel_id=1, source_target_pairs={{0,16},{16,32},{32,48},{48,64},{64,80},{80,96},{96,112},{24,8},{40... | collective-permute-start | bytes 688136 | tf_op jit(solution)/shard_map/ppermute | solution.py:18
  87.4 5.1 %collective-permute-start.11 = (bf16[448,256]{1,0:T(8,128)(2,1)S(1)}, bf16[448,256]{1,0:T(8,128)(2,1)S(1)}, u32[]{:S(2)}, u32[]{:S(2)}) collective-permute-start(bf16[448,256]{1,0:T(8,128)(2,1)S(1)} %fusion.18), channel_id=1, source_target_pairs={{16,0},{32,16},{48,32},{64,48},{80,64},{96,80},{112,96},{8,24},{24... | collective-permute-start | bytes 688136 | tf_op jit(solution)/shard_map/ppermute | solution.py:18
  92.5 0.9 collective-permute-done.10
  93.6 1.9 %collective-permute-start.12 = (bf16[448,256]{1,0:T(8,128)(2,1)S(1)}, bf16[448,256]{1,0:T(8,128)(2,1)S(1)}, u32[]{:S(2)}, u32[]{:S(2)}) collective-permute-start(bf16[448,256]{1,0:T(8,128)(2,1)S(1)} %fusion.19), channel_id=1, source_target_pairs={{0,16},{16,32},{32,48},{48,64},{64,80},{80,96},{96,112},{24,8},{40... | collective-permute-start | bytes 688136 | tf_op jit(solution)/shard_map/ppermute | solution.py:18
  96.3 5.4 %collective-permute-start.13 = (bf16[448,256]{1,0:T(8,128)(2,1)S(1)}, bf16[448,256]{1,0:T(8,128)(2,1)S(1)}, u32[]{:S(2)}, u32[]{:S(2)}) collective-permute-start(bf16[448,256]{1,0:T(8,128)(2,1)S(1)} %fusion.20), channel_id=1, source_target_pairs={{16,0},{32,16},{48,32},{64,48},{80,64},{96,80},{112,96},{8,24},{24... | collective-permute-start | bytes 688136 | tf_op jit(solution)/shard_map/ppermute | solution.py:18
  101.8 0.9 collective-permute-done.12
  102.8 1.9 %collective-permute-start.15 = (bf16[448,256]{1,0:T(8,128)(2,1)S(1)}, bf16[448,256]{1,0:T(8,128)(2,1)S(1)}, u32[]{:S(2)}, u32[]{:S(2)}) collective-permute-start(bf16[448,256]{1,0:T(8,128)(2,1)S(1)} %fusion.21), channel_id=1, source_target_pairs={{0,16},{16,32},{32,48},{48,64},{64,80},{80,96},{96,112},{24,8},{40... | collective-permute-start | bytes 688136 | tf_op jit(solution)/shard_map/ppermute | solution.py:18
  105.5 5.5 %collective-permute-start.14 = (bf16[448,256]{1,0:T(8,128)(2,1)S(1)}, bf16[448,256]{1,0:T(8,128)(2,1)S(1)}, u32[]{:S(2)}, u32[]{:S(2)}) collective-permute-start(bf16[448,256]{1,0:T(8,128)(2,1)S(1)} %fusion.22), channel_id=1, source_target_pairs={{16,0},{32,16},{48,32},{64,48},{80,64},{96,80},{112,96},{8,24},{24... | collective-permute-start | bytes 688136 | tf_op jit(solution)/shard_map/ppermute | solution.py:18
  111.0 0.9 collective-permute-done.15
  112.0 2.1 %collective-permute-start.16 = (bf16[448,256]{1,0:T(8,128)(2,1)S(1)}, bf16[448,256]{1,0:T(8,128)(2,1)S(1)}, u32[]{:S(2)}, u32[]{:S(2)}) collective-permute-start(bf16[448,256]{1,0:T(8,128)(2,1)S(1)} %fusion.23), channel_id=1, source_target_pairs={{0,16},{16,32},{32,48},{48,64},{64,80},{80,96},{96,112},{24,8},{40... | collective-permute-start | bytes 688136 | tf_op jit(solution)/shard_map/ppermute | solution.py:18
  114.8 6.5 %collective-permute-done.16 = bf16[448,256]{1,0:T(8,128)(2,1)S(1)} collective-permute-done((bf16[448,256]{1,0:T(8,128)(2,1)S(1)}, bf16[448,256]{1,0:T(8,128)(2,1)S(1)}, u32[]{:S(2)}, u32[]{:S(2)}) %collective-permute-start.16) | collective-permute-done | bytes 229408 | tf_op jit(solution)/shard_map/ppermute | solution.py:18
  121.3 1.4 %fusion.9 = (bf16[448,256]{1,0:T(8,128)(2,1)S(1)}, f32[448,256]{1,0:T(8,128)}, f32[448,256]{1,0:T(8,128)}) fusion(bf16[448,256]{1,0:T(8,128)(2,1)S(1)} %copy-done.1, f32[]{:T(128)S(6)} %sub.106, f32[]{:T(128)S(6)} %sub.105, bf16[448,256]{1,0:T(8,128)(2,1)S(1)} %collective-permute-done.16, f32[448,256]{1,0:T(8,128)S(1)} %convolution_bitcast_fusion.1, ...), kind=kLoop, calls=%fused_computation.22 | loop fusion | flops 2523136 | bytes 3211272 | tf_op jit(solution)/shard_map/convert_element_type | solution.py:95
  122.7 3.5 %collective-permute-start.17 = (bf16[224,256]{1,0:T(8,128)(2,1)S(1)}, bf16[224,256]{1,0:T(8,128)(2,1)S(1)}, u32[]{:S(2)}, u32[]{:S(2)}) collective-permute-start(bf16[224,256]{1,0:T(8,128)(2,1)S(1)} %get-tuple-element.9), channel_id=1, source_target_pairs={{0,128},{128,256},{256,384},{384,0},{1,129},{129,257},{257,385},{3... | collective-permute-start | bytes 344072 | tf_op jit(solution)/shard_map/ppermute | solution.py:100
  126.2 4.8 %collective-permute-start.18 = (bf16[224,256]{1,0:T(8,128)(2,1)S(1)}, bf16[224,256]{1,0:T(8,128)(2,1)S(1)}, u32[]{:S(2)}, u32[]{:S(2)}) collective-permute-start(bf16[224,256]{1,0:T(8,128)(2,1)S(1)} %get-tuple-element.10), channel_id=1, source_target_pairs={{0,256},{128,384},{256,0},{384,128},{1,257},{129,385},{257,1},{385... | collective-permute-start | bytes 344072 | tf_op jit(solution)/shard_map/ppermute | solution.py:101
  131.0 1.2 fusion.6
  132.2 2.1 %collective-permute-done.18 = bf16[224,256]{1,0:T(8,128)(2,1)S(1)} collective-permute-done((bf16[224,256]{1,0:T(8,128)(2,1)S(1)}, bf16[224,256]{1,0:T(8,128)(2,1)S(1)}, u32[]{:S(2)}, u32[]{:S(2)}) %collective-permute-start.18) | collective-permute-done | bytes 114720 | tf_op jit(solution)/shard_map/ppermute | solution.py:101
  134.4 0.8 multiply_convert_fusion
  (54 shorter events, 6.9 us)
Async XLA Ops:
  0.6 31.5 %copy-start = (bf16[448,448]{1,0:T(8,128)(2,1)S(1)}, bf16[448,448]{1,0:T(8,128)(2,1)}, u32[]{:S(2)}) copy-start(bf16[448,448]{1,0:T(8,128)(2,1)} %param.6) | copy-start | bytes 1204228
  0.6 32.8 %collective-permute-start = (bf16[448,256]{1,0:T(8,128)(2,1)}, bf16[448,256]{1,0:T(8,128)(2,1)S(1)}, u32[]{:S(2)}, u32[]{:S(2)}) collective-permute-start(bf16[448,256]{1,0:T(8,128)(2,1)} %param.8), channel_id=1, source_target_pairs={{0,16},{16,32},{32,48},{48,64},{64,80},{80,96},{96,112},{24,8},{40... | collective-permute-start | bytes 688136 | tf_op jit(solution)/shard_map/ppermute | solution.py:18
  4.6 28.9 %collective-permute-start.1 = (bf16[448,256]{1,0:T(8,128)(2,1)}, bf16[448,256]{1,0:T(8,128)(2,1)S(1)}, u32[]{:S(2)}, u32[]{:S(2)}) collective-permute-start(bf16[448,256]{1,0:T(8,128)(2,1)} %param.8), channel_id=1, source_target_pairs={{16,0},{32,16},{48,32},{64,48},{80,64},{96,80},{112,96},{8,24},{24... | collective-permute-start | bytes 688136 | tf_op jit(solution)/shard_map/ppermute | solution.py:18
  7.8 30.9 %collective-permute-start.2 = (bf16[448,128]{1,0:T(8,128)(2,1)}, bf16[448,128]{1,0:T(8,128)(2,1)S(1)}, u32[]{:S(2)}, u32[]{:S(2)}) collective-permute-start(bf16[448,128]{1,0:T(8,128)(2,1)} %param.7), channel_id=1, source_target_pairs={{0,8},{8,0},{1,9},{9,1},{2,10},{10,2},{3,11},{11,3},{4,12},{12,4},... | collective-permute-start | bytes 344072 | tf_op jit(solution)/shard_map/ppermute | solution.py:37
  33.6 22.4 %collective-permute-start.3 = (bf16[448,256]{1,0:T(8,128)(2,1)S(1)}, bf16[448,256]{1,0:T(8,128)(2,1)S(1)}, u32[]{:S(2)}, u32[]{:S(2)}) collective-permute-start(bf16[448,256]{1,0:T(8,128)(2,1)S(1)} %fusion.10), channel_id=1, source_target_pairs={{16,0},{32,16},{48,32},{64,48},{80,64},{96,80},{112,96},{8,24},{24... | collective-permute-start | bytes 688136 | tf_op jit(solution)/shard_map/ppermute | solution.py:18
  53.7 11.0 %collective-permute-start.4 = (bf16[448,256]{1,0:T(8,128)(2,1)S(1)}, bf16[448,256]{1,0:T(8,128)(2,1)S(1)}, u32[]{:S(2)}, u32[]{:S(2)}) collective-permute-start(bf16[448,256]{1,0:T(8,128)(2,1)S(1)} %fusion.11), channel_id=1, source_target_pairs={{0,16},{16,32},{32,48},{48,64},{64,80},{80,96},{96,112},{24,8},{40... | collective-permute-start | bytes 688136 | tf_op jit(solution)/shard_map/ppermute | solution.py:18
  56.1 10.9 %collective-permute-start.5 = (bf16[448,256]{1,0:T(8,128)(2,1)S(1)}, bf16[448,256]{1,0:T(8,128)(2,1)S(1)}, u32[]{:S(2)}, u32[]{:S(2)}) collective-permute-start(bf16[448,256]{1,0:T(8,128)(2,1)S(1)} %fusion.12), channel_id=1, source_target_pairs={{16,0},{32,16},{48,32},{64,48},{80,64},{96,80},{112,96},{8,24},{24... | collective-permute-start | bytes 688136 | tf_op jit(solution)/shard_map/ppermute | solution.py:18
  64.8 10.2 %collective-permute-start.6 = (bf16[448,256]{1,0:T(8,128)(2,1)S(1)}, bf16[448,256]{1,0:T(8,128)(2,1)S(1)}, u32[]{:S(2)}, u32[]{:S(2)}) collective-permute-start(bf16[448,256]{1,0:T(8,128)(2,1)S(1)} %fusion.13), channel_id=1, source_target_pairs={{0,16},{16,32},{32,48},{48,64},{64,80},{80,96},{96,112},{24,8},{40... | collective-permute-start | bytes 688136 | tf_op jit(solution)/shard_map/ppermute | solution.py:18
  67.1 9.8 %collective-permute-start.7 = (bf16[448,256]{1,0:T(8,128)(2,1)S(1)}, bf16[448,256]{1,0:T(8,128)(2,1)S(1)}, u32[]{:S(2)}, u32[]{:S(2)}) collective-permute-start(bf16[448,256]{1,0:T(8,128)(2,1)S(1)} %fusion.14), channel_id=1, source_target_pairs={{16,0},{32,16},{48,32},{64,48},{80,64},{96,80},{112,96},{8,24},{24... | collective-permute-start | bytes 688136 | tf_op jit(solution)/shard_map/ppermute | solution.py:18
  75.0 9.2 %collective-permute-start.8 = (bf16[448,256]{1,0:T(8,128)(2,1)S(1)}, bf16[448,256]{1,0:T(8,128)(2,1)S(1)}, u32[]{:S(2)}, u32[]{:S(2)}) collective-permute-start(bf16[448,256]{1,0:T(8,128)(2,1)S(1)} %fusion.15), channel_id=1, source_target_pairs={{0,16},{16,32},{32,48},{48,64},{64,80},{80,96},{96,112},{24,8},{40... | collective-permute-start | bytes 688136 | tf_op jit(solution)/shard_map/ppermute | solution.py:18
  77.0 9.9 %copy-start.1 = (bf16[448,256]{1,0:T(8,128)(2,1)S(1)}, bf16[448,256]{1,0:T(8,128)(2,1)}, u32[]{:S(2)}) copy-start(bf16[448,256]{1,0:T(8,128)(2,1)} %param.8) | copy-start | bytes 688132
  77.1 10.2 %collective-permute-start.9 = (bf16[448,256]{1,0:T(8,128)(2,1)S(1)}, bf16[448,256]{1,0:T(8,128)(2,1)S(1)}, u32[]{:S(2)}, u32[]{:S(2)}) collective-permute-start(bf16[448,256]{1,0:T(8,128)(2,1)S(1)} %fusion.16), channel_id=1, source_target_pairs={{16,0},{32,16},{48,32},{64,48},{80,64},{96,80},{112,96},{8,24},{24... | collective-permute-start | bytes 688136 | tf_op jit(solution)/shard_map/ppermute | solution.py:18
  84.3 9.1 %collective-permute-start.10 = (bf16[448,256]{1,0:T(8,128)(2,1)S(1)}, bf16[448,256]{1,0:T(8,128)(2,1)S(1)}, u32[]{:S(2)}, u32[]{:S(2)}) collective-permute-start(bf16[448,256]{1,0:T(8,128)(2,1)S(1)} %fusion.17), channel_id=1, source_target_pairs={{0,16},{16,32},{32,48},{48,64},{64,80},{80,96},{96,112},{24,8},{40... | collective-permute-start | bytes 688136 | tf_op jit(solution)/shard_map/ppermute | solution.py:18
  87.4 8.8 %collective-permute-start.11 = (bf16[448,256]{1,0:T(8,128)(2,1)S(1)}, bf16[448,256]{1,0:T(8,128)(2,1)S(1)}, u32[]{:S(2)}, u32[]{:S(2)}) collective-permute-start(bf16[448,256]{1,0:T(8,128)(2,1)S(1)} %fusion.18), channel_id=1, source_target_pairs={{16,0},{32,16},{48,32},{64,48},{80,64},{96,80},{112,96},{8,24},{24... | collective-permute-start | bytes 688136 | tf_op jit(solution)/shard_map/ppermute | solution.py:18
  93.6 9.1 %collective-permute-start.12 = (bf16[448,256]{1,0:T(8,128)(2,1)S(1)}, bf16[448,256]{1,0:T(8,128)(2,1)S(1)}, u32[]{:S(2)}, u32[]{:S(2)}) collective-permute-start(bf16[448,256]{1,0:T(8,128)(2,1)S(1)} %fusion.19), channel_id=1, source_target_pairs={{0,16},{16,32},{32,48},{48,64},{64,80},{80,96},{96,112},{24,8},{40... | collective-permute-start | bytes 688136 | tf_op jit(solution)/shard_map/ppermute | solution.py:18
  96.3 9.1 %collective-permute-start.13 = (bf16[448,256]{1,0:T(8,128)(2,1)S(1)}, bf16[448,256]{1,0:T(8,128)(2,1)S(1)}, u32[]{:S(2)}, u32[]{:S(2)}) collective-permute-start(bf16[448,256]{1,0:T(8,128)(2,1)S(1)} %fusion.20), channel_id=1, source_target_pairs={{16,0},{32,16},{48,32},{64,48},{80,64},{96,80},{112,96},{8,24},{24... | collective-permute-start | bytes 688136 | tf_op jit(solution)/shard_map/ppermute | solution.py:18
  102.8 9.1 %collective-permute-start.15 = (bf16[448,256]{1,0:T(8,128)(2,1)S(1)}, bf16[448,256]{1,0:T(8,128)(2,1)S(1)}, u32[]{:S(2)}, u32[]{:S(2)}) collective-permute-start(bf16[448,256]{1,0:T(8,128)(2,1)S(1)} %fusion.21), channel_id=1, source_target_pairs={{0,16},{16,32},{32,48},{48,64},{64,80},{80,96},{96,112},{24,8},{40... | collective-permute-start | bytes 688136 | tf_op jit(solution)/shard_map/ppermute | solution.py:18
  105.5 9.3 %collective-permute-start.14 = (bf16[448,256]{1,0:T(8,128)(2,1)S(1)}, bf16[448,256]{1,0:T(8,128)(2,1)S(1)}, u32[]{:S(2)}, u32[]{:S(2)}) collective-permute-start(bf16[448,256]{1,0:T(8,128)(2,1)S(1)} %fusion.22), channel_id=1, source_target_pairs={{16,0},{32,16},{48,32},{64,48},{80,64},{96,80},{112,96},{8,24},{24... | collective-permute-start | bytes 688136 | tf_op jit(solution)/shard_map/ppermute | solution.py:18
  112.0 9.3 %copy-start.2 = (f32[448,256]{1,0:T(8,128)S(1)}, f32[448,256]{1,0:T(8,128)}, u32[]{:S(2)}) copy-start(f32[448,256]{1,0:T(8,128)} %param.10) | copy-start | bytes 1376260
  112.0 9.3 %copy-start.3 = (f32[448,256]{1,0:T(8,128)S(1)}, f32[448,256]{1,0:T(8,128)}, u32[]{:S(2)}) copy-start(f32[448,256]{1,0:T(8,128)} %param.9) | copy-start | bytes 1376260
  112.0 9.3 %collective-permute-start.16 = (bf16[448,256]{1,0:T(8,128)(2,1)S(1)}, bf16[448,256]{1,0:T(8,128)(2,1)S(1)}, u32[]{:S(2)}, u32[]{:S(2)}) collective-permute-start(bf16[448,256]{1,0:T(8,128)(2,1)S(1)} %fusion.23), channel_id=1, source_target_pairs={{0,16},{16,32},{32,48},{48,64},{64,80},{80,96},{96,112},{24,8},{40... | collective-permute-start | bytes 688136 | tf_op jit(solution)/shard_map/ppermute | solution.py:18
  122.7 9.6 %collective-permute-start.17 = (bf16[224,256]{1,0:T(8,128)(2,1)S(1)}, bf16[224,256]{1,0:T(8,128)(2,1)S(1)}, u32[]{:S(2)}, u32[]{:S(2)}) collective-permute-start(bf16[224,256]{1,0:T(8,128)(2,1)S(1)} %get-tuple-element.9), channel_id=1, source_target_pairs={{0,128},{128,256},{256,384},{384,0},{1,129},{129,257},{257,385},{3... | collective-permute-start | bytes 344072 | tf_op jit(solution)/shard_map/ppermute | solution.py:100
  126.2 8.2 %collective-permute-start.18 = (bf16[224,256]{1,0:T(8,128)(2,1)S(1)}, bf16[224,256]{1,0:T(8,128)(2,1)S(1)}, u32[]{:S(2)}, u32[]{:S(2)}) collective-permute-start(bf16[224,256]{1,0:T(8,128)(2,1)S(1)} %get-tuple-element.10), channel_id=1, source_target_pairs={{0,256},{128,384},{256,0},{384,128},{1,257},{129,385},{257,1},{385... | collective-permute-start | bytes 344072 | tf_op jit(solution)/shard_map/ppermute | solution.py:101

commit v10 on v9

--- a/solution.py
+++ b/solution.py
@@ -34,9 +34,9 @@
     early_up = far_half == 1
     position = jnp.where(early_up, place, last - place)
 
-    up_other = lax.ppermute(upstream, "zh", [(0, 1), (1, 0)])
     hidden_t = lax.optimization_barrier(hidden.T)
     got = {True: [along(weights, True)], False: [along(weights, False)]}
+    up_other = lax.ppermute(upstream, "zh", [(0, 1), (1, 0)])
     sent = {}
 
     def send(early, turn, part):
@@ -77,7 +77,7 @@
     for turn in range(last):
         send(False, turn, part_of(last - 1 - turn, (False, turn - 1) if 0 < turn < last - 1 else (False, 3) if turn else None))
         if turn < last - 1:
-            send(True, turn + 1, part_of(turn + 1, (True, turn) if turn else None))
+            send(True, turn + 1, part_of(turn + 1, (True, turn) if turn else (False, 0)))
         for pair in {turn, last - 1 - turn} if turn >= last // 2 else ():
             block = jnp.where(pair < position, got[True][pair], got[False][last - 1 - pair])
             hg_total = hg_total + contract(features_of(pair), block, ((1,), (1,)))
@@ -97,8 +97,10 @@
     half = updated.shape[0] // 2
     even_step = step_index[0] % 2 == 0
     lower, upper = updated[:half], updated[half:]
-    near = lax.ppermute(jnp.where(even_step, lower, upper), "y", [(i, (i + 1) % 4) for i in range(4)])
-    far = lax.ppermute(jnp.where(even_step, upper, lower), "y", [(i, (i + 2) % 4) for i in range(4)])
+    far_sent = lax.optimization_barrier(jnp.where(even_step, upper, lower))
+    far = lax.ppermute(far_sent, "y", [(i, (i + 2) % 4) for i in range(4)])
+    near_sent = behind(jnp.where(even_step, lower, upper), far_sent)
+    near = lax.ppermute(near_sent, "y", [(i, (i + 1) % 4) for i in range(4)])
     partner = jnp.concatenate([jnp.where(even_step, near, far), jnp.where(even_step, far, near)], 0)
     mixed = ((updated.astype(F32) + partner.astype(F32)) * 0.5).astype(BF)
 

time: 136 us -> 137 us (level)
  waiting for transfers between devices: 18.7 us -> 20.3 us
    ppermute x2, waiting for transfers between devices: 2.13 us -> 4.06 us  [the longest x1 4.05 us: body(): near = lax.ppermute(near_sent, 'y', [(i, (i + 1) % 4) for i in range(4)])]
where the time goes in v10:
time: 137 us; the launch traced here: 136 us
  starting transfers between devices  75.2 us (55%)
  blocking collectives  28.4 us (21%)
  waiting for transfers between devices  20.3 us (15%)
  matrix products  6.61 us (5%)
  other arithmetic  3.57 us (3%)
  between operations  2 us (1%)
    ppermute x16, starting transfers between devices, along(): return lax.ppermute(value, ('zl', 'zh'), pairs)  57.6 us
    ppermute x16, waiting for transfers between devices, along(): return lax.ppermute(value, ('zl', 'zh'), pairs)  16.2 us
    all_gather x1, blocking collectives, body(): near_up = lax.all_gather(upstream, ('x', 'c'), axis=1, tiled=True)  14.4 us
    all_gather x1, blocking collectives, body(): far_up = lax.all_gather(up_other, ('x', 'c'), axis=1, tiled=True)  14 us
    ppermute x1, starting transfers between devices, body(): up_other = lax.ppermute(upstream, 'zh', [(0, 1), (1, 0)])  9.91 us
    dot_general x17, matrix products, contract(): lax.dot_general(left, right, (dims, ((), ())), preferred_element_type=F32)  6.61 us
    ppermute x1, starting transfers between devices, body(): far = lax.ppermute(far_sent, 'y', [(i, (i + 2) % 4) for i in range(4)])  5.1 us
    ppermute x1, waiting for transfers between devices, body(): near = lax.ppermute(near_sent, 'y', [(i, (i + 1) % 4) for i in range(4)])  4.05 us
  transfers between devices with their start and end apart: 19, of which 8 were waited for; matrix products, arithmetic and copies ran while one was open for 6% of the time, Pallas kernels for 0%

profile of v10, /device:TPU:128, one launch (start us, length us, event | category | flops | bytes accessed | tf_op | source)
XLA Modules:
  0.0 136.2 jit_solution(13039506661638018430)
XLA Ops:
  0.6 4.0 %collective-permute-start = (bf16[448,256]{1,0:T(8,128)(2,1)}, bf16[448,256]{1,0:T(8,128)(2,1)S(1)}, u32[]{:S(2)}, u32[]{:S(2)}) collective-permute-start(bf16[448,256]{1,0:T(8,128)(2,1)} %param.8), channel_id=1, source_target_pairs={{0,16},{16,32},{32,48},{48,64},{64,80},{80,96},{96,112},{24,8},{40... | collective-permute-start | bytes 688136 | tf_op jit(solution)/shard_map/ppermute | solution.py:18
  4.6 3.2 %collective-permute-start.1 = (bf16[448,256]{1,0:T(8,128)(2,1)}, bf16[448,256]{1,0:T(8,128)(2,1)S(1)}, u32[]{:S(2)}, u32[]{:S(2)}) collective-permute-start(bf16[448,256]{1,0:T(8,128)(2,1)} %param.8), channel_id=1, source_target_pairs={{16,0},{32,16},{48,32},{64,48},{80,64},{96,80},{112,96},{8,24},{24... | collective-permute-start | bytes 688136 | tf_op jit(solution)/shard_map/ppermute | solution.py:18
  7.8 9.9 %collective-permute-start.2 = (bf16[448,128]{1,0:T(8,128)(2,1)}, bf16[448,128]{1,0:T(8,128)(2,1)S(1)}, u32[]{:S(2)}, u32[]{:S(2)}) collective-permute-start(bf16[448,128]{1,0:T(8,128)(2,1)} %param.7), channel_id=1, source_target_pairs={{0,8},{8,0},{1,9},{9,1},{2,10},{10,2},{3,11},{11,3},{4,12},{12,4},... | collective-permute-start | bytes 344072 | tf_op jit(solution)/shard_map/ppermute | solution.py:39
  17.8 14.4 %all_gather.6 = bf16[448,1024]{1,0:T(8,128)(2,1)S(1)} all-gather(bf16[448,128]{1,0:T(8,128)(2,1)} %param.7), channel_id=1, replica_groups=mesh['y'=4,'zl'=8,'zh'=2,'x'=4,'c'=2] {'x','c'}, dimensions={1}, use_global_device_ids=true | all-gather | bytes 1032192 | tf_op jit(solution)/shard_map/all_gather | solution.py:53
  33.6 5.1 %collective-permute-start.3 = (bf16[448,256]{1,0:T(8,128)(2,1)S(1)}, bf16[448,256]{1,0:T(8,128)(2,1)S(1)}, u32[]{:S(2)}, u32[]{:S(2)}) collective-permute-start(bf16[448,256]{1,0:T(8,128)(2,1)S(1)} %fusion.10), channel_id=1, source_target_pairs={{16,0},{32,16},{48,32},{64,48},{80,64},{96,80},{112,96},{8,24},{24... | collective-permute-start | bytes 688136 | tf_op jit(solution)/shard_map/ppermute | solution.py:18
  38.8 14.0 %all_gather.7 = bf16[448,1024]{1,0:T(8,128)(2,1)S(1)} all-gather(bf16[448,128]{1,0:T(8,128)(2,1)S(1)} %slice_select_fusion), channel_id=1, replica_groups=mesh['y'=4,'zl'=8,'zh'=2,'x'=4,'c'=2] {'x','c'}, dimensions={1}, use_global_device_ids=true | all-gather | bytes 1032192 | tf_op jit(solution)/shard_map/all_gather | solution.py:57
  53.4 1.9 %collective-permute-start.4 = (bf16[448,256]{1,0:T(8,128)(2,1)S(1)}, bf16[448,256]{1,0:T(8,128)(2,1)S(1)}, u32[]{:S(2)}, u32[]{:S(2)}) collective-permute-start(bf16[448,256]{1,0:T(8,128)(2,1)S(1)} %fusion.11), channel_id=1, source_target_pairs={{0,16},{16,32},{32,48},{48,64},{64,80},{80,96},{96,112},{24,8},{40... | collective-permute-start | bytes 688136 | tf_op jit(solution)/shard_map/ppermute | solution.py:18
  56.1 5.1 %collective-permute-start.5 = (bf16[448,256]{1,0:T(8,128)(2,1)S(1)}, bf16[448,256]{1,0:T(8,128)(2,1)S(1)}, u32[]{:S(2)}, u32[]{:S(2)}) collective-permute-start(bf16[448,256]{1,0:T(8,128)(2,1)S(1)} %fusion.12), channel_id=1, source_target_pairs={{16,0},{32,16},{48,32},{64,48},{80,64},{96,80},{112,96},{8,24},{24... | collective-permute-start | bytes 688136 | tf_op jit(solution)/shard_map/ppermute | solution.py:18
  61.3 3.1 %collective-permute-done.4 = bf16[448,256]{1,0:T(8,128)(2,1)S(1)} collective-permute-done((bf16[448,256]{1,0:T(8,128)(2,1)S(1)}, bf16[448,256]{1,0:T(8,128)(2,1)S(1)}, u32[]{:S(2)}, u32[]{:S(2)}) %collective-permute-start.4) | collective-permute-done | bytes 229408 | tf_op jit(solution)/shard_map/ppermute | solution.py:18
  64.4 1.9 %collective-permute-start.6 = (bf16[448,256]{1,0:T(8,128)(2,1)S(1)}, bf16[448,256]{1,0:T(8,128)(2,1)S(1)}, u32[]{:S(2)}, u32[]{:S(2)}) collective-permute-start(bf16[448,256]{1,0:T(8,128)(2,1)S(1)} %fusion.13), channel_id=1, source_target_pairs={{0,16},{16,32},{32,48},{48,64},{64,80},{80,96},{96,112},{24,8},{40... | collective-permute-start | bytes 688136 | tf_op jit(solution)/shard_map/ppermute | solution.py:18
  67.2 5.1 %collective-permute-start.7 = (bf16[448,256]{1,0:T(8,128)(2,1)S(1)}, bf16[448,256]{1,0:T(8,128)(2,1)S(1)}, u32[]{:S(2)}, u32[]{:S(2)}) collective-permute-start(bf16[448,256]{1,0:T(8,128)(2,1)S(1)} %fusion.14), channel_id=1, source_target_pairs={{16,0},{32,16},{48,32},{64,48},{80,64},{96,80},{112,96},{8,24},{24... | collective-permute-start | bytes 688136 | tf_op jit(solution)/shard_map/ppermute | solution.py:18
  72.3 2.2 %collective-permute-done.6 = bf16[448,256]{1,0:T(8,128)(2,1)S(1)} collective-permute-done((bf16[448,256]{1,0:T(8,128)(2,1)S(1)}, bf16[448,256]{1,0:T(8,128)(2,1)S(1)}, u32[]{:S(2)}, u32[]{:S(2)}) %collective-permute-start.6) | collective-permute-done | bytes 229408 | tf_op jit(solution)/shard_map/ppermute | solution.py:18
  74.7 1.9 %collective-permute-start.8 = (bf16[448,256]{1,0:T(8,128)(2,1)S(1)}, bf16[448,256]{1,0:T(8,128)(2,1)S(1)}, u32[]{:S(2)}, u32[]{:S(2)}) collective-permute-start(bf16[448,256]{1,0:T(8,128)(2,1)S(1)} %fusion.15), channel_id=1, source_target_pairs={{0,16},{16,32},{32,48},{48,64},{64,80},{80,96},{96,112},{24,8},{40... | collective-permute-start | bytes 688136 | tf_op jit(solution)/shard_map/ppermute | solution.py:18
  77.1 5.3 %collective-permute-start.9 = (bf16[448,256]{1,0:T(8,128)(2,1)S(1)}, bf16[448,256]{1,0:T(8,128)(2,1)S(1)}, u32[]{:S(2)}, u32[]{:S(2)}) collective-permute-start(bf16[448,256]{1,0:T(8,128)(2,1)S(1)} %fusion.16), channel_id=1, source_target_pairs={{16,0},{32,16},{48,32},{64,48},{80,64},{96,80},{112,96},{8,24},{24... | collective-permute-start | bytes 688136 | tf_op jit(solution)/shard_map/ppermute | solution.py:18
  82.4 1.5 %collective-permute-done.8 = bf16[448,256]{1,0:T(8,128)(2,1)S(1)} collective-permute-done((bf16[448,256]{1,0:T(8,128)(2,1)S(1)}, bf16[448,256]{1,0:T(8,128)(2,1)S(1)}, u32[]{:S(2)}, u32[]{:S(2)}) %collective-permute-start.8) | collective-permute-done | bytes 229408 | tf_op jit(solution)/shard_map/ppermute | solution.py:18
  84.0 1.9 %collective-permute-start.10 = (bf16[448,256]{1,0:T(8,128)(2,1)S(1)}, bf16[448,256]{1,0:T(8,128)(2,1)S(1)}, u32[]{:S(2)}, u32[]{:S(2)}) collective-permute-start(bf16[448,256]{1,0:T(8,128)(2,1)S(1)} %fusion.17), channel_id=1, source_target_pairs={{0,16},{16,32},{32,48},{48,64},{64,80},{80,96},{96,112},{24,8},{40... | collective-permute-start | bytes 688136 | tf_op jit(solution)/shard_map/ppermute | solution.py:18
  87.1 5.1 %collective-permute-start.11 = (bf16[448,256]{1,0:T(8,128)(2,1)S(1)}, bf16[448,256]{1,0:T(8,128)(2,1)S(1)}, u32[]{:S(2)}, u32[]{:S(2)}) collective-permute-start(bf16[448,256]{1,0:T(8,128)(2,1)S(1)} %fusion.18), channel_id=1, source_target_pairs={{16,0},{32,16},{48,32},{64,48},{80,64},{96,80},{112,96},{8,24},{24... | collective-permute-start | bytes 688136 | tf_op jit(solution)/shard_map/ppermute | solution.py:18
  92.2 0.9 collective-permute-done.10
  93.3 1.9 %collective-permute-start.12 = (bf16[448,256]{1,0:T(8,128)(2,1)S(1)}, bf16[448,256]{1,0:T(8,128)(2,1)S(1)}, u32[]{:S(2)}, u32[]{:S(2)}) collective-permute-start(bf16[448,256]{1,0:T(8,128)(2,1)S(1)} %fusion.19), channel_id=1, source_target_pairs={{0,16},{16,32},{32,48},{48,64},{64,80},{80,96},{96,112},{24,8},{40... | collective-permute-start | bytes 688136 | tf_op jit(solution)/shard_map/ppermute | solution.py:18
  96.0 5.5 %collective-permute-start.13 = (bf16[448,256]{1,0:T(8,128)(2,1)S(1)}, bf16[448,256]{1,0:T(8,128)(2,1)S(1)}, u32[]{:S(2)}, u32[]{:S(2)}) collective-permute-start(bf16[448,256]{1,0:T(8,128)(2,1)S(1)} %fusion.20), channel_id=1, source_target_pairs={{16,0},{32,16},{48,32},{64,48},{80,64},{96,80},{112,96},{8,24},{24... | collective-permute-start | bytes 688136 | tf_op jit(solution)/shard_map/ppermute | solution.py:18
  101.4 0.9 collective-permute-done.12
  102.5 1.9 %collective-permute-start.15 = (bf16[448,256]{1,0:T(8,128)(2,1)S(1)}, bf16[448,256]{1,0:T(8,128)(2,1)S(1)}, u32[]{:S(2)}, u32[]{:S(2)}) collective-permute-start(bf16[448,256]{1,0:T(8,128)(2,1)S(1)} %fusion.21), channel_id=1, source_target_pairs={{0,16},{16,32},{32,48},{48,64},{64,80},{80,96},{96,112},{24,8},{40... | collective-permute-start | bytes 688136 | tf_op jit(solution)/shard_map/ppermute | solution.py:18
  105.2 5.5 %collective-permute-start.14 = (bf16[448,256]{1,0:T(8,128)(2,1)S(1)}, bf16[448,256]{1,0:T(8,128)(2,1)S(1)}, u32[]{:S(2)}, u32[]{:S(2)}) collective-permute-start(bf16[448,256]{1,0:T(8,128)(2,1)S(1)} %fusion.22), channel_id=1, source_target_pairs={{16,0},{32,16},{48,32},{64,48},{80,64},{96,80},{112,96},{8,24},{24... | collective-permute-start | bytes 688136 | tf_op jit(solution)/shard_map/ppermute | solution.py:18
  110.7 0.9 collective-permute-done.15
  111.7 2.1 %collective-permute-start.16 = (bf16[448,256]{1,0:T(8,128)(2,1)S(1)}, bf16[448,256]{1,0:T(8,128)(2,1)S(1)}, u32[]{:S(2)}, u32[]{:S(2)}) collective-permute-start(bf16[448,256]{1,0:T(8,128)(2,1)S(1)} %fusion.23), channel_id=1, source_target_pairs={{0,16},{16,32},{32,48},{48,64},{64,80},{80,96},{96,112},{24,8},{40... | collective-permute-start | bytes 688136 | tf_op jit(solution)/shard_map/ppermute | solution.py:18
  114.4 6.6 %collective-permute-done.16 = bf16[448,256]{1,0:T(8,128)(2,1)S(1)} collective-permute-done((bf16[448,256]{1,0:T(8,128)(2,1)S(1)}, bf16[448,256]{1,0:T(8,128)(2,1)S(1)}, u32[]{:S(2)}, u32[]{:S(2)}) %collective-permute-start.16) | collective-permute-done | bytes 229408 | tf_op jit(solution)/shard_map/ppermute | solution.py:18
  121.0 1.4 fusion.9
  122.4 5.1 %collective-permute-start.18 = (bf16[224,256]{1,0:T(8,128)(2,1)S(1)}, bf16[224,256]{1,0:T(8,128)(2,1)S(1)}, u32[]{:S(2)}, u32[]{:S(2)}) collective-permute-start(bf16[224,256]{1,0:T(8,128)(2,1)S(1)} %broadcast_select_fusion.2), channel_id=1, source_target_pairs={{0,256},{128,384},{256,0},{384,128},{1,257},{129,385},{257,1},{385... | collective-permute-start | bytes 344072 | tf_op jit(solution)/shard_map/ppermute | solution.py:101
  127.5 2.6 %collective-permute-start.17 = (bf16[224,256]{1,0:T(8,128)(2,1)S(1)}, bf16[224,256]{1,0:T(8,128)(2,1)S(1)}, u32[]{:S(2)}, u32[]{:S(2)}) collective-permute-start(bf16[224,256]{1,0:T(8,128)(2,1)S(1)} %select_select_fusion), channel_id=1, source_target_pairs={{0,128},{128,256},{256,384},{384,0},{1,129},{129,257},{257,385},{3... | collective-permute-start | bytes 344072 | tf_op jit(solution)/shard_map/ppermute | solution.py:103
  130.1 1.2 fusion.6
  131.4 4.1 %collective-permute-done.17 = bf16[224,256]{1,0:T(8,128)(2,1)S(1)} collective-permute-done((bf16[224,256]{1,0:T(8,128)(2,1)S(1)}, bf16[224,256]{1,0:T(8,128)(2,1)S(1)}, u32[]{:S(2)}, u32[]{:S(2)}) %collective-permute-start.17) | collective-permute-done | bytes 114720 | tf_op jit(solution)/shard_map/ppermute | solution.py:103
  135.4 0.8 multiply_convert_fusion
  (55 shorter events, 7.0 us)
Async XLA Ops:
  0.6 31.5 %copy-start = (bf16[448,448]{1,0:T(8,128)(2,1)S(1)}, bf16[448,448]{1,0:T(8,128)(2,1)}, u32[]{:S(2)}) copy-start(bf16[448,448]{1,0:T(8,128)(2,1)} %param.6) | copy-start | bytes 1204228
  0.6 32.8 %collective-permute-start = (bf16[448,256]{1,0:T(8,128)(2,1)}, bf16[448,256]{1,0:T(8,128)(2,1)S(1)}, u32[]{:S(2)}, u32[]{:S(2)}) collective-permute-start(bf16[448,256]{1,0:T(8,128)(2,1)} %param.8), channel_id=1, source_target_pairs={{0,16},{16,32},{32,48},{48,64},{64,80},{80,96},{96,112},{24,8},{40... | collective-permute-start | bytes 688136 | tf_op jit(solution)/shard_map/ppermute | solution.py:18
  4.6 28.9 %collective-permute-start.1 = (bf16[448,256]{1,0:T(8,128)(2,1)}, bf16[448,256]{1,0:T(8,128)(2,1)S(1)}, u32[]{:S(2)}, u32[]{:S(2)}) collective-permute-start(bf16[448,256]{1,0:T(8,128)(2,1)} %param.8), channel_id=1, source_target_pairs={{16,0},{32,16},{48,32},{64,48},{80,64},{96,80},{112,96},{8,24},{24... | collective-permute-start | bytes 688136 | tf_op jit(solution)/shard_map/ppermute | solution.py:18
  7.8 30.9 %collective-permute-start.2 = (bf16[448,128]{1,0:T(8,128)(2,1)}, bf16[448,128]{1,0:T(8,128)(2,1)S(1)}, u32[]{:S(2)}, u32[]{:S(2)}) collective-permute-start(bf16[448,128]{1,0:T(8,128)(2,1)} %param.7), channel_id=1, source_target_pairs={{0,8},{8,0},{1,9},{9,1},{2,10},{10,2},{3,11},{11,3},{4,12},{12,4},... | collective-permute-start | bytes 344072 | tf_op jit(solution)/shard_map/ppermute | solution.py:39
  33.6 22.4 %collective-permute-start.3 = (bf16[448,256]{1,0:T(8,128)(2,1)S(1)}, bf16[448,256]{1,0:T(8,128)(2,1)S(1)}, u32[]{:S(2)}, u32[]{:S(2)}) collective-permute-start(bf16[448,256]{1,0:T(8,128)(2,1)S(1)} %fusion.10), channel_id=1, source_target_pairs={{16,0},{32,16},{48,32},{64,48},{80,64},{96,80},{112,96},{8,24},{24... | collective-permute-start | bytes 688136 | tf_op jit(solution)/shard_map/ppermute | solution.py:18
  53.4 11.0 %collective-permute-start.4 = (bf16[448,256]{1,0:T(8,128)(2,1)S(1)}, bf16[448,256]{1,0:T(8,128)(2,1)S(1)}, u32[]{:S(2)}, u32[]{:S(2)}) collective-permute-start(bf16[448,256]{1,0:T(8,128)(2,1)S(1)} %fusion.11), channel_id=1, source_target_pairs={{0,16},{16,32},{32,48},{48,64},{64,80},{80,96},{96,112},{24,8},{40... | collective-permute-start | bytes 688136 | tf_op jit(solution)/shard_map/ppermute | solution.py:18
  56.1 11.0 %collective-permute-start.5 = (bf16[448,256]{1,0:T(8,128)(2,1)S(1)}, bf16[448,256]{1,0:T(8,128)(2,1)S(1)}, u32[]{:S(2)}, u32[]{:S(2)}) collective-permute-start(bf16[448,256]{1,0:T(8,128)(2,1)S(1)} %fusion.12), channel_id=1, source_target_pairs={{16,0},{32,16},{48,32},{64,48},{80,64},{96,80},{112,96},{8,24},{24... | collective-permute-start | bytes 688136 | tf_op jit(solution)/shard_map/ppermute | solution.py:18
  64.4 10.2 %collective-permute-start.6 = (bf16[448,256]{1,0:T(8,128)(2,1)S(1)}, bf16[448,256]{1,0:T(8,128)(2,1)S(1)}, u32[]{:S(2)}, u32[]{:S(2)}) collective-permute-start(bf16[448,256]{1,0:T(8,128)(2,1)S(1)} %fusion.13), channel_id=1, source_target_pairs={{0,16},{16,32},{32,48},{48,64},{64,80},{80,96},{96,112},{24,8},{40... | collective-permute-start | bytes 688136 | tf_op jit(solution)/shard_map/ppermute | solution.py:18
  67.2 9.8 %collective-permute-start.7 = (bf16[448,256]{1,0:T(8,128)(2,1)S(1)}, bf16[448,256]{1,0:T(8,128)(2,1)S(1)}, u32[]{:S(2)}, u32[]{:S(2)}) collective-permute-start(bf16[448,256]{1,0:T(8,128)(2,1)S(1)} %fusion.14), channel_id=1, source_target_pairs={{16,0},{32,16},{48,32},{64,48},{80,64},{96,80},{112,96},{8,24},{24... | collective-permute-start | bytes 688136 | tf_op jit(solution)/shard_map/ppermute | solution.py:18
  74.7 9.2 %collective-permute-start.8 = (bf16[448,256]{1,0:T(8,128)(2,1)S(1)}, bf16[448,256]{1,0:T(8,128)(2,1)S(1)}, u32[]{:S(2)}, u32[]{:S(2)}) collective-permute-start(bf16[448,256]{1,0:T(8,128)(2,1)S(1)} %fusion.15), channel_id=1, source_target_pairs={{0,16},{16,32},{32,48},{48,64},{64,80},{80,96},{96,112},{24,8},{40... | collective-permute-start | bytes 688136 | tf_op jit(solution)/shard_map/ppermute | solution.py:18
  77.1 9.5 %copy-start.1 = (bf16[448,256]{1,0:T(8,128)(2,1)S(1)}, bf16[448,256]{1,0:T(8,128)(2,1)}, u32[]{:S(2)}) copy-start(bf16[448,256]{1,0:T(8,128)(2,1)} %param.8) | copy-start | bytes 688132
  77.1 9.9 %collective-permute-start.9 = (bf16[448,256]{1,0:T(8,128)(2,1)S(1)}, bf16[448,256]{1,0:T(8,128)(2,1)S(1)}, u32[]{:S(2)}, u32[]{:S(2)}) collective-permute-start(bf16[448,256]{1,0:T(8,128)(2,1)S(1)} %fusion.16), channel_id=1, source_target_pairs={{16,0},{32,16},{48,32},{64,48},{80,64},{96,80},{112,96},{8,24},{24... | collective-permute-start | bytes 688136 | tf_op jit(solution)/shard_map/ppermute | solution.py:18
  84.0 9.1 %collective-permute-start.10 = (bf16[448,256]{1,0:T(8,128)(2,1)S(1)}, bf16[448,256]{1,0:T(8,128)(2,1)S(1)}, u32[]{:S(2)}, u32[]{:S(2)}) collective-permute-start(bf16[448,256]{1,0:T(8,128)(2,1)S(1)} %fusion.17), channel_id=1, source_target_pairs={{0,16},{16,32},{32,48},{48,64},{64,80},{80,96},{96,112},{24,8},{40... | collective-permute-start | bytes 688136 | tf_op jit(solution)/shard_map/ppermute | solution.py:18
  87.1 8.8 %collective-permute-start.11 = (bf16[448,256]{1,0:T(8,128)(2,1)S(1)}, bf16[448,256]{1,0:T(8,128)(2,1)S(1)}, u32[]{:S(2)}, u32[]{:S(2)}) collective-permute-start(bf16[448,256]{1,0:T(8,128)(2,1)S(1)} %fusion.18), channel_id=1, source_target_pairs={{16,0},{32,16},{48,32},{64,48},{80,64},{96,80},{112,96},{8,24},{24... | collective-permute-start | bytes 688136 | tf_op jit(solution)/shard_map/ppermute | solution.py:18
  93.3 9.1 %collective-permute-start.12 = (bf16[448,256]{1,0:T(8,128)(2,1)S(1)}, bf16[448,256]{1,0:T(8,128)(2,1)S(1)}, u32[]{:S(2)}, u32[]{:S(2)}) collective-permute-start(bf16[448,256]{1,0:T(8,128)(2,1)S(1)} %fusion.19), channel_id=1, source_target_pairs={{0,16},{16,32},{32,48},{48,64},{64,80},{80,96},{96,112},{24,8},{40... | collective-permute-start | bytes 688136 | tf_op jit(solution)/shard_map/ppermute | solution.py:18
  96.0 9.1 %collective-permute-start.13 = (bf16[448,256]{1,0:T(8,128)(2,1)S(1)}, bf16[448,256]{1,0:T(8,128)(2,1)S(1)}, u32[]{:S(2)}, u32[]{:S(2)}) collective-permute-start(bf16[448,256]{1,0:T(8,128)(2,1)S(1)} %fusion.20), channel_id=1, source_target_pairs={{16,0},{32,16},{48,32},{64,48},{80,64},{96,80},{112,96},{8,24},{24... | collective-permute-start | bytes 688136 | tf_op jit(solution)/shard_map/ppermute | solution.py:18
  102.5 9.1 %collective-permute-start.15 = (bf16[448,256]{1,0:T(8,128)(2,1)S(1)}, bf16[448,256]{1,0:T(8,128)(2,1)S(1)}, u32[]{:S(2)}, u32[]{:S(2)}) collective-permute-start(bf16[448,256]{1,0:T(8,128)(2,1)S(1)} %fusion.21), channel_id=1, source_target_pairs={{0,16},{16,32},{32,48},{48,64},{64,80},{80,96},{96,112},{24,8},{40... | collective-permute-start | bytes 688136 | tf_op jit(solution)/shard_map/ppermute | solution.py:18
  105.2 15.8 %collective-permute-start.14 = (bf16[448,256]{1,0:T(8,128)(2,1)S(1)}, bf16[448,256]{1,0:T(8,128)(2,1)S(1)}, u32[]{:S(2)}, u32[]{:S(2)}) collective-permute-start(bf16[448,256]{1,0:T(8,128)(2,1)S(1)} %fusion.22), channel_id=1, source_target_pairs={{16,0},{32,16},{48,32},{64,48},{80,64},{96,80},{112,96},{8,24},{24... | collective-permute-start | bytes 688136 | tf_op jit(solution)/shard_map/ppermute | solution.py:18
  111.7 9.3 %copy-start.2 = (f32[448,256]{1,0:T(8,128)S(1)}, f32[448,256]{1,0:T(8,128)}, u32[]{:S(2)}) copy-start(f32[448,256]{1,0:T(8,128)} %param.10) | copy-start | bytes 1376260
  111.7 9.3 %copy-start.3 = (f32[448,256]{1,0:T(8,128)S(1)}, f32[448,256]{1,0:T(8,128)}, u32[]{:S(2)}) copy-start(f32[448,256]{1,0:T(8,128)} %param.9) | copy-start | bytes 1376260
  111.7 9.3 %collective-permute-start.16 = (bf16[448,256]{1,0:T(8,128)(2,1)S(1)}, bf16[448,256]{1,0:T(8,128)(2,1)S(1)}, u32[]{:S(2)}, u32[]{:S(2)}) collective-permute-start(bf16[448,256]{1,0:T(8,128)(2,1)S(1)} %fusion.23), channel_id=1, source_target_pairs={{0,16},{16,32},{32,48},{48,64},{64,80},{80,96},{96,112},{24,8},{40... | collective-permute-start | bytes 688136 | tf_op jit(solution)/shard_map/ppermute | solution.py:18
  122.4 13.0 %collective-permute-start.18 = (bf16[224,256]{1,0:T(8,128)(2,1)S(1)}, bf16[224,256]{1,0:T(8,128)(2,1)S(1)}, u32[]{:S(2)}, u32[]{:S(2)}) collective-permute-start(bf16[224,256]{1,0:T(8,128)(2,1)S(1)} %broadcast_select_fusion.2), channel_id=1, source_target_pairs={{0,256},{128,384},{256,0},{384,128},{1,257},{129,385},{257,1},{385... | collective-permute-start | bytes 344072 | tf_op jit(solution)/shard_map/ppermute | solution.py:101
  127.5 7.9 %collective-permute-start.17 = (bf16[224,256]{1,0:T(8,128)(2,1)S(1)}, bf16[224,256]{1,0:T(8,128)(2,1)S(1)}, u32[]{:S(2)}, u32[]{:S(2)}) collective-permute-start(bf16[224,256]{1,0:T(8,128)(2,1)S(1)} %select_select_fusion), channel_id=1, source_target_pairs={{0,128},{128,256},{256,384},{384,0},{1,129},{129,257},{257,385},{3... | collective-permute-start | bytes 344072 | tf_op jit(solution)/shard_map/ppermute | solution.py:103

commit v11 on v9

--- a/solution.py
+++ b/solution.py
@@ -77,7 +77,7 @@
     for turn in range(last):
         send(False, turn, part_of(last - 1 - turn, (False, turn - 1) if 0 < turn < last - 1 else (False, 3) if turn else None))
         if turn < last - 1:
-            send(True, turn + 1, part_of(turn + 1, (True, turn) if turn else None))
+            send(True, turn + 1, part_of(turn + 1, (True, turn) if turn else (False, 0)))
         for pair in {turn, last - 1 - turn} if turn >= last // 2 else ():
             block = jnp.where(pair < position, got[True][pair], got[False][last - 1 - pair])
             hg_total = hg_total + contract(features_of(pair), block, ((1,), (1,)))
@@ -86,22 +86,40 @@
     grads = (own_part + got[True][-1].astype(F32) + got[False][-1].astype(F32)) * scale_hid
 
     count = (step_index[0] + 1).astype(F32)
-    first_new = 0.9 * first_moment + 0.1 * grads
-    second_new = 0.999 * second_moment + 0.001 * grads * grads
     correct_one = 1.0 - jnp.power(F32(0.9), count)
     correct_two = 1.0 - jnp.power(F32(0.999), count)
-    weights_f = weights.astype(F32)
-    step_size = first_new / correct_one / (jnp.sqrt(second_new / correct_two) + 1e-08) + 0.1 * weights_f
-    updated = (weights_f - 0.05 * step_size).astype(BF)
 
-    half = updated.shape[0] // 2
+    def moments(first, second, grad):
+        return 0.9 * first + 0.1 * grad, 0.999 * second + 0.001 * grad * grad
+
+    half = weights.shape[0] // 2
     even_step = step_index[0] % 2 == 0
-    lower, upper = updated[:half], updated[half:]
-    near = lax.ppermute(jnp.where(even_step, lower, upper), "y", [(i, (i + 1) % 4) for i in range(4)])
-    far = lax.ppermute(jnp.where(even_step, upper, lower), "y", [(i, (i + 2) % 4) for i in range(4)])
-    partner = jnp.concatenate([jnp.where(even_step, near, far), jnp.where(even_step, far, near)], 0)
-    mixed = ((updated.astype(F32) + partner.astype(F32)) * 0.5).astype(BF)
+    near_at = jnp.where(even_step, 0, half)
 
+    def updated_rows(at, after=None):
+        first, second, weight, *sums = [
+            lax.dynamic_slice_in_dim(x, at, half, 0)
+            for x in (first_moment, second_moment, weights, own_part, got[True][-1], got[False][-1])
+        ]
+        weight = weight if after is None else behind(weight, after)
+        grad = (sums[0] + sums[1].astype(F32) + sums[2].astype(F32)) * scale_hid
+        first_new, second_new = moments(first, second, grad)
+        weight = weight.astype(F32)
+        step_size = first_new / correct_one / (jnp.sqrt(second_new / correct_two) + 1e-08) + 0.1 * weight
+        return lax.optimization_barrier((weight - 0.05 * step_size).astype(BF))
+
+    def mix(own, partner):
+        return ((own.astype(F32) + partner.astype(F32)) * 0.5).astype(BF)
+
+    near_rows = updated_rows(near_at)
+    near = lax.ppermute(near_rows, "y", [(i, (i + 1) % 4) for i in range(4)])
+    far_rows = updated_rows(half - near_at, near_rows)
+    far = lax.ppermute(far_rows, "y", [(i, (i + 2) % 4) for i in range(4)])
+    first_new, second_new = moments(first_moment, second_moment, grads)
+    near_mixed, far_mixed = mix(near_rows, near), mix(far_rows, far)
+    mixed = jnp.concatenate(
+        [jnp.where(even_step, near_mixed, far_mixed), jnp.where(even_step, far_mixed, near_mixed)], 0
+    )
     in_grad = (hg_total * scale_hid).astype(BF)
     return mixed, first_new, second_new, in_grad
 

time: 136 us -> 133 us (0.978)
  the two profiles are of different devices: /device:TPU:128 before, /device:TPU:136 now
where the time goes in v11:
time: 133 us
  starting transfers between devices  72.7 us (55%)
  blocking collectives  28.3 us (21%)
  waiting for transfers between devices  19.1 us (14%)
  matrix products  6.63 us (5%)
  other arithmetic  3.84 us (3%)
  between operations  2 us (2%)
    ppermute x16, starting transfers between devices, along(): return lax.ppermute(value, ('zl', 'zh'), pairs)  54.2 us
    ppermute x16, waiting for transfers between devices, along(): return lax.ppermute(value, ('zl', 'zh'), pairs)  14.9 us
    all_gather x1, blocking collectives, body(): near_up = lax.all_gather(upstream, ('x', 'c'), axis=1, tiled=True)  14.4 us
    all_gather x1, blocking collectives, body(): far_up = lax.all_gather(up_other, ('x', 'c'), axis=1, tiled=True)  13.9 us
    ppermute x1, starting transfers between devices, body(): up_other = lax.ppermute(upstream, 'zh', [(0, 1), (1, 0)])  12.1 us
    dot_general x17, matrix products, contract(): lax.dot_general(left, right, (dims, ((), ())), preferred_element_type=F32)  6.63 us
    ppermute x1, waiting for transfers between devices, body(): far = lax.ppermute(far_rows, 'y', [(i, (i + 2) % 4) for i in range(4)])  4.22 us
    ppermute x1, starting transfers between devices, body(): near = lax.ppermute(near_rows, 'y', [(i, (i + 1) % 4) for i in range(4)])  3.49 us
  transfers between devices with their start and end apart: 19, of which 8 were waited for; matrix products, arithmetic and copies ran while one was open for 7% of the time, Pallas kernels for 0%

profile of v11, /device:TPU:136, one launch (start us, length us, event | category | flops | bytes accessed | tf_op | source)
XLA Modules:
  0.0 132.7 jit_solution(8835506744854413181)
XLA Ops:
  0.6 2.2 %collective-permute-start.1 = (bf16[448,256]{1,0:T(8,128)(2,1)}, bf16[448,256]{1,0:T(8,128)(2,1)S(1)}, u32[]{:S(2)}, u32[]{:S(2)}) collective-permute-start(bf16[448,256]{1,0:T(8,128)(2,1)} %param.8), channel_id=1, source_target_pairs={{16,0},{32,16},{48,32},{64,48},{80,64},{96,80},{112,96},{8,24},{24... | collective-permute-start | bytes 688136 | tf_op jit(solution)/shard_map/ppermute | solution.py:18
  2.8 3.8 %collective-permute-start = (bf16[448,256]{1,0:T(8,128)(2,1)}, bf16[448,256]{1,0:T(8,128)(2,1)S(1)}, u32[]{:S(2)}, u32[]{:S(2)}) collective-permute-start(bf16[448,256]{1,0:T(8,128)(2,1)} %param.8), channel_id=1, source_target_pairs={{0,16},{16,32},{32,48},{48,64},{64,80},{80,96},{96,112},{24,8},{40... | collective-permute-start | bytes 688136 | tf_op jit(solution)/shard_map/ppermute | solution.py:18
  6.6 12.1 %collective-permute-start.2 = (bf16[448,128]{1,0:T(8,128)(2,1)}, bf16[448,128]{1,0:T(8,128)(2,1)S(1)}, u32[]{:S(2)}, u32[]{:S(2)}) collective-permute-start(bf16[448,128]{1,0:T(8,128)(2,1)} %param.7), channel_id=1, source_target_pairs={{0,8},{8,0},{1,9},{9,1},{2,10},{10,2},{3,11},{11,3},{4,12},{12,4},... | collective-permute-start | bytes 344072 | tf_op jit(solution)/shard_map/ppermute | solution.py:37
  18.8 14.4 %all_gather.6 = bf16[448,1024]{1,0:T(8,128)(2,1)S(1)} all-gather(bf16[448,128]{1,0:T(8,128)(2,1)} %param.7), channel_id=1, replica_groups=mesh['y'=4,'zl'=8,'zh'=2,'x'=4,'c'=2] {'x','c'}, dimensions={1}, use_global_device_ids=true | all-gather | bytes 1032192 | tf_op jit(solution)/shard_map/all_gather | solution.py:53
  34.6 3.1 %collective-permute-start.3 = (bf16[448,256]{1,0:T(8,128)(2,1)S(1)}, bf16[448,256]{1,0:T(8,128)(2,1)S(1)}, u32[]{:S(2)}, u32[]{:S(2)}) collective-permute-start(bf16[448,256]{1,0:T(8,128)(2,1)S(1)} %fusion.7), channel_id=1, source_target_pairs={{16,0},{32,16},{48,32},{64,48},{80,64},{96,80},{112,96},{8,24},{24... | collective-permute-start | bytes 688136 | tf_op jit(solution)/shard_map/ppermute | solution.py:18
  37.8 13.9 %all_gather.7 = bf16[448,1024]{1,0:T(8,128)(2,1)S(1)} all-gather(bf16[448,128]{1,0:T(8,128)(2,1)S(1)} %slice_select_fusion), channel_id=1, replica_groups=mesh['y'=4,'zl'=8,'zh'=2,'x'=4,'c'=2] {'x','c'}, dimensions={1}, use_global_device_ids=true | all-gather | bytes 1032192 | tf_op jit(solution)/shard_map/all_gather | solution.py:57
  52.2 3.2 %collective-permute-start.4 = (bf16[448,256]{1,0:T(8,128)(2,1)S(1)}, bf16[448,256]{1,0:T(8,128)(2,1)S(1)}, u32[]{:S(2)}, u32[]{:S(2)}) collective-permute-start(bf16[448,256]{1,0:T(8,128)(2,1)S(1)} %fusion.8), channel_id=1, source_target_pairs={{0,16},{16,32},{32,48},{48,64},{64,80},{80,96},{96,112},{24,8},{40... | collective-permute-start | bytes 688136 | tf_op jit(solution)/shard_map/ppermute | solution.py:18
  56.2 3.9 %collective-permute-start.5 = (bf16[448,256]{1,0:T(8,128)(2,1)S(1)}, bf16[448,256]{1,0:T(8,128)(2,1)S(1)}, u32[]{:S(2)}, u32[]{:S(2)}) collective-permute-start(bf16[448,256]{1,0:T(8,128)(2,1)S(1)} %fusion.9), channel_id=1, source_target_pairs={{16,0},{32,16},{48,32},{64,48},{80,64},{96,80},{112,96},{8,24},{24... | collective-permute-start | bytes 688136 | tf_op jit(solution)/shard_map/ppermute | solution.py:18
  60.1 3.1 %collective-permute-done.4 = bf16[448,256]{1,0:T(8,128)(2,1)S(1)} collective-permute-done((bf16[448,256]{1,0:T(8,128)(2,1)S(1)}, bf16[448,256]{1,0:T(8,128)(2,1)S(1)}, u32[]{:S(2)}, u32[]{:S(2)}) %collective-permute-start.4) | collective-permute-done | bytes 229408 | tf_op jit(solution)/shard_map/ppermute | solution.py:18
  63.3 2.0 %collective-permute-start.6 = (bf16[448,256]{1,0:T(8,128)(2,1)S(1)}, bf16[448,256]{1,0:T(8,128)(2,1)S(1)}, u32[]{:S(2)}, u32[]{:S(2)}) collective-permute-start(bf16[448,256]{1,0:T(8,128)(2,1)S(1)} %fusion.10), channel_id=1, source_target_pairs={{0,16},{16,32},{32,48},{48,64},{64,80},{80,96},{96,112},{24,8},{40... | collective-permute-start | bytes 688136 | tf_op jit(solution)/shard_map/ppermute | solution.py:18
  66.1 5.1 %collective-permute-start.7 = (bf16[448,256]{1,0:T(8,128)(2,1)S(1)}, bf16[448,256]{1,0:T(8,128)(2,1)S(1)}, u32[]{:S(2)}, u32[]{:S(2)}) collective-permute-start(bf16[448,256]{1,0:T(8,128)(2,1)S(1)} %fusion.11), channel_id=1, source_target_pairs={{16,0},{32,16},{48,32},{64,48},{80,64},{96,80},{112,96},{8,24},{24... | collective-permute-start | bytes 688136 | tf_op jit(solution)/shard_map/ppermute | solution.py:18
  71.2 2.3 %collective-permute-done.6 = bf16[448,256]{1,0:T(8,128)(2,1)S(1)} collective-permute-done((bf16[448,256]{1,0:T(8,128)(2,1)S(1)}, bf16[448,256]{1,0:T(8,128)(2,1)S(1)}, u32[]{:S(2)}, u32[]{:S(2)}) %collective-permute-start.6) | collective-permute-done | bytes 229408 | tf_op jit(solution)/shard_map/ppermute | solution.py:18
  73.5 1.9 %collective-permute-start.8 = (bf16[448,256]{1,0:T(8,128)(2,1)S(1)}, bf16[448,256]{1,0:T(8,128)(2,1)S(1)}, u32[]{:S(2)}, u32[]{:S(2)}) collective-permute-start(bf16[448,256]{1,0:T(8,128)(2,1)S(1)} %fusion.12), channel_id=1, source_target_pairs={{0,16},{16,32},{32,48},{48,64},{64,80},{80,96},{96,112},{24,8},{40... | collective-permute-start | bytes 688136 | tf_op jit(solution)/shard_map/ppermute | solution.py:18
  76.0 5.3 %collective-permute-start.9 = (bf16[448,256]{1,0:T(8,128)(2,1)S(1)}, bf16[448,256]{1,0:T(8,128)(2,1)S(1)}, u32[]{:S(2)}, u32[]{:S(2)}) collective-permute-start(bf16[448,256]{1,0:T(8,128)(2,1)S(1)} %fusion.13), channel_id=1, source_target_pairs={{16,0},{32,16},{48,32},{64,48},{80,64},{96,80},{112,96},{8,24},{24... | collective-permute-start | bytes 688136 | tf_op jit(solution)/shard_map/ppermute | solution.py:18
  81.3 1.5 %collective-permute-done.8 = bf16[448,256]{1,0:T(8,128)(2,1)S(1)} collective-permute-done((bf16[448,256]{1,0:T(8,128)(2,1)S(1)}, bf16[448,256]{1,0:T(8,128)(2,1)S(1)}, u32[]{:S(2)}, u32[]{:S(2)}) %collective-permute-start.8) | collective-permute-done | bytes 229408 | tf_op jit(solution)/shard_map/ppermute | solution.py:18
  82.9 1.9 %collective-permute-start.10 = (bf16[448,256]{1,0:T(8,128)(2,1)S(1)}, bf16[448,256]{1,0:T(8,128)(2,1)S(1)}, u32[]{:S(2)}, u32[]{:S(2)}) collective-permute-start(bf16[448,256]{1,0:T(8,128)(2,1)S(1)} %fusion.14), channel_id=1, source_target_pairs={{0,16},{16,32},{32,48},{48,64},{64,80},{80,96},{96,112},{24,8},{40... | collective-permute-start | bytes 688136 | tf_op jit(solution)/shard_map/ppermute | solution.py:18
  85.9 5.1 %collective-permute-start.11 = (bf16[448,256]{1,0:T(8,128)(2,1)S(1)}, bf16[448,256]{1,0:T(8,128)(2,1)S(1)}, u32[]{:S(2)}, u32[]{:S(2)}) collective-permute-start(bf16[448,256]{1,0:T(8,128)(2,1)S(1)} %fusion.15), channel_id=1, source_target_pairs={{16,0},{32,16},{48,32},{64,48},{80,64},{96,80},{112,96},{8,24},{24... | collective-permute-start | bytes 688136 | tf_op jit(solution)/shard_map/ppermute | solution.py:18
  91.1 0.9 collective-permute-done.10
  92.1 1.9 %collective-permute-start.12 = (bf16[448,256]{1,0:T(8,128)(2,1)S(1)}, bf16[448,256]{1,0:T(8,128)(2,1)S(1)}, u32[]{:S(2)}, u32[]{:S(2)}) collective-permute-start(bf16[448,256]{1,0:T(8,128)(2,1)S(1)} %fusion.16), channel_id=1, source_target_pairs={{0,16},{16,32},{32,48},{48,64},{64,80},{80,96},{96,112},{24,8},{40... | collective-permute-start | bytes 688136 | tf_op jit(solution)/shard_map/ppermute | solution.py:18
  94.8 5.5 %collective-permute-start.13 = (bf16[448,256]{1,0:T(8,128)(2,1)S(1)}, bf16[448,256]{1,0:T(8,128)(2,1)S(1)}, u32[]{:S(2)}, u32[]{:S(2)}) collective-permute-start(bf16[448,256]{1,0:T(8,128)(2,1)S(1)} %fusion.17), channel_id=1, source_target_pairs={{16,0},{32,16},{48,32},{64,48},{80,64},{96,80},{112,96},{8,24},{24... | collective-permute-start | bytes 688136 | tf_op jit(solution)/shard_map/ppermute | solution.py:18
  100.3 0.9 collective-permute-done.12
  101.3 1.9 %collective-permute-start.15 = (bf16[448,256]{1,0:T(8,128)(2,1)S(1)}, bf16[448,256]{1,0:T(8,128)(2,1)S(1)}, u32[]{:S(2)}, u32[]{:S(2)}) collective-permute-start(bf16[448,256]{1,0:T(8,128)(2,1)S(1)} %fusion.18), channel_id=1, source_target_pairs={{0,16},{16,32},{32,48},{48,64},{64,80},{80,96},{96,112},{24,8},{40... | collective-permute-start | bytes 688136 | tf_op jit(solution)/shard_map/ppermute | solution.py:18
  104.0 5.5 %collective-permute-start.14 = (bf16[448,256]{1,0:T(8,128)(2,1)S(1)}, bf16[448,256]{1,0:T(8,128)(2,1)S(1)}, u32[]{:S(2)}, u32[]{:S(2)}) collective-permute-start(bf16[448,256]{1,0:T(8,128)(2,1)S(1)} %fusion.19), channel_id=1, source_target_pairs={{16,0},{32,16},{48,32},{64,48},{80,64},{96,80},{112,96},{8,24},{24... | collective-permute-start | bytes 688136 | tf_op jit(solution)/shard_map/ppermute | solution.py:18
  109.5 0.9 collective-permute-done.15
  110.6 1.9 %collective-permute-start.16 = (bf16[448,256]{1,0:T(8,128)(2,1)S(1)}, bf16[448,256]{1,0:T(8,128)(2,1)S(1)}, u32[]{:S(2)}, u32[]{:S(2)}) collective-permute-start(bf16[448,256]{1,0:T(8,128)(2,1)S(1)} %fusion.20), channel_id=1, source_target_pairs={{0,16},{16,32},{32,48},{48,64},{64,80},{80,96},{96,112},{24,8},{40... | collective-permute-start | bytes 688136 | tf_op jit(solution)/shard_map/ppermute | solution.py:18
  113.1 1.2 fusion.6
  114.4 5.3 %collective-permute-done.16 = bf16[448,256]{1,0:T(8,128)(2,1)S(1)} collective-permute-done((bf16[448,256]{1,0:T(8,128)(2,1)S(1)}, bf16[448,256]{1,0:T(8,128)(2,1)S(1)}, u32[]{:S(2)}, u32[]{:S(2)}) %collective-permute-start.16) | collective-permute-done | bytes 229408 | tf_op jit(solution)/shard_map/ppermute | solution.py:18
  119.9 3.5 %collective-permute-start.17 = (bf16[224,256]{1,0:T(8,128)(2,1)S(1)}, bf16[224,256]{1,0:T(8,128)(2,1)S(1)}, u32[]{:S(2)}, u32[]{:S(2)}) collective-permute-start(bf16[224,256]{1,0:T(8,128)(2,1)S(1)} %fusion.23), channel_id=1, source_target_pairs={{0,128},{128,256},{256,384},{384,0},{1,129},{129,257},{257,385},{3... | collective-permute-start | bytes 344072 | tf_op jit(solution)/shard_map/ppermute | solution.py:115
  123.7 2.8 %collective-permute-start.18 = (bf16[224,256]{1,0:T(8,128)(2,1)S(1)}, bf16[224,256]{1,0:T(8,128)(2,1)S(1)}, u32[]{:S(2)}, u32[]{:S(2)}) collective-permute-start(bf16[224,256]{1,0:T(8,128)(2,1)S(1)} %fusion.26), channel_id=1, source_target_pairs={{0,256},{128,384},{256,0},{384,128},{1,257},{129,385},{257,1},{385... | collective-permute-start | bytes 344072 | tf_op jit(solution)/shard_map/ppermute | solution.py:117
  126.6 1.1 multiply_add_fusion
  127.7 4.2 %collective-permute-done.18 = bf16[224,256]{1,0:T(8,128)(2,1)S(1)} collective-permute-done((bf16[224,256]{1,0:T(8,128)(2,1)S(1)}, bf16[224,256]{1,0:T(8,128)(2,1)S(1)}, u32[]{:S(2)}, u32[]{:S(2)}) %collective-permute-start.18) | collective-permute-done | bytes 114720 | tf_op jit(solution)/shard_map/ppermute | solution.py:117
  132.0 0.7 pad_maximum_fusion
  (55 shorter events, 7.6 us)
Async XLA Ops:
  0.6 32.5 %copy-start = (bf16[448,448]{1,0:T(8,128)(2,1)S(1)}, bf16[448,448]{1,0:T(8,128)(2,1)}, u32[]{:S(2)}) copy-start(bf16[448,448]{1,0:T(8,128)(2,1)} %param.6) | copy-start | bytes 1204228
  0.6 33.8 %collective-permute-start.1 = (bf16[448,256]{1,0:T(8,128)(2,1)}, bf16[448,256]{1,0:T(8,128)(2,1)S(1)}, u32[]{:S(2)}, u32[]{:S(2)}) collective-permute-start(bf16[448,256]{1,0:T(8,128)(2,1)} %param.8), channel_id=1, source_target_pairs={{16,0},{32,16},{48,32},{64,48},{80,64},{96,80},{112,96},{8,24},{24... | collective-permute-start | bytes 688136 | tf_op jit(solution)/shard_map/ppermute | solution.py:18
  2.8 31.7 %collective-permute-start = (bf16[448,256]{1,0:T(8,128)(2,1)}, bf16[448,256]{1,0:T(8,128)(2,1)S(1)}, u32[]{:S(2)}, u32[]{:S(2)}) collective-permute-start(bf16[448,256]{1,0:T(8,128)(2,1)} %param.8), channel_id=1, source_target_pairs={{0,16},{16,32},{32,48},{48,64},{64,80},{80,96},{96,112},{24,8},{40... | collective-permute-start | bytes 688136 | tf_op jit(solution)/shard_map/ppermute | solution.py:18
  6.6 31.1 %collective-permute-start.2 = (bf16[448,128]{1,0:T(8,128)(2,1)}, bf16[448,128]{1,0:T(8,128)(2,1)S(1)}, u32[]{:S(2)}, u32[]{:S(2)}) collective-permute-start(bf16[448,128]{1,0:T(8,128)(2,1)} %param.7), channel_id=1, source_target_pairs={{0,8},{8,0},{1,9},{9,1},{2,10},{10,2},{3,11},{11,3},{4,12},{12,4},... | collective-permute-start | bytes 344072 | tf_op jit(solution)/shard_map/ppermute | solution.py:37
  34.6 21.5 %collective-permute-start.3 = (bf16[448,256]{1,0:T(8,128)(2,1)S(1)}, bf16[448,256]{1,0:T(8,128)(2,1)S(1)}, u32[]{:S(2)}, u32[]{:S(2)}) collective-permute-start(bf16[448,256]{1,0:T(8,128)(2,1)S(1)} %fusion.7), channel_id=1, source_target_pairs={{16,0},{32,16},{48,32},{64,48},{80,64},{96,80},{112,96},{8,24},{24... | collective-permute-start | bytes 688136 | tf_op jit(solution)/shard_map/ppermute | solution.py:18
  52.2 11.0 %collective-permute-start.4 = (bf16[448,256]{1,0:T(8,128)(2,1)S(1)}, bf16[448,256]{1,0:T(8,128)(2,1)S(1)}, u32[]{:S(2)}, u32[]{:S(2)}) collective-permute-start(bf16[448,256]{1,0:T(8,128)(2,1)S(1)} %fusion.8), channel_id=1, source_target_pairs={{0,16},{16,32},{32,48},{48,64},{64,80},{80,96},{96,112},{24,8},{40... | collective-permute-start | bytes 688136 | tf_op jit(solution)/shard_map/ppermute | solution.py:18
  56.2 9.7 %collective-permute-start.5 = (bf16[448,256]{1,0:T(8,128)(2,1)S(1)}, bf16[448,256]{1,0:T(8,128)(2,1)S(1)}, u32[]{:S(2)}, u32[]{:S(2)}) collective-permute-start(bf16[448,256]{1,0:T(8,128)(2,1)S(1)} %fusion.9), channel_id=1, source_target_pairs={{16,0},{32,16},{48,32},{64,48},{80,64},{96,80},{112,96},{8,24},{24... | collective-permute-start | bytes 688136 | tf_op jit(solution)/shard_map/ppermute | solution.py:18
  63.3 10.2 %collective-permute-start.6 = (bf16[448,256]{1,0:T(8,128)(2,1)S(1)}, bf16[448,256]{1,0:T(8,128)(2,1)S(1)}, u32[]{:S(2)}, u32[]{:S(2)}) collective-permute-start(bf16[448,256]{1,0:T(8,128)(2,1)S(1)} %fusion.10), channel_id=1, source_target_pairs={{0,16},{16,32},{32,48},{48,64},{64,80},{80,96},{96,112},{24,8},{40... | collective-permute-start | bytes 688136 | tf_op jit(solution)/shard_map/ppermute | solution.py:18
  66.1 9.7 %collective-permute-start.7 = (bf16[448,256]{1,0:T(8,128)(2,1)S(1)}, bf16[448,256]{1,0:T(8,128)(2,1)S(1)}, u32[]{:S(2)}, u32[]{:S(2)}) collective-permute-start(bf16[448,256]{1,0:T(8,128)(2,1)S(1)} %fusion.11), channel_id=1, source_target_pairs={{16,0},{32,16},{48,32},{64,48},{80,64},{96,80},{112,96},{8,24},{24... | collective-permute-start | bytes 688136 | tf_op jit(solution)/shard_map/ppermute | solution.py:18
  73.5 9.2 %collective-permute-start.8 = (bf16[448,256]{1,0:T(8,128)(2,1)S(1)}, bf16[448,256]{1,0:T(8,128)(2,1)S(1)}, u32[]{:S(2)}, u32[]{:S(2)}) collective-permute-start(bf16[448,256]{1,0:T(8,128)(2,1)S(1)} %fusion.12), channel_id=1, source_target_pairs={{0,16},{16,32},{32,48},{48,64},{64,80},{80,96},{96,112},{24,8},{40... | collective-permute-start | bytes 688136 | tf_op jit(solution)/shard_map/ppermute | solution.py:18
  75.9 9.5 %copy-start.3 = (bf16[448,256]{1,0:T(8,128)(2,1)S(1)}, bf16[448,256]{1,0:T(8,128)(2,1)}, u32[]{:S(2)}) copy-start(bf16[448,256]{1,0:T(8,128)(2,1)} %param.8) | copy-start | bytes 688132
  76.0 9.9 %collective-permute-start.9 = (bf16[448,256]{1,0:T(8,128)(2,1)S(1)}, bf16[448,256]{1,0:T(8,128)(2,1)S(1)}, u32[]{:S(2)}, u32[]{:S(2)}) collective-permute-start(bf16[448,256]{1,0:T(8,128)(2,1)S(1)} %fusion.13), channel_id=1, source_target_pairs={{16,0},{32,16},{48,32},{64,48},{80,64},{96,80},{112,96},{8,24},{24... | collective-permute-start | bytes 688136 | tf_op jit(solution)/shard_map/ppermute | solution.py:18
  82.9 9.1 %collective-permute-start.10 = (bf16[448,256]{1,0:T(8,128)(2,1)S(1)}, bf16[448,256]{1,0:T(8,128)(2,1)S(1)}, u32[]{:S(2)}, u32[]{:S(2)}) collective-permute-start(bf16[448,256]{1,0:T(8,128)(2,1)S(1)} %fusion.14), channel_id=1, source_target_pairs={{0,16},{16,32},{32,48},{48,64},{64,80},{80,96},{96,112},{24,8},{40... | collective-permute-start | bytes 688136 | tf_op jit(solution)/shard_map/ppermute | solution.py:18
  85.9 8.8 %collective-permute-start.11 = (bf16[448,256]{1,0:T(8,128)(2,1)S(1)}, bf16[448,256]{1,0:T(8,128)(2,1)S(1)}, u32[]{:S(2)}, u32[]{:S(2)}) collective-permute-start(bf16[448,256]{1,0:T(8,128)(2,1)S(1)} %fusion.15), channel_id=1, source_target_pairs={{16,0},{32,16},{48,32},{64,48},{80,64},{96,80},{112,96},{8,24},{24... | collective-permute-start | bytes 688136 | tf_op jit(solution)/shard_map/ppermute | solution.py:18
  92.1 9.1 %collective-permute-start.12 = (bf16[448,256]{1,0:T(8,128)(2,1)S(1)}, bf16[448,256]{1,0:T(8,128)(2,1)S(1)}, u32[]{:S(2)}, u32[]{:S(2)}) collective-permute-start(bf16[448,256]{1,0:T(8,128)(2,1)S(1)} %fusion.16), channel_id=1, source_target_pairs={{0,16},{16,32},{32,48},{48,64},{64,80},{80,96},{96,112},{24,8},{40... | collective-permute-start | bytes 688136 | tf_op jit(solution)/shard_map/ppermute | solution.py:18
  94.8 9.1 %collective-permute-start.13 = (bf16[448,256]{1,0:T(8,128)(2,1)S(1)}, bf16[448,256]{1,0:T(8,128)(2,1)S(1)}, u32[]{:S(2)}, u32[]{:S(2)}) collective-permute-start(bf16[448,256]{1,0:T(8,128)(2,1)S(1)} %fusion.17), channel_id=1, source_target_pairs={{16,0},{32,16},{48,32},{64,48},{80,64},{96,80},{112,96},{8,24},{24... | collective-permute-start | bytes 688136 | tf_op jit(solution)/shard_map/ppermute | solution.py:18
  101.3 9.1 %collective-permute-start.15 = (bf16[448,256]{1,0:T(8,128)(2,1)S(1)}, bf16[448,256]{1,0:T(8,128)(2,1)S(1)}, u32[]{:S(2)}, u32[]{:S(2)}) collective-permute-start(bf16[448,256]{1,0:T(8,128)(2,1)S(1)} %fusion.18), channel_id=1, source_target_pairs={{0,16},{16,32},{32,48},{48,64},{64,80},{80,96},{96,112},{24,8},{40... | collective-permute-start | bytes 688136 | tf_op jit(solution)/shard_map/ppermute | solution.py:18
  104.0 15.7 %collective-permute-start.14 = (bf16[448,256]{1,0:T(8,128)(2,1)S(1)}, bf16[448,256]{1,0:T(8,128)(2,1)S(1)}, u32[]{:S(2)}, u32[]{:S(2)}) collective-permute-start(bf16[448,256]{1,0:T(8,128)(2,1)S(1)} %fusion.19), channel_id=1, source_target_pairs={{16,0},{32,16},{48,32},{64,48},{80,64},{96,80},{112,96},{8,24},{24... | collective-permute-start | bytes 688136 | tf_op jit(solution)/shard_map/ppermute | solution.py:18
  110.6 9.1 %collective-permute-start.16 = (bf16[448,256]{1,0:T(8,128)(2,1)S(1)}, bf16[448,256]{1,0:T(8,128)(2,1)S(1)}, u32[]{:S(2)}, u32[]{:S(2)}) collective-permute-start(bf16[448,256]{1,0:T(8,128)(2,1)S(1)} %fusion.20), channel_id=1, source_target_pairs={{0,16},{16,32},{32,48},{48,64},{64,80},{80,96},{96,112},{24,8},{40... | collective-permute-start | bytes 688136 | tf_op jit(solution)/shard_map/ppermute | solution.py:18
  113.1 6.6 %copy-start.1 = (f32[448,256]{1,0:T(8,128)S(1)}, f32[448,256]{1,0:T(8,128)}, u32[]{:S(2)}) copy-start(f32[448,256]{1,0:T(8,128)} %param.10) | copy-start | bytes 1376260
  113.1 6.6 %copy-start.2 = (f32[448,256]{1,0:T(8,128)S(1)}, f32[448,256]{1,0:T(8,128)}, u32[]{:S(2)}) copy-start(f32[448,256]{1,0:T(8,128)} %param.9) | copy-start | bytes 1376260
  119.9 11.9 %collective-permute-start.17 = (bf16[224,256]{1,0:T(8,128)(2,1)S(1)}, bf16[224,256]{1,0:T(8,128)(2,1)S(1)}, u32[]{:S(2)}, u32[]{:S(2)}) collective-permute-start(bf16[224,256]{1,0:T(8,128)(2,1)S(1)} %fusion.23), channel_id=1, source_target_pairs={{0,128},{128,256},{256,384},{384,0},{1,129},{129,257},{257,385},{3... | collective-permute-start | bytes 344072 | tf_op jit(solution)/shard_map/ppermute | solution.py:115
  123.7 8.2 %collective-permute-start.18 = (bf16[224,256]{1,0:T(8,128)(2,1)S(1)}, bf16[224,256]{1,0:T(8,128)(2,1)S(1)}, u32[]{:S(2)}, u32[]{:S(2)}) collective-permute-start(bf16[224,256]{1,0:T(8,128)(2,1)S(1)} %fusion.26), channel_id=1, source_target_pairs={{0,256},{128,384},{256,0},{384,128},{1,257},{129,385},{257,1},{385... | collective-permute-start | bytes 344072 | tf_op jit(solution)/shard_map/ppermute | solution.py:117

commit v12 on v11

--- a/solution.py
+++ b/solution.py
@@ -51,9 +51,8 @@
         return lax.optimization_barrier(contract(hidden_t, features, ((1,), (0,))))
 
     near_up = lax.all_gather(upstream, ("x", "c"), axis=1, tiled=True)
-    first = lax.dynamic_slice_in_dim(near_up, jnp.where(early_up, 3, 0) * width, width, 1)
-    send(True, 0, product(first))
-    up_other = behind(up_other, sent[True, 0][:, : up_other.shape[1]])
+    for early in (True, False):
+        up_other = behind(up_other, got[early][0][:, : up_other.shape[1]])
     far_up = lax.all_gather(up_other, ("x", "c"), axis=1, tiled=True)
     full_up = jnp.concatenate([near_up, far_up], axis=1)
 
@@ -73,6 +72,7 @@
             parts[pair] = product(features if after is None else behind(features, sent[after]))
         return parts[pair]
 
+    send(True, 0, part_of(0, None))
     hg_total = contract(behind(up_block(place), sent[True, 0]), weights, ((1,), (1,)))
     for turn in range(last):
         send(False, turn, part_of(last - 1 - turn, (False, turn - 1) if 0 < turn < last - 1 else (False, 3) if turn else None))

time: 133 us -> 134 us (level)
  the two profiles are of different devices: /device:TPU:136 before, /device:TPU:128 now
where the time goes in v12:
time: 134 us; the launch traced here: 133 us
  starting transfers between devices  75.8 us (57%)
  blocking collectives  28.9 us (22%)
  waiting for transfers between devices  16.5 us (12%)
  matrix products  6.25 us (5%)
  other arithmetic  3.76 us (3%)
  between operations  1.85 us (1%)
    ppermute x16, starting transfers between devices, along(): return lax.ppermute(value, ('zl', 'zh'), pairs)  55.4 us
    all_gather x1, blocking collectives, body(): far_up = lax.all_gather(up_other, ('x', 'c'), axis=1, tiled=True)  14.5 us
    all_gather x1, blocking collectives, body(): near_up = lax.all_gather(upstream, ('x', 'c'), axis=1, tiled=True)  14.4 us
    ppermute x16, waiting for transfers between devices, along(): return lax.ppermute(value, ('zl', 'zh'), pairs)  14.2 us
    ppermute x1, starting transfers between devices, body(): up_other = lax.ppermute(upstream, 'zh', [(0, 1), (1, 0)])  12.1 us
    dot_general x16, matrix products, contract(): lax.dot_general(left, right, (dims, ((), ())), preferred_element_type=F32)  6.25 us
    ppermute x1, starting transfers between devices, body(): far = lax.ppermute(far_rows, 'y', [(i, (i + 2) % 4) for i in range(4)])  4.81 us
    ppermute x1, starting transfers between devices, body(): near = lax.ppermute(near_rows, 'y', [(i, (i + 1) % 4) for i in range(4)])  3.48 us
  transfers between devices with their start and end apart: 19, of which 9 were waited for; matrix products, arithmetic and copies ran while one was open for 6% of the time, Pallas kernels for 0%

profile of v12, /device:TPU:128, one launch (start us, length us, event | category | flops | bytes accessed | tf_op | source)
XLA Modules:
  0.0 133.2 jit_solution(10666048553580795754)
XLA Ops:
  0.6 2.2 %collective-permute-start.1 = (bf16[448,256]{1,0:T(8,128)(2,1)}, bf16[448,256]{1,0:T(8,128)(2,1)S(1)}, u32[]{:S(2)}, u32[]{:S(2)}) collective-permute-start(bf16[448,256]{1,0:T(8,128)(2,1)} %param.8), channel_id=1, source_target_pairs={{16,0},{32,16},{48,32},{64,48},{80,64},{96,80},{112,96},{8,24},{24... | collective-permute-start | bytes 688136 | tf_op jit(solution)/shard_map/ppermute | solution.py:18
  2.8 3.8 %collective-permute-start = (bf16[448,256]{1,0:T(8,128)(2,1)}, bf16[448,256]{1,0:T(8,128)(2,1)S(1)}, u32[]{:S(2)}, u32[]{:S(2)}) collective-permute-start(bf16[448,256]{1,0:T(8,128)(2,1)} %param.8), channel_id=1, source_target_pairs={{0,16},{16,32},{32,48},{48,64},{64,80},{80,96},{96,112},{24,8},{40... | collective-permute-start | bytes 688136 | tf_op jit(solution)/shard_map/ppermute | solution.py:18
  6.6 12.1 %collective-permute-start.2 = (bf16[448,128]{1,0:T(8,128)(2,1)}, bf16[448,128]{1,0:T(8,128)(2,1)S(1)}, u32[]{:S(2)}, u32[]{:S(2)}) collective-permute-start(bf16[448,128]{1,0:T(8,128)(2,1)} %param.7), channel_id=1, source_target_pairs={{0,8},{8,0},{1,9},{9,1},{2,10},{10,2},{3,11},{11,3},{4,12},{12,4},... | collective-permute-start | bytes 344072 | tf_op jit(solution)/shard_map/ppermute | solution.py:37
  18.8 14.4 %all_gather.6 = bf16[448,1024]{1,0:T(8,128)(2,1)S(1)} all-gather(bf16[448,128]{1,0:T(8,128)(2,1)} %param.7), channel_id=1, replica_groups=mesh['y'=4,'zl'=8,'zh'=2,'x'=4,'c'=2] {'x','c'}, dimensions={1}, use_global_device_ids=true | all-gather | bytes 1032192 | tf_op jit(solution)/shard_map/all_gather | solution.py:53
  34.1 14.5 %all_gather.7 = bf16[448,1024]{1,0:T(8,128)(2,1)S(1)} all-gather(bf16[448,128]{1,0:T(8,128)(2,1)S(1)} %fusion.77), channel_id=1, replica_groups=mesh['y'=4,'zl'=8,'zh'=2,'x'=4,'c'=2] {'x','c'}, dimensions={1}, use_global_device_ids=true | all-gather | bytes 1032192 | tf_op jit(solution)/shard_map/all_gather | solution.py:56
  49.5 3.0 %collective-permute-start.3 = (bf16[448,256]{1,0:T(8,128)(2,1)S(1)}, bf16[448,256]{1,0:T(8,128)(2,1)S(1)}, u32[]{:S(2)}, u32[]{:S(2)}) collective-permute-start(bf16[448,256]{1,0:T(8,128)(2,1)S(1)} %fusion.7), channel_id=1, source_target_pairs={{16,0},{32,16},{48,32},{64,48},{80,64},{96,80},{112,96},{8,24},{24... | collective-permute-start | bytes 688136 | tf_op jit(solution)/shard_map/ppermute | solution.py:18
  52.6 2.8 %collective-permute-start.4 = (bf16[448,256]{1,0:T(8,128)(2,1)S(1)}, bf16[448,256]{1,0:T(8,128)(2,1)S(1)}, u32[]{:S(2)}, u32[]{:S(2)}) collective-permute-start(bf16[448,256]{1,0:T(8,128)(2,1)S(1)} %fusion.8), channel_id=1, source_target_pairs={{0,16},{16,32},{32,48},{48,64},{64,80},{80,96},{96,112},{24,8},{40... | collective-permute-start | bytes 688136 | tf_op jit(solution)/shard_map/ppermute | solution.py:18
  56.1 3.1 %collective-permute-done.3 = bf16[448,256]{1,0:T(8,128)(2,1)S(1)} collective-permute-done((bf16[448,256]{1,0:T(8,128)(2,1)S(1)}, bf16[448,256]{1,0:T(8,128)(2,1)S(1)}, u32[]{:S(2)}, u32[]{:S(2)}) %collective-permute-start.3) | collective-permute-done | bytes 229408 | tf_op jit(solution)/shard_map/ppermute | solution.py:18
  59.3 4.2 %collective-permute-start.5 = (bf16[448,256]{1,0:T(8,128)(2,1)S(1)}, bf16[448,256]{1,0:T(8,128)(2,1)S(1)}, u32[]{:S(2)}, u32[]{:S(2)}) collective-permute-start(bf16[448,256]{1,0:T(8,128)(2,1)S(1)} %fusion.9), channel_id=1, source_target_pairs={{16,0},{32,16},{48,32},{64,48},{80,64},{96,80},{112,96},{8,24},{24... | collective-permute-start | bytes 688136 | tf_op jit(solution)/shard_map/ppermute | solution.py:18
  63.6 1.9 %collective-permute-start.6 = (bf16[448,256]{1,0:T(8,128)(2,1)S(1)}, bf16[448,256]{1,0:T(8,128)(2,1)S(1)}, u32[]{:S(2)}, u32[]{:S(2)}) collective-permute-start(bf16[448,256]{1,0:T(8,128)(2,1)S(1)} %fusion.10), channel_id=1, source_target_pairs={{0,16},{16,32},{32,48},{48,64},{64,80},{80,96},{96,112},{24,8},{40... | collective-permute-start | bytes 688136 | tf_op jit(solution)/shard_map/ppermute | solution.py:18
  66.3 2.0 %collective-permute-done.5 = bf16[448,256]{1,0:T(8,128)(2,1)S(1)} collective-permute-done((bf16[448,256]{1,0:T(8,128)(2,1)S(1)}, bf16[448,256]{1,0:T(8,128)(2,1)S(1)}, u32[]{:S(2)}, u32[]{:S(2)}) %collective-permute-start.5) | collective-permute-done | bytes 229408 | tf_op jit(solution)/shard_map/ppermute | solution.py:18
  68.3 5.4 %collective-permute-start.7 = (bf16[448,256]{1,0:T(8,128)(2,1)S(1)}, bf16[448,256]{1,0:T(8,128)(2,1)S(1)}, u32[]{:S(2)}, u32[]{:S(2)}) collective-permute-start(bf16[448,256]{1,0:T(8,128)(2,1)S(1)} %fusion.11), channel_id=1, source_target_pairs={{16,0},{32,16},{48,32},{64,48},{80,64},{96,80},{112,96},{8,24},{24... | collective-permute-start | bytes 688136 | tf_op jit(solution)/shard_map/ppermute | solution.py:18
  73.9 1.9 %collective-permute-start.8 = (bf16[448,256]{1,0:T(8,128)(2,1)S(1)}, bf16[448,256]{1,0:T(8,128)(2,1)S(1)}, u32[]{:S(2)}, u32[]{:S(2)}) collective-permute-start(bf16[448,256]{1,0:T(8,128)(2,1)S(1)} %fusion.12), channel_id=1, source_target_pairs={{0,16},{16,32},{32,48},{48,64},{64,80},{80,96},{96,112},{24,8},{40... | collective-permute-start | bytes 688136 | tf_op jit(solution)/shard_map/ppermute | solution.py:18
  76.2 1.2 collective-permute-done.7
  77.5 5.6 %collective-permute-start.9 = (bf16[448,256]{1,0:T(8,128)(2,1)S(1)}, bf16[448,256]{1,0:T(8,128)(2,1)S(1)}, u32[]{:S(2)}, u32[]{:S(2)}) collective-permute-start(bf16[448,256]{1,0:T(8,128)(2,1)S(1)} %fusion.13), channel_id=1, source_target_pairs={{16,0},{32,16},{48,32},{64,48},{80,64},{96,80},{112,96},{8,24},{24... | collective-permute-start | bytes 688136 | tf_op jit(solution)/shard_map/ppermute | solution.py:18
  83.2 1.9 %collective-permute-start.10 = (bf16[448,256]{1,0:T(8,128)(2,1)S(1)}, bf16[448,256]{1,0:T(8,128)(2,1)S(1)}, u32[]{:S(2)}, u32[]{:S(2)}) collective-permute-start(bf16[448,256]{1,0:T(8,128)(2,1)S(1)} %fusion.14), channel_id=1, source_target_pairs={{0,16},{16,32},{32,48},{48,64},{64,80},{80,96},{96,112},{24,8},{40... | collective-permute-start | bytes 688136 | tf_op jit(solution)/shard_map/ppermute | solution.py:18
  85.8 0.8 collective-permute-done.9
  86.8 5.6 %collective-permute-start.11 = (bf16[448,256]{1,0:T(8,128)(2,1)S(1)}, bf16[448,256]{1,0:T(8,128)(2,1)S(1)}, u32[]{:S(2)}, u32[]{:S(2)}) collective-permute-start(bf16[448,256]{1,0:T(8,128)(2,1)S(1)} %fusion.15), channel_id=1, source_target_pairs={{16,0},{32,16},{48,32},{64,48},{80,64},{96,80},{112,96},{8,24},{24... | collective-permute-start | bytes 688136 | tf_op jit(solution)/shard_map/ppermute | solution.py:18
  92.5 1.9 %collective-permute-start.12 = (bf16[448,256]{1,0:T(8,128)(2,1)S(1)}, bf16[448,256]{1,0:T(8,128)(2,1)S(1)}, u32[]{:S(2)}, u32[]{:S(2)}) collective-permute-start(bf16[448,256]{1,0:T(8,128)(2,1)S(1)} %fusion.16), channel_id=1, source_target_pairs={{0,16},{16,32},{32,48},{48,64},{64,80},{80,96},{96,112},{24,8},{40... | collective-permute-start | bytes 688136 | tf_op jit(solution)/shard_map/ppermute | solution.py:18
  95.1 0.8 collective-permute-done.11
  96.0 5.6 %collective-permute-start.13 = (bf16[448,256]{1,0:T(8,128)(2,1)S(1)}, bf16[448,256]{1,0:T(8,128)(2,1)S(1)}, u32[]{:S(2)}, u32[]{:S(2)}) collective-permute-start(bf16[448,256]{1,0:T(8,128)(2,1)S(1)} %fusion.17), channel_id=1, source_target_pairs={{16,0},{32,16},{48,32},{64,48},{80,64},{96,80},{112,96},{8,24},{24... | collective-permute-start | bytes 688136 | tf_op jit(solution)/shard_map/ppermute | solution.py:18
  101.7 1.9 %collective-permute-start.15 = (bf16[448,256]{1,0:T(8,128)(2,1)S(1)}, bf16[448,256]{1,0:T(8,128)(2,1)S(1)}, u32[]{:S(2)}, u32[]{:S(2)}) collective-permute-start(bf16[448,256]{1,0:T(8,128)(2,1)S(1)} %fusion.18), channel_id=1, source_target_pairs={{0,16},{16,32},{32,48},{48,64},{64,80},{80,96},{96,112},{24,8},{40... | collective-permute-start | bytes 688136 | tf_op jit(solution)/shard_map/ppermute | solution.py:18
  104.3 0.8 collective-permute-done.13
  105.2 5.6 %collective-permute-start.14 = (bf16[448,256]{1,0:T(8,128)(2,1)S(1)}, bf16[448,256]{1,0:T(8,128)(2,1)S(1)}, u32[]{:S(2)}, u32[]{:S(2)}) collective-permute-start(bf16[448,256]{1,0:T(8,128)(2,1)S(1)} %fusion.19), channel_id=1, source_target_pairs={{16,0},{32,16},{48,32},{64,48},{80,64},{96,80},{112,96},{8,24},{24... | collective-permute-start | bytes 688136 | tf_op jit(solution)/shard_map/ppermute | solution.py:18
  111.1 1.9 %collective-permute-start.16 = (bf16[448,256]{1,0:T(8,128)(2,1)S(1)}, bf16[448,256]{1,0:T(8,128)(2,1)S(1)}, u32[]{:S(2)}, u32[]{:S(2)}) collective-permute-start(bf16[448,256]{1,0:T(8,128)(2,1)S(1)} %fusion.20), channel_id=1, source_target_pairs={{0,16},{16,32},{32,48},{48,64},{64,80},{80,96},{96,112},{24,8},{40... | collective-permute-start | bytes 688136 | tf_op jit(solution)/shard_map/ppermute | solution.py:18
  113.7 1.2 fusion.6
  114.9 5.3 %collective-permute-done.16 = bf16[448,256]{1,0:T(8,128)(2,1)S(1)} collective-permute-done((bf16[448,256]{1,0:T(8,128)(2,1)S(1)}, bf16[448,256]{1,0:T(8,128)(2,1)S(1)}, u32[]{:S(2)}, u32[]{:S(2)}) %collective-permute-start.16) | collective-permute-done | bytes 229408 | tf_op jit(solution)/shard_map/ppermute | solution.py:18
  120.5 3.5 %collective-permute-start.17 = (bf16[224,256]{1,0:T(8,128)(2,1)S(1)}, bf16[224,256]{1,0:T(8,128)(2,1)S(1)}, u32[]{:S(2)}, u32[]{:S(2)}) collective-permute-start(bf16[224,256]{1,0:T(8,128)(2,1)S(1)} %fusion.23), channel_id=1, source_target_pairs={{0,128},{128,256},{256,384},{384,0},{1,129},{129,257},{257,385},{3... | collective-permute-start | bytes 344072 | tf_op jit(solution)/shard_map/ppermute | solution.py:115
  124.2 4.8 %collective-permute-start.18 = (bf16[224,256]{1,0:T(8,128)(2,1)S(1)}, bf16[224,256]{1,0:T(8,128)(2,1)S(1)}, u32[]{:S(2)}, u32[]{:S(2)}) collective-permute-start(bf16[224,256]{1,0:T(8,128)(2,1)S(1)} %fusion.26), channel_id=1, source_target_pairs={{0,256},{128,384},{256,0},{384,128},{1,257},{129,385},{257,1},{385... | collective-permute-start | bytes 344072 | tf_op jit(solution)/shard_map/ppermute | solution.py:117
  129.0 1.1 multiply_add_fusion
  130.2 2.3 %collective-permute-done.18 = bf16[224,256]{1,0:T(8,128)(2,1)S(1)} collective-permute-done((bf16[224,256]{1,0:T(8,128)(2,1)S(1)}, bf16[224,256]{1,0:T(8,128)(2,1)S(1)}, u32[]{:S(2)}, u32[]{:S(2)}) %collective-permute-start.18) | collective-permute-done | bytes 114720 | tf_op jit(solution)/shard_map/ppermute | solution.py:117
  132.5 0.7 pad_maximum_fusion
  (54 shorter events, 7.3 us)
Async XLA Ops:
  0.6 33.3 %copy-start = (bf16[448,448]{1,0:T(8,128)(2,1)S(1)}, bf16[448,448]{1,0:T(8,128)(2,1)}, u32[]{:S(2)}) copy-start(bf16[448,448]{1,0:T(8,128)(2,1)} %param.6) | copy-start | bytes 1204228
  0.6 33.4 %collective-permute-start.1 = (bf16[448,256]{1,0:T(8,128)(2,1)}, bf16[448,256]{1,0:T(8,128)(2,1)S(1)}, u32[]{:S(2)}, u32[]{:S(2)}) collective-permute-start(bf16[448,256]{1,0:T(8,128)(2,1)} %param.8), channel_id=1, source_target_pairs={{16,0},{32,16},{48,32},{64,48},{80,64},{96,80},{112,96},{8,24},{24... | collective-permute-start | bytes 688136 | tf_op jit(solution)/shard_map/ppermute | solution.py:18
  2.8 31.2 %collective-permute-start = (bf16[448,256]{1,0:T(8,128)(2,1)}, bf16[448,256]{1,0:T(8,128)(2,1)S(1)}, u32[]{:S(2)}, u32[]{:S(2)}) collective-permute-start(bf16[448,256]{1,0:T(8,128)(2,1)} %param.8), channel_id=1, source_target_pairs={{0,16},{16,32},{32,48},{48,64},{64,80},{80,96},{96,112},{24,8},{40... | collective-permute-start | bytes 688136 | tf_op jit(solution)/shard_map/ppermute | solution.py:18
  6.6 27.4 %collective-permute-start.2 = (bf16[448,128]{1,0:T(8,128)(2,1)}, bf16[448,128]{1,0:T(8,128)(2,1)S(1)}, u32[]{:S(2)}, u32[]{:S(2)}) collective-permute-start(bf16[448,128]{1,0:T(8,128)(2,1)} %param.7), channel_id=1, source_target_pairs={{0,8},{8,0},{1,9},{9,1},{2,10},{10,2},{3,11},{11,3},{4,12},{12,4},... | collective-permute-start | bytes 344072 | tf_op jit(solution)/shard_map/ppermute | solution.py:37
  49.5 9.7 %collective-permute-start.3 = (bf16[448,256]{1,0:T(8,128)(2,1)S(1)}, bf16[448,256]{1,0:T(8,128)(2,1)S(1)}, u32[]{:S(2)}, u32[]{:S(2)}) collective-permute-start(bf16[448,256]{1,0:T(8,128)(2,1)S(1)} %fusion.7), channel_id=1, source_target_pairs={{16,0},{32,16},{48,32},{64,48},{80,64},{96,80},{112,96},{8,24},{24... | collective-permute-start | bytes 688136 | tf_op jit(solution)/shard_map/ppermute | solution.py:18
  52.6 11.0 %collective-permute-start.4 = (bf16[448,256]{1,0:T(8,128)(2,1)S(1)}, bf16[448,256]{1,0:T(8,128)(2,1)S(1)}, u32[]{:S(2)}, u32[]{:S(2)}) collective-permute-start(bf16[448,256]{1,0:T(8,128)(2,1)S(1)} %fusion.8), channel_id=1, source_target_pairs={{0,16},{16,32},{32,48},{48,64},{64,80},{80,96},{96,112},{24,8},{40... | collective-permute-start | bytes 688136 | tf_op jit(solution)/shard_map/ppermute | solution.py:18
  59.3 8.9 %collective-permute-start.5 = (bf16[448,256]{1,0:T(8,128)(2,1)S(1)}, bf16[448,256]{1,0:T(8,128)(2,1)S(1)}, u32[]{:S(2)}, u32[]{:S(2)}) collective-permute-start(bf16[448,256]{1,0:T(8,128)(2,1)S(1)} %fusion.9), channel_id=1, source_target_pairs={{16,0},{32,16},{48,32},{64,48},{80,64},{96,80},{112,96},{8,24},{24... | collective-permute-start | bytes 688136 | tf_op jit(solution)/shard_map/ppermute | solution.py:18
  63.6 10.1 %collective-permute-start.6 = (bf16[448,256]{1,0:T(8,128)(2,1)S(1)}, bf16[448,256]{1,0:T(8,128)(2,1)S(1)}, u32[]{:S(2)}, u32[]{:S(2)}) collective-permute-start(bf16[448,256]{1,0:T(8,128)(2,1)S(1)} %fusion.10), channel_id=1, source_target_pairs={{0,16},{16,32},{32,48},{48,64},{64,80},{80,96},{96,112},{24,8},{40... | collective-permute-start | bytes 688136 | tf_op jit(solution)/shard_map/ppermute | solution.py:18
  68.3 9.1 %collective-permute-start.7 = (bf16[448,256]{1,0:T(8,128)(2,1)S(1)}, bf16[448,256]{1,0:T(8,128)(2,1)S(1)}, u32[]{:S(2)}, u32[]{:S(2)}) collective-permute-start(bf16[448,256]{1,0:T(8,128)(2,1)S(1)} %fusion.11), channel_id=1, source_target_pairs={{16,0},{32,16},{48,32},{64,48},{80,64},{96,80},{112,96},{8,24},{24... | collective-permute-start | bytes 688136 | tf_op jit(solution)/shard_map/ppermute | solution.py:18
  73.9 9.2 %collective-permute-start.8 = (bf16[448,256]{1,0:T(8,128)(2,1)S(1)}, bf16[448,256]{1,0:T(8,128)(2,1)S(1)}, u32[]{:S(2)}, u32[]{:S(2)}) collective-permute-start(bf16[448,256]{1,0:T(8,128)(2,1)S(1)} %fusion.12), channel_id=1, source_target_pairs={{0,16},{16,32},{32,48},{48,64},{64,80},{80,96},{96,112},{24,8},{40... | collective-permute-start | bytes 688136 | tf_op jit(solution)/shard_map/ppermute | solution.py:18
  76.2 9.3 %copy-start.3 = (bf16[448,256]{1,0:T(8,128)(2,1)S(1)}, bf16[448,256]{1,0:T(8,128)(2,1)}, u32[]{:S(2)}) copy-start(bf16[448,256]{1,0:T(8,128)(2,1)} %param.8) | copy-start | bytes 688132
  77.5 9.1 %collective-permute-start.9 = (bf16[448,256]{1,0:T(8,128)(2,1)S(1)}, bf16[448,256]{1,0:T(8,128)(2,1)S(1)}, u32[]{:S(2)}, u32[]{:S(2)}) collective-permute-start(bf16[448,256]{1,0:T(8,128)(2,1)S(1)} %fusion.13), channel_id=1, source_target_pairs={{16,0},{32,16},{48,32},{64,48},{80,64},{96,80},{112,96},{8,24},{24... | collective-permute-start | bytes 688136 | tf_op jit(solution)/shard_map/ppermute | solution.py:18
  83.2 9.1 %collective-permute-start.10 = (bf16[448,256]{1,0:T(8,128)(2,1)S(1)}, bf16[448,256]{1,0:T(8,128)(2,1)S(1)}, u32[]{:S(2)}, u32[]{:S(2)}) collective-permute-start(bf16[448,256]{1,0:T(8,128)(2,1)S(1)} %fusion.14), channel_id=1, source_target_pairs={{0,16},{16,32},{32,48},{48,64},{64,80},{80,96},{96,112},{24,8},{40... | collective-permute-start | bytes 688136 | tf_op jit(solution)/shard_map/ppermute | solution.py:18
  86.8 9.1 %collective-permute-start.11 = (bf16[448,256]{1,0:T(8,128)(2,1)S(1)}, bf16[448,256]{1,0:T(8,128)(2,1)S(1)}, u32[]{:S(2)}, u32[]{:S(2)}) collective-permute-start(bf16[448,256]{1,0:T(8,128)(2,1)S(1)} %fusion.15), channel_id=1, source_target_pairs={{16,0},{32,16},{48,32},{64,48},{80,64},{96,80},{112,96},{8,24},{24... | collective-permute-start | bytes 688136 | tf_op jit(solution)/shard_map/ppermute | solution.py:18
  92.5 9.1 %collective-permute-start.12 = (bf16[448,256]{1,0:T(8,128)(2,1)S(1)}, bf16[448,256]{1,0:T(8,128)(2,1)S(1)}, u32[]{:S(2)}, u32[]{:S(2)}) collective-permute-start(bf16[448,256]{1,0:T(8,128)(2,1)S(1)} %fusion.16), channel_id=1, source_target_pairs={{0,16},{16,32},{32,48},{48,64},{64,80},{80,96},{96,112},{24,8},{40... | collective-permute-start | bytes 688136 | tf_op jit(solution)/shard_map/ppermute | solution.py:18
  96.0 9.1 %collective-permute-start.13 = (bf16[448,256]{1,0:T(8,128)(2,1)S(1)}, bf16[448,256]{1,0:T(8,128)(2,1)S(1)}, u32[]{:S(2)}, u32[]{:S(2)}) collective-permute-start(bf16[448,256]{1,0:T(8,128)(2,1)S(1)} %fusion.17), channel_id=1, source_target_pairs={{16,0},{32,16},{48,32},{64,48},{80,64},{96,80},{112,96},{8,24},{24... | collective-permute-start | bytes 688136 | tf_op jit(solution)/shard_map/ppermute | solution.py:18
  101.7 9.3 %collective-permute-start.15 = (bf16[448,256]{1,0:T(8,128)(2,1)S(1)}, bf16[448,256]{1,0:T(8,128)(2,1)S(1)}, u32[]{:S(2)}, u32[]{:S(2)}) collective-permute-start(bf16[448,256]{1,0:T(8,128)(2,1)S(1)} %fusion.18), channel_id=1, source_target_pairs={{0,16},{16,32},{32,48},{48,64},{64,80},{80,96},{96,112},{24,8},{40... | collective-permute-start | bytes 688136 | tf_op jit(solution)/shard_map/ppermute | solution.py:18
  105.2 15.0 %collective-permute-start.14 = (bf16[448,256]{1,0:T(8,128)(2,1)S(1)}, bf16[448,256]{1,0:T(8,128)(2,1)S(1)}, u32[]{:S(2)}, u32[]{:S(2)}) collective-permute-start(bf16[448,256]{1,0:T(8,128)(2,1)S(1)} %fusion.19), channel_id=1, source_target_pairs={{16,0},{32,16},{48,32},{64,48},{80,64},{96,80},{112,96},{8,24},{24... | collective-permute-start | bytes 688136 | tf_op jit(solution)/shard_map/ppermute | solution.py:18
  111.1 9.1 %collective-permute-start.16 = (bf16[448,256]{1,0:T(8,128)(2,1)S(1)}, bf16[448,256]{1,0:T(8,128)(2,1)S(1)}, u32[]{:S(2)}, u32[]{:S(2)}) collective-permute-start(bf16[448,256]{1,0:T(8,128)(2,1)S(1)} %fusion.20), channel_id=1, source_target_pairs={{0,16},{16,32},{32,48},{48,64},{64,80},{80,96},{96,112},{24,8},{40... | collective-permute-start | bytes 688136 | tf_op jit(solution)/shard_map/ppermute | solution.py:18
  113.6 6.6 %copy-start.1 = (f32[448,256]{1,0:T(8,128)S(1)}, f32[448,256]{1,0:T(8,128)}, u32[]{:S(2)}) copy-start(f32[448,256]{1,0:T(8,128)} %param.10) | copy-start | bytes 1376260
  113.7 6.6 %copy-start.2 = (f32[448,256]{1,0:T(8,128)S(1)}, f32[448,256]{1,0:T(8,128)}, u32[]{:S(2)}) copy-start(f32[448,256]{1,0:T(8,128)} %param.9) | copy-start | bytes 1376260
  120.5 11.9 %collective-permute-start.17 = (bf16[224,256]{1,0:T(8,128)(2,1)S(1)}, bf16[224,256]{1,0:T(8,128)(2,1)S(1)}, u32[]{:S(2)}, u32[]{:S(2)}) collective-permute-start(bf16[224,256]{1,0:T(8,128)(2,1)S(1)} %fusion.23), channel_id=1, source_target_pairs={{0,128},{128,256},{256,384},{384,0},{1,129},{129,257},{257,385},{3... | collective-permute-start | bytes 344072 | tf_op jit(solution)/shard_map/ppermute | solution.py:115
  124.2 8.2 %collective-permute-start.18 = (bf16[224,256]{1,0:T(8,128)(2,1)S(1)}, bf16[224,256]{1,0:T(8,128)(2,1)S(1)}, u32[]{:S(2)}, u32[]{:S(2)}) collective-permute-start(bf16[224,256]{1,0:T(8,128)(2,1)S(1)} %fusion.26), channel_id=1, source_target_pairs={{0,256},{128,384},{256,0},{384,128},{1,257},{129,385},{257,1},{385... | collective-permute-start | bytes 344072 | tf_op jit(solution)/shard_map/ppermute | solution.py:117
